TPU v7x, 32 devices: a whole 2x2x4 slice. The times are simulated.
32 devices in a mesh: dp: 4 (over y, x), rows: 8 (over z, core).
Axes of the slice: x: 2, y: 2, z: 4, core: 2. Of those that a mesh axis runs over, the one named last changes fastest.
Arguments:
- grads: bfloat16 [4, 8, 1024, 1024], P('dp', None, 'rows'), may hold values from -6 to 6
- weight: bfloat16 [8, 1024, 1024], P(None, 'rows'), may hold values from -6 to 6
- basis: float32 [8, 1024, 256], P(None, 'rows'), may hold values from -6 to 6
- first_moment: float32 [32, 256, 1024], P('rows', None, 'dp'), may hold values from -6 to 6
- second_moment: float32 [32, 256, 1024], P('rows', None, 'dp'), may hold values from 0.5 to 4
- sketch: bfloat16 [1024, 256], replicated, may hold values from -6 to 6
- owner: int32 [8], replicated, may hold values from 0 to 7, as said below
- rank: int32 [8], replicated, may hold values from 128 to 256
Outputs:
- new_weight: bfloat16 [8, 1024, 1024], P(None, 'rows')
- new_basis: float32 [8, 1024, 256], P(None, 'rows')
- first_out: float32 [32, 256, 1024], P('rows', None, 'dp')
- second_out: float32 [32, 256, 1024], P('rows', None, 'dp')
Inputs may be any that keep to these rules, and one draw needn't show every extreme that they name: No owner is named by more than 4 matrices, and some owner is named by exactly 4.
All inputs are finite; a program needn't handle non-finite values.
Results may differ from a plain program's by a relative error of at most 0.012.
Values may be sent and summed in bfloat16 or wider, within the bound.
No kernel may reach another device: no remote copies, remote signals or barrier semaphores. Data moves between devices by JAX's collectives and lax.ppermute only.
A program may use at most 128 MiB of HBM per device.

v0:
```python
import jax
import jax.numpy as jnp
from jax import lax
from jax.sharding import PartitionSpec as P

beta_one = 0.9
beta_two = 0.95
bias_one = 1.0 - 0.9**10
bias_two = 1.0 - 0.95**10
step_size = 0.5
epsilon = 1e-08


def slot_of(owner, capacity):
    same = owner[:, None] == owner[None, :]
    places = jnp.arange(owner.shape[0], dtype=jnp.int32)
    earlier = places[None, :] < places[:, None]
    within = jnp.sum((same & earlier).astype(jnp.int32), axis=1)
    return owner * capacity + within


def spread_half(placing, data, capacity, owners):
    flat = data.reshape(data.shape[0], -1)
    moved = jnp.dot(placing.T, flat, preferred_element_type=jnp.float32).astype(jnp.bfloat16)
    return moved.reshape(capacity, owners, data.shape[1], data.shape[2])


def spread_full(placing, data, capacity, owners):
    flat = data.reshape(data.shape[0], -1)
    moved = jnp.dot(placing.T, flat, precision=lax.Precision.HIGHEST)
    return moved.reshape(capacity, owners, data.shape[1], data.shape[2])


def collect_half(placing, data):
    flat = data.reshape(placing.shape[1], -1)
    picked = jnp.dot(placing, flat, preferred_element_type=jnp.float32).astype(jnp.bfloat16)
    return picked.reshape(placing.shape[0], data.shape[2], data.shape[3])


def collect_full(placing, data):
    flat = data.reshape(placing.shape[1], -1)
    picked = jnp.dot(placing, flat, precision=lax.Precision.HIGHEST)
    return picked.reshape(placing.shape[0], data.shape[2], data.shape[3])


def per_device(grads, weight, basis, first_moment, second_moment, sketch, owner, rank):
    owners = lax.axis_size("rows")
    here = lax.axis_index("rows")
    group = lax.axis_index("dp")
    capacity = first_moment.shape[0]
    rank_full = first_moment.shape[1]
    quarter = first_moment.shape[2]
    shard = weight.shape[1]
    width = weight.shape[2]
    total_rows = shard * owners
    root = float(total_rows) ** 0.5
    inverse_root = float(total_rows) ** (-0.5)
    slots = slot_of(owner, capacity)
    column = slots % capacity * owners + slots // capacity
    placing = column[:, None] == jnp.arange(capacity * owners, dtype=jnp.int32)[None, :]
    place_half = placing.astype(jnp.bfloat16)
    place_full = placing.astype(jnp.float32)
    sent_basis = lax.all_to_all(
        spread_full(place_full, basis, capacity, owners),
        "rows",
        split_axis=1,
        concat_axis=1,
        tiled=True,
    )
    old_basis = sent_basis.reshape(capacity, total_rows, rank_full)
    total = lax.psum(grads[0], "dp").astype(jnp.float32).astype(jnp.bfloat16)
    sent_grad = lax.all_to_all(
        spread_half(place_half, total, capacity, owners),
        "rows",
        split_axis=1,
        concat_axis=1,
        tiled=True,
    )
    whole = sent_grad.reshape(capacity, total_rows, width)
    own = lax.dynamic_slice_in_dim(whole, group * quarter, quarter, 2)
    sample = jnp.einsum("cmd,dr->cmr", whole, sketch, preferred_element_type=jnp.float32)
    matched = slots[:, None] == (here * capacity + jnp.arange(capacity, dtype=jnp.int32))[None, :]
    valid = jnp.any(matched, axis=0).astype(jnp.float32)
    rank_slot = jnp.sum(jnp.where(matched, rank[:, None], 0), axis=0)
    projected = (
        jnp.einsum(
            "cmr,cmd->crd", old_basis, own.astype(jnp.float32), precision=lax.Precision.HIGHEST
        )
        * inverse_root
    )
    first_new = beta_one * first_moment + (1.0 - beta_one) * projected
    second_new = beta_two * second_moment + (1.0 - beta_two) * projected * projected
    keeping = (jnp.arange(rank_full, dtype=jnp.int32)[None, :] < rank_slot[:, None]).astype(
        jnp.float32
    )[:, :, None]
    update = keeping * (first_new / bias_one) / (jnp.sqrt(second_new / bias_two) + epsilon)
    delta = (
        jnp.einsum("cmr,crd->cmd", old_basis, update, precision=lax.Precision.HIGHEST)
        * inverse_root
    ).astype(jnp.bfloat16)
    gram = jnp.einsum("cmr,cms->crs", sample, sample, precision=lax.Precision.HIGHEST)
    gram = gram + (1.0 - valid)[:, None, None] * jnp.eye(rank_full, dtype=jnp.float32)[None, :, :]
    lower = jnp.linalg.cholesky(gram)
    new_basis = (
        lax.linalg.triangular_solve(lower, sample, left_side=False, lower=True, transpose_a=True)
        * root
    )
    back_delta = lax.all_to_all(
        delta.reshape(capacity, owners, shard, quarter),
        "rows",
        split_axis=1,
        concat_axis=1,
        tiled=True,
    )
    full_delta = lax.all_gather(collect_half(place_half, back_delta), "dp", axis=2, tiled=True)
    back_basis = lax.all_to_all(
        new_basis.reshape(capacity, owners, shard, rank_full),
        "rows",
        split_axis=1,
        concat_axis=1,
        tiled=True,
    )
    mine_basis = collect_full(place_full, back_basis)
    new_weight = (weight.astype(jnp.float32) - step_size * full_delta.astype(jnp.float32)).astype(
        jnp.bfloat16
    )
    scale_slot = valid[:, None, None]
    return (new_weight, mine_basis, first_new * scale_slot, second_new * scale_slot)


def solution(mesh):
    in_specs = (
        P("dp", None, "rows", None),
        P(None, "rows", None),
        P(None, "rows", None),
        P("rows", None, "dp"),
        P("rows", None, "dp"),
        P(),
        P(),
        P(),
    )
    out_specs = (
        P(None, "rows", None),
        P(None, "rows", None),
        P("rows", None, "dp"),
        P("rows", None, "dp"),
    )
    return jax.shard_map(
        per_device, mesh=mesh, in_specs=in_specs, out_specs=out_specs, check_vma=False
    )
```

profile of v0, /device:TPU:0, one launch (start us, length us, event | category | flops | bytes accessed | tf_op | source)
XLA Modules:
  0.0 695.3 jit_solution(10074540307929962039)
XLA Ops:
  8.8 3.2 fusion.27
  12.0 3.3 copy.74
  15.3 6.5 all-to-all-start
  22.0 2.5 copy.108
  24.5 72.9 %all-reduce.3.cloned.1.call-done = bf16[8,131072]{1,0:T(8,128)(2,1)} async-done(((bf16[8,131072]{1,0:T(8,128)(2,1)}), bf16[8,131072]{1,0:T(8,128)(2,1)}) %all-reduce.3.cloned.1.call-update) | async-done | bytes 2097168 | tf_op jit(solution)/shard_map/psum | solution.py:71
  97.4 7.3 %convolution_convert_fusion = bf16[32,131072]{1,0:T(8,128)(2,1)} fusion(bf16[8,131072]{1,0:T(8,128)(2,1)} %all-reduce.3.cloned.1.call-done, s32[8]{0:T(128)S(1)} %get-tuple-element.42), kind=kOutput, calls=%fused_computation.2 | convolution fusion | flops 71303424 | bytes 10485792 | tf_op jit(solution)/shard_map/dot_general | solution.py:24
  104.7 11.3 %copy.76 = bf16[4,8,128,1024]{3,2,0,1:T(8,128)(2,1)} copy(bf16[4,8,128,1024]{3,1,2,0:T(8,128)(2,1)} %bitcast.94) | data formatting | bytes 16777216 | tf_op jit(solution)/shard_map/reshape | solution.py:25
  116.0 5.6 all-to-all-start.1
  122.3 4.6 copy.75
  126.9 178.2 %all-to-all-done.1 = bf16[4,8,128,1024]{3,2,0,1:T(8,128)(2,1)} async-done(((bf16[4,8,128,1024]{3,2,0,1:T(8,128)(2,1)}), bf16[4,8,128,1024]{3,2,0,1:T(8,128)(2,1)}, u32[]{:S(2)}, u32[]{:S(2)}) %all-to-all-start.1) | async-done | bytes 8388640 | tf_op jit(solution)/shard_map/all_to_all | solution.py:72
  305.1 8.2 %copy.77 = bf16[4,8,128,1024]{3,2,1,0:T(8,128)(2,1)} copy(bf16[4,8,128,1024]{3,2,0,1:T(8,128)(2,1)} %all-to-all-done.1) | data formatting | bytes 16777216 | tf_op jit(solution)/shard_map/all_to_all | solution.py:72
  313.3 5.8 fusion.15
  321.0 7.1 %fusion.53 = f32[4,256,256]{2,1,0:T(8,128)S(1)} fusion(f32[4,1024,256]{2,1,0:T(8,128)S(1)} %fusion.15), kind=kOutput, calls=%fused_computation.101 | convolution fusion | flops 3221225472 | bytes 5242880 | tf_op jit(solution)/shard_map/cmr,cms->crs/dot_general | solution.py:101
  328.5 8.7 %broadcast_multiply_fusion = (f32[4,256,256]{2,1,0:T(8,128)}, f32[4,256,256]{2,1,0:T(8,128)}, f32[4,256,256]{2,1,0:T(8,128)S(1)}) fusion(f32[4]{0:T(128)S(1)} %convert_element_type.58, f32[4,256,256]{2,1,0:T(8,128)} %param.12, f32[4,256,256]{2,1,0:T(8,128)} %param.11, f32[4,1024,256]{2,1,0:T(8,128)} %bitcast.96, bf16[4,1024,1024]{2,1,0:T(8,128)(2,1)} %bitcast.99, ...), kind=kOutput, calls=%fused_computation.33 | convolution fusion | flops 3223846912 | bytes 11534356 | tf_op jit(solution)/shard_map/cmr,cmd->crd/dot_general | solution.py:86
  337.2 4.7 multiply_convert_fusion
  343.4 4.4 all-to-all-start.2
  349.1 46.9 %custom-call.16 = f32[4,128,128]{2,1,0:T(8,128)S(1)} custom-call(f32[4,128,128]{2,1,0:T(8,128)S(1)} %cholesky.122), custom_call_target="Cholesky" | custom-call | tf_op jit(solution)/shard_map/jit(cholesky)/cholesky | solution.py:103
  396.1 39.3 %custom-call.17 = f32[4,1,128,128]{2,3,1,0:T(8,128)S(1)} custom-call(f32[4,1,128,128]{3,2,1,0:T(8,128)S(1)} %select_bitcast_fusion), custom_call_target="InvertDiagBlocksLowerTriangular" | custom-call | tf_op jit(solution)/shard_map/jit(cholesky)/cholesky | solution.py:103
  438.4 46.9 %custom-call.18 = f32[4,128,128]{2,1,0:T(8,128)S(1)} custom-call(f32[4,128,128]{2,1,0:T(8,128)S(1)} %convolution_subtract_fusion), custom_call_target="Cholesky" | custom-call | tf_op jit(solution)/shard_map/jit(cholesky)/cholesky | solution.py:103
  485.9 5.6 while.1
  486.5 2.2 bitcast_dynamic-update-slice_fusion.2
  489.3 2.2 bitcast_dynamic-update-slice_fusion.2
  491.5 79.6 %custom-call.19 = f32[4,2,128,128]{2,3,1,0:T(8,128)S(1)} custom-call(f32[4,2,128,128]{3,2,1,0:T(8,128)} %bitcast.106), custom_call_target="InvertDiagBlocksLowerTriangular" | custom-call | tf_op jit(solution)/shard_map/triangular_solve | solution.py:105
  571.1 3.6 fusion.4
  576.7 2.0 fusion.3
  578.7 2.4 copy_multiply_fusion
  581.1 5.0 all-to-all-start.3
  590.7 36.5 %all-gather.2.cloned.1.call-done = bf16[8,128,1024]{2,1,0:T(8,128)(2,1)} async-done(((bf16[8,128,256]{2,1,0:T(8,128)(2,1)}), bf16[8,128,1024]{2,1,0:T(8,128)(2,1)}) %all-gather.2.cloned.1.call-update) | async-done | bytes 2097168 | tf_op jit(solution)/shard_map/all_gather | solution.py:115
  627.2 3.9 subtract_convert_fusion
  631.1 49.1 %all-to-all-done.3 = f32[4,8,128,256]{3,2,0,1:T(8,128)} async-done(((f32[4,8,128,256]{3,2,0,1:T(8,128)}), f32[4,8,128,256]{3,2,0,1:T(8,128)}, u32[]{:S(2)}, u32[]{:S(2)}) %all-to-all-start.3) | async-done | bytes 4194336 | tf_op jit(solution)/shard_map/all_to_all | solution.py:116
  680.2 2.6 copy.125
  682.8 3.9 fusion
  (67 shorter events, 20.1 us)
Async XLA Ops:
  7.2 306.1 %copy-start = (bf16[1024,256]{1,0:T(8,128)(2,1)S(1)}, bf16[1024,256]{1,0:T(8,128)(2,1)}, u32[]{:S(2)}) copy-start(bf16[1024,256]{1,0:T(8,128)(2,1)} %param.13) | copy-start | bytes 1572868
  15.3 6.7 copy-start.7
  15.3 100.7 %all-to-all-start = ((f32[4,8,128,256]{3,2,0,1:T(8,128)}), f32[4,8,128,256]{3,2,0,1:T(8,128)}, u32[]{:S(2)}, u32[]{:S(2)}) async-start(f32[4,8,128,256]{3,2,0,1:T(8,128)} %copy.74), calls=%async_computation | async-start | bytes 8388608 | tf_op jit(solution)/shard_map/all_to_all | solution.py:63
  21.8 75.7 %all-reduce.3.cloned.1.call-start = ((), (), s32[]{:S(2)}) async-start(), calls=%async_computation.4 | async-start | bytes 4194304 | tf_op jit(solution)/shard_map/psum | solution.py:71
  116.0 5.9 copy-start.10
  116.0 189.1 %all-to-all-start.1 = ((bf16[4,8,128,1024]{3,2,0,1:T(8,128)(2,1)}), bf16[4,8,128,1024]{3,2,0,1:T(8,128)(2,1)}, u32[]{:S(2)}, u32[]{:S(2)}) async-start(bf16[4,8,128,1024]{3,2,0,1:T(8,128)(2,1)} %copy.76), calls=%async_computation.1 | async-start | bytes 16777216 | tf_op jit(solution)/shard_map/all_to_all | solution.py:72
  319.1 2.0 copy-start.2
  328.5 8.7 %copy-start.4 = (f32[4,8,128,256]{3,2,1,0:T(8,128)S(1)}, f32[4,8,128,256]{3,2,1,0:T(8,128)}, u32[]{:S(2)}) copy-start(f32[4,8,128,256]{3,2,1,0:T(8,128)} %copy.75) | copy-start | bytes 12582916
  328.5 8.7 %copy-start.8 = (f32[4,256,256]{2,1,0:T(8,128)S(1)}, f32[4,256,256]{2,1,0:T(8,128)}, u32[]{:S(2)}) copy-start(f32[4,256,256]{2,1,0:T(8,128)} %param.12) | copy-start | bytes 3145732
  328.5 8.7 %copy-start.9 = (f32[4,256,256]{2,1,0:T(8,128)S(1)}, f32[4,256,256]{2,1,0:T(8,128)}, u32[]{:S(2)}) copy-start(f32[4,256,256]{2,1,0:T(8,128)} %param.11) | copy-start | bytes 3145732
  343.4 237.7 %all-to-all-start.2 = ((bf16[4,8,128,256]{3,2,0,1:T(8,128)(2,1)}), bf16[4,8,128,256]{3,2,0,1:T(8,128)(2,1)}, u32[]{:S(2)}, u32[]{:S(2)}) async-start(bf16[4,8,128,256]{3,2,0,1:T(8,128)(2,1)} %copy.79), calls=%async_computation.2 | async-start | bytes 4194304 | tf_op jit(solution)/shard_map/all_to_all | solution.py:108
  348.1 1.0 copy-start.5
  571.1 5.6 copy-start.3
  581.1 99.1 %all-to-all-start.3 = ((f32[4,8,128,256]{3,2,0,1:T(8,128)}), f32[4,8,128,256]{3,2,0,1:T(8,128)}, u32[]{:S(2)}, u32[]{:S(2)}) async-start(f32[4,8,128,256]{3,2,0,1:T(8,128)} %copy_multiply_fusion), calls=%async_computation.3 | async-start | bytes 8388608 | tf_op jit(solution)/shard_map/all_to_all | solution.py:116
  586.1 41.1 %all-gather.2.cloned.1.call-start = ((), (), s32[]{:S(2)}) async-start(), calls=%async_computation.5 | async-start | bytes 2621440 | tf_op jit(solution)/shard_map/all_gather | solution.py:115
  588.1 39.1 %copy-start.6 = (bf16[8,128,1024]{2,1,0:T(8,128)(2,1)S(1)}, bf16[8,128,1024]{2,1,0:T(8,128)(2,1)}, u32[]{:S(2)}) copy-start(bf16[8,128,1024]{2,1,0:T(8,128)(2,1)} %param.9) | copy-start | bytes 6291460
  680.2 7.9 %copy-start.1 = (bf16[1024,256]{1,0:T(8,128)(2,1)S(1)}, bf16[1024,256]{1,0:T(8,128)(2,1)}, u32[]{:S(2)}) copy-start(bf16[1024,256]{1,0:T(8,128)(2,1)} %param.13) | copy-start | bytes 1572868
Sparse Core Ops, SparseCore 0:
  26.3 71.1 all-reduce.2
  590.8 36.3 all-gather.1
where the time goes:
time: 700 us; the launch traced here: 695 us
  waiting for transfers between devices  337 us (48%)
  other arithmetic  222 us (32%)
  matrix products  51.7 us (7%)
  local copies, waits for them, and re-layouts  48.1 us (7%)
  starting transfers between devices  22 us (3%)
  between operations  14.8 us (2%)
    all_to_all x1, waiting for transfers between devices, per_device(): lax.all_to_all(spread_half(place_half, total, capacity, owners), 'rows',...  178 us
    another operation x10, other arithmetic, per_device(): lower = jnp.linalg.cholesky(gram)  133 us
    another operation x4, other arithmetic, per_device(): lax.linalg.triangular_solve(lower, sample, left_side=False, lower=True, t...  79.8 us
    psum x1, waiting for transfers between devices, per_device(): total = lax.psum(grads[0], 'dp').astype(jnp.float32).astype(jnp.bfloat16)  72.9 us
    all_to_all x1, waiting for transfers between devices, per_device(): lax.all_to_all(new_basis.reshape(capacity, owners, shard, rank_full), 'ro...  49.1 us
    all_gather x1, waiting for transfers between devices, per_device(): lax.all_gather(collect_half(place_half, back_delta), 'dp', axis=2, tiled=...  36.5 us
  transfers between devices with their start and end apart: 6, of which 4 were waited for; matrix products, arithmetic and copies ran while one was open for 38% of the time, Pallas kernels for 0%

commit v1 on v0

v1 whole, which is shorter than its diff:
```python
import functools

import jax
import jax.numpy as jnp
from jax import lax
from jax.experimental import pallas as pl
from jax.experimental.pallas import tpu as pltpu
from jax.sharding import PartitionSpec as P

beta_one = 0.9
beta_two = 0.95
bias_one = 1.0 - 0.9**10
bias_two = 1.0 - 0.95**10
step_size = 0.5
epsilon = 1e-08
BLOCK = 64
HIGHEST = lax.Precision.HIGHEST
VMEM_LIMIT = 48 * 1024 * 1024


def slot_of(owner, capacity):
    same = owner[:, None] == owner[None, :]
    places = jnp.arange(owner.shape[0], dtype=jnp.int32)
    earlier = places[None, :] < places[:, None]
    within = jnp.sum((same & earlier).astype(jnp.int32), axis=1)
    return owner * capacity + within


def factor_kernel(gram_ref, rows_ref, out_ref, work, *, scale):
    pair, size = gram_ref.shape[0], gram_ref.shape[1]
    lane = lax.broadcasted_iota(jnp.int32, (BLOCK, 2 * BLOCK), 1)
    sub = lax.broadcasted_iota(jnp.int32, (BLOCK, 2 * BLOCK), 0)
    eye_right = (lane - BLOCK == sub).astype(jnp.float32)
    wide_row = lax.broadcasted_iota(jnp.int32, (size, size), 0)
    wide_col = lax.broadcasted_iota(jnp.int32, (size, size), 1)
    eye = (wide_row == wide_col).astype(jnp.float32)
    for b in range(pair):
        work[b, :, :size] = gram_ref[b]
        work[b, :, size:] = eye
    blocks = size // BLOCK
    for j in range(blocks):
        lo = j * BLOCK
        tiles = []
        for b in range(pair):
            base = lo // 128 * 128
            slab = work[b, lo : lo + BLOCK, base : base + 128]
            if lo > base:
                slab = pltpu.roll(slab, 128 - (lo - base), 1)
            tiles.append(jnp.where(lane < BLOCK, slab, eye_right))
        for k in range(BLOCK - 1):
            for b in range(pair):
                tile = tiles[b]
                column = jnp.where(sub[:, :1] > k, tile[:, k : k + 1], 0.0)
                row = tile[k : k + 1, :] * (1.0 / tile[k : k + 1, k : k + 1])
                tiles[b] = tile - column * row
        for b in range(pair):
            tile = tiles[b]
            diagonal = jnp.sum(jnp.where(lane == sub, tile, 0.0), axis=1, keepdims=True)
            inverse = pltpu.roll(tile, BLOCK, 1)[:, :BLOCK] * lax.rsqrt(diagonal)
            solved = jnp.dot(
                inverse,
                work[b, lo : lo + BLOCK, :],
                precision=HIGHEST,
                preferred_element_type=jnp.float32,
            )
            work[b, lo : lo + BLOCK, size:] = solved[:, size:]
            if j + 1 < blocks:
                change = lax.dot_general(
                    solved[:, :size],
                    solved,
                    (((0,), (0,)), ((), ())),
                    precision=HIGHEST,
                    preferred_element_type=jnp.float32,
                )
                work[b, lo + BLOCK :, :] = work[b, lo + BLOCK :, :] - change[lo + BLOCK :, :]
    for b in range(pair):
        basis = lax.dot_general(
            rows_ref[b].astype(jnp.float32),
            work[b, :, size:],
            (((1,), (1,)), ((), ())),
            precision=HIGHEST,
            preferred_element_type=jnp.float32,
        )
        out_ref[b] = (basis * scale).astype(out_ref.dtype)


def factor(gram, rows, scale):
    count, size, _ = gram.shape
    pair = 2 if count % 2 == 0 else 1
    shard = rows.shape[1]
    return pl.pallas_call(
        functools.partial(factor_kernel, scale=scale),
        out_shape=jax.ShapeDtypeStruct((count, shard, size), jnp.bfloat16),
        grid=(count // pair,),
        in_specs=[
            pl.BlockSpec((pair, size, size), lambda i: (i, 0, 0)),
            pl.BlockSpec((pair, shard, size), lambda i: (i, 0, 0)),
        ],
        out_specs=pl.BlockSpec((pair, shard, size), lambda i: (i, 0, 0)),
        scratch_shapes=[pltpu.VMEM((pair, size, 2 * size), jnp.float32)],
        compiler_params=pltpu.CompilerParams(vmem_limit_bytes=VMEM_LIMIT),
        cost_estimate=pl.CostEstimate(
            flops=4_000_000_000, bytes_accessed=count * size * size * 8, transcendentals=0
        ),
    )(gram, rows)


def pick_kernel(index_ref, first_ref, second_ref, out_ref):
    out_ref[0, 0] = first_ref[0].astype(out_ref.dtype)
    out_ref[0, 1] = second_ref[0].astype(out_ref.dtype)


def pick_moments(index, first, second):
    count = index.shape[0]
    _, rank, width = first.shape
    spec = pl.BlockSpec((1, rank, width), lambda i, index: (index[i], 0, 0))
    return pl.pallas_call(
        pick_kernel,
        out_shape=jax.ShapeDtypeStruct((count, 2, rank, width), jnp.bfloat16),
        grid_spec=pltpu.PrefetchScalarGridSpec(
            num_scalar_prefetch=1,
            grid=(count,),
            in_specs=[spec, spec],
            out_specs=pl.BlockSpec((1, 2, rank, width), lambda i, index: (i, 0, 0, 0)),
        ),
        cost_estimate=pl.CostEstimate(
            flops=0, bytes_accessed=count * rank * width * 12, transcendentals=0
        ),
    )(index, first, second)


def project_kernel(grad_ref, basis_ref, out_ref, *, scale):
    total = grad_ref[0, 0].astype(jnp.float32)
    for g in range(1, grad_ref.shape[0]):
        total = total + grad_ref[g, 0].astype(jnp.float32)
    product = lax.dot_general(
        basis_ref[0],
        total,
        (((0,), (0,)), ((), ())),
        precision=HIGHEST,
        preferred_element_type=jnp.float32,
    )
    out_ref[0] = (product * scale).astype(out_ref.dtype)


def project(parts, basis, scale):
    groups, count, shard, quarter = parts.shape
    rank = basis.shape[2]
    return pl.pallas_call(
        functools.partial(project_kernel, scale=scale),
        out_shape=jax.ShapeDtypeStruct((count, rank, quarter), jnp.bfloat16),
        grid=(count,),
        in_specs=[
            pl.BlockSpec((groups, 1, shard, quarter), lambda i: (0, i, 0, 0)),
            pl.BlockSpec((1, shard, rank), lambda i: (i, 0, 0)),
        ],
        out_specs=pl.BlockSpec((1, rank, quarter), lambda i: (i, 0, 0)),
        cost_estimate=pl.CostEstimate(
            flops=12 * count * shard * quarter * rank,
            bytes_accessed=count * (shard * quarter * 12 + rank * quarter * 2),
            transcendentals=0,
        ),
    )(parts, basis)


def moment_kernel(index_ref, valid_ref, proj_ref, first_ref, second_ref, first_out, second_out):
    keep = valid_ref[pl.program_id(0)] > 0
    projected = proj_ref[0].astype(jnp.float32)
    first_new = beta_one * first_ref[0] + (1.0 - beta_one) * projected
    second_new = beta_two * second_ref[0] + (1.0 - beta_two) * projected * projected
    first_out[0] = jnp.where(keep, first_new, 0.0)
    second_out[0] = jnp.where(keep, second_new, 0.0)


def update_moments(index, valid, projected, first, second):
    capacity, rank, width = first.shape
    spec = pl.BlockSpec((1, rank, width), lambda i, index, valid: (i, 0, 0))
    picked = pl.BlockSpec((1, rank, width), lambda i, index, valid: (index[i], 0, 0))
    shape = jax.ShapeDtypeStruct(first.shape, jnp.float32)
    return pl.pallas_call(
        moment_kernel,
        out_shape=(shape, shape),
        grid_spec=pltpu.PrefetchScalarGridSpec(
            num_scalar_prefetch=2,
            grid=(capacity,),
            in_specs=[picked, spec, spec],
            out_specs=(spec, spec),
        ),
        cost_estimate=pl.CostEstimate(
            flops=0, bytes_accessed=capacity * rank * width * 18, transcendentals=0
        ),
    )(index, valid, projected, first, second)


def per_device(grads, weight, basis, first_moment, second_moment, sketch, owner, rank):
    owners = lax.axis_size("rows")
    groups = lax.axis_size("dp")
    here = lax.axis_index("rows")
    capacity, rank_full, quarter = first_moment.shape
    count, shard, width = weight.shape
    per = count // owners
    total_rows = shard * owners
    root = float(total_rows) ** 0.5
    inverse_root = float(total_rows) ** (-0.5)
    local = grads[0]
    slots = slot_of(owner, capacity)

    sent = lax.all_to_all(
        local.reshape(count, shard, groups, quarter), "dp", split_axis=2, concat_axis=0
    )
    part = jnp.einsum("mrd,dk->mrk", local, sketch, preferred_element_type=jnp.float32)
    part = part.astype(jnp.bfloat16).reshape(groups, count // groups, shard, rank_full)
    got = lax.all_to_all(part, "dp", split_axis=0, concat_axis=0)
    sample = jnp.sum(got.astype(jnp.float32), axis=0).astype(jnp.bfloat16)
    whole = lax.all_gather(sample, "rows", axis=1, tiled=True)

    offset = slots - here * capacity
    held = pick_moments(jnp.clip(offset, 0, capacity - 1), first_moment, second_moment)
    moved = lax.all_to_all(
        held.reshape(owners, per, 2, rank_full, quarter), "rows", split_axis=0, concat_axis=0
    )
    mine = here * per + jnp.arange(per, dtype=jnp.int32)
    from_owner = owner[mine]
    moments = jnp.stack([moved[from_owner[i], i] for i in range(per)]).astype(jnp.float32)

    partial = project(sent, basis, inverse_root)
    terms = lax.all_to_all(
        partial.reshape(owners, per, rank_full, quarter), "rows", split_axis=0, concat_axis=0
    )
    projected = jnp.sum(terms.astype(jnp.float32), axis=0)
    first_new = beta_one * moments[:, 0] + (1.0 - beta_one) * projected
    second_new = beta_two * moments[:, 1] + (1.0 - beta_two) * projected * projected
    keeping = jnp.arange(rank_full, dtype=jnp.int32)[None, :] < rank[mine][:, None]
    update = (first_new / bias_one) / (jnp.sqrt(second_new / bias_two) + epsilon)
    update = jnp.where(keeping[:, :, None], update, 0.0).astype(jnp.bfloat16)
    updates = lax.all_gather(update, "rows", axis=0, tiled=True)
    all_projected = lax.all_gather(projected.astype(jnp.bfloat16), "rows", axis=0, tiled=True)

    delta = jnp.einsum(
        "mrk,mkd->mrd",
        basis.astype(jnp.bfloat16),
        updates,
        preferred_element_type=jnp.float32,
    )
    delta = (delta * inverse_root).astype(jnp.bfloat16)
    full_delta = lax.all_gather(delta, "dp", axis=2, tiled=True)
    new_weight = (weight.astype(jnp.float32) - step_size * full_delta.astype(jnp.float32)).astype(
        jnp.bfloat16
    )

    gram = jnp.einsum("cmr,cms->crs", whole, whole, preferred_element_type=jnp.float32)
    rows_basis = factor(gram, sample, root)
    new_basis = lax.all_gather(rows_basis, "dp", axis=0, tiled=True).astype(jnp.float32)

    matched = slots[None, :] == (here * capacity + jnp.arange(capacity, dtype=jnp.int32))[:, None]
    valid = jnp.any(matched, axis=1).astype(jnp.int32)
    index = jnp.sum(
        jnp.where(matched, jnp.arange(count, dtype=jnp.int32)[None, :], 0), axis=1
    )
    first_out, second_out = update_moments(
        index, valid, all_projected, first_moment, second_moment
    )
    return (new_weight, new_basis, first_out, second_out)


def solution(mesh):
    in_specs = (
        P("dp", None, "rows", None),
        P(None, "rows", None),
        P(None, "rows", None),
        P("rows", None, "dp"),
        P("rows", None, "dp"),
        P(),
        P(),
        P(),
    )
    out_specs = (
        P(None, "rows", None),
        P(None, "rows", None),
        P("rows", None, "dp"),
        P("rows", None, "dp"),
    )
    return jax.shard_map(
        per_device, mesh=mesh, in_specs=in_specs, out_specs=out_specs, check_vma=False
    )
```

time: 700 us -> 261 us (0.37)
  waiting for transfers between devices: 337 us -> 98.7 us
  other arithmetic: 222 us -> 10.9 us
  blocking collectives: 0 us -> 56.3 us
  Pallas kernels: 0 us -> 46.3 us
  matrix products: 51.7 us -> 6.95 us
  local copies, waits for them, and re-layouts: 48.1 us -> 15.2 us
  starting transfers between devices: 22 us -> 9.63 us
    another operation x14 -> x0, other arithmetic: 213 us -> none  [the longest x10 133 us: per_device(): lower = jnp.linalg.cholesky(gram)]
    all_to_all x4 -> x2, waiting for transfers between devices: 227 us -> 65.3 us  [the longest x1 45.1 us: per_device(): lax.all_to_all(held.reshape(owners, per, 2, rank_full, quarter), 'rows',...]
    psum x1 -> x0, waiting for transfers between devices: 72.9 us -> none  [per_device(): total = lax.psum(grads[0], 'dp').astype(jnp.float32).astype(jnp.bfloat16)]
    pallas_call x0 -> x4, Pallas kernels: none -> 46.3 us  [the longest x1 28.8 us: factor(): pl.pallas_call(functools.partial(factor_kernel, scale=scale), out_shape=j...]
    all_to_all x0 -> x2, blocking collectives: none -> 41.4 us  [the longest x1 30.4 us: per_device(): lax.all_to_all(local.reshape(count, shard, groups, quarter), 'dp', split_...]
    dot_general x8 -> x3, matrix products: 41.2 us -> 6.95 us  [the longest x1 2.52 us: per_device(): jnp.einsum('mrk,mkd->mrd', basis.astype(jnp.bfloat16), updates, preferred...]
    all_to_all x4 -> x0, local copies, waits for them, and re-layouts: 17.2 us -> none  [the longest x1 8.2 us: per_device(): lax.all_to_all(spread_half(place_half, total, capacity, owners), 'rows',...]
    all_gather x0 -> x1, blocking collectives: none -> 14.9 us  [per_device(): lax.all_gather(rows_basis, 'dp', axis=0, tiled=True).astype(jnp.float32)]
  transfers between devices with their start and end apart: 6 -> 6, of which waited for: 4 -> 5; matrix products, arithmetic and copies ran while one was open for 38% -> 6% of each run, Pallas kernels for 0% -> 15%
where the time goes in v1:
time: 261 us; the launch traced here: 260 us
  waiting for transfers between devices  98.7 us (38%)
  blocking collectives  56.3 us (22%)
  Pallas kernels  46.3 us (18%)
  between operations  15.8 us (6%)
  local copies, waits for them, and re-layouts  15.2 us (6%)
  other arithmetic  10.9 us (4%)
  starting transfers between devices  9.63 us (4%)
  matrix products  6.95 us (3%)
    all_to_all x1, waiting for transfers between devices, per_device(): lax.all_to_all(held.reshape(owners, per, 2, rank_full, quarter), 'rows',...  45.1 us
    all_to_all x1, blocking collectives, per_device(): lax.all_to_all(local.reshape(count, shard, groups, quarter), 'dp', split_...  30.4 us
    pallas_call x1, Pallas kernels, factor(): pl.pallas_call(functools.partial(factor_kernel, scale=scale), out_shape=j...  28.8 us
    all_to_all x1, waiting for transfers between devices, per_device(): lax.all_to_all(partial.reshape(owners, per, rank_full, quarter), 'rows',...  20.2 us
    all_gather x1, waiting for transfers between devices, per_device(): whole = lax.all_gather(sample, 'rows', axis=1, tiled=True)  16.6 us
    all_gather x1, blocking collectives, per_device(): lax.all_gather(rows_basis, 'dp', axis=0, tiled=True).astype(jnp.float32)  14.9 us
    all_gather x1, waiting for transfers between devices, per_device(): full_delta = lax.all_gather(delta, 'dp', axis=2, tiled=True)  12.2 us
    unnamed x13, local copies, waits for them, and re-layouts  11.1 us
  transfers between devices with their start and end apart: 6, of which 5 were waited for; matrix products, arithmetic and copies ran while one was open for 6% of the time, Pallas kernels for 15%

profile of v1, /device:TPU:0, one launch (start us, length us, event | category | flops | bytes accessed | tf_op | source)
XLA Modules:
  0.0 259.8 jit_solution(17007115914789143110)
XLA Ops:
  7.2 4.0 %copy.39 = bf16[1,8,128,1024]{2,3,1,0:T(8,128)(2,1)} copy(bf16[1,8,128,1024]{3,2,1,0:T(8,128)(2,1)} %param.8) | data formatting | bytes 4194304 | tf_op args[0]
  11.1 2.9 %copy.40 = bf16[1,8,128,4,256]{4,2,1,0,3:T(8,128)(2,1)S(1)} copy(bf16[1,8,128,4,256]{2,4,3,1,0:T(8,128)(2,1)} %bitcast.59) | data formatting | bytes 4194304 | tf_op jit(solution)/shard_map/broadcast_in_dim;reshape;squeeze | solution.py:208
  14.0 30.4 %all_to_all.30 = bf16[1,8,128,4,256]{4,2,1,0,3:T(8,128)(2,1)} all-to-all(bf16[1,8,128,4,256]{4,2,1,0,3:T(8,128)(2,1)S(1)} %copy.40), channel_id=1, replica_groups=mesh['dp'=4,'rows'=8] {'dp'}, dimensions={3} | all-to-all | bytes 4194304 | tf_op jit(solution)/shard_map/all_to_all | solution.py:208
  44.5 7.1 %shard_map.112 = bf16[8,256,256]{2,1,0:T(8,128)(2,1)} custom-call(bf16[4,8,128,256]{3,2,1,0:T(8,128)(2,1)} %bitcast.58, f32[8,128,256]{2,1,0:T(8,128)} %basis_ref.1), custom_call_target="tpu_custom_call" | custom-call | flops 805306368 | bytes 4194304 | tf_op jit(solution)/shard_map/pallas_call | solution.py:149
  51.6 5.0 %all-to-all-start.2 = ((bf16[8,1,256,256]{3,2,1,0:T(8,128)(2,1)}), bf16[8,1,256,256]{3,2,1,0:T(8,128)(2,1)S(1)}, u32[]{:S(2)}, u32[]{:S(2)}) async-start(bf16[8,1,256,256]{3,2,1,0:T(8,128)(2,1)} %bitcast.60), calls=%async_computation.2 | async-start | bytes 2097152 | tf_op jit(solution)/shard_map/all_to_all | solution.py:227
  57.3 5.7 %shard_map.111 = bf16[8,2,256,256]{3,2,1,0:T(8,128)(2,1)} custom-call(s32[8]{0:T(128)} %get-tuple-element.50.index_ref, f32[4,256,256]{2,1,0:T(8,128)} %first_ref.3, f32[4,256,256]{2,1,0:T(8,128)} %second_ref.3), custom_call_target="tpu_custom_call" | custom-call | bytes 6291456 | tf_op jit(solution)/shard_map/pallas_call | solution.py:117
  63.0 20.2 %all-to-all-done.2 = bf16[8,1,256,256]{3,2,1,0:T(8,128)(2,1)S(1)} async-done(((bf16[8,1,256,256]{3,2,1,0:T(8,128)(2,1)}), bf16[8,1,256,256]{3,2,1,0:T(8,128)(2,1)S(1)}, u32[]{:S(2)}, u32[]{:S(2)}) %all-to-all-start.2) | async-done | bytes 1048608 | tf_op jit(solution)/shard_map/all_to_all | solution.py:227
  83.2 4.5 %all-to-all-start = ((bf16[8,1,2,256,256]{4,3,2,1,0:T(8,128)(2,1)}), bf16[8,1,2,256,256]{4,3,2,1,0:T(8,128)(2,1)}, u32[]{:S(2)}, u32[]{:S(2)}) async-start(bf16[8,1,2,256,256]{4,3,2,1,0:T(8,128)(2,1)} %bitcast.57), calls=%async_computation | async-start | bytes 4194304 | tf_op jit(solution)/shard_map/all_to_all | solution.py:219
  87.7 0.6 dynamic-slice.5
  89.6 0.6 dynamic-slice.4
  90.8 0.7 iota_compare_fusion.1
  91.7 45.1 %all-to-all-done = bf16[8,1,2,256,256]{4,3,2,1,0:T(8,128)(2,1)} async-done(((bf16[8,1,2,256,256]{4,3,2,1,0:T(8,128)(2,1)}), bf16[8,1,2,256,256]{4,3,2,1,0:T(8,128)(2,1)}, u32[]{:S(2)}, u32[]{:S(2)}) %all-to-all-start) | async-done | bytes 2097184 | tf_op jit(solution)/shard_map/all_to_all | solution.py:219
  136.7 1.0 bitcast_convert_fusion
  137.7 0.9 fusion.19
  138.7 2.4 fusion.3
  141.0 11.0 %all_to_all.31 = bf16[4,2,128,256]{3,2,1,0:T(8,128)(2,1)S(1)} all-to-all(bf16[4,2,128,256]{3,2,1,0:T(8,128)(2,1)S(1)} %bitcast.61), channel_id=1, replica_groups=mesh['dp'=4,'rows'=8] {'dp'}, dimensions={0} | all-to-all | bytes 1048576 | tf_op jit(solution)/shard_map/all_to_all | solution.py:213
  152.0 0.7 reduce_sum.44.rows_ref
  152.9 0.7 bitcast_convert_fusion.1
  153.6 4.6 %all-gather.5.cloned.1.call-done = bf16[8,256,256]{2,1,0:T(8,128)(2,1)} async-done(((bf16[1,256,256]{2,1,0:T(8,128)(2,1)}), bf16[8,256,256]{2,1,0:T(8,128)(2,1)}) %all-gather.5.cloned.1.call-update) | async-done | bytes 1048592 | tf_op jit(solution)/shard_map/all_gather | solution.py:236
  158.2 2.5 fusion.6
  160.8 3.2 %copy.37 = bf16[8,128,1024]{1,2,0:T(8,128)(2,1)S(1)} copy(bf16[8,128,1024]{2,1,0:T(8,128)(2,1)} %param.9) | data formatting | bytes 4194304 | tf_op args[1]
  164.2 0.6 convert_element_type.84.valid_ref
  164.8 0.8 fusion.21.index_ref
  165.5 16.6 %all-gather.9.cloned.1.call-done = bf16[2,1024,256]{2,1,0:T(8,128)(2,1)} async-done(((bf16[2,128,256]{2,1,0:T(8,128)(2,1)}), bf16[2,1024,256]{2,1,0:T(8,128)(2,1)}) %all-gather.9.cloned.1.call-update) | async-done | bytes 1048592 | tf_op jit(solution)/shard_map/all_gather | solution.py:215
  182.1 2.1 fusion.22.gram_ref
  184.2 28.8 %shard_map.113 = bf16[2,128,256]{2,1,0:T(8,128)(2,1)S(1)} custom-call(f32[2,256,256]{2,1,0:T(8,128)S(1)} %fusion.22.gram_ref, bf16[2,128,256]{2,1,0:T(8,128)(2,1)S(1)} %copy-done.1), custom_call_target="tpu_custom_call" | custom-call | flops 4000000000 | bytes 1048576 | tf_op jit(solution)/shard_map/pallas_call | solution.py:91
  213.0 14.9 %all_gather.18 = bf16[8,128,256]{2,1,0:T(8,128)(2,1)S(1)} all-gather(bf16[2,128,256]{2,1,0:T(8,128)(2,1)S(1)} %shard_map.113), channel_id=1, replica_groups=mesh['dp'=4,'rows'=8] {'dp'}, dimensions={0}, use_global_device_ids=true | all-gather | bytes 655360 | tf_op jit(solution)/shard_map/all_gather | solution.py:253
  227.9 1.1 convert_element_type.83
  228.9 4.6 %shard_map.114 = (f32[4,256,256]{2,1,0:T(8,128)}, f32[4,256,256]{2,1,0:T(8,128)}) custom-call(s32[4]{0:T(128)} %fusion.21.index_ref, s32[4]{0:T(128)} %convert_element_type.84.valid_ref, bf16[8,256,256]{2,1,0:T(8,128)(2,1)} %all-gather.11.cloned.1.call-done.proj_ref, f32[4,256,256]{2,1,0:T(8,128)} %first_ref.3, f32[4,256,256]{2,1,0:T(8,128)} %second_ref.3), custom_call_target="tpu_custom_call" | custom-call | bytes 4718592 | tf_op jit(solution)/shard_map/pallas_call | solution.py:180
  233.6 12.2 %all-gather.7.cloned.1.call-done = bf16[8,128,1024]{1,2,0:T(8,128)(2,1)} async-done(((bf16[8,128,256]{1,2,0:T(8,128)(2,1)}), bf16[8,128,1024]{1,2,0:T(8,128)(2,1)}) %all-gather.7.cloned.1.call-update) | async-done | bytes 2097168 | tf_op jit(solution)/shard_map/all_gather | solution.py:246
  245.8 3.6 %subtract_convert_fusion = bf16[8,128,1024]{1,2,0:T(8,128)(2,1)} fusion(bf16[8,128,1024]{1,2,0:T(8,128)(2,1)} %all-gather.7.cloned.1.call-done, bf16[8,128,1024]{1,2,0:T(8,128)(2,1)S(1)} %copy.37), kind=kLoop, calls=%fused_computation | loop fusion | flops 5242880 | bytes 6291456 | tf_op jit(solution)/shard_map/convert_element_type | solution.py:247
  249.4 3.9 %copy.44 = bf16[8,128,1024]{2,1,0:T(8,128)(2,1)} copy(bf16[8,128,1024]{1,2,0:T(8,128)(2,1)} %subtract_convert_fusion) | data formatting | bytes 4194304
  (24 shorter events, 1.3 us)
Async XLA Ops:
  7.2 131.5 %copy-start = (bf16[1024,256]{1,0:T(8,128)(2,1)S(1)}, bf16[1024,256]{1,0:T(8,128)(2,1)}, u32[]{:S(2)}) copy-start(bf16[1024,256]{1,0:T(8,128)(2,1)} %param.13) | copy-start | bytes 1572868
  51.6 5.0 %copy-start.3 = (s32[8]{0:T(128)S(1)}, s32[8]{0:T(128)}, u32[]{:S(2)}) copy-start(s32[8]{0:T(128)} %param.14) | copy-start | bytes 100
  51.6 31.6 %all-to-all-start.2 = ((bf16[8,1,256,256]{3,2,1,0:T(8,128)(2,1)}), bf16[8,1,256,256]{3,2,1,0:T(8,128)(2,1)S(1)}, u32[]{:S(2)}, u32[]{:S(2)}) async-start(bf16[8,1,256,256]{3,2,1,0:T(8,128)(2,1)} %bitcast.60), calls=%async_computation.2 | async-start | bytes 2097152 | tf_op jit(solution)/shard_map/all_to_all | solution.py:227
  83.2 6.4 %copy-start.4 = (s32[8]{0:T(128)S(1)}, s32[8]{0:T(128)}, u32[]{:S(2)}) copy-start(s32[8]{0:T(128)} %param.15) | copy-start | bytes 100
  83.2 53.5 %all-to-all-start = ((bf16[8,1,2,256,256]{4,3,2,1,0:T(8,128)(2,1)}), bf16[8,1,2,256,256]{4,3,2,1,0:T(8,128)(2,1)}, u32[]{:S(2)}, u32[]{:S(2)}) async-start(bf16[8,1,2,256,256]{4,3,2,1,0:T(8,128)(2,1)} %bitcast.57), calls=%async_computation | async-start | bytes 4194304 | tf_op jit(solution)/shard_map/all_to_all | solution.py:219
  87.7 70.6 %all-gather.5.cloned.1.call-start = ((), (), s32[]{:S(2)}) async-start(), calls=%async_computation.4 | async-start | bytes 1179648 | tf_op jit(solution)/shard_map/all_gather | solution.py:236
  138.6 19.6 %copy-start.2 = (f32[8,128,256]{2,1,0:T(8,128)S(1)}, f32[8,128,256]{2,1,0:T(8,128)}, u32[]{:S(2)}) copy-start(f32[8,128,256]{2,1,0:T(8,128)} %basis_ref.1) | copy-start | bytes 3145732
  138.6 43.5 %all-gather.9.cloned.1.call-start = ((), (), s32[]{:S(2)}) async-start(), calls=%async_computation.6 | async-start | bytes 1179648 | tf_op jit(solution)/shard_map/all_gather | solution.py:215
  152.8 76.1 %all-gather.11.cloned.1.call-start = ((), (), s32[]{:S(2)}) async-start(), calls=%async_computation.7 | async-start | bytes 1179648 | tf_op jit(solution)/shard_map/all_gather | solution.py:237
  153.6 92.2 %all-gather.7.cloned.1.call-start = ((), (), s32[]{:S(2)}) async-start(), calls=%async_computation.5 | async-start | bytes 2621440 | tf_op jit(solution)/shard_map/all_gather | solution.py:246
  164.0 20.2 %copy-start.1 = (bf16[2,128,256]{2,1,0:T(8,128)(2,1)S(1)}, bf16[2,128,256]{2,1,0:T(8,128)(2,1)}, u32[]{:S(2)}) copy-start(bf16[2,128,256]{2,1,0:T(8,128)(2,1)} %reduce_sum.44.rows_ref) | copy-start | bytes 393220
Sparse Core Ops, SparseCore 0:
  138.7 19.4 all-gather.4
  160.4 21.6 all-gather.8
  183.7 21.7 all-gather.10
  207.8 37.9 all-gather.6

commit v2 on v0

v2 whole, which is shorter than its diff:
```python
import functools

import jax
import jax.numpy as jnp
from jax import lax
from jax.experimental import pallas as pl
from jax.experimental.pallas import tpu as pltpu
from jax.sharding import PartitionSpec as P

beta_one = 0.9
beta_two = 0.95
bias_one = 1.0 - 0.9**10
bias_two = 1.0 - 0.95**10
step_size = 0.5
epsilon = 1e-08
BLOCK = 64
CHUNKS = 1
HIGHEST = lax.Precision.HIGHEST
VMEM_LIMIT = 48 * 1024 * 1024
VMEM = pl.BlockSpec(memory_space=pltpu.VMEM)
SMEM = pl.BlockSpec(memory_space=pltpu.SMEM)
f32 = jnp.float32
bf16 = jnp.bfloat16


def call(kernel, out_shape, args, scalars=0, us=2.0, aliases=None, scratch=()):
    many = isinstance(out_shape, (tuple, list))
    return pl.pallas_call(
        kernel,
        out_shape=out_shape,
        in_specs=[SMEM] * scalars + [VMEM] * (len(args) - scalars),
        out_specs=[VMEM] * len(out_shape) if many else VMEM,
        scratch_shapes=list(scratch),
        input_output_aliases=aliases or {},
        compiler_params=pltpu.CompilerParams(vmem_limit_bytes=VMEM_LIMIT),
        cost_estimate=pl.CostEstimate(
            flops=0, bytes_accessed=int(us * 3_000_000), transcendentals=0
        ),
    )(*args)


def swap(x, axis, mask):
    size = lax.axis_size(axis)
    return lax.ppermute(x, axis, [(i, i ^ mask) for i in range(size)])


def split_kernel(place, grad_ref, *outs, groups, chunks):
    width = outs[0].shape[2]
    for h in range(chunks):
        for k in range(groups):
            start = ((place[0] ^ k) * chunks + h) * width
            columns = pl.ds(pl.multiple_of(start, 128), width)
            outs[h * groups + k][...] = grad_ref[0, :, :, columns]


def sample_kernel(place, grad_ref, sketch_ref, *outs):
    each = outs[0].shape[0]
    for k, out in enumerate(outs):
        for i in range(each):
            m = (place[0] ^ k) * each + i
            out[i] = jnp.dot(
                grad_ref[0, m], sketch_ref[...], preferred_element_type=f32
            ).astype(bf16)


def sum_kernel(*refs):
    out = refs[-1]
    total = refs[0][...].astype(f32)
    for ref in refs[1:-1]:
        total = total + ref[...].astype(f32)
    out[...] = total.astype(bf16)


def gram_kernel(*refs):
    out = refs[-1]
    for i in range(out.shape[0]):
        total = None
        for ref in refs[:-1]:
            term = lax.dot_general(
                ref[i], ref[i], (((0,), (0,)), ((), ())), preferred_element_type=f32
            )
            total = term if total is None else total + term
        out[i] = total


def eliminate(work, j):
    pair, size = work.shape[0], work.shape[1]
    lane = lax.broadcasted_iota(jnp.int32, (BLOCK, 2 * BLOCK), 1)
    sub = lax.broadcasted_iota(jnp.int32, (BLOCK, 2 * BLOCK), 0)
    eye_right = (lane - BLOCK == sub).astype(f32)
    lo = j * BLOCK
    base = lo // 128 * 128
    tiles = []
    for b in range(pair):
        slab = work[b, lo : lo + BLOCK, base : base + 128]
        if lo > base:
            slab = pltpu.roll(slab, 128 - (lo - base), 1)
        tiles.append(jnp.where(lane < BLOCK, slab, eye_right))
    for k in range(BLOCK - 1):
        for b in range(pair):
            tile = tiles[b]
            column = jnp.where(sub[:, :1] > k, tile[:, k : k + 1], 0.0)
            row = tile[k : k + 1, :] * (1.0 / tile[k : k + 1, k : k + 1])
            tiles[b] = tile - column * row
    for b in range(pair):
        tile = tiles[b]
        diagonal = jnp.sum(jnp.where(lane == sub, tile, 0.0), axis=1, keepdims=True)
        inverse = pltpu.roll(tile, BLOCK, 1)[:, :BLOCK] * lax.rsqrt(diagonal)
        solved = jnp.dot(
            inverse, work[b, lo : lo + BLOCK, :], precision=HIGHEST, preferred_element_type=f32
        )
        work[b, lo : lo + BLOCK, size:] = solved[:, size:]
        if lo + BLOCK < size:
            change = lax.dot_general(
                solved[:, :size],
                solved,
                (((0,), (0,)), ((), ())),
                precision=HIGHEST,
                preferred_element_type=f32,
            )
            work[b, lo + BLOCK :, :] = work[b, lo + BLOCK :, :] - change[lo + BLOCK :, :]


def start_kernel(own_ref, other_ref, work):
    pair, size = own_ref.shape[0], own_ref.shape[1]
    row = lax.broadcasted_iota(jnp.int32, (size, size), 0)
    col = lax.broadcasted_iota(jnp.int32, (size, size), 1)
    eye = (row == col).astype(f32)
    for b in range(pair):
        work[b, :, :size] = own_ref[b] + other_ref[b]
        work[b, :, size:] = eye
    eliminate(work, 0)


def middle_kernel(work_in, work, *, j):
    work[...] = work_in[...]
    eliminate(work, j)


def finish_kernel(work_in, rows_ref, out_ref, work, *, j, scale):
    work[...] = work_in[...]
    eliminate(work, j)
    size = work.shape[1]
    for b in range(work.shape[0]):
        basis = lax.dot_general(
            rows_ref[b].astype(f32),
            work[b, :, size:],
            (((1,), (1,)), ((), ())),
            precision=HIGHEST,
            preferred_element_type=f32,
        )
        out_ref[b] = (basis * scale).astype(out_ref.dtype)


def factor(own, other, rows, scale):
    pair, size, _ = own.shape
    shape = jax.ShapeDtypeStruct((pair, size, 2 * size), f32)
    blocks = size // BLOCK
    work = call(start_kernel, shape, (own, other), us=8.0)
    for j in range(1, blocks - 1):
        work = call(functools.partial(middle_kernel, j=j), shape, (work,), us=7.0)
    return call(
        functools.partial(finish_kernel, j=blocks - 1, scale=scale),
        jax.ShapeDtypeStruct(rows.shape, bf16),
        (work, rows),
        us=8.0,
        scratch=[pltpu.VMEM(shape.shape, f32)],
    )


def pick_kernel(place, owner, first_ref, second_ref, mine_ref, other_ref):
    here, core = place[1] * 2 + place[2], place[2]
    capacity = first_ref.shape[0]
    seen = jnp.int32(0)
    at = []
    for m in range(owner.shape[0]):
        at.append(jnp.minimum(seen, capacity - 1))
        seen = seen + (owner[m] == here).astype(jnp.int32)
    for i in range(mine_ref.shape[0]):
        even, odd = at[2 * i], at[2 * i + 1]
        for out, want in ((mine_ref, core), (other_ref, 1 - core)):
            slot = jnp.where(want == 0, even, odd)
            out[i, 0] = first_ref[slot].astype(bf16)
            out[i, 1] = second_ref[slot].astype(bf16)


def merge_kernel(place, owner, mine_ref, other_ref, *outs):
    z, core = place[1], place[2]
    for k, out in enumerate(outs):
        i = z ^ k
        local = owner[2 * i + core] == 2 * z + core
        out[...] = jnp.where(local, mine_ref[i], other_ref[i])


def project_kernel(place, *refs, scale):
    *grad_refs, basis_ref, mine_ref, other_ref = refs
    core = place[2]
    for i in range(mine_ref.shape[0]):
        for out, want in ((other_ref, 1 - core), (mine_ref, core)):
            m = 2 * i + want
            total = grad_refs[0][m].astype(f32)
            for ref in grad_refs[1:]:
                total = total + ref[m].astype(f32)
            product = lax.dot_general(
                (basis_ref[m] * scale).astype(bf16),
                total.astype(bf16),
                (((0,), (0,)), ((), ())),
                preferred_element_type=f32,
            )
            out[i] = product.astype(out.dtype)


def pair_kernel(place, mine_ref, other_ref, *outs):
    for k, out in enumerate(outs):
        i = place[1] ^ k
        out[...] = (mine_ref[i] + other_ref[i].astype(f32)).astype(out.dtype)


def update_kernel(place, owner, rank, *refs, chips, start):
    terms, moments = refs[:chips], refs[chips : 2 * chips]
    update_ref, projected_ref = refs[2 * chips :]
    z, core = place[1], place[2]
    m = 2 * z + core
    projected = terms[0][...].astype(f32)
    for ref in terms[1:]:
        projected = projected + ref[...].astype(f32)
    width = projected.shape[1]
    columns = slice(start, start + width)
    source = (owner[m] // 2) ^ z
    first = moments[0][0, :, columns]
    second = moments[0][1, :, columns]
    for k in range(1, chips):
        first = jnp.where(source == k, moments[k][0, :, columns], first)
        second = jnp.where(source == k, moments[k][1, :, columns], second)
    first_new = beta_one * first.astype(f32) + (1.0 - beta_one) * projected
    second_new = beta_two * second.astype(f32) + (1.0 - beta_two) * projected * projected
    update = (first_new / bias_one) / (jnp.sqrt(second_new / bias_two) + epsilon)
    row = lax.broadcasted_iota(jnp.int32, update.shape, 0)
    update_ref[...] = jnp.where(row < rank[m], update, 0.0).astype(bf16)
    projected_ref[...] = projected.astype(bf16)


def delta_kernel(place, *refs, chips, scale):
    near, far = refs[:chips], refs[chips : 2 * chips]
    basis_ref, out_ref = refs[2 * chips :]
    z, core = place[1], place[2]
    for k in range(chips):
        for ref, want in ((near[k], core), (far[k], 1 - core)):
            m = 2 * (z ^ k) + want
            product = jnp.dot(
                (basis_ref[m] * scale).astype(bf16), ref[...], preferred_element_type=f32
            )
            out_ref[m] = product.astype(bf16)


def weight_kernel(place, weight_ref, *refs, groups, chunks):
    out_ref = refs[-1]
    width = refs[0].shape[2]
    for h in range(chunks):
        for k in range(groups):
            start = ((place[0] ^ k) * chunks + h) * width
            columns = pl.ds(pl.multiple_of(start, 128), width)
            for m in range(out_ref.shape[0]):
                delta = refs[h * groups + k][m].astype(f32)
                old = weight_ref[m, :, columns].astype(f32)
                out_ref[m, :, columns] = (old - step_size * delta).astype(bf16)


def basis_kernel(place, *refs):
    out_ref = refs[-1]
    each = refs[0].shape[0]
    for k, ref in enumerate(refs[:-1]):
        for i in range(each):
            out_ref[(place[0] ^ k) * each + i] = ref[i].astype(f32)


def moment_kernel(place, owner, *refs, chunks):
    projected_refs = refs[:chunks]
    first_ref, second_ref, first_out, second_out = refs[chunks:]
    here = place[1] * 2 + place[2]
    capacity, rank_full, _ = first_out.shape
    width = projected_refs[0].shape[2]
    seen = jnp.int32(0)
    index = [jnp.int32(0)] * capacity
    for m in range(owner.shape[0]):
        hit = owner[m] == here
        for s in range(capacity):
            index[s] = jnp.where(hit & (seen == s), m, index[s])
        seen = seen + hit.astype(jnp.int32)
    for s in range(capacity):
        keep = seen > s
        for h in range(chunks):
            columns = slice(h * width, (h + 1) * width)
            projected = projected_refs[h][index[s]].astype(f32)
            first_new = beta_one * first_ref[s, :, columns] + (1.0 - beta_one) * projected
            second_new = (
                beta_two * second_ref[s, :, columns] + (1.0 - beta_two) * projected * projected
            )
            first_out[s, :, columns] = jnp.where(keep, first_new, 0.0)
            second_out[s, :, columns] = jnp.where(keep, second_new, 0.0)


def per_device(grads, weight, basis, first_moment, second_moment, sketch, owner, rank):
    owners = lax.axis_size("rows")
    groups = lax.axis_size("dp")
    here = lax.axis_index("rows")
    group = lax.axis_index("dp")
    capacity, rank_full, quarter = first_moment.shape
    count, shard, width = weight.shape
    chips = owners // 2
    each = count // groups
    piece = quarter // CHUNKS
    total_rows = shard * owners
    root = float(total_rows) ** 0.5
    inverse_root = float(total_rows) ** (-0.5)
    place = jnp.stack([group, here // 2, here % 2]).astype(jnp.int32)
    struct = jax.ShapeDtypeStruct

    parts = call(
        sample_kernel,
        [struct((each, shard, rank_full), bf16)] * groups,
        (place, grads, sketch),
        scalars=1,
        us=2.0,
    )
    blocks = call(
        functools.partial(split_kernel, groups=groups, chunks=CHUNKS),
        [struct((count, shard, piece), bf16)] * (groups * CHUNKS),
        (place, grads),
        scalars=1,
        us=2.0,
    )
    parts = [parts[0]] + [swap(parts[k], "dp", k) for k in range(1, groups)]
    moved = []
    for h in range(CHUNKS):
        mine = blocks[h * groups : (h + 1) * groups]
        moved.append([mine[0]] + [swap(mine[k], "dp", k) for k in range(1, groups)])

    picked, lent = call(
        pick_kernel,
        [struct((chips, 2, rank_full, quarter), bf16)] * 2,
        (place, owner, first_moment, second_moment),
        scalars=2,
        us=2.5,
    )
    lent = swap(lent, "rows", 1)
    sample = call(sum_kernel, struct((each, shard, rank_full), bf16), tuple(parts), us=0.5)
    samples = [sample] + [swap(sample, "rows", 2 * k) for k in range(1, chips)]
    ready = call(
        merge_kernel,
        [struct((2, rank_full, quarter), bf16)] * chips,
        (place, owner, picked, lent),
        scalars=2,
        us=1.5,
    )
    moments = [ready[0]] + [swap(ready[k], "rows", 2 * k) for k in range(1, chips)]
    gram = call(
        gram_kernel, struct((each, rank_full, rank_full), f32), tuple(samples), us=1.0
    )
    rows_basis = factor(gram, swap(gram, "rows", 1), sample, root)

    deltas, gathered = [], []
    for h in range(CHUNKS):
        mine, other = call(
            functools.partial(project_kernel, scale=inverse_root),
            [struct((chips, rank_full, piece), f32), struct((chips, rank_full, piece), bf16)],
            (place, *moved[h], basis),
            scalars=1,
            us=2.0,
        )
        other = swap(other, "rows", 1)
        terms = call(
            pair_kernel,
            [struct((rank_full, piece), f32)] + [struct((rank_full, piece), bf16)] * (chips - 1),
            (place, mine, other),
            scalars=1,
            us=0.7,
        )
        terms = [terms[0]] + [swap(terms[k], "rows", 2 * k) for k in range(1, chips)]
        update, projected = call(
            functools.partial(update_kernel, chips=chips, start=h * piece),
            [struct((rank_full, piece), bf16)] * 2,
            (place, owner, rank, *terms, *moments),
            scalars=3,
            us=0.7,
        )
        near = [update] + [swap(update, "rows", 2 * k) for k in range(1, chips)]
        far = [swap(x, "rows", 1) for x in near]
        gathered.append(lax.all_gather(projected, "rows", axis=0))
        delta = call(
            functools.partial(delta_kernel, chips=chips, scale=inverse_root),
            struct((count, shard, piece), bf16),
            (place, *near, *far, basis),
            scalars=1,
            us=1.5,
        )
        deltas += [delta] + [swap(delta, "dp", k) for k in range(1, groups)]

    first_out, second_out = call(
        functools.partial(moment_kernel, chunks=CHUNKS),
        [struct(first_moment.shape, f32)] * 2,
        (place, owner, *gathered, first_moment, second_moment),
        scalars=2,
        us=3.0,
    )
    shared = [rows_basis] + [swap(rows_basis, "dp", k) for k in range(1, groups)]
    new_basis = call(
        basis_kernel, struct(basis.shape, f32), (place, *shared), scalars=1, us=1.5
    )
    new_weight = call(
        functools.partial(weight_kernel, groups=groups, chunks=CHUNKS),
        struct(weight.shape, bf16),
        (place, weight, *deltas),
        scalars=1,
        us=3.0,
    )
    return (new_weight, new_basis, first_out, second_out)


def solution(mesh):
    in_specs = (
        P("dp", None, "rows", None),
        P(None, "rows", None),
        P(None, "rows", None),
        P("rows", None, "dp"),
        P("rows", None, "dp"),
        P(),
        P(),
        P(),
    )
    out_specs = (
        P(None, "rows", None),
        P(None, "rows", None),
        P("rows", None, "dp"),
        P("rows", None, "dp"),
    )
    return jax.shard_map(
        per_device, mesh=mesh, in_specs=in_specs, out_specs=out_specs, check_vma=False
    )
```

time: 700 us -> 187 us (0.27)
  waiting for transfers between devices: 337 us -> 85.2 us
  other arithmetic: 222 us -> 0.08 us
  matrix products: 51.7 us -> 0 us
  Pallas kernels: 0 us -> 44.4 us
  local copies, waits for them, and re-layouts: 48.1 us -> 5.12 us
  starting transfers between devices: 22 us -> 37.6 us
    all_to_all x4 -> x0, waiting for transfers between devices: 227 us -> none  [the longest x1 178 us: per_device(): lax.all_to_all(spread_half(place_half, total, capacity, owners), 'rows',...]
    another operation x14 -> x1, other arithmetic: 213 us -> 0.08 us  [per_device(): place = jnp.stack([group, here // 2, here % 2]).astype(jnp.int32)]
    ppermute x0 -> x31, waiting for transfers between devices: none -> 85.2 us  [swap(): return lax.ppermute(x, axis, [(i, i ^ mask) for i in range(size)])]
    psum x1 -> x0, waiting for transfers between devices: 72.9 us -> none  [per_device(): total = lax.psum(grads[0], 'dp').astype(jnp.float32).astype(jnp.bfloat16)]
    pallas_call x0 -> x17, Pallas kernels: none -> 44.4 us  [call(): pl.pallas_call(kernel, out_shape=out_shape, in_specs=[SMEM] * scalars + [...]
    dot_general x8 -> x0, matrix products: 41.2 us -> none  [the longest x1 8.68 us: per_device(): jnp.einsum('cmr,cmd->crd', old_basis, own.astype(jnp.float32), precision=...]
    ppermute x0 -> x31, starting transfers between devices: none -> 37.5 us  [swap(): return lax.ppermute(x, axis, [(i, i ^ mask) for i in range(size)])]
    all_gather x1, waiting for transfers between devices: 36.5 us -> 0.01 us  [per_device(): gathered.append(lax.all_gather(projected, 'rows', axis=0))]
  transfers between devices with their start and end apart: 6 -> 32, of which waited for: 4 -> 17; matrix products, arithmetic and copies ran while one was open for 38% -> 0% of each run, Pallas kernels for 0% -> 21%
where the time goes in v2:
time: 187 us
  waiting for transfers between devices  85.2 us (46%)
  Pallas kernels  44.4 us (24%)
  starting transfers between devices  37.6 us (20%)
  between operations  14.3 us (8%)
  local copies, waits for them, and re-layouts  5.12 us (3%)
    ppermute x31, waiting for transfers between devices, swap(): return lax.ppermute(x, axis, [(i, i ^ mask) for i in range(size)])  85.2 us
    pallas_call x17, Pallas kernels, call(): pl.pallas_call(kernel, out_shape=out_shape, in_specs=[SMEM] * scalars + [...  44.4 us
    ppermute x31, starting transfers between devices, swap(): return lax.ppermute(x, axis, [(i, i ^ mask) for i in range(size)])  37.5 us
    unnamed x24, local copies, waits for them, and re-layouts  5.12 us
  transfers between devices with their start and end apart: 32, of which 17 were waited for; matrix products, arithmetic and copies ran while one was open for 0% of the time, Pallas kernels for 21%

profile of v2, /device:TPU:0, one launch (start us, length us, event | category | flops | bytes accessed | tf_op | source)
XLA Modules:
  0.0 186.7 jit_solution(1840784171038527593)
XLA Ops:
  7.3 1.6 copy-done
  9.7 3.0 %collective-permute-start = (bf16[8,128,256]{2,1,0:T(8,128)(2,1)S(1)}, bf16[8,128,256]{2,1,0:T(8,128)(2,1)S(1)}, u32[]{:S(2)}, u32[]{:S(2)}) collective-permute-start(bf16[8,128,256]{2,1,0:T(8,128)(2,1)S(1)} %get-tuple-element.29), channel_id=1, source_target_pairs={{0,8},{8,0},{16,24},{24,16},{1,9},{9,1},{17,25},{25,17},{2,10},{10... | collective-permute-start | bytes 1572872 | tf_op jit(solution)/shard_map/ppermute | solution.py:44
  12.7 1.5 collective-permute-start.1
  16.4 9.1 %collective-permute-done.refs_1_ = bf16[8,128,256]{2,1,0:T(8,128)(2,1)S(1)} collective-permute-done((bf16[8,128,256]{2,1,0:T(8,128)(2,1)S(1)}, bf16[8,128,256]{2,1,0:T(8,128)(2,1)S(1)}, u32[]{:S(2)}, u32[]{:S(2)}) %collective-permute-start) | collective-permute-done | bytes 524320 | tf_op jit(solution)/shard_map/ppermute | solution.py:44
  25.5 11.9 %collective-permute-done.1.refs_2_ = bf16[8,128,256]{2,1,0:T(8,128)(2,1)S(1)} collective-permute-done((bf16[8,128,256]{2,1,0:T(8,128)(2,1)S(1)}, bf16[8,128,256]{2,1,0:T(8,128)(2,1)S(1)}, u32[]{:S(2)}, u32[]{:S(2)}) %collective-permute-start.1) | collective-permute-done | bytes 524320 | tf_op jit(solution)/shard_map/ppermute | solution.py:44
  38.6 1.9 %collective-permute-done.3.other_ref = bf16[4,256,256]{2,1,0:T(8,128)(2,1)S(1)} collective-permute-done((bf16[4,256,256]{2,1,0:T(8,128)(2,1)S(1)}, bf16[4,256,256]{2,1,0:T(8,128)(2,1)S(1)}, u32[]{:S(2)}, u32[]{:S(2)}) %collective-permute-start.3) | collective-permute-done | bytes 524320 | tf_op jit(solution)/shard_map/ppermute | solution.py:44
  41.1 1.6 collective-permute-start.4
  43.9 2.6 %collective-permute-start.9 = (bf16[2,256,256]{2,1,0:T(8,128)(2,1)S(1)}, bf16[2,256,256]{2,1,0:T(8,128)(2,1)S(1)}, u32[]{:S(2)}, u32[]{:S(2)}) collective-permute-start(bf16[2,256,256]{2,1,0:T(8,128)(2,1)S(1)} %get-tuple-element.42), channel_id=1, source_target_pairs={{0,4},{1,5},{2,6},{3,7},{4,0},{5,1},{6,2},{7,3},{8,12},{9,13},{10,... | collective-permute-start | bytes 786440 | tf_op jit(solution)/shard_map/ppermute | solution.py:44
  47.9 1.7 collective-permute-start.5
  49.6 2.5 %collective-permute-done.4.refs_1_ = bf16[256,256]{1,0:T(8,128)(2,1)S(1)} collective-permute-done((bf16[256,256]{1,0:T(8,128)(2,1)S(1)}, bf16[256,256]{1,0:T(8,128)(2,1)S(1)}, u32[]{:S(2)}, u32[]{:S(2)}) %collective-permute-start.4) | collective-permute-done | bytes 131104 | tf_op jit(solution)/shard_map/ppermute | solution.py:44
  52.1 3.4 %collective-permute-start.6 = (bf16[256,256]{1,0:T(8,128)(2,1)S(1)}, bf16[256,256]{1,0:T(8,128)(2,1)S(1)}, u32[]{:S(2)}, u32[]{:S(2)}) collective-permute-start(bf16[256,256]{1,0:T(8,128)(2,1)S(1)} %get-tuple-element.37), channel_id=1, source_target_pairs={{0,6},{1,7},{2,4},{3,5},{4,2},{5,3},{6,0},{7,1},{8,14},{9,15},{10,... | collective-permute-start | bytes 393224 | tf_op jit(solution)/shard_map/ppermute | solution.py:44
  55.5 23.9 %collective-permute-done.5.refs_2_ = bf16[256,256]{1,0:T(8,128)(2,1)S(1)} collective-permute-done((bf16[256,256]{1,0:T(8,128)(2,1)S(1)}, bf16[256,256]{1,0:T(8,128)(2,1)S(1)}, u32[]{:S(2)}, u32[]{:S(2)}) %collective-permute-start.5) | collective-permute-done | bytes 131104 | tf_op jit(solution)/shard_map/ppermute | solution.py:44
  89.4 1.7 collective-permute-done.23.refs_3_
  91.2 3.7 %collective-permute-start.26 = (bf16[2,128,256]{2,1,0:T(8,128)(2,1)S(1)}, bf16[2,128,256]{2,1,0:T(8,128)(2,1)S(1)}, u32[]{:S(2)}, u32[]{:S(2)}) collective-permute-start(bf16[2,128,256]{2,1,0:T(8,128)(2,1)S(1)} %shard_map.120.refs_0_.rows_ref), channel_id=1, source_target_pairs={{0,6},{1,7},{2,4},{3,5},{4,2},{5,3},{6,0},{7,1},{8,14},{9,15},{10,... | collective-permute-start | bytes 393224 | tf_op jit(solution)/shard_map/ppermute | solution.py:44
  95.9 6.2 %collective-permute-done.26.refs_3_ = bf16[2,128,256]{2,1,0:T(8,128)(2,1)S(1)} collective-permute-done((bf16[2,128,256]{2,1,0:T(8,128)(2,1)S(1)}, bf16[2,128,256]{2,1,0:T(8,128)(2,1)S(1)}, u32[]{:S(2)}, u32[]{:S(2)}) %collective-permute-start.26) | collective-permute-done | bytes 131104 | tf_op jit(solution)/shard_map/ppermute | solution.py:44
  102.0 9.0 %collective-permute-done.25.refs_2_ = bf16[2,128,256]{2,1,0:T(8,128)(2,1)S(1)} collective-permute-done((bf16[2,128,256]{2,1,0:T(8,128)(2,1)S(1)}, bf16[2,128,256]{2,1,0:T(8,128)(2,1)S(1)}, u32[]{:S(2)}, u32[]{:S(2)}) %collective-permute-start.25) | collective-permute-done | bytes 131104 | tf_op jit(solution)/shard_map/ppermute | solution.py:44
  111.6 2.7 %collective-permute-start.13 = (bf16[256,256]{1,0:T(8,128)(2,1)S(1)}, bf16[256,256]{1,0:T(8,128)(2,1)S(1)}, u32[]{:S(2)}, u32[]{:S(2)}) collective-permute-start(bf16[256,256]{1,0:T(8,128)(2,1)S(1)} %get-tuple-element.44.refs_0_), channel_id=1, source_target_pairs={{0,6},{1,7},{2,4},{3,5},{4,2},{5,3},{6,0},{7,1},{8,14},{9,15},{10,... | collective-permute-start | bytes 393224 | tf_op jit(solution)/shard_map/ppermute | solution.py:44
  114.3 1.8 collective-permute-start.11
  116.1 3.8 %collective-permute-done.13.refs_3_ = bf16[256,256]{1,0:T(8,128)(2,1)S(1)} collective-permute-done((bf16[256,256]{1,0:T(8,128)(2,1)S(1)}, bf16[256,256]{1,0:T(8,128)(2,1)S(1)}, u32[]{:S(2)}, u32[]{:S(2)}) %collective-permute-start.13) | collective-permute-done | bytes 131104 | tf_op jit(solution)/shard_map/ppermute | solution.py:44
  119.9 5.3 %collective-permute-done.12.refs_2_ = bf16[256,256]{1,0:T(8,128)(2,1)S(1)} collective-permute-done((bf16[256,256]{1,0:T(8,128)(2,1)S(1)}, bf16[256,256]{1,0:T(8,128)(2,1)S(1)}, u32[]{:S(2)}, u32[]{:S(2)}) %collective-permute-start.12) | collective-permute-done | bytes 131104 | tf_op jit(solution)/shard_map/ppermute | solution.py:44
  127.6 2.6 %collective-permute-start.20 = (bf16[8,128,256]{2,1,0:T(8,128)(2,1)S(1)}, bf16[8,128,256]{2,1,0:T(8,128)(2,1)S(1)}, u32[]{:S(2)}, u32[]{:S(2)}) collective-permute-start(bf16[8,128,256]{2,1,0:T(8,128)(2,1)S(1)} %shard_map.117.refs_0_), channel_id=1, source_target_pairs={{0,24},{8,16},{16,8},{24,0},{1,25},{9,17},{17,9},{25,1},{2,26},{10... | collective-permute-start | bytes 1572872 | tf_op jit(solution)/shard_map/ppermute | solution.py:44
  131.1 7.9 %shard_map.122.work_in = f32[2,256,512]{2,1,0:T(8,128)S(1)} custom-call(f32[2,256,256]{2,1,0:T(8,128)S(1)} %shard_map.121.own_ref, f32[2,256,256]{2,1,0:T(8,128)S(1)} %collective-permute-done.27.other_ref), custom_call_target="tpu_custom_call" | custom-call | bytes 24000000 | tf_op jit(solution)/shard_map/pallas_call | solution.py:28
  139.0 8.0 %shard_map.123.work_in = f32[2,256,512]{2,1,0:T(8,128)S(1)} custom-call(f32[2,256,512]{2,1,0:T(8,128)S(1)} %shard_map.122.work_in), custom_call_target="tpu_custom_call" | custom-call | bytes 21000000 | tf_op jit(solution)/shard_map/pallas_call | solution.py:28
  147.0 8.0 %shard_map.124.work_in = f32[2,256,512]{2,1,0:T(8,128)S(1)} custom-call(f32[2,256,512]{2,1,0:T(8,128)S(1)} %shard_map.123.work_in), custom_call_target="tpu_custom_call" | custom-call | bytes 21000000 | tf_op jit(solution)/shard_map/pallas_call | solution.py:28
  155.0 6.3 %shard_map.125.refs_0_ = bf16[2,128,256]{2,1,0:T(8,128)(2,1)S(1)} custom-call(f32[2,256,512]{2,1,0:T(8,128)S(1)} %shard_map.124.work_in, bf16[2,128,256]{2,1,0:T(8,128)(2,1)S(1)} %shard_map.120.refs_0_.rows_ref), custom_call_target="tpu_custom_call" | custom-call | bytes 24000000 | tf_op jit(solution)/shard_map/pallas_call | solution.py:28
  161.3 2.6 %collective-permute-start.30 = (bf16[2,128,256]{2,1,0:T(8,128)(2,1)S(1)}, bf16[2,128,256]{2,1,0:T(8,128)(2,1)S(1)}, u32[]{:S(2)}, u32[]{:S(2)}) collective-permute-start(bf16[2,128,256]{2,1,0:T(8,128)(2,1)S(1)} %shard_map.125.refs_0_), channel_id=1, source_target_pairs={{0,24},{8,16},{16,8},{24,0},{1,25},{9,17},{17,9},{25,1},{2,26},{10... | collective-permute-start | bytes 393224 | tf_op jit(solution)/shard_map/ppermute | solution.py:44
  164.5 2.8 %collective-permute-done.30.refs_3_ = bf16[2,128,256]{2,1,0:T(8,128)(2,1)S(1)} collective-permute-done((bf16[2,128,256]{2,1,0:T(8,128)(2,1)S(1)}, bf16[2,128,256]{2,1,0:T(8,128)(2,1)S(1)}, u32[]{:S(2)}, u32[]{:S(2)}) %collective-permute-start.30) | collective-permute-done | bytes 131104 | tf_op jit(solution)/shard_map/ppermute | solution.py:44
  167.3 1.6 collective-permute-start.28
  170.0 2.3 %collective-permute-done.28.refs_1_ = bf16[2,128,256]{2,1,0:T(8,128)(2,1)S(1)} collective-permute-done((bf16[2,128,256]{2,1,0:T(8,128)(2,1)S(1)}, bf16[2,128,256]{2,1,0:T(8,128)(2,1)S(1)}, u32[]{:S(2)}, u32[]{:S(2)}) %collective-permute-start.28) | collective-permute-done | bytes 131104 | tf_op jit(solution)/shard_map/ppermute | solution.py:44
  172.3 1.6 shard_map.126
  173.9 2.5 %shard_map.118 = bf16[8,128,1024]{2,1,0:T(8,128)(2,1)} custom-call(s32[3]{0:T(128)S(1)} %pad_add_fusion.place, bf16[8,128,1024]{2,1,0:T(8,128)(2,1)S(1)} %copy-done.7, bf16[8,128,256]{2,1,0:T(8,128)(2,1)S(1)} %shard_map.117.refs_0_, bf16[8,128,256]{2,1,0:T(8,128)(2,1)S(1)} %collective-permute-done.18.refs_1_, ...), custom_call_target="tpu_custom_call" | custom-call | bytes 9000000 | tf_op jit(solution)/shard_map/pallas_call | solution.py:28
  177.6 2.2 %shard_map.127 = (f32[4,256,256]{2,1,0:T(8,128)}, f32[4,256,256]{2,1,0:T(8,128)}) custom-call(s32[3]{0:T(128)S(1)} %pad_add_fusion.place, s32[8]{0:T(128)S(1)} %copy-done.10, bf16[8,256,256]{2,1,0:T(8,128)(2,1)S(1)} %bitcast.4, f32[4,256,256]{2,1,0:T(8,128)S(1)} %copy-done.4, f32[4,256,256]{2,1,0:T(8,128)S(1)} %copy-done.6), custom_call_target="tpu_custom_call" | custom-call | bytes 9000000 | tf_op jit(solution)/shard_map/pallas_call | solution.py:28
  (75 shorter events, 25.2 us)
Async XLA Ops:
  7.2 169.2 %all-gather.3.cloned.1.call-start = ((), (), s32[]{:S(2)}) async-start(), calls=%async_computation | async-start | bytes 1179648 | tf_op jit(solution)/shard_map/all_gather | solution.py:389
  9.7 15.8 %collective-permute-start = (bf16[8,128,256]{2,1,0:T(8,128)(2,1)S(1)}, bf16[8,128,256]{2,1,0:T(8,128)(2,1)S(1)}, u32[]{:S(2)}, u32[]{:S(2)}) collective-permute-start(bf16[8,128,256]{2,1,0:T(8,128)(2,1)S(1)} %get-tuple-element.29), channel_id=1, source_target_pairs={{0,8},{8,0},{16,24},{24,16},{1,9},{9,1},{17,25},{25,17},{2,10},{10... | collective-permute-start | bytes 1572872 | tf_op jit(solution)/shard_map/ppermute | solution.py:44
  12.7 24.6 %collective-permute-start.1 = (bf16[8,128,256]{2,1,0:T(8,128)(2,1)S(1)}, bf16[8,128,256]{2,1,0:T(8,128)(2,1)S(1)}, u32[]{:S(2)}, u32[]{:S(2)}) collective-permute-start(bf16[8,128,256]{2,1,0:T(8,128)(2,1)S(1)} %get-tuple-element.30), channel_id=1, source_target_pairs={{0,16},{8,24},{16,0},{24,8},{1,17},{9,25},{17,1},{25,9},{2,18},{10... | collective-permute-start | bytes 1572872 | tf_op jit(solution)/shard_map/ppermute | solution.py:44
  14.3 23.1 %collective-permute-start.2 = (bf16[8,128,256]{2,1,0:T(8,128)(2,1)S(1)}, bf16[8,128,256]{2,1,0:T(8,128)(2,1)S(1)}, u32[]{:S(2)}, u32[]{:S(2)}) collective-permute-start(bf16[8,128,256]{2,1,0:T(8,128)(2,1)S(1)} %get-tuple-element.31), channel_id=1, source_target_pairs={{0,24},{8,16},{16,8},{24,0},{1,25},{9,17},{17,9},{25,1},{2,26},{10... | collective-permute-start | bytes 1572872 | tf_op jit(solution)/shard_map/ppermute | solution.py:44
  16.3 26.5 %collective-permute-start.7 = (bf16[4,2,256,256]{3,2,1,0:T(8,128)(2,1)S(1)}, bf16[4,2,256,256]{3,2,1,0:T(8,128)(2,1)S(1)}, u32[]{:S(2)}, u32[]{:S(2)}) collective-permute-start(bf16[4,2,256,256]{3,2,1,0:T(8,128)(2,1)S(1)} %get-tuple-element.39), channel_id=1, source_target_pairs={{0,1},{1,0},{2,3},{3,2},{4,5},{5,4},{6,7},{7,6},{8,9},{9,8},{10,11... | collective-permute-start | bytes 3145736 | tf_op jit(solution)/shard_map/ppermute | solution.py:44
  38.5 2.0 %collective-permute-start.3 = (bf16[4,256,256]{2,1,0:T(8,128)(2,1)S(1)}, bf16[4,256,256]{2,1,0:T(8,128)(2,1)S(1)}, u32[]{:S(2)}, u32[]{:S(2)}) collective-permute-start(bf16[4,256,256]{2,1,0:T(8,128)(2,1)S(1)} %get-tuple-element.33), channel_id=1, source_target_pairs={{0,1},{1,0},{2,3},{3,2},{4,5},{5,4},{6,7},{7,6},{8,9},{9,8},{10,11... | collective-permute-start | bytes 1572872 | tf_op jit(solution)/shard_map/ppermute | solution.py:44
  41.1 11.0 %collective-permute-start.4 = (bf16[256,256]{1,0:T(8,128)(2,1)S(1)}, bf16[256,256]{1,0:T(8,128)(2,1)S(1)}, u32[]{:S(2)}, u32[]{:S(2)}) collective-permute-start(bf16[256,256]{1,0:T(8,128)(2,1)S(1)} %get-tuple-element.35), channel_id=1, source_target_pairs={{0,2},{1,3},{2,0},{3,1},{4,6},{5,7},{6,4},{7,5},{8,10},{9,11},{10,... | collective-permute-start | bytes 393224 | tf_op jit(solution)/shard_map/ppermute | solution.py:44
  43.4 35.9 %collective-permute-start.8 = (bf16[2,256,256]{2,1,0:T(8,128)(2,1)S(1)}, bf16[2,256,256]{2,1,0:T(8,128)(2,1)S(1)}, u32[]{:S(2)}, u32[]{:S(2)}) collective-permute-start(bf16[2,256,256]{2,1,0:T(8,128)(2,1)S(1)} %get-tuple-element.41), channel_id=1, source_target_pairs={{0,2},{1,3},{2,0},{3,1},{4,6},{5,7},{6,4},{7,5},{8,10},{9,11},{10,... | collective-permute-start | bytes 786440 | tf_op jit(solution)/shard_map/ppermute | solution.py:44
  43.9 35.4 %collective-permute-start.9 = (bf16[2,256,256]{2,1,0:T(8,128)(2,1)S(1)}, bf16[2,256,256]{2,1,0:T(8,128)(2,1)S(1)}, u32[]{:S(2)}, u32[]{:S(2)}) collective-permute-start(bf16[2,256,256]{2,1,0:T(8,128)(2,1)S(1)} %get-tuple-element.42), channel_id=1, source_target_pairs={{0,4},{1,5},{2,6},{3,7},{4,0},{5,1},{6,2},{7,3},{8,12},{9,13},{10,... | collective-permute-start | bytes 786440 | tf_op jit(solution)/shard_map/ppermute | solution.py:44
  46.5 32.8 %collective-permute-start.10 = (bf16[2,256,256]{2,1,0:T(8,128)(2,1)S(1)}, bf16[2,256,256]{2,1,0:T(8,128)(2,1)S(1)}, u32[]{:S(2)}, u32[]{:S(2)}) collective-permute-start(bf16[2,256,256]{2,1,0:T(8,128)(2,1)S(1)} %get-tuple-element.43), channel_id=1, source_target_pairs={{0,6},{1,7},{2,4},{3,5},{4,2},{5,3},{6,0},{7,1},{8,14},{9,15},{10,... | collective-permute-start | bytes 786440 | tf_op jit(solution)/shard_map/ppermute | solution.py:44
  47.9 31.5 %collective-permute-start.5 = (bf16[256,256]{1,0:T(8,128)(2,1)S(1)}, bf16[256,256]{1,0:T(8,128)(2,1)S(1)}, u32[]{:S(2)}, u32[]{:S(2)}) collective-permute-start(bf16[256,256]{1,0:T(8,128)(2,1)S(1)} %get-tuple-element.36), channel_id=1, source_target_pairs={{0,4},{1,5},{2,6},{3,7},{4,0},{5,1},{6,2},{7,3},{8,12},{9,13},{10,... | collective-permute-start | bytes 393224 | tf_op jit(solution)/shard_map/ppermute | solution.py:44
  52.1 27.3 %collective-permute-start.6 = (bf16[256,256]{1,0:T(8,128)(2,1)S(1)}, bf16[256,256]{1,0:T(8,128)(2,1)S(1)}, u32[]{:S(2)}, u32[]{:S(2)}) collective-permute-start(bf16[256,256]{1,0:T(8,128)(2,1)S(1)} %get-tuple-element.37), channel_id=1, source_target_pairs={{0,6},{1,7},{2,4},{3,5},{4,2},{5,3},{6,0},{7,1},{8,14},{9,15},{10,... | collective-permute-start | bytes 393224 | tf_op jit(solution)/shard_map/ppermute | solution.py:44
  83.1 5.0 %collective-permute-start.21 = (bf16[2,128,256]{2,1,0:T(8,128)(2,1)S(1)}, bf16[2,128,256]{2,1,0:T(8,128)(2,1)S(1)}, u32[]{:S(2)}, u32[]{:S(2)}) collective-permute-start(bf16[2,128,256]{2,1,0:T(8,128)(2,1)S(1)} %get-tuple-element.46), channel_id=1, source_target_pairs={{0,8},{8,0},{16,24},{24,16},{1,9},{9,1},{17,25},{25,17},{2,10},{10... | collective-permute-start | bytes 393224 | tf_op jit(solution)/shard_map/ppermute | solution.py:44
  84.4 5.0 %collective-permute-start.22 = (bf16[2,128,256]{2,1,0:T(8,128)(2,1)S(1)}, bf16[2,128,256]{2,1,0:T(8,128)(2,1)S(1)}, u32[]{:S(2)}, u32[]{:S(2)}) collective-permute-start(bf16[2,128,256]{2,1,0:T(8,128)(2,1)S(1)} %get-tuple-element.47), channel_id=1, source_target_pairs={{0,16},{8,24},{16,0},{24,8},{1,17},{9,25},{17,1},{25,9},{2,18},{10... | collective-permute-start | bytes 393224 | tf_op jit(solution)/shard_map/ppermute | solution.py:44
  85.2 5.9 %collective-permute-start.23 = (bf16[2,128,256]{2,1,0:T(8,128)(2,1)S(1)}, bf16[2,128,256]{2,1,0:T(8,128)(2,1)S(1)}, u32[]{:S(2)}, u32[]{:S(2)}) collective-permute-start(bf16[2,128,256]{2,1,0:T(8,128)(2,1)S(1)} %get-tuple-element.48), channel_id=1, source_target_pairs={{0,24},{8,16},{16,8},{24,0},{1,25},{9,17},{17,9},{25,1},{2,26},{10... | collective-permute-start | bytes 393224 | tf_op jit(solution)/shard_map/ppermute | solution.py:44
  91.2 10.9 %collective-permute-start.26 = (bf16[2,128,256]{2,1,0:T(8,128)(2,1)S(1)}, bf16[2,128,256]{2,1,0:T(8,128)(2,1)S(1)}, u32[]{:S(2)}, u32[]{:S(2)}) collective-permute-start(bf16[2,128,256]{2,1,0:T(8,128)(2,1)S(1)} %shard_map.120.refs_0_.rows_ref), channel_id=1, source_target_pairs={{0,6},{1,7},{2,4},{3,5},{4,2},{5,3},{6,0},{7,1},{8,14},{9,15},{10,... | collective-permute-start | bytes 393224 | tf_op jit(solution)/shard_map/ppermute | solution.py:44
  94.8 16.2 %collective-permute-start.25 = (bf16[2,128,256]{2,1,0:T(8,128)(2,1)S(1)}, bf16[2,128,256]{2,1,0:T(8,128)(2,1)S(1)}, u32[]{:S(2)}, u32[]{:S(2)}) collective-permute-start(bf16[2,128,256]{2,1,0:T(8,128)(2,1)S(1)} %shard_map.120.refs_0_.rows_ref), channel_id=1, source_target_pairs={{0,4},{1,5},{2,6},{3,7},{4,0},{5,1},{6,2},{7,3},{8,12},{9,13},{10,... | collective-permute-start | bytes 393224 | tf_op jit(solution)/shard_map/ppermute | solution.py:44
  95.4 15.7 %collective-permute-start.24 = (bf16[2,128,256]{2,1,0:T(8,128)(2,1)S(1)}, bf16[2,128,256]{2,1,0:T(8,128)(2,1)S(1)}, u32[]{:S(2)}, u32[]{:S(2)}) collective-permute-start(bf16[2,128,256]{2,1,0:T(8,128)(2,1)S(1)} %shard_map.120.refs_0_.rows_ref), channel_id=1, source_target_pairs={{0,2},{1,3},{2,0},{3,1},{4,6},{5,7},{6,4},{7,5},{8,10},{9,11},{10,... | collective-permute-start | bytes 393224 | tf_op jit(solution)/shard_map/ppermute | solution.py:44
  111.5 19.6 %collective-permute-start.27 = (f32[2,256,256]{2,1,0:T(8,128)S(1)}, f32[2,256,256]{2,1,0:T(8,128)S(1)}, u32[]{:S(2)}, u32[]{:S(2)}) collective-permute-start(f32[2,256,256]{2,1,0:T(8,128)S(1)} %shard_map.121.own_ref), channel_id=1, source_target_pairs={{0,1},{1,0},{2,3},{3,2},{4,5},{5,4},{6,7},{7,6},{8,9},{9,8},{10,11... | collective-permute-start | bytes 1572872 | tf_op jit(solution)/shard_map/ppermute | solution.py:44
  111.6 8.3 %collective-permute-start.13 = (bf16[256,256]{1,0:T(8,128)(2,1)S(1)}, bf16[256,256]{1,0:T(8,128)(2,1)S(1)}, u32[]{:S(2)}, u32[]{:S(2)}) collective-permute-start(bf16[256,256]{1,0:T(8,128)(2,1)S(1)} %get-tuple-element.44.refs_0_), channel_id=1, source_target_pairs={{0,6},{1,7},{2,4},{3,5},{4,2},{5,3},{6,0},{7,1},{8,14},{9,15},{10,... | collective-permute-start | bytes 393224 | tf_op jit(solution)/shard_map/ppermute | solution.py:44
  114.3 10.9 %collective-permute-start.12 = (bf16[256,256]{1,0:T(8,128)(2,1)S(1)}, bf16[256,256]{1,0:T(8,128)(2,1)S(1)}, u32[]{:S(2)}, u32[]{:S(2)}) collective-permute-start(bf16[256,256]{1,0:T(8,128)(2,1)S(1)} %get-tuple-element.44.refs_0_), channel_id=1, source_target_pairs={{0,4},{1,5},{2,6},{3,7},{4,0},{5,1},{6,2},{7,3},{8,12},{9,13},{10,... | collective-permute-start | bytes 393224 | tf_op jit(solution)/shard_map/ppermute | solution.py:44
  114.3 10.9 %collective-permute-start.11 = (bf16[256,256]{1,0:T(8,128)(2,1)S(1)}, bf16[256,256]{1,0:T(8,128)(2,1)S(1)}, u32[]{:S(2)}, u32[]{:S(2)}) collective-permute-start(bf16[256,256]{1,0:T(8,128)(2,1)S(1)} %get-tuple-element.44.refs_0_), channel_id=1, source_target_pairs={{0,2},{1,3},{2,0},{3,1},{4,6},{5,7},{6,4},{7,5},{8,10},{9,11},{10,... | collective-permute-start | bytes 393224 | tf_op jit(solution)/shard_map/ppermute | solution.py:44
  116.1 9.6 %collective-permute-start.14 = (bf16[256,256]{1,0:T(8,128)(2,1)S(1)}, bf16[256,256]{1,0:T(8,128)(2,1)S(1)}, u32[]{:S(2)}, u32[]{:S(2)}) collective-permute-start(bf16[256,256]{1,0:T(8,128)(2,1)S(1)} %get-tuple-element.44.refs_0_), channel_id=1, source_target_pairs={{0,1},{1,0},{2,3},{3,2},{4,5},{5,4},{6,7},{7,6},{8,9},{9,8},{10,11... | collective-permute-start | bytes 393224 | tf_op jit(solution)/shard_map/ppermute | solution.py:44
  119.9 5.8 %collective-permute-start.17 = (bf16[256,256]{1,0:T(8,128)(2,1)S(1)}, bf16[256,256]{1,0:T(8,128)(2,1)S(1)}, u32[]{:S(2)}, u32[]{:S(2)}) collective-permute-start(bf16[256,256]{1,0:T(8,128)(2,1)S(1)} %collective-permute-done.13.refs_3_), channel_id=1, source_target_pairs={{0,1},{1,0},{2,3},{3,2},{4,5},{5,4},{6,7},{7,6},{8,9},{9,8},{10,11... | collective-permute-start | bytes 393224 | tf_op jit(solution)/shard_map/ppermute | solution.py:44
  125.2 1.3 collective-permute-start.16
  125.2 1.5 collective-permute-start.15
  127.6 46.3 %collective-permute-start.20 = (bf16[8,128,256]{2,1,0:T(8,128)(2,1)S(1)}, bf16[8,128,256]{2,1,0:T(8,128)(2,1)S(1)}, u32[]{:S(2)}, u32[]{:S(2)}) collective-permute-start(bf16[8,128,256]{2,1,0:T(8,128)(2,1)S(1)} %shard_map.117.refs_0_), channel_id=1, source_target_pairs={{0,24},{8,16},{16,8},{24,0},{1,25},{9,17},{17,9},{25,1},{2,26},{10... | collective-permute-start | bytes 1572872 | tf_op jit(solution)/shard_map/ppermute | solution.py:44
  130.2 43.7 %collective-permute-start.19 = (bf16[8,128,256]{2,1,0:T(8,128)(2,1)S(1)}, bf16[8,128,256]{2,1,0:T(8,128)(2,1)S(1)}, u32[]{:S(2)}, u32[]{:S(2)}) collective-permute-start(bf16[8,128,256]{2,1,0:T(8,128)(2,1)S(1)} %shard_map.117.refs_0_), channel_id=1, source_target_pairs={{0,16},{8,24},{16,0},{24,8},{1,17},{9,25},{17,1},{25,9},{2,18},{10... | collective-permute-start | bytes 1572872 | tf_op jit(solution)/shard_map/ppermute | solution.py:44
  130.7 43.2 %collective-permute-start.18 = (bf16[8,128,256]{2,1,0:T(8,128)(2,1)S(1)}, bf16[8,128,256]{2,1,0:T(8,128)(2,1)S(1)}, u32[]{:S(2)}, u32[]{:S(2)}) collective-permute-start(bf16[8,128,256]{2,1,0:T(8,128)(2,1)S(1)} %shard_map.117.refs_0_), channel_id=1, source_target_pairs={{0,8},{8,0},{16,24},{24,16},{1,9},{9,1},{17,25},{25,17},{2,10},{10... | collective-permute-start | bytes 1572872 | tf_op jit(solution)/shard_map/ppermute | solution.py:44
  161.3 6.0 %collective-permute-start.30 = (bf16[2,128,256]{2,1,0:T(8,128)(2,1)S(1)}, bf16[2,128,256]{2,1,0:T(8,128)(2,1)S(1)}, u32[]{:S(2)}, u32[]{:S(2)}) collective-permute-start(bf16[2,128,256]{2,1,0:T(8,128)(2,1)S(1)} %shard_map.125.refs_0_), channel_id=1, source_target_pairs={{0,24},{8,16},{16,8},{24,0},{1,25},{9,17},{17,9},{25,1},{2,26},{10... | collective-permute-start | bytes 393224 | tf_op jit(solution)/shard_map/ppermute | solution.py:44
  163.9 6.1 %collective-permute-start.29 = (bf16[2,128,256]{2,1,0:T(8,128)(2,1)S(1)}, bf16[2,128,256]{2,1,0:T(8,128)(2,1)S(1)}, u32[]{:S(2)}, u32[]{:S(2)}) collective-permute-start(bf16[2,128,256]{2,1,0:T(8,128)(2,1)S(1)} %shard_map.125.refs_0_), channel_id=1, source_target_pairs={{0,16},{8,24},{16,0},{24,8},{1,17},{9,25},{17,1},{25,9},{2,18},{10... | collective-permute-start | bytes 393224 | tf_op jit(solution)/shard_map/ppermute | solution.py:44
  167.3 5.0 %collective-permute-start.28 = (bf16[2,128,256]{2,1,0:T(8,128)(2,1)S(1)}, bf16[2,128,256]{2,1,0:T(8,128)(2,1)S(1)}, u32[]{:S(2)}, u32[]{:S(2)}) collective-permute-start(bf16[2,128,256]{2,1,0:T(8,128)(2,1)S(1)} %shard_map.125.refs_0_), channel_id=1, source_target_pairs={{0,8},{8,0},{16,24},{24,16},{1,9},{9,1},{17,25},{25,17},{2,10},{10... | collective-permute-start | bytes 393224 | tf_op jit(solution)/shard_map/ppermute | solution.py:44
  (12 other events, 158.6 us)
Sparse Core Ops, SparseCore 0:
  80.9 29.7 all-gather.2

commit v3 on v2

--- a/solution.py
+++ b/solution.py
@@ -23,20 +23,34 @@
 bf16 = jnp.bfloat16
 
 
-def call(kernel, out_shape, args, scalars=0, us=2.0, aliases=None, scratch=()):
-    many = isinstance(out_shape, (tuple, list))
-    return pl.pallas_call(
-        kernel,
-        out_shape=out_shape,
-        in_specs=[SMEM] * scalars + [VMEM] * (len(args) - scalars),
-        out_specs=[VMEM] * len(out_shape) if many else VMEM,
-        scratch_shapes=list(scratch),
-        input_output_aliases=aliases or {},
-        compiler_params=pltpu.CompilerParams(vmem_limit_bytes=VMEM_LIMIT),
-        cost_estimate=pl.CostEstimate(
-            flops=0, bytes_accessed=int(us * 3_000_000), transcendentals=0
-        ),
-    )(*args)
+class Sequence:
+    def __init__(self):
+        self.last = None
+
+    def __call__(self, kernel, out_shape, args, scalars=0, us=2.0, scratch=()):
+        many = isinstance(out_shape, (tuple, list))
+        specs = [SMEM] * scalars + [VMEM] * (len(args) - scalars)
+        body = kernel
+        if self.last is not None:
+            specs = [pl.BlockSpec(memory_space=pl.ANY)] + specs
+            args = (self.last, *args)
+
+            def body(_, *refs):
+                kernel(*refs)
+
+        result = pl.pallas_call(
+            body,
+            out_shape=out_shape,
+            in_specs=specs,
+            out_specs=[VMEM] * len(out_shape) if many else VMEM,
+            scratch_shapes=list(scratch),
+            compiler_params=pltpu.CompilerParams(vmem_limit_bytes=VMEM_LIMIT),
+            cost_estimate=pl.CostEstimate(
+                flops=0, bytes_accessed=int(us * 3_000_000), transcendentals=0
+            ),
+        )(*args)
+        self.last = result[-1] if many else result
+        return result
 
 
 def swap(x, axis, mask):
@@ -71,15 +85,24 @@
     out[...] = total.astype(bf16)
 
 
+def stack_kernel(own_ref, other_ref, out_ref):
+    half = own_ref.shape[0]
+    out_ref[:half] = own_ref[...]
+    out_ref[half:] = other_ref[...]
+
+
 def gram_kernel(*refs):
     out = refs[-1]
-    for i in range(out.shape[0]):
+    each = out.shape[0]
+    for i in range(each):
         total = None
         for ref in refs[:-1]:
-            term = lax.dot_general(
-                ref[i], ref[i], (((0,), (0,)), ((), ())), preferred_element_type=f32
-            )
-            total = term if total is None else total + term
+            for j in range(i, ref.shape[0], each):
+                block = ref[j]
+                term = lax.dot_general(
+                    block, block, (((0,), (0,)), ((), ())), preferred_element_type=f32
+                )
+                total = term if total is None else total + term
         out[i] = total
 
 
@@ -152,22 +175,6 @@
         out_ref[b] = (basis * scale).astype(out_ref.dtype)
 
 
-def factor(own, other, rows, scale):
-    pair, size, _ = own.shape
-    shape = jax.ShapeDtypeStruct((pair, size, 2 * size), f32)
-    blocks = size // BLOCK
-    work = call(start_kernel, shape, (own, other), us=8.0)
-    for j in range(1, blocks - 1):
-        work = call(functools.partial(middle_kernel, j=j), shape, (work,), us=7.0)
-    return call(
-        functools.partial(finish_kernel, j=blocks - 1, scale=scale),
-        jax.ShapeDtypeStruct(rows.shape, bf16),
-        (work, rows),
-        us=8.0,
-        scratch=[pltpu.VMEM(shape.shape, f32)],
-    )
-
-
 def pick_kernel(place, owner, first_ref, second_ref, mine_ref, other_ref):
     here, core = place[1] * 2 + place[2], place[2]
     capacity = first_ref.shape[0]
@@ -176,20 +183,28 @@
     for m in range(owner.shape[0]):
         at.append(jnp.minimum(seen, capacity - 1))
         seen = seen + (owner[m] == here).astype(jnp.int32)
-    for i in range(mine_ref.shape[0]):
-        even, odd = at[2 * i], at[2 * i + 1]
+    chips = mine_ref.shape[0]
+    for i in range(chips):
         for out, want in ((mine_ref, core), (other_ref, 1 - core)):
-            slot = jnp.where(want == 0, even, odd)
+            slot = jnp.int32(0)
+            m = 2 * (place[1] ^ i) + want
+            for j in range(owner.shape[0]):
+                slot = jnp.where(m == j, at[j], slot)
             out[i, 0] = first_ref[slot].astype(bf16)
             out[i, 1] = second_ref[slot].astype(bf16)
 
 
-def merge_kernel(place, owner, mine_ref, other_ref, *outs):
+def merge_kernel(place, owner, mine_ref, other_ref, *outs, bit):
     z, core = place[1], place[2]
-    for k, out in enumerate(outs):
-        i = z ^ k
-        local = owner[2 * i + core] == 2 * z + core
-        out[...] = jnp.where(local, mine_ref[i], other_ref[i])
+    stride = 1 if bit < 0 else 2 << bit
+    split = len(outs)
+    for i in range(mine_ref.shape[0]):
+        source = owner[2 * (z ^ (i * stride)) + core]
+        if bit < 0:
+            local = (source & 1) == core
+        else:
+            local = (((source >> 1) ^ z) >> bit) & 1 == 0
+        outs[i % split][i // split] = jnp.where(local, mine_ref[i], other_ref[i])
 
 
 def project_kernel(place, *refs, scale):
@@ -216,9 +231,9 @@
         out[...] = (mine_ref[i] + other_ref[i].astype(f32)).astype(out.dtype)
 
 
-def update_kernel(place, owner, rank, *refs, chips, start):
-    terms, moments = refs[:chips], refs[chips : 2 * chips]
-    update_ref, projected_ref = refs[2 * chips :]
+def update_kernel(place, rank, *refs, chips, start):
+    terms = refs[:chips]
+    moment_ref, update_ref, projected_ref = refs[chips:]
     z, core = place[1], place[2]
     m = 2 * z + core
     projected = terms[0][...].astype(f32)
@@ -226,12 +241,8 @@
         projected = projected + ref[...].astype(f32)
     width = projected.shape[1]
     columns = slice(start, start + width)
-    source = (owner[m] // 2) ^ z
-    first = moments[0][0, :, columns]
-    second = moments[0][1, :, columns]
-    for k in range(1, chips):
-        first = jnp.where(source == k, moments[k][0, :, columns], first)
-        second = jnp.where(source == k, moments[k][1, :, columns], second)
+    first = moment_ref[0, 0, :, columns]
+    second = moment_ref[0, 1, :, columns]
     first_new = beta_one * first.astype(f32) + (1.0 - beta_one) * projected
     second_new = beta_two * second.astype(f32) + (1.0 - beta_two) * projected * projected
     update = (first_new / bias_one) / (jnp.sqrt(second_new / bias_two) + epsilon)
@@ -316,6 +327,7 @@
     place = jnp.stack([group, here // 2, here % 2]).astype(jnp.int32)
     struct = jax.ShapeDtypeStruct
 
+    call = Sequence()
     parts = call(
         sample_kernel,
         [struct((each, shard, rank_full), bf16)] * groups,
@@ -323,6 +335,7 @@
         scalars=1,
         us=2.0,
     )
+    parts = [parts[0]] + [swap(parts[k], "dp", k) for k in range(1, groups)]
     blocks = call(
         functools.partial(split_kernel, groups=groups, chunks=CHUNKS),
         [struct((count, shard, piece), bf16)] * (groups * CHUNKS),
@@ -330,72 +343,116 @@
         scalars=1,
         us=2.0,
     )
-    parts = [parts[0]] + [swap(parts[k], "dp", k) for k in range(1, groups)]
     moved = []
     for h in range(CHUNKS):
         mine = blocks[h * groups : (h + 1) * groups]
         moved.append([mine[0]] + [swap(mine[k], "dp", k) for k in range(1, groups)])
-
-    picked, lent = call(
+    sample = call(sum_kernel, struct((each, shard, rank_full), bf16), tuple(parts), us=0.5)
+    stacked = sample
+    mask = 1
+    while mask < chips // 2:
+        other = swap(stacked, "rows", 2 * mask)
+        both = struct((2 * stacked.shape[0], shard, rank_full), bf16)
+        stacked = call(stack_kernel, both, (stacked, other), us=0.5)
+        mask *= 2
+    far_samples = swap(stacked, "rows", 2 * mask)
+
+    moment_shape = struct((chips, 2, rank_full, quarter), bf16)
+    moments, lent = call(
         pick_kernel,
-        [struct((chips, 2, rank_full, quarter), bf16)] * 2,
+        [moment_shape] * 2,
         (place, owner, first_moment, second_moment),
         scalars=2,
-        us=2.5,
+        us=2.0,
     )
     lent = swap(lent, "rows", 1)
-    sample = call(sum_kernel, struct((each, shard, rank_full), bf16), tuple(parts), us=0.5)
-    samples = [sample] + [swap(sample, "rows", 2 * k) for k in range(1, chips)]
-    ready = call(
-        merge_kernel,
-        [struct((2, rank_full, quarter), bf16)] * chips,
-        (place, owner, picked, lent),
+    halves = [struct((chips // 2, 2, rank_full, quarter), bf16)] * 2
+    moments, lent_next = call(
+        functools.partial(merge_kernel, bit=-1),
+        halves,
+        (place, owner, moments, lent),
         scalars=2,
+        us=1.0,
+    )
+    lent = swap(lent_next, "rows", 2)
+    gram = call(
+        gram_kernel,
+        struct((each, rank_full, rank_full), f32),
+        (stacked, far_samples),
+        us=1.0,
+    )
+    other_gram = swap(gram, "rows", 1)
+    bit = 0
+    while moments.shape[0] > 1:
+        halves = [struct((moments.shape[0] // 2, 2, rank_full, quarter), bf16)] * 2
+        moments, lent_next = call(
+            functools.partial(merge_kernel, bit=bit),
+            halves,
+            (place, owner, moments, lent),
+            scalars=2,
+            us=1.0,
+        )
+        bit += 1
+        lent = swap(lent_next, "rows", 2 << bit)
+    work_shape = struct((each, rank_full, 2 * rank_full), f32)
+    work = call(start_kernel, work_shape, (gram, other_gram), us=8.0)
+    last = rank_full // BLOCK - 1
+
+    deltas, gathered = [], []
+    h = 0
+    mine, other = call(
+        functools.partial(project_kernel, scale=inverse_root),
+        [struct((chips, rank_full, piece), f32), struct((chips, rank_full, piece), bf16)],
+        (place, *moved[h], basis),
+        scalars=1,
+        us=2.0,
+    )
+    other = swap(other, "rows", 1)
+    terms = call(
+        pair_kernel,
+        [struct((rank_full, piece), f32)] + [struct((rank_full, piece), bf16)] * (chips - 1),
+        (place, mine, other),
+        scalars=1,
+        us=0.7,
+    )
+    terms = [terms[0]] + [swap(terms[k], "rows", 2 * k) for k in range(1, chips)]
+    for j in range(1, 2):
+        work = call(functools.partial(middle_kernel, j=j), work_shape, (work,), us=8.0)
+    moments = call(
+        functools.partial(merge_kernel, bit=bit),
+        [struct((1, 2, rank_full, quarter), bf16)],
+        (place, owner, moments, lent),
+        scalars=2,
+        us=0.5,
+    )[0]
+    update, projected = call(
+        functools.partial(update_kernel, chips=chips, start=h * piece),
+        [struct((rank_full, piece), bf16)] * 2,
+        (place, rank, *terms, moments),
+        scalars=2,
+        us=0.7,
+    )
+    near = [update] + [swap(update, "rows", 2 * k) for k in range(1, chips)]
+    far = [swap(x, "rows", 1) for x in near]
+    gathered.append(lax.all_gather(projected, "rows", axis=0))
+    for j in range(2, last):
+        work = call(functools.partial(middle_kernel, j=j), work_shape, (work,), us=8.0)
+    rows_basis = call(
+        functools.partial(finish_kernel, j=last, scale=root),
+        struct(sample.shape, bf16),
+        (work, sample),
+        us=6.0,
+        scratch=[pltpu.VMEM(work_shape.shape, f32)],
+    )
+    delta = call(
+        functools.partial(delta_kernel, chips=chips, scale=inverse_root),
+        struct((count, shard, piece), bf16),
+        (place, *near, *far, basis),
+        scalars=1,
         us=1.5,
     )
-    moments = [ready[0]] + [swap(ready[k], "rows", 2 * k) for k in range(1, chips)]
-    gram = call(
-        gram_kernel, struct((each, rank_full, rank_full), f32), tuple(samples), us=1.0
-    )
-    rows_basis = factor(gram, swap(gram, "rows", 1), sample, root)
-
-    deltas, gathered = [], []
-    for h in range(CHUNKS):
-        mine, other = call(
-            functools.partial(project_kernel, scale=inverse_root),
-            [struct((chips, rank_full, piece), f32), struct((chips, rank_full, piece), bf16)],
-            (place, *moved[h], basis),
-            scalars=1,
-            us=2.0,
-        )
-        other = swap(other, "rows", 1)
-        terms = call(
-            pair_kernel,
-            [struct((rank_full, piece), f32)] + [struct((rank_full, piece), bf16)] * (chips - 1),
-            (place, mine, other),
-            scalars=1,
-            us=0.7,
-        )
-        terms = [terms[0]] + [swap(terms[k], "rows", 2 * k) for k in range(1, chips)]
-        update, projected = call(
-            functools.partial(update_kernel, chips=chips, start=h * piece),
-            [struct((rank_full, piece), bf16)] * 2,
-            (place, owner, rank, *terms, *moments),
-            scalars=3,
-            us=0.7,
-        )
-        near = [update] + [swap(update, "rows", 2 * k) for k in range(1, chips)]
-        far = [swap(x, "rows", 1) for x in near]
-        gathered.append(lax.all_gather(projected, "rows", axis=0))
-        delta = call(
-            functools.partial(delta_kernel, chips=chips, scale=inverse_root),
-            struct((count, shard, piece), bf16),
-            (place, *near, *far, basis),
-            scalars=1,
-            us=1.5,
-        )
-        deltas += [delta] + [swap(delta, "dp", k) for k in range(1, groups)]
-
+    deltas += [delta] + [swap(delta, "dp", k) for k in range(1, groups)]
+    shared = [rows_basis] + [swap(rows_basis, "dp", k) for k in range(1, groups)]
     first_out, second_out = call(
         functools.partial(moment_kernel, chunks=CHUNKS),
         [struct(first_moment.shape, f32)] * 2,
@@ -403,7 +460,6 @@
         scalars=2,
         us=3.0,
     )
-    shared = [rows_basis] + [swap(rows_basis, "dp", k) for k in range(1, groups)]
     new_basis = call(
         basis_kernel, struct(basis.shape, f32), (place, *shared), scalars=1, us=1.5
     )

time: 187 us -> 185 us (0.989)
  starting transfers between devices: 37.6 us -> 29.1 us
  local copies, waits for them, and re-layouts: 5.12 us -> 7.76 us
  Pallas kernels: 44.4 us -> 46.6 us
    ppermute x31 -> x29, starting transfers between devices: 37.5 us -> 29 us  [swap(): return lax.ppermute(x, axis, [(i, i ^ mask) for i in range(size)])]
    unnamed x24, local copies, waits for them, and re-layouts: 5.12 us -> 7.76 us
    pallas_call x17 -> x20, Pallas kernels: 44.4 us -> 46.6 us  [__call__(): pl.pallas_call(body, out_shape=out_shape, in_specs=specs, out_specs=[VMEM...]
    ppermute x31 -> x29, waiting for transfers between devices: 85.2 us -> 86.9 us  [swap(): return lax.ppermute(x, axis, [(i, i ^ mask) for i in range(size)])]
  transfers between devices with their start and end apart: 32 -> 30, of which waited for: 17 -> 15; matrix products, arithmetic and copies ran while one was open for 0% -> 0% of each run, Pallas kernels for 21% -> 21%
where the time goes in v3:
time: 185 us
  waiting for transfers between devices  86.9 us (47%)
  Pallas kernels  46.6 us (25%)
  starting transfers between devices  29.1 us (16%)
  between operations  14.3 us (8%)
  local copies, waits for them, and re-layouts  7.76 us (4%)
    ppermute x29, waiting for transfers between devices, swap(): return lax.ppermute(x, axis, [(i, i ^ mask) for i in range(size)])  86.9 us
    pallas_call x20, Pallas kernels, __call__(): pl.pallas_call(body, out_shape=out_shape, in_specs=specs, out_specs=[VMEM...  46.6 us
    ppermute x29, starting transfers between devices, swap(): return lax.ppermute(x, axis, [(i, i ^ mask) for i in range(size)])  29 us
    unnamed x24, local copies, waits for them, and re-layouts  7.76 us
  transfers between devices with their start and end apart: 30, of which 15 were waited for; matrix products, arithmetic and copies ran while one was open for 0% of the time, Pallas kernels for 21%

profile of v3, /device:TPU:0, one launch (start us, length us, event | category | flops | bytes accessed | tf_op | source)
XLA Modules:
  0.0 184.8 jit_solution(6804014400244832600)
XLA Ops:
  7.3 1.6 copy-done
  11.2 3.0 %collective-permute-start = (bf16[2,128,256]{2,1,0:T(8,128)(2,1)S(1)}, bf16[2,128,256]{2,1,0:T(8,128)(2,1)S(1)}, u32[]{:S(2)}, u32[]{:S(2)}) collective-permute-start(bf16[2,128,256]{2,1,0:T(8,128)(2,1)S(1)} %get-tuple-element.31), channel_id=1, source_target_pairs={{0,8},{8,0},{16,24},{24,16},{1,9},{9,1},{17,25},{25,17},{2,10},{10... | collective-permute-start | bytes 393224 | tf_op jit(solution)/shard_map/ppermute | solution.py:58
  14.3 1.5 collective-permute-start.1
  16.6 1.5 collective-permute-done.refs_1_
  18.2 3.9 %collective-permute-done.1.refs_2_ = bf16[2,128,256]{2,1,0:T(8,128)(2,1)S(1)} collective-permute-done((bf16[2,128,256]{2,1,0:T(8,128)(2,1)S(1)}, bf16[2,128,256]{2,1,0:T(8,128)(2,1)S(1)}, u32[]{:S(2)}, u32[]{:S(2)}) %collective-permute-start.1) | collective-permute-done | bytes 131104 | tf_op jit(solution)/shard_map/ppermute | solution.py:58
  22.1 1.6 collective-permute-start.3
  23.7 3.4 %collective-permute-done.3.refs_1_ = bf16[2,128,256]{2,1,0:T(8,128)(2,1)S(1)} collective-permute-done((bf16[2,128,256]{2,1,0:T(8,128)(2,1)S(1)}, bf16[2,128,256]{2,1,0:T(8,128)(2,1)S(1)}, u32[]{:S(2)}, u32[]{:S(2)}) %collective-permute-start.3) | collective-permute-done | bytes 131104 | tf_op jit(solution)/shard_map/ppermute | solution.py:58
  28.1 2.6 %collective-permute-start.5 = (bf16[4,128,256]{2,1,0:T(8,128)(2,1)S(1)}, bf16[4,128,256]{2,1,0:T(8,128)(2,1)S(1)}, u32[]{:S(2)}, u32[]{:S(2)}) collective-permute-start(bf16[4,128,256]{2,1,0:T(8,128)(2,1)S(1)} %shard_map.114._.refs_0_), channel_id=1, source_target_pairs={{0,4},{1,5},{2,6},{3,7},{4,0},{5,1},{6,2},{7,3},{8,12},{9,13},{10,... | collective-permute-start | bytes 786440 | tf_op jit(solution)/shard_map/ppermute | solution.py:58
  31.4 1.6 collective-permute-start.6
  33.0 10.4 %collective-permute-done.5.refs_1_ = bf16[4,128,256]{2,1,0:T(8,128)(2,1)S(1)} collective-permute-done((bf16[4,128,256]{2,1,0:T(8,128)(2,1)S(1)}, bf16[4,128,256]{2,1,0:T(8,128)(2,1)S(1)}, u32[]{:S(2)}, u32[]{:S(2)}) %collective-permute-start.5) | collective-permute-done | bytes 262176 | tf_op jit(solution)/shard_map/ppermute | solution.py:58
  46.1 1.4 collective-permute-start.10
  47.5 2.4 %collective-permute-done.6.refs_3_ = bf16[2,2,256,256]{3,2,1,0:T(8,128)(2,1)S(1)} collective-permute-done((bf16[2,2,256,256]{3,2,1,0:T(8,128)(2,1)S(1)}, bf16[2,2,256,256]{3,2,1,0:T(8,128)(2,1)S(1)}, u32[]{:S(2)}, u32[]{:S(2)}) %collective-permute-start.6) | collective-permute-done | bytes 524320 | tf_op jit(solution)/shard_map/ppermute | solution.py:58
  50.6 7.9 %shard_map.119._.refs_0_ = f32[2,256,512]{2,1,0:T(8,128)S(1)} custom-call(bf16[1,2,256,256]{3,2,1,0:T(8,128)(2,1)S(1)} %get-tuple-element.37._, f32[2,256,256]{2,1,0:T(8,128)S(1)} %shard_map.117._.refs_0_, f32[2,256,256]{2,1,0:T(8,128)S(1)} %collective-permute-done.7.refs_1_), custom_call_target="tpu_custom_call" | custom-call | bytes 24000000 | tf_op jit(solution)/shard_map/pallas_call | solution.py:41
  58.7 10.1 %collective-permute-done.9.refs_3_ = bf16[8,128,256]{2,1,0:T(8,128)(2,1)S(1)} collective-permute-done((bf16[8,128,256]{2,1,0:T(8,128)(2,1)S(1)}, bf16[8,128,256]{2,1,0:T(8,128)(2,1)S(1)}, u32[]{:S(2)}, u32[]{:S(2)}) %collective-permute-start.9) | collective-permute-done | bytes 524320 | tf_op jit(solution)/shard_map/ppermute | solution.py:58
  68.8 1.6 collective-permute-done.10.refs_4_
  71.7 1.8 collective-permute-done.11.refs_2_
  74.2 2.3 %collective-permute-start.13 = (bf16[256,256]{1,0:T(8,128)(2,1)S(1)}, bf16[256,256]{1,0:T(8,128)(2,1)S(1)}, u32[]{:S(2)}, u32[]{:S(2)}) collective-permute-start(bf16[256,256]{1,0:T(8,128)(2,1)S(1)} %get-tuple-element.46), channel_id=1, source_target_pairs={{0,2},{1,3},{2,0},{3,1},{4,6},{5,7},{6,4},{7,5},{8,10},{9,11},{10,... | collective-permute-start | bytes 393224 | tf_op jit(solution)/shard_map/ppermute | solution.py:58
  76.5 1.8 collective-permute-start.14
  79.0 8.0 %shard_map.122._.refs_0_ = f32[2,256,512]{2,1,0:T(8,128)S(1)} custom-call(bf16[256,256]{1,0:T(8,128)(2,1)S(1)} %get-tuple-element.43._, f32[2,256,512]{2,1,0:T(8,128)S(1)} %shard_map.119._.refs_0_), custom_call_target="tpu_custom_call" | custom-call | bytes 24000000 | tf_op jit(solution)/shard_map/pallas_call | solution.py:41
  86.9 6.1 %collective-permute-done.12.refs_3_ = bf16[1,2,256,256]{3,2,1,0:T(8,128)(2,1)S(1)} collective-permute-done((bf16[1,2,256,256]{3,2,1,0:T(8,128)(2,1)S(1)}, bf16[1,2,256,256]{3,2,1,0:T(8,128)(2,1)S(1)}, u32[]{:S(2)}, u32[]{:S(2)}) %collective-permute-start.12) | collective-permute-done | bytes 262176 | tf_op jit(solution)/shard_map/ppermute | solution.py:58
  93.6 2.2 %collective-permute-done.14.refs_4_ = bf16[256,256]{1,0:T(8,128)(2,1)S(1)} collective-permute-done((bf16[256,256]{1,0:T(8,128)(2,1)S(1)}, bf16[256,256]{1,0:T(8,128)(2,1)S(1)}, u32[]{:S(2)}, u32[]{:S(2)}) %collective-permute-start.14) | collective-permute-done | bytes 131104 | tf_op jit(solution)/shard_map/ppermute | solution.py:58
  98.0 3.6 %collective-permute-start.17 = (bf16[256,256]{1,0:T(8,128)(2,1)S(1)}, bf16[256,256]{1,0:T(8,128)(2,1)S(1)}, u32[]{:S(2)}, u32[]{:S(2)}) collective-permute-start(bf16[256,256]{1,0:T(8,128)(2,1)S(1)} %get-tuple-element.49.refs_1_), channel_id=1, source_target_pairs={{0,4},{1,5},{2,6},{3,7},{4,0},{5,1},{6,2},{7,3},{8,12},{9,13},{10,... | collective-permute-start | bytes 393224 | tf_op jit(solution)/shard_map/ppermute | solution.py:58
  101.6 3.3 %collective-permute-done.18.refs_4_ = bf16[256,256]{1,0:T(8,128)(2,1)S(1)} collective-permute-done((bf16[256,256]{1,0:T(8,128)(2,1)S(1)}, bf16[256,256]{1,0:T(8,128)(2,1)S(1)}, u32[]{:S(2)}, u32[]{:S(2)}) %collective-permute-start.18) | collective-permute-done | bytes 131104 | tf_op jit(solution)/shard_map/ppermute | solution.py:58
  104.9 15.5 %collective-permute-done.17.refs_3_ = bf16[256,256]{1,0:T(8,128)(2,1)S(1)} collective-permute-done((bf16[256,256]{1,0:T(8,128)(2,1)S(1)}, bf16[256,256]{1,0:T(8,128)(2,1)S(1)}, u32[]{:S(2)}, u32[]{:S(2)}) %collective-permute-start.17) | collective-permute-done | bytes 131104 | tf_op jit(solution)/shard_map/ppermute | solution.py:58
  120.9 8.0 %shard_map.125._.refs_0_ = f32[2,256,512]{2,1,0:T(8,128)S(1)} custom-call(bf16[256,256]{1,0:T(8,128)(2,1)} %get-tuple-element.48._, f32[2,256,512]{2,1,0:T(8,128)S(1)} %shard_map.122._.refs_0_), custom_call_target="tpu_custom_call" | custom-call | bytes 24000000 | tf_op jit(solution)/shard_map/pallas_call | solution.py:41
  128.9 6.3 %shard_map.126._.refs_1_ = bf16[2,128,256]{2,1,0:T(8,128)(2,1)S(1)} custom-call(f32[2,256,512]{2,1,0:T(8,128)S(1)} %shard_map.125._.refs_0_, f32[2,256,512]{2,1,0:T(8,128)S(1)} %shard_map.125._.refs_0_, bf16[2,128,256]{2,1,0:T(8,128)(2,1)S(1)} %shard_map.113._.refs_0_.refs_1_), custom_call_target="tpu_custom_call" | custom-call | bytes 18000000 | tf_op jit(solution)/shard_map/pallas_call | solution.py:41
  137.3 2.4 %collective-permute-start.26 = (bf16[8,128,256]{2,1,0:T(8,128)(2,1)S(1)}, bf16[8,128,256]{2,1,0:T(8,128)(2,1)}, u32[]{:S(2)}, u32[]{:S(2)}) collective-permute-start(bf16[8,128,256]{2,1,0:T(8,128)(2,1)S(1)} %shard_map.127._.refs_2_), channel_id=1, source_target_pairs={{0,8},{8,0},{16,24},{24,16},{1,9},{9,1},{17,25},{25,17},{2,10},{10... | collective-permute-start | bytes 1572872 | tf_op jit(solution)/shard_map/ppermute | solution.py:58
  141.1 24.0 %collective-permute-done.25.refs_4_ = bf16[2,128,256]{2,1,0:T(8,128)(2,1)S(1)} collective-permute-done((bf16[2,128,256]{2,1,0:T(8,128)(2,1)S(1)}, bf16[2,128,256]{2,1,0:T(8,128)(2,1)S(1)}, u32[]{:S(2)}, u32[]{:S(2)}) %collective-permute-start.25) | collective-permute-done | bytes 131104 | tf_op jit(solution)/shard_map/ppermute | solution.py:58
  167.6 2.2 %shard_map.128 = (f32[4,256,256]{2,1,0:T(8,128)}, f32[4,256,256]{2,1,0:T(8,128)}) custom-call(bf16[8,128,256]{2,1,0:T(8,128)(2,1)S(1)} %shard_map.127._.refs_2_, s32[3]{0:T(128)S(1)} %pad_add_fusion.place.refs_0_, s32[8]{0:T(128)S(1)} %copy-done.10, bf16[8,256,256]{2,1,0:T(8,128)(2,1)S(1)} %bitcast.4, f32[4,256,256]{2,1,0:T(8,128)S(1)} %copy-done.2, ...), custom_call_target="tpu_custom_call" | custom-call | bytes 9000000 | tf_op jit(solution)/shard_map/pallas_call | solution.py:41
  170.2 1.4 copy-done.7
  171.6 2.0 %shard_map.129._ = f32[8,128,256]{2,1,0:T(8,128)} custom-call(f32[4,256,256]{2,1,0:T(8,128)S(1)} %copy-done.7, s32[3]{0:T(128)S(1)} %pad_add_fusion.place.refs_0_, bf16[2,128,256]{2,1,0:T(8,128)(2,1)S(1)} %shard_map.126._.refs_1_, bf16[2,128,256]{2,1,0:T(8,128)(2,1)} %collective-permute-done.23.refs_2_, ...), custom_call_target="tpu_custom_call" | custom-call | bytes 4500000 | tf_op jit(solution)/shard_map/pallas_call | solution.py:41
  174.8 3.2 %shard_map.130 = bf16[8,128,1024]{2,1,0:T(8,128)(2,1)} custom-call(f32[8,128,256]{2,1,0:T(8,128)S(1)} %copy-done.5, s32[3]{0:T(128)S(1)} %pad_add_fusion.place.refs_0_, bf16[8,128,1024]{2,1,0:T(8,128)(2,1)S(1)} %copy-done.6, bf16[8,128,256]{2,1,0:T(8,128)(2,1)S(1)} %shard_map.127._.refs_2_, bf16[8,128,256]{2,1,0:T(8,128)(2,1)} %collective-permute-done.26.refs_3_, ...), custom_call_target="tpu_custom_call" | custom-call | bytes 9000000 | tf_op jit(solution)/shard_map/pallas_call | solution.py:41
  (74 shorter events, 21.9 us)
Async XLA Ops:
  7.2 158.0 %all-gather.3.cloned.1.call-start = ((), (), s32[]{:S(2)}) async-start(), calls=%async_computation | async-start | bytes 1179648 | tf_op jit(solution)/shard_map/all_gather | solution.py:437
  11.2 6.9 %collective-permute-start = (bf16[2,128,256]{2,1,0:T(8,128)(2,1)S(1)}, bf16[2,128,256]{2,1,0:T(8,128)(2,1)S(1)}, u32[]{:S(2)}, u32[]{:S(2)}) collective-permute-start(bf16[2,128,256]{2,1,0:T(8,128)(2,1)S(1)} %get-tuple-element.31), channel_id=1, source_target_pairs={{0,8},{8,0},{16,24},{24,16},{1,9},{9,1},{17,25},{25,17},{2,10},{10... | collective-permute-start | bytes 393224 | tf_op jit(solution)/shard_map/ppermute | solution.py:58
  14.3 7.8 %collective-permute-start.1 = (bf16[2,128,256]{2,1,0:T(8,128)(2,1)S(1)}, bf16[2,128,256]{2,1,0:T(8,128)(2,1)S(1)}, u32[]{:S(2)}, u32[]{:S(2)}) collective-permute-start(bf16[2,128,256]{2,1,0:T(8,128)(2,1)S(1)} %get-tuple-element.32), channel_id=1, source_target_pairs={{0,16},{8,24},{16,0},{24,8},{1,17},{9,25},{17,1},{25,9},{2,18},{10... | collective-permute-start | bytes 393224 | tf_op jit(solution)/shard_map/ppermute | solution.py:58
  15.8 6.3 %collective-permute-start.2 = (bf16[2,128,256]{2,1,0:T(8,128)(2,1)S(1)}, bf16[2,128,256]{2,1,0:T(8,128)(2,1)S(1)}, u32[]{:S(2)}, u32[]{:S(2)}) collective-permute-start(bf16[2,128,256]{2,1,0:T(8,128)(2,1)S(1)} %get-tuple-element.28._), channel_id=1, source_target_pairs={{0,24},{8,16},{16,8},{24,0},{1,25},{9,17},{17,9},{25,1},{2,26},{10... | collective-permute-start | bytes 393224 | tf_op jit(solution)/shard_map/ppermute | solution.py:58
  22.1 5.0 %collective-permute-start.3 = (bf16[2,128,256]{2,1,0:T(8,128)(2,1)S(1)}, bf16[2,128,256]{2,1,0:T(8,128)(2,1)S(1)}, u32[]{:S(2)}, u32[]{:S(2)}) collective-permute-start(bf16[2,128,256]{2,1,0:T(8,128)(2,1)S(1)} %shard_map.113._.refs_0_.refs_1_), channel_id=1, source_target_pairs={{0,2},{1,3},{2,0},{3,1},{4,6},{5,7},{6,4},{7,5},{8,10},{9,11},{10,... | collective-permute-start | bytes 393224 | tf_op jit(solution)/shard_map/ppermute | solution.py:58
  28.0 2.7 %collective-permute-start.4 = (bf16[4,2,256,256]{3,2,1,0:T(8,128)(2,1)S(1)}, bf16[4,2,256,256]{3,2,1,0:T(8,128)(2,1)S(1)}, u32[]{:S(2)}, u32[]{:S(2)}) collective-permute-start(bf16[4,2,256,256]{3,2,1,0:T(8,128)(2,1)S(1)} %get-tuple-element.33._), channel_id=1, source_target_pairs={{0,1},{1,0},{2,3},{3,2},{4,5},{5,4},{6,7},{7,6},{8,9},{9,8},{10,11... | collective-permute-start | bytes 3145736 | tf_op jit(solution)/shard_map/ppermute | solution.py:58
  28.1 15.3 %collective-permute-start.5 = (bf16[4,128,256]{2,1,0:T(8,128)(2,1)S(1)}, bf16[4,128,256]{2,1,0:T(8,128)(2,1)S(1)}, u32[]{:S(2)}, u32[]{:S(2)}) collective-permute-start(bf16[4,128,256]{2,1,0:T(8,128)(2,1)S(1)} %shard_map.114._.refs_0_), channel_id=1, source_target_pairs={{0,4},{1,5},{2,6},{3,7},{4,0},{5,1},{6,2},{7,3},{8,12},{9,13},{10,... | collective-permute-start | bytes 786440 | tf_op jit(solution)/shard_map/ppermute | solution.py:58
  31.4 18.6 %collective-permute-start.6 = (bf16[2,2,256,256]{3,2,1,0:T(8,128)(2,1)S(1)}, bf16[2,2,256,256]{3,2,1,0:T(8,128)(2,1)S(1)}, u32[]{:S(2)}, u32[]{:S(2)}) collective-permute-start(bf16[2,2,256,256]{3,2,1,0:T(8,128)(2,1)S(1)} %get-tuple-element.35._), channel_id=1, source_target_pairs={{0,2},{1,3},{2,0},{3,1},{4,6},{5,7},{6,4},{7,5},{8,10},{9,11},{10,... | collective-permute-start | bytes 1572872 | tf_op jit(solution)/shard_map/ppermute | solution.py:58
  43.9 26.6 %copy-start.1 = (f32[8,128,256]{2,1,0:T(8,128)S(1)}, f32[8,128,256]{2,1,0:T(8,128)}, u32[]{:S(2)}) copy-start(f32[8,128,256]{2,1,0:T(8,128)} %refs_9_.1) | copy-start | bytes 3145732
  43.9 6.7 %collective-permute-start.7 = (f32[2,256,256]{2,1,0:T(8,128)S(1)}, f32[2,256,256]{2,1,0:T(8,128)S(1)}, u32[]{:S(2)}, u32[]{:S(2)}) collective-permute-start(f32[2,256,256]{2,1,0:T(8,128)S(1)} %shard_map.117._.refs_0_), channel_id=1, source_target_pairs={{0,1},{1,0},{2,3},{3,2},{4,5},{5,4},{6,7},{7,6},{8,9},{9,8},{10,11... | collective-permute-start | bytes 1572872 | tf_op jit(solution)/shard_map/ppermute | solution.py:58
  44.0 14.8 %collective-permute-start.8 = (bf16[8,128,256]{2,1,0:T(8,128)(2,1)S(1)}, bf16[8,128,256]{2,1,0:T(8,128)(2,1)S(1)}, u32[]{:S(2)}, u32[]{:S(2)}) collective-permute-start(bf16[8,128,256]{2,1,0:T(8,128)(2,1)S(1)} %get-tuple-element.39), channel_id=1, source_target_pairs={{0,8},{8,0},{16,24},{24,16},{1,9},{9,1},{17,25},{25,17},{2,10},{10... | collective-permute-start | bytes 1572872 | tf_op jit(solution)/shard_map/ppermute | solution.py:58
  45.2 23.6 %collective-permute-start.9 = (bf16[8,128,256]{2,1,0:T(8,128)(2,1)S(1)}, bf16[8,128,256]{2,1,0:T(8,128)(2,1)S(1)}, u32[]{:S(2)}, u32[]{:S(2)}) collective-permute-start(bf16[8,128,256]{2,1,0:T(8,128)(2,1)S(1)} %get-tuple-element.40), channel_id=1, source_target_pairs={{0,16},{8,24},{16,0},{24,8},{1,17},{9,25},{17,1},{25,9},{2,18},{10... | collective-permute-start | bytes 1572872 | tf_op jit(solution)/shard_map/ppermute | solution.py:58
  46.1 24.4 %collective-permute-start.10 = (bf16[8,128,256]{2,1,0:T(8,128)(2,1)S(1)}, bf16[8,128,256]{2,1,0:T(8,128)(2,1)S(1)}, u32[]{:S(2)}, u32[]{:S(2)}) collective-permute-start(bf16[8,128,256]{2,1,0:T(8,128)(2,1)S(1)} %get-tuple-element.29._), channel_id=1, source_target_pairs={{0,24},{8,16},{16,8},{24,0},{1,25},{9,17},{17,9},{25,1},{2,26},{10... | collective-permute-start | bytes 1572872 | tf_op jit(solution)/shard_map/ppermute | solution.py:58
  71.6 2.0 %collective-permute-start.11 = (bf16[4,256,256]{2,1,0:T(8,128)(2,1)S(1)}, bf16[4,256,256]{2,1,0:T(8,128)(2,1)S(1)}, u32[]{:S(2)}, u32[]{:S(2)}) collective-permute-start(bf16[4,256,256]{2,1,0:T(8,128)(2,1)S(1)} %get-tuple-element.41._), channel_id=1, source_target_pairs={{0,1},{1,0},{2,3},{3,2},{4,5},{5,4},{6,7},{7,6},{8,9},{9,8},{10,11... | collective-permute-start | bytes 1572872 | tf_op jit(solution)/shard_map/ppermute | solution.py:58
  71.7 21.3 %collective-permute-start.12 = (bf16[1,2,256,256]{3,2,1,0:T(8,128)(2,1)S(1)}, bf16[1,2,256,256]{3,2,1,0:T(8,128)(2,1)S(1)}, u32[]{:S(2)}, u32[]{:S(2)}) collective-permute-start(bf16[1,2,256,256]{3,2,1,0:T(8,128)(2,1)S(1)} %get-tuple-element.37._), channel_id=1, source_target_pairs={{0,4},{1,5},{2,6},{3,7},{4,0},{5,1},{6,2},{7,3},{8,12},{9,13},{10,... | collective-permute-start | bytes 786440 | tf_op jit(solution)/shard_map/ppermute | solution.py:58
  74.2 21.6 %copy-start.11 = (s32[8]{0:T(128)S(1)}, s32[8]{0:T(128)}, u32[]{:S(2)}) copy-start(s32[8]{0:T(128)} %refs_1_.13) | copy-start | bytes 100
  74.2 19.3 %collective-permute-start.13 = (bf16[256,256]{1,0:T(8,128)(2,1)S(1)}, bf16[256,256]{1,0:T(8,128)(2,1)S(1)}, u32[]{:S(2)}, u32[]{:S(2)}) collective-permute-start(bf16[256,256]{1,0:T(8,128)(2,1)S(1)} %get-tuple-element.46), channel_id=1, source_target_pairs={{0,2},{1,3},{2,0},{3,1},{4,6},{5,7},{6,4},{7,5},{8,10},{9,11},{10,... | collective-permute-start | bytes 393224 | tf_op jit(solution)/shard_map/ppermute | solution.py:58
  76.5 19.3 %collective-permute-start.14 = (bf16[256,256]{1,0:T(8,128)(2,1)S(1)}, bf16[256,256]{1,0:T(8,128)(2,1)S(1)}, u32[]{:S(2)}, u32[]{:S(2)}) collective-permute-start(bf16[256,256]{1,0:T(8,128)(2,1)S(1)} %get-tuple-element.47), channel_id=1, source_target_pairs={{0,4},{1,5},{2,6},{3,7},{4,0},{5,1},{6,2},{7,3},{8,12},{9,13},{10,... | collective-permute-start | bytes 393224 | tf_op jit(solution)/shard_map/ppermute | solution.py:58
  78.3 17.4 %collective-permute-start.15 = (bf16[256,256]{1,0:T(8,128)(2,1)S(1)}, bf16[256,256]{1,0:T(8,128)(2,1)S(1)}, u32[]{:S(2)}, u32[]{:S(2)}) collective-permute-start(bf16[256,256]{1,0:T(8,128)(2,1)S(1)} %get-tuple-element.43._), channel_id=1, source_target_pairs={{0,6},{1,7},{2,4},{3,5},{4,2},{5,3},{6,0},{7,1},{8,14},{9,15},{10,... | collective-permute-start | bytes 393224 | tf_op jit(solution)/shard_map/ppermute | solution.py:58
  97.1 7.8 %collective-permute-start.18 = (bf16[256,256]{1,0:T(8,128)(2,1)S(1)}, bf16[256,256]{1,0:T(8,128)(2,1)S(1)}, u32[]{:S(2)}, u32[]{:S(2)}) collective-permute-start(bf16[256,256]{1,0:T(8,128)(2,1)S(1)} %get-tuple-element.49.refs_1_), channel_id=1, source_target_pairs={{0,6},{1,7},{2,4},{3,5},{4,2},{5,3},{6,0},{7,1},{8,14},{9,15},{10,... | collective-permute-start | bytes 393224 | tf_op jit(solution)/shard_map/ppermute | solution.py:58
  98.0 22.4 %collective-permute-start.17 = (bf16[256,256]{1,0:T(8,128)(2,1)S(1)}, bf16[256,256]{1,0:T(8,128)(2,1)S(1)}, u32[]{:S(2)}, u32[]{:S(2)}) collective-permute-start(bf16[256,256]{1,0:T(8,128)(2,1)S(1)} %get-tuple-element.49.refs_1_), channel_id=1, source_target_pairs={{0,4},{1,5},{2,6},{3,7},{4,0},{5,1},{6,2},{7,3},{8,12},{9,13},{10,... | collective-permute-start | bytes 393224 | tf_op jit(solution)/shard_map/ppermute | solution.py:58
  101.6 18.8 %collective-permute-start.16 = (bf16[256,256]{1,0:T(8,128)(2,1)S(1)}, bf16[256,256]{1,0:T(8,128)(2,1)S(1)}, u32[]{:S(2)}, u32[]{:S(2)}) collective-permute-start(bf16[256,256]{1,0:T(8,128)(2,1)S(1)} %get-tuple-element.49.refs_1_), channel_id=1, source_target_pairs={{0,2},{1,3},{2,0},{3,1},{4,6},{5,7},{6,4},{7,5},{8,10},{9,11},{10,... | collective-permute-start | bytes 393224 | tf_op jit(solution)/shard_map/ppermute | solution.py:58
  101.6 33.6 %collective-permute-start.19 = (bf16[256,256]{1,0:T(8,128)(2,1)S(1)}, bf16[256,256]{1,0:T(8,128)(2,1)S(1)}, u32[]{:S(2)}, u32[]{:S(2)}) collective-permute-start(bf16[256,256]{1,0:T(8,128)(2,1)S(1)} %get-tuple-element.49.refs_1_), channel_id=1, source_target_pairs={{0,1},{1,0},{2,3},{3,2},{4,5},{5,4},{6,7},{7,6},{8,9},{9,8},{10,11... | collective-permute-start | bytes 393224 | tf_op jit(solution)/shard_map/ppermute | solution.py:58
  104.9 30.4 %collective-permute-start.22 = (bf16[256,256]{1,0:T(8,128)(2,1)S(1)}, bf16[256,256]{1,0:T(8,128)(2,1)S(1)}, u32[]{:S(2)}, u32[]{:S(2)}) collective-permute-start(bf16[256,256]{1,0:T(8,128)(2,1)S(1)} %collective-permute-done.18.refs_4_), channel_id=1, source_target_pairs={{0,1},{1,0},{2,3},{3,2},{4,5},{5,4},{6,7},{7,6},{8,9},{9,8},{10,11... | collective-permute-start | bytes 393224 | tf_op jit(solution)/shard_map/ppermute | solution.py:58
  120.3 14.9 %collective-permute-start.21 = (bf16[256,256]{1,0:T(8,128)(2,1)S(1)}, bf16[256,256]{1,0:T(8,128)(2,1)S(1)}, u32[]{:S(2)}, u32[]{:S(2)}) collective-permute-start(bf16[256,256]{1,0:T(8,128)(2,1)S(1)} %collective-permute-done.17.refs_3_), channel_id=1, source_target_pairs={{0,1},{1,0},{2,3},{3,2},{4,5},{5,4},{6,7},{7,6},{8,9},{9,8},{10,11... | collective-permute-start | bytes 393224 | tf_op jit(solution)/shard_map/ppermute | solution.py:58
  120.4 14.9 %collective-permute-start.20 = (bf16[256,256]{1,0:T(8,128)(2,1)S(1)}, bf16[256,256]{1,0:T(8,128)(2,1)S(1)}, u32[]{:S(2)}, u32[]{:S(2)}) collective-permute-start(bf16[256,256]{1,0:T(8,128)(2,1)S(1)} %collective-permute-done.16.refs_2_), channel_id=1, source_target_pairs={{0,1},{1,0},{2,3},{3,2},{4,5},{5,4},{6,7},{7,6},{8,9},{9,8},{10,11... | collective-permute-start | bytes 393224 | tf_op jit(solution)/shard_map/ppermute | solution.py:58
  136.1 37.4 %collective-permute-start.28 = (bf16[8,128,256]{2,1,0:T(8,128)(2,1)S(1)}, bf16[8,128,256]{2,1,0:T(8,128)(2,1)S(1)}, u32[]{:S(2)}, u32[]{:S(2)}) collective-permute-start(bf16[8,128,256]{2,1,0:T(8,128)(2,1)S(1)} %shard_map.127._.refs_2_), channel_id=1, source_target_pairs={{0,24},{8,16},{16,8},{24,0},{1,25},{9,17},{17,9},{25,1},{2,26},{10... | collective-permute-start | bytes 1572872 | tf_op jit(solution)/shard_map/ppermute | solution.py:58
  136.8 36.7 %collective-permute-start.27 = (bf16[8,128,256]{2,1,0:T(8,128)(2,1)S(1)}, bf16[8,128,256]{2,1,0:T(8,128)(2,1)}, u32[]{:S(2)}, u32[]{:S(2)}) collective-permute-start(bf16[8,128,256]{2,1,0:T(8,128)(2,1)S(1)} %shard_map.127._.refs_2_), channel_id=1, source_target_pairs={{0,16},{8,24},{16,0},{24,8},{1,17},{9,25},{17,1},{25,9},{2,18},{10... | collective-permute-start | bytes 1572872 | tf_op jit(solution)/shard_map/ppermute | solution.py:58
  137.3 36.3 %collective-permute-start.26 = (bf16[8,128,256]{2,1,0:T(8,128)(2,1)S(1)}, bf16[8,128,256]{2,1,0:T(8,128)(2,1)}, u32[]{:S(2)}, u32[]{:S(2)}) collective-permute-start(bf16[8,128,256]{2,1,0:T(8,128)(2,1)S(1)} %shard_map.127._.refs_2_), channel_id=1, source_target_pairs={{0,8},{8,0},{16,24},{24,16},{1,9},{9,1},{17,25},{25,17},{2,10},{10... | collective-permute-start | bytes 1572872 | tf_op jit(solution)/shard_map/ppermute | solution.py:58
  139.7 25.4 %collective-permute-start.25 = (bf16[2,128,256]{2,1,0:T(8,128)(2,1)S(1)}, bf16[2,128,256]{2,1,0:T(8,128)(2,1)S(1)}, u32[]{:S(2)}, u32[]{:S(2)}) collective-permute-start(bf16[2,128,256]{2,1,0:T(8,128)(2,1)S(1)} %shard_map.126._.refs_1_), channel_id=1, source_target_pairs={{0,24},{8,16},{16,8},{24,0},{1,25},{9,17},{17,9},{25,1},{2,26},{10... | collective-permute-start | bytes 393224 | tf_op jit(solution)/shard_map/ppermute | solution.py:58
  140.3 29.4 %collective-permute-start.24 = (bf16[2,128,256]{2,1,0:T(8,128)(2,1)S(1)}, bf16[2,128,256]{2,1,0:T(8,128)(2,1)S(1)}, u32[]{:S(2)}, u32[]{:S(2)}) collective-permute-start(bf16[2,128,256]{2,1,0:T(8,128)(2,1)S(1)} %shard_map.126._.refs_1_), channel_id=1, source_target_pairs={{0,16},{8,24},{16,0},{24,8},{1,17},{9,25},{17,1},{25,9},{2,18},{10... | collective-permute-start | bytes 393224 | tf_op jit(solution)/shard_map/ppermute | solution.py:58
  165.1 5.1 %collective-permute-start.23 = (bf16[2,128,256]{2,1,0:T(8,128)(2,1)S(1)}, bf16[2,128,256]{2,1,0:T(8,128)(2,1)}, u32[]{:S(2)}, u32[]{:S(2)}) collective-permute-start(bf16[2,128,256]{2,1,0:T(8,128)(2,1)S(1)} %shard_map.126._.refs_1_), channel_id=1, source_target_pairs={{0,8},{8,0},{16,24},{24,16},{1,9},{9,1},{17,25},{25,17},{2,10},{10... | collective-permute-start | bytes 393224 | tf_op jit(solution)/shard_map/ppermute | solution.py:58
  (10 other events, 59.4 us)
Sparse Core Ops, SparseCore 0:
  97.2 24.7 all-gather.2

commit v4 on v3

--- a/solution.py
+++ b/solution.py
@@ -14,7 +14,7 @@
 step_size = 0.5
 epsilon = 1e-08
 BLOCK = 64
-CHUNKS = 1
+COST = 10_000
 HIGHEST = lax.Precision.HIGHEST
 VMEM_LIMIT = 48 * 1024 * 1024
 VMEM = pl.BlockSpec(memory_space=pltpu.VMEM)
@@ -27,16 +27,19 @@
     def __init__(self):
         self.last = None
 
-    def __call__(self, kernel, out_shape, args, scalars=0, us=2.0, scratch=()):
+    def __call__(self, kernel, out_shape, args, scalars=0, us=2.0, scratch=(), after=()):
         many = isinstance(out_shape, (tuple, list))
         specs = [SMEM] * scalars + [VMEM] * (len(args) - scalars)
         body = kernel
         if self.last is not None:
-            specs = [pl.BlockSpec(memory_space=pl.ANY)] + specs
-            args = (self.last, *args)
-
-            def body(_, *refs):
-                kernel(*refs)
+            after = (self.last, *after)
+        unread = len(after)
+        if unread:
+            specs = [pl.BlockSpec(memory_space=pl.ANY)] * unread + specs
+            args = (*after, *args)
+
+            def body(*refs):
+                kernel(*refs[unread:])
 
         result = pl.pallas_call(
             body,
@@ -46,7 +49,7 @@
             scratch_shapes=list(scratch),
             compiler_params=pltpu.CompilerParams(vmem_limit_bytes=VMEM_LIMIT),
             cost_estimate=pl.CostEstimate(
-                flops=0, bytes_accessed=int(us * 3_000_000), transcendentals=0
+                flops=0, bytes_accessed=int(us * COST), transcendentals=0
             ),
         )(*args)
         self.last = result[-1] if many else result
@@ -67,28 +70,41 @@
             outs[h * groups + k][...] = grad_ref[0, :, :, columns]
 
 
-def sample_kernel(place, grad_ref, sketch_ref, *outs):
-    each = outs[0].shape[0]
-    for k, out in enumerate(outs):
+def sample_kernel(place, grad_ref, sketch_ref, keep_ref, send_ref):
+    half, each = keep_ref.shape[0], keep_ref.shape[1]
+    for k in range(2 * half):
+        out = (keep_ref, send_ref)[k % 2]
         for i in range(each):
             m = (place[0] ^ k) * each + i
-            out[i] = jnp.dot(
-                grad_ref[0, m], sketch_ref[...], preferred_element_type=f32
-            ).astype(bf16)
-
-
-def sum_kernel(*refs):
+            product = jnp.dot(grad_ref[0, m], sketch_ref[...], preferred_element_type=f32)
+            out[k // 2, i] = product.astype(out.dtype)
+
+
+def halve_kernel(keep_ref, other_ref, *outs):
+    for k in range(keep_ref.shape[0]):
+        total = keep_ref[k] + other_ref[k].astype(f32)
+        out = outs[k % len(outs)]
+        out[k // len(outs)] = total.astype(out.dtype)
+
+
+def add_kernel(*refs):
     out = refs[-1]
-    total = refs[0][...].astype(f32)
-    for ref in refs[1:-1]:
-        total = total + ref[...].astype(f32)
-    out[...] = total.astype(bf16)
+    for m in range(out.shape[0]):
+        total = refs[0][m].astype(f32)
+        for ref in refs[1:-1]:
+            total = total + ref[m].astype(f32)
+        out[m] = total
 
 
 def stack_kernel(own_ref, other_ref, out_ref):
     half = own_ref.shape[0]
     out_ref[:half] = own_ref[...]
     out_ref[half:] = other_ref[...]
+
+
+def gather_kernel(*refs):
+    for k, ref in enumerate(refs[:-1]):
+        refs[-1][k] = ref[...]
 
 
 def gram_kernel(*refs):
@@ -231,9 +247,9 @@
         out[...] = (mine_ref[i] + other_ref[i].astype(f32)).astype(out.dtype)
 
 
-def update_kernel(place, rank, *refs, chips, start):
+def update_kernel(place, owner, rank, *refs, chips, bit, start):
     terms = refs[:chips]
-    moment_ref, update_ref, projected_ref = refs[chips:]
+    moment_ref, lent_ref, update_ref, projected_ref = refs[chips:]
     z, core = place[1], place[2]
     m = 2 * z + core
     projected = terms[0][...].astype(f32)
@@ -241,8 +257,9 @@
         projected = projected + ref[...].astype(f32)
     width = projected.shape[1]
     columns = slice(start, start + width)
-    first = moment_ref[0, 0, :, columns]
-    second = moment_ref[0, 1, :, columns]
+    local = (((owner[m] >> 1) ^ z) >> bit) & 1 == 0
+    first = jnp.where(local, moment_ref[0, 0, :, columns], lent_ref[0, 0, :, columns])
+    second = jnp.where(local, moment_ref[0, 1, :, columns], lent_ref[0, 1, :, columns])
     first_new = beta_one * first.astype(f32) + (1.0 - beta_one) * projected
     second_new = beta_two * second.astype(f32) + (1.0 - beta_two) * projected * projected
     update = (first_new / bias_one) / (jnp.sqrt(second_new / bias_two) + epsilon)
@@ -252,14 +269,14 @@
 
 
 def delta_kernel(place, *refs, chips, scale):
-    near, far = refs[:chips], refs[chips : 2 * chips]
-    basis_ref, out_ref = refs[2 * chips :]
+    near, far, basis_ref, projected_ref, out_ref, passed_ref = refs
     z, core = place[1], place[2]
+    passed_ref[...] = projected_ref[...]
     for k in range(chips):
-        for ref, want in ((near[k], core), (far[k], 1 - core)):
+        for ref, want in ((near, core), (far, 1 - core)):
             m = 2 * (z ^ k) + want
             product = jnp.dot(
-                (basis_ref[m] * scale).astype(bf16), ref[...], preferred_element_type=f32
+                (basis_ref[m] * scale).astype(bf16), ref[k], preferred_element_type=f32
             )
             out_ref[m] = product.astype(bf16)
 
@@ -320,7 +337,6 @@
     count, shard, width = weight.shape
     chips = owners // 2
     each = count // groups
-    piece = quarter // CHUNKS
     total_rows = shard * owners
     root = float(total_rows) ** 0.5
     inverse_root = float(total_rows) ** (-0.5)
@@ -328,148 +344,136 @@
     struct = jax.ShapeDtypeStruct
 
     call = Sequence()
-    parts = call(
-        sample_kernel,
-        [struct((each, shard, rank_full), bf16)] * groups,
-        (place, grads, sketch),
-        scalars=1,
-        us=2.0,
-    )
-    parts = [parts[0]] + [swap(parts[k], "dp", k) for k in range(1, groups)]
-    blocks = call(
-        functools.partial(split_kernel, groups=groups, chunks=CHUNKS),
-        [struct((count, shard, piece), bf16)] * (groups * CHUNKS),
-        (place, grads),
-        scalars=1,
-        us=2.0,
-    )
-    moved = []
-    for h in range(CHUNKS):
-        mine = blocks[h * groups : (h + 1) * groups]
-        moved.append([mine[0]] + [swap(mine[k], "dp", k) for k in range(1, groups)])
-    sample = call(sum_kernel, struct((each, shard, rank_full), bf16), tuple(parts), us=0.5)
-    stacked = sample
-    mask = 1
-    while mask < chips // 2:
-        other = swap(stacked, "rows", 2 * mask)
-        both = struct((2 * stacked.shape[0], shard, rank_full), bf16)
-        stacked = call(stack_kernel, both, (stacked, other), us=0.5)
-        mask *= 2
-    far_samples = swap(stacked, "rows", 2 * mask)
-
-    moment_shape = struct((chips, 2, rank_full, quarter), bf16)
+    half = chips
     moments, lent = call(
         pick_kernel,
-        [moment_shape] * 2,
+        [struct((half, 2, rank_full, quarter), bf16)] * 2,
         (place, owner, first_moment, second_moment),
         scalars=2,
-        us=2.0,
     )
     lent = swap(lent, "rows", 1)
-    halves = [struct((chips // 2, 2, rank_full, quarter), bf16)] * 2
-    moments, lent_next = call(
+    blocks = call(
+        functools.partial(split_kernel, groups=groups, chunks=1),
+        [struct((count, shard, quarter), bf16)] * groups,
+        (place, grads),
+        scalars=1,
+    )
+    keep, send = call(
+        sample_kernel,
+        [struct((groups // 2, each, shard, rank_full), kind) for kind in (f32, bf16)],
+        (place, grads, sketch),
+        scalars=1,
+    )
+    half //= 2
+    moments, lent = call(
         functools.partial(merge_kernel, bit=-1),
-        halves,
+        [struct((half, 2, rank_full, quarter), bf16)] * 2,
         (place, owner, moments, lent),
         scalars=2,
-        us=1.0,
-    )
-    lent = swap(lent_next, "rows", 2)
-    gram = call(
-        gram_kernel,
-        struct((each, rank_full, rank_full), f32),
-        (stacked, far_samples),
-        us=1.0,
-    )
-    other_gram = swap(gram, "rows", 1)
+    )
+    lent = swap(lent, "rows", 2)
+    sides = [1 << i for i in range(groups.bit_length() - 1)]
+    corners = [k for k in range(1, groups) if k not in sides]
+    beside = [swap(blocks[k], "dp", k) for k in sides]
+    send = swap(send, "dp", 1)
+    part = groups // 2
+    mask = 1
+    while part > 1:
+        part //= 2
+        keep, send = call(
+            halve_kernel,
+            [struct((part, each, shard, rank_full), kind) for kind in (f32, bf16)],
+            (keep, send),
+        )
+        mask *= 2
+        send = swap(send, "dp", mask)
+    total = call(add_kernel, struct((count, shard, quarter), f32), (blocks[0], *beside))
+    across = [swap(blocks[k], "dp", k) for k in corners]
     bit = 0
-    while moments.shape[0] > 1:
-        halves = [struct((moments.shape[0] // 2, 2, rank_full, quarter), bf16)] * 2
-        moments, lent_next = call(
+    while half > 1:
+        half //= 2
+        moments, lent = call(
             functools.partial(merge_kernel, bit=bit),
-            halves,
+            [struct((half, 2, rank_full, quarter), bf16)] * 2,
             (place, owner, moments, lent),
             scalars=2,
-            us=1.0,
         )
         bit += 1
-        lent = swap(lent_next, "rows", 2 << bit)
-    work_shape = struct((each, rank_full, 2 * rank_full), f32)
-    work = call(start_kernel, work_shape, (gram, other_gram), us=8.0)
-    last = rank_full // BLOCK - 1
-
-    deltas, gathered = [], []
-    h = 0
+        lent = swap(lent, "rows", 2 << bit)
+    sample = call(
+        halve_kernel,
+        [struct((1, each, shard, rank_full), bf16)],
+        (keep, send),
+    )[0].reshape(each, shard, rank_full)
     mine, other = call(
         functools.partial(project_kernel, scale=inverse_root),
-        [struct((chips, rank_full, piece), f32), struct((chips, rank_full, piece), bf16)],
-        (place, *moved[h], basis),
-        scalars=1,
-        us=2.0,
+        [struct((chips, rank_full, quarter), f32), struct((chips, rank_full, quarter), bf16)],
+        (place, total, *across, basis),
+        scalars=1,
+        after=(lent,),
     )
     other = swap(other, "rows", 1)
+    mask = 1
+    arrived = swap(sample, "rows", 2)
     terms = call(
         pair_kernel,
-        [struct((rank_full, piece), f32)] + [struct((rank_full, piece), bf16)] * (chips - 1),
+        [struct((rank_full, quarter), f32)] + [struct((rank_full, quarter), bf16)] * (chips - 1),
         (place, mine, other),
         scalars=1,
-        us=0.7,
     )
     terms = [terms[0]] + [swap(terms[k], "rows", 2 * k) for k in range(1, chips)]
-    for j in range(1, 2):
-        work = call(functools.partial(middle_kernel, j=j), work_shape, (work,), us=8.0)
-    moments = call(
-        functools.partial(merge_kernel, bit=bit),
-        [struct((1, 2, rank_full, quarter), bf16)],
-        (place, owner, moments, lent),
-        scalars=2,
-        us=0.5,
-    )[0]
+    stacked = sample
+    while mask < chips // 2:
+        both = struct((2 * stacked.shape[0], shard, rank_full), bf16)
+        stacked = call(stack_kernel, both, (stacked, arrived))
+        mask *= 2
+        arrived = swap(stacked, "rows", 2 * mask)
+    work_shape = struct((each, rank_full, 2 * rank_full), f32)
+    last = rank_full // BLOCK - 1
     update, projected = call(
-        functools.partial(update_kernel, chips=chips, start=h * piece),
-        [struct((rank_full, piece), bf16)] * 2,
-        (place, rank, *terms, moments),
-        scalars=2,
-        us=0.7,
+        functools.partial(update_kernel, chips=chips, bit=bit, start=0),
+        [struct((rank_full, quarter), bf16)] * 2,
+        (place, owner, rank, *terms, moments, lent),
+        scalars=3,
     )
     near = [update] + [swap(update, "rows", 2 * k) for k in range(1, chips)]
-    far = [swap(x, "rows", 1) for x in near]
-    gathered.append(lax.all_gather(projected, "rows", axis=0))
-    for j in range(2, last):
-        work = call(functools.partial(middle_kernel, j=j), work_shape, (work,), us=8.0)
+    gram = call(
+        gram_kernel, struct((each, rank_full, rank_full), f32), (stacked, arrived)
+    )
+    other_gram = swap(gram, "rows", 1)
+    work = call(start_kernel, work_shape, (gram, other_gram))
+    near = call(gather_kernel, struct((chips, rank_full, quarter), bf16), tuple(near))
+    far = swap(near, "rows", 1)
+    delta, projected = call(
+        functools.partial(delta_kernel, chips=chips, scale=inverse_root),
+        [struct((count, shard, quarter), bf16), struct((rank_full, quarter), bf16)],
+        (place, near, far, basis, projected),
+        scalars=1,
+    )
+    deltas = [delta] + [swap(delta, "dp", k) for k in range(1, groups)]
+    gathered = lax.all_gather(projected, "rows", axis=0)
+    for j in range(1, last):
+        work = call(functools.partial(middle_kernel, j=j), work_shape, (work,))
     rows_basis = call(
         functools.partial(finish_kernel, j=last, scale=root),
         struct(sample.shape, bf16),
         (work, sample),
-        us=6.0,
         scratch=[pltpu.VMEM(work_shape.shape, f32)],
     )
-    delta = call(
-        functools.partial(delta_kernel, chips=chips, scale=inverse_root),
-        struct((count, shard, piece), bf16),
-        (place, *near, *far, basis),
-        scalars=1,
-        us=1.5,
-    )
-    deltas += [delta] + [swap(delta, "dp", k) for k in range(1, groups)]
     shared = [rows_basis] + [swap(rows_basis, "dp", k) for k in range(1, groups)]
     first_out, second_out = call(
-        functools.partial(moment_kernel, chunks=CHUNKS),
+        functools.partial(moment_kernel, chunks=1),
         [struct(first_moment.shape, f32)] * 2,
-        (place, owner, *gathered, first_moment, second_moment),
+        (place, owner, gathered, first_moment, second_moment),
         scalars=2,
-        us=3.0,
-    )
-    new_basis = call(
-        basis_kernel, struct(basis.shape, f32), (place, *shared), scalars=1, us=1.5
     )
     new_weight = call(
-        functools.partial(weight_kernel, groups=groups, chunks=CHUNKS),
+        functools.partial(weight_kernel, groups=groups, chunks=1),
         struct(weight.shape, bf16),
         (place, weight, *deltas),
         scalars=1,
-        us=3.0,
-    )
+    )
+    new_basis = call(basis_kernel, struct(basis.shape, f32), (place, *shared), scalars=1)
     return (new_weight, new_basis, first_out, second_out)
 
 

time: 185 us -> 149 us (0.81)
  waiting for transfers between devices: 86.9 us -> 45.8 us
  starting transfers between devices: 29.1 us -> 34 us
    ppermute x29 -> x25, waiting for transfers between devices: 86.9 us -> 45.8 us  [swap(): return lax.ppermute(x, axis, [(i, i ^ mask) for i in range(size)])]
    ppermute x29 -> x25, starting transfers between devices: 29 us -> 34 us  [swap(): return lax.ppermute(x, axis, [(i, i ^ mask) for i in range(size)])]
    unnamed x24 -> x28, local copies, waits for them, and re-layouts: 7.76 us -> 7.44 us
    pallas_call x20 -> x22, Pallas kernels: 46.6 us -> 46.3 us  [__call__(): pl.pallas_call(body, out_shape=out_shape, in_specs=specs, out_specs=[VMEM...]
  transfers between devices with their start and end apart: 30 -> 26, of which waited for: 15 -> 9; matrix products, arithmetic and copies ran while one was open for 0% -> 0% of each run, Pallas kernels for 21% -> 27%
where the time goes in v4:
time: 149 us; the launch traced here: 148 us
  Pallas kernels  46.3 us (31%)
  waiting for transfers between devices  45.8 us (31%)
  starting transfers between devices  34 us (23%)
  between operations  14.4 us (10%)
  local copies, waits for them, and re-layouts  7.44 us (5%)
    pallas_call x22, Pallas kernels, __call__(): pl.pallas_call(body, out_shape=out_shape, in_specs=specs, out_specs=[VMEM...  46.3 us
    ppermute x25, waiting for transfers between devices, swap(): return lax.ppermute(x, axis, [(i, i ^ mask) for i in range(size)])  45.8 us
    ppermute x25, starting transfers between devices, swap(): return lax.ppermute(x, axis, [(i, i ^ mask) for i in range(size)])  34 us
    unnamed x28, local copies, waits for them, and re-layouts  7.44 us
  transfers between devices with their start and end apart: 26, of which 9 were waited for; matrix products, arithmetic and copies ran while one was open for 0% of the time, Pallas kernels for 27%

profile of v4, /device:TPU:0, one launch (start us, length us, event | category | flops | bytes accessed | tf_op | source)
XLA Modules:
  0.0 148.0 jit_solution(3143446539810712809)
XLA Ops:
  12.7 2.6 %collective-permute-start.2 = (bf16[8,128,256]{2,1,0:T(8,128)(2,1)S(1)}, bf16[8,128,256]{2,1,0:T(8,128)(2,1)S(1)}, u32[]{:S(2)}, u32[]{:S(2)}) collective-permute-start(bf16[8,128,256]{2,1,0:T(8,128)(2,1)S(1)} %get-tuple-element.38), channel_id=1, source_target_pairs={{0,8},{8,0},{16,24},{24,16},{1,9},{9,1},{17,25},{25,17},{2,10},{10... | collective-permute-start | bytes 1572872 | tf_op jit(solution)/shard_map/ppermute | solution.py:61
  15.3 1.5 %collective-permute-start.3 = (bf16[8,128,256]{2,1,0:T(8,128)(2,1)S(1)}, bf16[8,128,256]{2,1,0:T(8,128)(2,1)S(1)}, u32[]{:S(2)}, u32[]{:S(2)}) collective-permute-start(bf16[8,128,256]{2,1,0:T(8,128)(2,1)S(1)} %get-tuple-element.39), channel_id=1, source_target_pairs={{0,16},{8,24},{16,0},{24,8},{1,17},{9,25},{17,1},{25,9},{2,18},{10... | collective-permute-start | bytes 1572872 | tf_op jit(solution)/shard_map/ppermute | solution.py:61
  18.7 1.6 %collective-permute-start.4 = (bf16[2,2,256,256]{3,2,1,0:T(8,128)(2,1)S(1)}, bf16[2,2,256,256]{3,2,1,0:T(8,128)(2,1)S(1)}, u32[]{:S(2)}, u32[]{:S(2)}) collective-permute-start(bf16[2,2,256,256]{3,2,1,0:T(8,128)(2,1)S(1)} %get-tuple-element.34.refs_0_), channel_id=1, source_target_pairs={{0,2},{1,3},{2,0},{3,1},{4,6},{5,7},{6,4},{7,5},{8,10},{9,11},{10,... | collective-permute-start | bytes 1572872 | tf_op jit(solution)/shard_map/ppermute | solution.py:61
  20.9 1.4 collective-permute-start.7
  22.4 11.3 %collective-permute-done.1.refs_2_ = bf16[2,2,128,256]{3,2,1,0:T(8,128)(2,1)S(1)} collective-permute-done((bf16[2,2,128,256]{3,2,1,0:T(8,128)(2,1)S(1)}, bf16[2,2,128,256]{3,2,1,0:T(8,128)(2,1)S(1)}, u32[]{:S(2)}, u32[]{:S(2)}) %collective-permute-start.1) | collective-permute-done | bytes 262176 | tf_op jit(solution)/shard_map/ppermute | solution.py:61
  34.5 3.1 %collective-permute-start.6 = (bf16[1,2,256,256]{3,2,1,0:T(8,128)(2,1)S(1)}, bf16[1,2,256,256]{3,2,1,0:T(8,128)(2,1)S(1)}, u32[]{:S(2)}, u32[]{:S(2)}) collective-permute-start(bf16[1,2,256,256]{3,2,1,0:T(8,128)(2,1)S(1)} %get-tuple-element.41.refs_0_), channel_id=1, source_target_pairs={{0,4},{1,5},{2,6},{3,7},{4,0},{5,1},{6,2},{7,3},{8,12},{9,13},{10,... | collective-permute-start | bytes 786440 | tf_op jit(solution)/shard_map/ppermute | solution.py:61
  37.6 1.5 %collective-permute-start.5 = (bf16[1,2,128,256]{3,2,1,0:T(8,128)(2,1)S(1)}, bf16[1,2,128,256]{3,2,1,0:T(8,128)(2,1)S(1)}, u32[]{:S(2)}, u32[]{:S(2)}) collective-permute-start(bf16[1,2,128,256]{3,2,1,0:T(8,128)(2,1)S(1)} %get-tuple-element.36.refs_0_), channel_id=1, source_target_pairs={{0,16},{8,24},{16,0},{24,8},{1,17},{9,25},{17,1},{25,9},{2,18},{10... | collective-permute-start | bytes 393224 | tf_op jit(solution)/shard_map/ppermute | solution.py:61
  39.2 9.5 %collective-permute-done.5.refs_2_ = bf16[1,2,128,256]{3,2,1,0:T(8,128)(2,1)S(1)} collective-permute-done((bf16[1,2,128,256]{3,2,1,0:T(8,128)(2,1)S(1)}, bf16[1,2,128,256]{3,2,1,0:T(8,128)(2,1)S(1)}, u32[]{:S(2)}, u32[]{:S(2)}) %collective-permute-start.5) | collective-permute-done | bytes 131104 | tf_op jit(solution)/shard_map/ppermute | solution.py:61
  52.7 3.4 %collective-permute-done.9.refs_2_ = bf16[2,128,256]{2,1,0:T(8,128)(2,1)S(1)} collective-permute-done((bf16[2,128,256]{2,1,0:T(8,128)(2,1)S(1)}, bf16[2,128,256]{2,1,0:T(8,128)(2,1)S(1)}, u32[]{:S(2)}, u32[]{:S(2)}) %collective-permute-start.9) | collective-permute-done | bytes 131104 | tf_op jit(solution)/shard_map/ppermute | solution.py:61
  56.1 2.4 %collective-permute-start.13 = (bf16[4,128,256]{2,1,0:T(8,128)(2,1)S(1)}, bf16[4,128,256]{2,1,0:T(8,128)(2,1)S(1)}, u32[]{:S(2)}, u32[]{:S(2)}) collective-permute-start(bf16[4,128,256]{2,1,0:T(8,128)(2,1)S(1)} %shard_map.121.refs_0_.refs_1_), channel_id=1, source_target_pairs={{0,4},{1,5},{2,6},{3,7},{4,0},{5,1},{6,2},{7,3},{8,12},{9,13},{10,... | collective-permute-start | bytes 786440 | tf_op jit(solution)/shard_map/ppermute | solution.py:61
  58.5 1.8 %collective-permute-start.10 = (bf16[256,256]{1,0:T(8,128)(2,1)S(1)}, bf16[256,256]{1,0:T(8,128)(2,1)S(1)}, u32[]{:S(2)}, u32[]{:S(2)}) collective-permute-start(bf16[256,256]{1,0:T(8,128)(2,1)S(1)} %get-tuple-element.47), channel_id=1, source_target_pairs={{0,2},{1,3},{2,0},{3,1},{4,6},{5,7},{6,4},{7,5},{8,10},{9,11},{10,... | collective-permute-start | bytes 393224 | tf_op jit(solution)/shard_map/ppermute | solution.py:61
  60.4 2.5 %collective-permute-start.12 = (bf16[256,256]{1,0:T(8,128)(2,1)S(1)}, bf16[256,256]{1,0:T(8,128)(2,1)S(1)}, u32[]{:S(2)}, u32[]{:S(2)}) collective-permute-start(bf16[256,256]{1,0:T(8,128)(2,1)S(1)} %get-tuple-element.45.refs_0_), channel_id=1, source_target_pairs={{0,6},{1,7},{2,4},{3,5},{4,2},{5,3},{6,0},{7,1},{8,14},{9,15},{10,... | collective-permute-start | bytes 393224 | tf_op jit(solution)/shard_map/ppermute | solution.py:61
  62.9 5.2 %collective-permute-done.10.refs_5_ = bf16[256,256]{1,0:T(8,128)(2,1)S(1)} collective-permute-done((bf16[256,256]{1,0:T(8,128)(2,1)S(1)}, bf16[256,256]{1,0:T(8,128)(2,1)S(1)}, u32[]{:S(2)}, u32[]{:S(2)}) %collective-permute-start.10) | collective-permute-done | bytes 131104 | tf_op jit(solution)/shard_map/ppermute | solution.py:61
  68.1 11.9 %collective-permute-done.11.refs_6_ = bf16[256,256]{1,0:T(8,128)(2,1)S(1)} collective-permute-done((bf16[256,256]{1,0:T(8,128)(2,1)S(1)}, bf16[256,256]{1,0:T(8,128)(2,1)S(1)}, u32[]{:S(2)}, u32[]{:S(2)}) %collective-permute-start.11) | collective-permute-done | bytes 131104 | tf_op jit(solution)/shard_map/ppermute | solution.py:61
  81.4 2.4 %collective-permute-start.15 = (bf16[256,256]{1,0:T(8,128)(2,1)S(1)}, bf16[256,256]{1,0:T(8,128)(2,1)S(1)}, u32[]{:S(2)}, u32[]{:S(2)}) collective-permute-start(bf16[256,256]{1,0:T(8,128)(2,1)S(1)} %get-tuple-element.51.refs_1_), channel_id=1, source_target_pairs={{0,2},{1,3},{2,0},{3,1},{4,6},{5,7},{6,4},{7,5},{8,10},{9,11},{10,... | collective-permute-start | bytes 393224 | tf_op jit(solution)/shard_map/ppermute | solution.py:61
  83.8 1.9 %collective-permute-start.16 = (bf16[256,256]{1,0:T(8,128)(2,1)S(1)}, bf16[256,256]{1,0:T(8,128)(2,1)S(1)}, u32[]{:S(2)}, u32[]{:S(2)}) collective-permute-start(bf16[256,256]{1,0:T(8,128)(2,1)S(1)} %get-tuple-element.51.refs_1_), channel_id=1, source_target_pairs={{0,4},{1,5},{2,6},{3,7},{4,0},{5,1},{6,2},{7,3},{8,12},{9,13},{10,... | collective-permute-start | bytes 393224 | tf_op jit(solution)/shard_map/ppermute | solution.py:61
  85.7 1.4 collective-permute-start.17
  87.1 7.9 %shard_map.124.refs_0_.refs_1_ = f32[2,256,512]{2,1,0:T(8,128)S(1)} custom-call(f32[2,256,256]{2,1,0:T(8,128)S(1)} %shard_map.123.refs_0_.refs_1_, f32[2,256,256]{2,1,0:T(8,128)S(1)} %shard_map.123.refs_0_.refs_1_, f32[2,256,256]{2,1,0:T(8,128)S(1)} %collective-permute-done.14.refs_2_), custom_call_target="tpu_custom_call" | custom-call | bytes 20000 | tf_op jit(solution)/shard_map/pallas_call | solution.py:44
  95.0 1.7 %collective-permute-done.16.refs_3_ = bf16[256,256]{1,0:T(8,128)(2,1)S(1)} collective-permute-done((bf16[256,256]{1,0:T(8,128)(2,1)S(1)}, bf16[256,256]{1,0:T(8,128)(2,1)S(1)}, u32[]{:S(2)}, u32[]{:S(2)}) %collective-permute-start.16) | collective-permute-done | bytes 131104 | tf_op jit(solution)/shard_map/ppermute | solution.py:61
  96.8 1.9 %collective-permute-done.18.refs_3_ = bf16[4,256,256]{2,1,0:T(8,128)(2,1)S(1)} collective-permute-done((bf16[4,256,256]{2,1,0:T(8,128)(2,1)S(1)}, bf16[4,256,256]{2,1,0:T(8,128)(2,1)S(1)}, u32[]{:S(2)}, u32[]{:S(2)}) %collective-permute-start.18) | collective-permute-done | bytes 524320 | tf_op jit(solution)/shard_map/ppermute | solution.py:61
  98.7 1.5 shard_map.126
  100.2 1.6 %collective-permute-start.19 = (bf16[8,128,256]{2,1,0:T(8,128)(2,1)S(1)}, bf16[8,128,256]{2,1,0:T(8,128)(2,1)S(1)}, u32[]{:S(2)}, u32[]{:S(2)}) collective-permute-start(bf16[8,128,256]{2,1,0:T(8,128)(2,1)S(1)} %get-tuple-element.54.refs_3_), channel_id=1, source_target_pairs={{0,8},{8,0},{16,24},{24,16},{1,9},{9,1},{17,25},{25,17},{2,10},{10... | collective-permute-start | bytes 1572872 | tf_op jit(solution)/shard_map/ppermute | solution.py:61
  101.8 1.5 %collective-permute-start.20 = (bf16[8,128,256]{2,1,0:T(8,128)(2,1)S(1)}, bf16[8,128,256]{2,1,0:T(8,128)(2,1)}, u32[]{:S(2)}, u32[]{:S(2)}) collective-permute-start(bf16[8,128,256]{2,1,0:T(8,128)(2,1)S(1)} %get-tuple-element.54.refs_3_), channel_id=1, source_target_pairs={{0,16},{8,24},{16,0},{24,8},{1,17},{9,25},{17,1},{25,9},{2,18},{10... | collective-permute-start | bytes 1572872 | tf_op jit(solution)/shard_map/ppermute | solution.py:61
  103.7 8.0 %shard_map.127.refs_0_.refs_1_ = f32[2,256,512]{2,1,0:T(8,128)S(1)} custom-call(bf16[256,256]{1,0:T(8,128)(2,1)} %get-tuple-element.52.refs_0_, f32[2,256,512]{2,1,0:T(8,128)S(1)} %shard_map.124.refs_0_.refs_1_), custom_call_target="tpu_custom_call" | custom-call | bytes 20000 | tf_op jit(solution)/shard_map/pallas_call | solution.py:44
  111.7 8.0 %shard_map.128.refs_0_.refs_1_ = f32[2,256,512]{2,1,0:T(8,128)S(1)} custom-call(f32[2,256,512]{2,1,0:T(8,128)S(1)} %shard_map.127.refs_0_.refs_1_, f32[2,256,512]{2,1,0:T(8,128)S(1)} %shard_map.127.refs_0_.refs_1_), custom_call_target="tpu_custom_call" | custom-call | bytes 20000 | tf_op jit(solution)/shard_map/pallas_call | solution.py:44
  119.8 6.3 %shard_map.129.refs_0_.refs_2_ = bf16[2,128,256]{2,1,0:T(8,128)(2,1)S(1)} custom-call(f32[2,256,512]{2,1,0:T(8,128)S(1)} %shard_map.128.refs_0_.refs_1_, f32[2,256,512]{2,1,0:T(8,128)S(1)} %shard_map.128.refs_0_.refs_1_, bf16[2,128,256]{2,1,0:T(8,128)(2,1)S(1)} %bitcast.7), custom_call_target="tpu_custom_call" | custom-call | bytes 20000 | tf_op jit(solution)/shard_map/pallas_call | solution.py:44
  126.1 1.6 %collective-permute-start.22 = (bf16[2,128,256]{2,1,0:T(8,128)(2,1)S(1)}, bf16[2,128,256]{2,1,0:T(8,128)(2,1)S(1)}, u32[]{:S(2)}, u32[]{:S(2)}) collective-permute-start(bf16[2,128,256]{2,1,0:T(8,128)(2,1)S(1)} %shard_map.129.refs_0_.refs_2_), channel_id=1, source_target_pairs={{0,8},{8,0},{16,24},{24,16},{1,9},{9,1},{17,25},{25,17},{2,10},{10... | collective-permute-start | bytes 393224 | tf_op jit(solution)/shard_map/ppermute | solution.py:61
  127.7 1.5 %collective-permute-start.23 = (bf16[2,128,256]{2,1,0:T(8,128)(2,1)S(1)}, bf16[2,128,256]{2,1,0:T(8,128)(2,1)S(1)}, u32[]{:S(2)}, u32[]{:S(2)}) collective-permute-start(bf16[2,128,256]{2,1,0:T(8,128)(2,1)S(1)} %shard_map.129.refs_0_.refs_2_), channel_id=1, source_target_pairs={{0,16},{8,24},{16,0},{24,8},{1,17},{9,25},{17,1},{25,9},{2,18},{10... | collective-permute-start | bytes 393224 | tf_op jit(solution)/shard_map/ppermute | solution.py:61
  131.0 2.2 %shard_map.130 = (f32[4,256,256]{2,1,0:T(8,128)}, f32[4,256,256]{2,1,0:T(8,128)}) custom-call(bf16[2,128,256]{2,1,0:T(8,128)(2,1)S(1)} %shard_map.129.refs_0_.refs_2_, s32[3]{0:T(128)S(1)} %pad_add_fusion.place.refs_1_.refs_2_, s32[8]{0:T(128)S(1)} %copy-done.12, bf16[8,256,256]{2,1,0:T(8,128)(2,1)S(1)} %bitcast.8, f32[4,256,256]{2,1,0:T(8,128)S(1)} %copy-done.4, ...), custom_call_target="tpu_custom_call" | custom-call | bytes 20000 | tf_op jit(solution)/shard_map/pallas_call | solution.py:44
  134.5 3.2 %shard_map.131.refs_0_ = bf16[8,128,1024]{2,1,0:T(8,128)(2,1)} custom-call(f32[4,256,256]{2,1,0:T(8,128)S(1)} %copy-done.9, s32[3]{0:T(128)S(1)} %pad_add_fusion.place.refs_1_.refs_2_, bf16[8,128,1024]{2,1,0:T(8,128)(2,1)S(1)} %copy-done.7, bf16[8,128,256]{2,1,0:T(8,128)(2,1)S(1)} %get-tuple-element.54.refs_3_, ...), custom_call_target="tpu_custom_call" | custom-call | bytes 20000 | tf_op jit(solution)/shard_map/pallas_call | solution.py:44
  137.7 1.6 %copy-done.1 = bf16[8,128,1024]{2,1,0:T(8,128)(2,1)S(1)} copy-done((bf16[8,128,1024]{2,1,0:T(8,128)(2,1)S(1)}, bf16[8,128,1024]{2,1,0:T(8,128)(2,1)}, u32[]{:S(2)}) %copy-start.1) | copy-done | bytes 2097176
  139.2 2.0 %shard_map.132 = f32[8,128,256]{2,1,0:T(8,128)} custom-call(bf16[8,128,1024]{2,1,0:T(8,128)(2,1)S(1)} %copy-done.1, s32[3]{0:T(128)S(1)} %pad_add_fusion.place.refs_1_.refs_2_, bf16[2,128,256]{2,1,0:T(8,128)(2,1)S(1)} %shard_map.129.refs_0_.refs_2_, bf16[2,128,256]{2,1,0:T(8,128)(2,1)S(1)} %collective-permute-done.22.refs_3_, ...), custom_call_target="tpu_custom_call" | custom-call | bytes 20000 | tf_op jit(solution)/shard_map/pallas_call | solution.py:44
  (72 shorter events, 17.7 us)
Async XLA Ops:
  7.2 122.5 %all-gather.3.cloned.1.call-start = ((), (), s32[]{:S(2)}) async-start(), calls=%async_computation | async-start | bytes 1179648 | tf_op jit(solution)/shard_map/all_gather | solution.py:454
  11.3 5.5 %copy-start.10 = (bf16[1024,256]{1,0:T(8,128)(2,1)S(1)}, bf16[1024,256]{1,0:T(8,128)(2,1)}, u32[]{:S(2)}) copy-start(bf16[1024,256]{1,0:T(8,128)(2,1)} %refs_3_.2) | copy-start | bytes 1572868
  11.3 6.7 %collective-permute-start = (bf16[4,2,256,256]{3,2,1,0:T(8,128)(2,1)S(1)}, bf16[4,2,256,256]{3,2,1,0:T(8,128)(2,1)S(1)}, u32[]{:S(2)}, u32[]{:S(2)}) collective-permute-start(bf16[4,2,256,256]{3,2,1,0:T(8,128)(2,1)S(1)} %get-tuple-element.30.refs_0_), channel_id=1, source_target_pairs={{0,1},{1,0},{2,3},{3,2},{4,5},{5,4},{6,7},{7,6},{8,9},{9,8},{10,11... | collective-permute-start | bytes 3145736 | tf_op jit(solution)/shard_map/ppermute | solution.py:61
  12.7 21.0 %collective-permute-start.2 = (bf16[8,128,256]{2,1,0:T(8,128)(2,1)S(1)}, bf16[8,128,256]{2,1,0:T(8,128)(2,1)S(1)}, u32[]{:S(2)}, u32[]{:S(2)}) collective-permute-start(bf16[8,128,256]{2,1,0:T(8,128)(2,1)S(1)} %get-tuple-element.38), channel_id=1, source_target_pairs={{0,8},{8,0},{16,24},{24,16},{1,9},{9,1},{17,25},{25,17},{2,10},{10... | collective-permute-start | bytes 1572872 | tf_op jit(solution)/shard_map/ppermute | solution.py:61
  15.3 18.5 %collective-permute-start.3 = (bf16[8,128,256]{2,1,0:T(8,128)(2,1)S(1)}, bf16[8,128,256]{2,1,0:T(8,128)(2,1)S(1)}, u32[]{:S(2)}, u32[]{:S(2)}) collective-permute-start(bf16[8,128,256]{2,1,0:T(8,128)(2,1)S(1)} %get-tuple-element.39), channel_id=1, source_target_pairs={{0,16},{8,24},{16,0},{24,8},{1,17},{9,25},{17,1},{25,9},{2,18},{10... | collective-permute-start | bytes 1572872 | tf_op jit(solution)/shard_map/ppermute | solution.py:61
  18.7 15.2 %collective-permute-start.4 = (bf16[2,2,256,256]{3,2,1,0:T(8,128)(2,1)S(1)}, bf16[2,2,256,256]{3,2,1,0:T(8,128)(2,1)S(1)}, u32[]{:S(2)}, u32[]{:S(2)}) collective-permute-start(bf16[2,2,256,256]{3,2,1,0:T(8,128)(2,1)S(1)} %get-tuple-element.34.refs_0_), channel_id=1, source_target_pairs={{0,2},{1,3},{2,0},{3,1},{4,6},{5,7},{6,4},{7,5},{8,10},{9,11},{10,... | collective-permute-start | bytes 1572872 | tf_op jit(solution)/shard_map/ppermute | solution.py:61
  20.4 13.3 %collective-permute-start.1 = (bf16[2,2,128,256]{3,2,1,0:T(8,128)(2,1)S(1)}, bf16[2,2,128,256]{3,2,1,0:T(8,128)(2,1)S(1)}, u32[]{:S(2)}, u32[]{:S(2)}) collective-permute-start(bf16[2,2,128,256]{3,2,1,0:T(8,128)(2,1)S(1)} %get-tuple-element.32.refs_0_), channel_id=1, source_target_pairs={{0,8},{8,0},{16,24},{24,16},{1,9},{9,1},{17,25},{25,17},{2,10},{10... | collective-permute-start | bytes 786440 | tf_op jit(solution)/shard_map/ppermute | solution.py:61
  20.9 27.8 %collective-permute-start.7 = (bf16[8,128,256]{2,1,0:T(8,128)(2,1)S(1)}, bf16[8,128,256]{2,1,0:T(8,128)(2,1)S(1)}, u32[]{:S(2)}, u32[]{:S(2)}) collective-permute-start(bf16[8,128,256]{2,1,0:T(8,128)(2,1)S(1)} %get-tuple-element.31.refs_0_), channel_id=1, source_target_pairs={{0,24},{8,16},{16,8},{24,0},{1,25},{9,17},{17,9},{25,1},{2,26},{10... | collective-permute-start | bytes 1572872 | tf_op jit(solution)/shard_map/ppermute | solution.py:61
  33.9 15.1 %copy-start.2 = (f32[8,128,256]{2,1,0:T(8,128)S(1)}, f32[8,128,256]{2,1,0:T(8,128)}, u32[]{:S(2)}) copy-start(f32[8,128,256]{2,1,0:T(8,128)} %refs_4_.2) | copy-start | bytes 3145732
  34.5 14.5 %collective-permute-start.6 = (bf16[1,2,256,256]{3,2,1,0:T(8,128)(2,1)S(1)}, bf16[1,2,256,256]{3,2,1,0:T(8,128)(2,1)S(1)}, u32[]{:S(2)}, u32[]{:S(2)}) collective-permute-start(bf16[1,2,256,256]{3,2,1,0:T(8,128)(2,1)S(1)} %get-tuple-element.41.refs_0_), channel_id=1, source_target_pairs={{0,4},{1,5},{2,6},{3,7},{4,0},{5,1},{6,2},{7,3},{8,12},{9,13},{10,... | collective-permute-start | bytes 786440 | tf_op jit(solution)/shard_map/ppermute | solution.py:61
  37.6 11.1 %collective-permute-start.5 = (bf16[1,2,128,256]{3,2,1,0:T(8,128)(2,1)S(1)}, bf16[1,2,128,256]{3,2,1,0:T(8,128)(2,1)S(1)}, u32[]{:S(2)}, u32[]{:S(2)}) collective-permute-start(bf16[1,2,128,256]{3,2,1,0:T(8,128)(2,1)S(1)} %get-tuple-element.36.refs_0_), channel_id=1, source_target_pairs={{0,16},{8,24},{16,0},{24,8},{1,17},{9,25},{17,1},{25,9},{2,18},{10... | collective-permute-start | bytes 393224 | tf_op jit(solution)/shard_map/ppermute | solution.py:61
  50.1 29.9 %copy-start.13 = (s32[8]{0:T(128)S(1)}, s32[8]{0:T(128)}, u32[]{:S(2)}) copy-start(s32[8]{0:T(128)} %refs_3_.3) | copy-start | bytes 100
  50.1 2.0 %collective-permute-start.8 = (bf16[4,256,256]{2,1,0:T(8,128)(2,1)S(1)}, bf16[4,256,256]{2,1,0:T(8,128)(2,1)S(1)}, u32[]{:S(2)}, u32[]{:S(2)}) collective-permute-start(bf16[4,256,256]{2,1,0:T(8,128)(2,1)S(1)} %get-tuple-element.43.refs_0_), channel_id=1, source_target_pairs={{0,1},{1,0},{2,3},{3,2},{4,5},{5,4},{6,7},{7,6},{8,9},{9,8},{10,11... | collective-permute-start | bytes 1572872 | tf_op jit(solution)/shard_map/ppermute | solution.py:61
  50.2 5.9 %collective-permute-start.9 = (bf16[2,128,256]{2,1,0:T(8,128)(2,1)S(1)}, bf16[2,128,256]{2,1,0:T(8,128)(2,1)S(1)}, u32[]{:S(2)}, u32[]{:S(2)}) collective-permute-start(bf16[2,128,256]{2,1,0:T(8,128)(2,1)S(1)} %bitcast.5), channel_id=1, source_target_pairs={{0,2},{1,3},{2,0},{3,1},{4,6},{5,7},{6,4},{7,5},{8,10},{9,11},{10,... | collective-permute-start | bytes 393224 | tf_op jit(solution)/shard_map/ppermute | solution.py:61
  56.1 24.8 %collective-permute-start.13 = (bf16[4,128,256]{2,1,0:T(8,128)(2,1)S(1)}, bf16[4,128,256]{2,1,0:T(8,128)(2,1)S(1)}, u32[]{:S(2)}, u32[]{:S(2)}) collective-permute-start(bf16[4,128,256]{2,1,0:T(8,128)(2,1)S(1)} %shard_map.121.refs_0_.refs_1_), channel_id=1, source_target_pairs={{0,4},{1,5},{2,6},{3,7},{4,0},{5,1},{6,2},{7,3},{8,12},{9,13},{10,... | collective-permute-start | bytes 786440 | tf_op jit(solution)/shard_map/ppermute | solution.py:61
  58.5 9.6 %collective-permute-start.10 = (bf16[256,256]{1,0:T(8,128)(2,1)S(1)}, bf16[256,256]{1,0:T(8,128)(2,1)S(1)}, u32[]{:S(2)}, u32[]{:S(2)}) collective-permute-start(bf16[256,256]{1,0:T(8,128)(2,1)S(1)} %get-tuple-element.47), channel_id=1, source_target_pairs={{0,2},{1,3},{2,0},{3,1},{4,6},{5,7},{6,4},{7,5},{8,10},{9,11},{10,... | collective-permute-start | bytes 393224 | tf_op jit(solution)/shard_map/ppermute | solution.py:61
  60.3 19.7 %collective-permute-start.11 = (bf16[256,256]{1,0:T(8,128)(2,1)S(1)}, bf16[256,256]{1,0:T(8,128)(2,1)S(1)}, u32[]{:S(2)}, u32[]{:S(2)}) collective-permute-start(bf16[256,256]{1,0:T(8,128)(2,1)S(1)} %get-tuple-element.48), channel_id=1, source_target_pairs={{0,4},{1,5},{2,6},{3,7},{4,0},{5,1},{6,2},{7,3},{8,12},{9,13},{10,... | collective-permute-start | bytes 393224 | tf_op jit(solution)/shard_map/ppermute | solution.py:61
  60.4 19.6 %collective-permute-start.12 = (bf16[256,256]{1,0:T(8,128)(2,1)S(1)}, bf16[256,256]{1,0:T(8,128)(2,1)S(1)}, u32[]{:S(2)}, u32[]{:S(2)}) collective-permute-start(bf16[256,256]{1,0:T(8,128)(2,1)S(1)} %get-tuple-element.45.refs_0_), channel_id=1, source_target_pairs={{0,6},{1,7},{2,4},{3,5},{4,2},{5,3},{6,0},{7,1},{8,14},{9,15},{10,... | collective-permute-start | bytes 393224 | tf_op jit(solution)/shard_map/ppermute | solution.py:61
  81.3 5.8 %collective-permute-start.14 = (f32[2,256,256]{2,1,0:T(8,128)S(1)}, f32[2,256,256]{2,1,0:T(8,128)S(1)}, u32[]{:S(2)}, u32[]{:S(2)}) collective-permute-start(f32[2,256,256]{2,1,0:T(8,128)S(1)} %shard_map.123.refs_0_.refs_1_), channel_id=1, source_target_pairs={{0,1},{1,0},{2,3},{3,2},{4,5},{5,4},{6,7},{7,6},{8,9},{9,8},{10,11... | collective-permute-start | bytes 1572872 | tf_op jit(solution)/shard_map/ppermute | solution.py:61
  81.4 13.6 %collective-permute-start.15 = (bf16[256,256]{1,0:T(8,128)(2,1)S(1)}, bf16[256,256]{1,0:T(8,128)(2,1)S(1)}, u32[]{:S(2)}, u32[]{:S(2)}) collective-permute-start(bf16[256,256]{1,0:T(8,128)(2,1)S(1)} %get-tuple-element.51.refs_1_), channel_id=1, source_target_pairs={{0,2},{1,3},{2,0},{3,1},{4,6},{5,7},{6,4},{7,5},{8,10},{9,11},{10,... | collective-permute-start | bytes 393224 | tf_op jit(solution)/shard_map/ppermute | solution.py:61
  83.8 12.9 %collective-permute-start.16 = (bf16[256,256]{1,0:T(8,128)(2,1)S(1)}, bf16[256,256]{1,0:T(8,128)(2,1)S(1)}, u32[]{:S(2)}, u32[]{:S(2)}) collective-permute-start(bf16[256,256]{1,0:T(8,128)(2,1)S(1)} %get-tuple-element.51.refs_1_), channel_id=1, source_target_pairs={{0,4},{1,5},{2,6},{3,7},{4,0},{5,1},{6,2},{7,3},{8,12},{9,13},{10,... | collective-permute-start | bytes 393224 | tf_op jit(solution)/shard_map/ppermute | solution.py:61
  85.7 11.0 %collective-permute-start.17 = (bf16[256,256]{1,0:T(8,128)(2,1)S(1)}, bf16[256,256]{1,0:T(8,128)(2,1)S(1)}, u32[]{:S(2)}, u32[]{:S(2)}) collective-permute-start(bf16[256,256]{1,0:T(8,128)(2,1)S(1)} %get-tuple-element.51.refs_1_), channel_id=1, source_target_pairs={{0,6},{1,7},{2,4},{3,5},{4,2},{5,3},{6,0},{7,1},{8,14},{9,15},{10,... | collective-permute-start | bytes 393224 | tf_op jit(solution)/shard_map/ppermute | solution.py:61
  96.7 2.0 %collective-permute-start.18 = (bf16[4,256,256]{2,1,0:T(8,128)(2,1)S(1)}, bf16[4,256,256]{2,1,0:T(8,128)(2,1)S(1)}, u32[]{:S(2)}, u32[]{:S(2)}) collective-permute-start(bf16[4,256,256]{2,1,0:T(8,128)(2,1)S(1)} %shard_map.125.refs_0_.refs_2_), channel_id=1, source_target_pairs={{0,1},{1,0},{2,3},{3,2},{4,5},{5,4},{6,7},{7,6},{8,9},{9,8},{10,11... | collective-permute-start | bytes 1572872 | tf_op jit(solution)/shard_map/ppermute | solution.py:61
  100.2 29.1 %collective-permute-start.19 = (bf16[8,128,256]{2,1,0:T(8,128)(2,1)S(1)}, bf16[8,128,256]{2,1,0:T(8,128)(2,1)S(1)}, u32[]{:S(2)}, u32[]{:S(2)}) collective-permute-start(bf16[8,128,256]{2,1,0:T(8,128)(2,1)S(1)} %get-tuple-element.54.refs_3_), channel_id=1, source_target_pairs={{0,8},{8,0},{16,24},{24,16},{1,9},{9,1},{17,25},{25,17},{2,10},{10... | collective-permute-start | bytes 1572872 | tf_op jit(solution)/shard_map/ppermute | solution.py:61
  101.8 31.4 %collective-permute-start.20 = (bf16[8,128,256]{2,1,0:T(8,128)(2,1)S(1)}, bf16[8,128,256]{2,1,0:T(8,128)(2,1)}, u32[]{:S(2)}, u32[]{:S(2)}) collective-permute-start(bf16[8,128,256]{2,1,0:T(8,128)(2,1)S(1)} %get-tuple-element.54.refs_3_), channel_id=1, source_target_pairs={{0,16},{8,24},{16,0},{24,8},{1,17},{9,25},{17,1},{25,9},{2,18},{10... | collective-permute-start | bytes 1572872 | tf_op jit(solution)/shard_map/ppermute | solution.py:61
  103.3 29.9 %collective-permute-start.21 = (bf16[8,128,256]{2,1,0:T(8,128)(2,1)S(1)}, bf16[8,128,256]{2,1,0:T(8,128)(2,1)}, u32[]{:S(2)}, u32[]{:S(2)}) collective-permute-start(bf16[8,128,256]{2,1,0:T(8,128)(2,1)S(1)} %get-tuple-element.54.refs_3_), channel_id=1, source_target_pairs={{0,24},{8,16},{16,8},{24,0},{1,25},{9,17},{17,9},{25,1},{2,26},{10... | collective-permute-start | bytes 1572872 | tf_op jit(solution)/shard_map/ppermute | solution.py:61
  111.7 18.0 %copy-start.4 = (f32[4,256,256]{2,1,0:T(8,128)S(1)}, f32[4,256,256]{2,1,0:T(8,128)}, u32[]{:S(2)}) copy-start(f32[4,256,256]{2,1,0:T(8,128)} %refs_4_.3) | copy-start | bytes 3145732
  111.7 17.9 %copy-start.6 = (f32[4,256,256]{2,1,0:T(8,128)S(1)}, f32[4,256,256]{2,1,0:T(8,128)}, u32[]{:S(2)}) copy-start(f32[4,256,256]{2,1,0:T(8,128)} %refs_5_.3) | copy-start | bytes 3145732
  111.7 17.9 %copy-start.12 = (s32[8]{0:T(128)S(1)}, s32[8]{0:T(128)}, u32[]{:S(2)}) copy-start(s32[8]{0:T(128)} %refs_2_.12) | copy-start | bytes 100
  126.1 11.6 %collective-permute-start.22 = (bf16[2,128,256]{2,1,0:T(8,128)(2,1)S(1)}, bf16[2,128,256]{2,1,0:T(8,128)(2,1)S(1)}, u32[]{:S(2)}, u32[]{:S(2)}) collective-permute-start(bf16[2,128,256]{2,1,0:T(8,128)(2,1)S(1)} %shard_map.129.refs_0_.refs_2_), channel_id=1, source_target_pairs={{0,8},{8,0},{16,24},{24,16},{1,9},{9,1},{17,25},{25,17},{2,10},{10... | collective-permute-start | bytes 393224 | tf_op jit(solution)/shard_map/ppermute | solution.py:61
  127.7 9.9 %collective-permute-start.23 = (bf16[2,128,256]{2,1,0:T(8,128)(2,1)S(1)}, bf16[2,128,256]{2,1,0:T(8,128)(2,1)S(1)}, u32[]{:S(2)}, u32[]{:S(2)}) collective-permute-start(bf16[2,128,256]{2,1,0:T(8,128)(2,1)S(1)} %shard_map.129.refs_0_.refs_2_), channel_id=1, source_target_pairs={{0,16},{8,24},{16,0},{24,8},{1,17},{9,25},{17,1},{25,9},{2,18},{10... | collective-permute-start | bytes 393224 | tf_op jit(solution)/shard_map/ppermute | solution.py:61
  129.3 8.4 %collective-permute-start.24 = (bf16[2,128,256]{2,1,0:T(8,128)(2,1)S(1)}, bf16[2,128,256]{2,1,0:T(8,128)(2,1)}, u32[]{:S(2)}, u32[]{:S(2)}) collective-permute-start(bf16[2,128,256]{2,1,0:T(8,128)(2,1)S(1)} %shard_map.129.refs_0_.refs_2_), channel_id=1, source_target_pairs={{0,24},{8,16},{16,8},{24,0},{1,25},{9,17},{17,9},{25,1},{2,26},{10... | collective-permute-start | bytes 393224 | tf_op jit(solution)/shard_map/ppermute | solution.py:61
  (8 other events, 15.7 us)
Sparse Core Ops, SparseCore 0:
  100.3 24.2 all-gather.2

commit v5 on v4

--- a/solution.py
+++ b/solution.py
@@ -14,6 +14,7 @@
 step_size = 0.5
 epsilon = 1e-08
 BLOCK = 64
+GROUP = 4
 COST = 10_000
 HIGHEST = lax.Precision.HIGHEST
 VMEM_LIMIT = 48 * 1024 * 1024
@@ -61,13 +62,26 @@
     return lax.ppermute(x, axis, [(i, i ^ mask) for i in range(size)])
 
 
-def split_kernel(place, grad_ref, *outs, groups, chunks):
-    width = outs[0].shape[2]
-    for h in range(chunks):
-        for k in range(groups):
-            start = ((place[0] ^ k) * chunks + h) * width
-            columns = pl.ds(pl.multiple_of(start, 128), width)
-            outs[h * groups + k][...] = grad_ref[0, :, :, columns]
+def split_kernel(place, grad_ref, *outs):
+    half = outs[0].shape[3]
+    for side, out in enumerate(outs):
+        for i, k in enumerate((1 << side, 3)):
+            start = (place[0] ^ k) * 2 + side
+            columns = pl.ds(pl.multiple_of(start * half, half), half)
+            out[i] = grad_ref[0, :, :, columns]
+
+
+def add_kernel(place, grad_ref, *refs):
+    sides = len(refs) // 3
+    arrived, sums, sends = refs[:sides], refs[sides : 2 * sides], refs[2 * sides :]
+    half = sums[0].shape[2]
+    for side in range(sides):
+        for i, (k, out) in enumerate(((0, sums[side]), (2 >> side, sends[side]))):
+            start = (place[0] ^ k) * 2 + side
+            columns = pl.ds(pl.multiple_of(start * half, half), half)
+            for m in range(out.shape[0]):
+                total = grad_ref[0, m, :, columns].astype(f32) + arrived[side][i, m].astype(f32)
+                out[m] = total.astype(out.dtype)
 
 
 def sample_kernel(place, grad_ref, sketch_ref, keep_ref, send_ref):
@@ -85,15 +99,6 @@
         total = keep_ref[k] + other_ref[k].astype(f32)
         out = outs[k % len(outs)]
         out[k // len(outs)] = total.astype(out.dtype)
-
-
-def add_kernel(*refs):
-    out = refs[-1]
-    for m in range(out.shape[0]):
-        total = refs[0][m].astype(f32)
-        for ref in refs[1:-1]:
-            total = total + ref[m].astype(f32)
-        out[m] = total
 
 
 def stack_kernel(own_ref, other_ref, out_ref):
@@ -135,12 +140,27 @@
         if lo > base:
             slab = pltpu.roll(slab, 128 - (lo - base), 1)
         tiles.append(jnp.where(lane < BLOCK, slab, eye_right))
-    for k in range(BLOCK - 1):
+    for first in range(0, BLOCK, GROUP):
         for b in range(pair):
             tile = tiles[b]
-            column = jnp.where(sub[:, :1] > k, tile[:, k : k + 1], 0.0)
-            row = tile[k : k + 1, :] * (1.0 / tile[k : k + 1, k : k + 1])
-            tiles[b] = tile - column * row
+            columns = [
+                jnp.broadcast_to(tile[:, k : k + 1], tile.shape)
+                for k in range(first, first + GROUP)
+            ]
+            rows = []
+            for i in range(GROUP):
+                k = first + i
+                inverse = 1.0 / columns[i][k : k + 1, :]
+                row = tile[k : k + 1, :]
+                for j in range(i):
+                    row = row - columns[j][k : k + 1, :] * rows[j]
+                rows.append(row * inverse)
+                columns[i] = jnp.where(sub > k, columns[i], 0.0)
+                for j in range(i + 1, GROUP):
+                    columns[j] = columns[j] - columns[i] * (columns[j][k : k + 1, :] * inverse)
+            for i in range(GROUP):
+                tile = tile - columns[i] * rows[i]
+            tiles[b] = tile
     for b in range(pair):
         tile = tiles[b]
         diagonal = jnp.sum(jnp.where(lane == sub, tile, 0.0), axis=1, keepdims=True)
@@ -224,21 +244,22 @@
 
 
 def project_kernel(place, *refs, scale):
-    *grad_refs, basis_ref, mine_ref, other_ref = refs
+    *sums, basis_ref, mine_ref, other_ref = refs
     core = place[2]
+    half = sums[0].shape[2]
     for i in range(mine_ref.shape[0]):
         for out, want in ((other_ref, 1 - core), (mine_ref, core)):
             m = 2 * i + want
-            total = grad_refs[0][m].astype(f32)
-            for ref in grad_refs[1:]:
-                total = total + ref[m].astype(f32)
-            product = lax.dot_general(
-                (basis_ref[m] * scale).astype(bf16),
-                total.astype(bf16),
-                (((0,), (0,)), ((), ())),
-                preferred_element_type=f32,
-            )
-            out[i] = product.astype(out.dtype)
+            scaled = (basis_ref[m] * scale).astype(bf16)
+            for side in range(2):
+                total = sums[side][m] + sums[2 + side][m].astype(f32)
+                product = lax.dot_general(
+                    scaled,
+                    total.astype(bf16),
+                    (((0,), (0,)), ((), ())),
+                    preferred_element_type=f32,
+                )
+                out[i, :, side * half : (side + 1) * half] = product.astype(out.dtype)
 
 
 def pair_kernel(place, mine_ref, other_ref, *outs):
@@ -344,6 +365,8 @@
     struct = jax.ShapeDtypeStruct
 
     call = Sequence()
+    halved = struct((2, count, shard, quarter // 2), bf16)
+    sides = call(split_kernel, [halved] * 2, (place, grads), scalars=1)
     half = chips
     moments, lent = call(
         pick_kernel,
@@ -352,12 +375,6 @@
         scalars=2,
     )
     lent = swap(lent, "rows", 1)
-    blocks = call(
-        functools.partial(split_kernel, groups=groups, chunks=1),
-        [struct((count, shard, quarter), bf16)] * groups,
-        (place, grads),
-        scalars=1,
-    )
     keep, send = call(
         sample_kernel,
         [struct((groups // 2, each, shard, rank_full), kind) for kind in (f32, bf16)],
@@ -372,9 +389,7 @@
         scalars=2,
     )
     lent = swap(lent, "rows", 2)
-    sides = [1 << i for i in range(groups.bit_length() - 1)]
-    corners = [k for k in range(1, groups) if k not in sides]
-    beside = [swap(blocks[k], "dp", k) for k in sides]
+    sides = [swap(sides[i], "dp", 1 << i) for i in range(2)]
     send = swap(send, "dp", 1)
     part = groups // 2
     mask = 1
@@ -387,8 +402,13 @@
         )
         mask *= 2
         send = swap(send, "dp", mask)
-    total = call(add_kernel, struct((count, shard, quarter), f32), (blocks[0], *beside))
-    across = [swap(blocks[k], "dp", k) for k in corners]
+    *sums, left, right = call(
+        add_kernel,
+        [struct((count, shard, quarter // 2), kind) for kind in (f32, f32, bf16, bf16)],
+        (place, grads, *sides),
+        scalars=1,
+    )
+    left, right = swap(left, "dp", 2), swap(right, "dp", 1)
     bit = 0
     while half > 1:
         half //= 2
@@ -408,13 +428,13 @@
     mine, other = call(
         functools.partial(project_kernel, scale=inverse_root),
         [struct((chips, rank_full, quarter), f32), struct((chips, rank_full, quarter), bf16)],
-        (place, total, *across, basis),
+        (place, *sums, left, right, basis),
         scalars=1,
         after=(lent,),
     )
     other = swap(other, "rows", 1)
-    mask = 1
-    arrived = swap(sample, "rows", 2)
+    mask = chips // 2
+    arrived = swap(sample, "rows", 2 * mask)
     terms = call(
         pair_kernel,
         [struct((rank_full, quarter), f32)] + [struct((rank_full, quarter), bf16)] * (chips - 1),
@@ -423,10 +443,10 @@
     )
     terms = [terms[0]] + [swap(terms[k], "rows", 2 * k) for k in range(1, chips)]
     stacked = sample
-    while mask < chips // 2:
+    while mask > 1:
         both = struct((2 * stacked.shape[0], shard, rank_full), bf16)
         stacked = call(stack_kernel, both, (stacked, arrived))
-        mask *= 2
+        mask //= 2
         arrived = swap(stacked, "rows", 2 * mask)
     work_shape = struct((each, rank_full, 2 * rank_full), f32)
     last = rank_full // BLOCK - 1
@@ -461,17 +481,17 @@
         scratch=[pltpu.VMEM(work_shape.shape, f32)],
     )
     shared = [rows_basis] + [swap(rows_basis, "dp", k) for k in range(1, groups)]
+    new_weight = call(
+        functools.partial(weight_kernel, groups=groups, chunks=1),
+        struct(weight.shape, bf16),
+        (place, weight, *deltas),
+        scalars=1,
+    )
     first_out, second_out = call(
         functools.partial(moment_kernel, chunks=1),
         [struct(first_moment.shape, f32)] * 2,
         (place, owner, gathered, first_moment, second_moment),
         scalars=2,
-    )
-    new_weight = call(
-        functools.partial(weight_kernel, groups=groups, chunks=1),
-        struct(weight.shape, bf16),
-        (place, weight, *deltas),
-        scalars=1,
     )
     new_basis = call(basis_kernel, struct(basis.shape, f32), (place, *shared), scalars=1)
     return (new_weight, new_basis, first_out, second_out)

time: 149 us -> 143 us (0.960)
  Pallas kernels: 46.3 us -> 32.8 us
  waiting for transfers between devices: 45.8 us -> 57.8 us
  starting transfers between devices: 34 us -> 29.5 us
    pallas_call x22, Pallas kernels: 46.3 us -> 32.8 us  [__call__(): pl.pallas_call(body, out_shape=out_shape, in_specs=specs, out_specs=[VMEM...]
    ppermute x25 -> x26, waiting for transfers between devices: 45.8 us -> 57.8 us  [swap(): return lax.ppermute(x, axis, [(i, i ^ mask) for i in range(size)])]
    ppermute x25 -> x26, starting transfers between devices: 34 us -> 29.4 us  [swap(): return lax.ppermute(x, axis, [(i, i ^ mask) for i in range(size)])]
  transfers between devices with their start and end apart: 26 -> 27, of which waited for: 9 -> 9; matrix products, arithmetic and copies ran while one was open for 0% -> 0% of each run, Pallas kernels for 27% -> 19%
where the time goes in v5:
time: 143 us
  waiting for transfers between devices  57.8 us (40%)
  Pallas kernels  32.8 us (23%)
  starting transfers between devices  29.5 us (21%)
  between operations  14.4 us (10%)
  local copies, waits for them, and re-layouts  8.11 us (6%)
    ppermute x26, waiting for transfers between devices, swap(): return lax.ppermute(x, axis, [(i, i ^ mask) for i in range(size)])  57.8 us
    pallas_call x22, Pallas kernels, __call__(): pl.pallas_call(body, out_shape=out_shape, in_specs=specs, out_specs=[VMEM...  32.8 us
    ppermute x26, starting transfers between devices, swap(): return lax.ppermute(x, axis, [(i, i ^ mask) for i in range(size)])  29.4 us
    unnamed x28, local copies, waits for them, and re-layouts  8.11 us
  transfers between devices with their start and end apart: 27, of which 9 were waited for; matrix products, arithmetic and copies ran while one was open for 0% of the time, Pallas kernels for 19%

profile of v5, /device:TPU:0, one launch (start us, length us, event | category | flops | bytes accessed | tf_op | source)
XLA Modules:
  0.0 142.6 jit_solution(13967105189188907766)
XLA Ops:
  7.3 1.6 %copy-done = bf16[1,8,128,1024]{3,2,1,0:T(8,128)(2,1)S(1)} copy-done((bf16[1,8,128,1024]{3,2,1,0:T(8,128)(2,1)S(1)}, bf16[1,8,128,1024]{3,2,1,0:T(8,128)(2,1)}, u32[]{:S(2)}) %copy-start) | copy-done | bytes 2097176
  13.5 2.6 %collective-permute-start.3 = (bf16[2,8,128,128]{3,2,1,0:T(8,128)(2,1)S(1)}, bf16[2,8,128,128]{3,2,1,0:T(8,128)(2,1)S(1)}, u32[]{:S(2)}, u32[]{:S(2)}) collective-permute-start(bf16[2,8,128,128]{3,2,1,0:T(8,128)(2,1)S(1)} %get-tuple-element.32.refs_0_), channel_id=1, source_target_pairs={{0,16},{8,24},{16,0},{24,8},{1,17},{9,25},{17,1},{25,9},{2,18},{10... | collective-permute-start | bytes 1572872 | tf_op jit(solution)/shard_map/ppermute | solution.py:62
  16.1 1.5 %collective-permute-start.2 = (bf16[2,8,128,128]{3,2,1,0:T(8,128)(2,1)S(1)}, bf16[2,8,128,128]{3,2,1,0:T(8,128)(2,1)S(1)}, u32[]{:S(2)}, u32[]{:S(2)}) collective-permute-start(bf16[2,8,128,128]{3,2,1,0:T(8,128)(2,1)S(1)} %get-tuple-element.39), channel_id=1, source_target_pairs={{0,8},{8,0},{16,24},{24,16},{1,9},{9,1},{17,25},{25,17},{2,10},{10... | collective-permute-start | bytes 1572872 | tf_op jit(solution)/shard_map/ppermute | solution.py:62
  19.6 1.6 %collective-permute-start.4 = (bf16[2,2,256,256]{3,2,1,0:T(8,128)(2,1)S(1)}, bf16[2,2,256,256]{3,2,1,0:T(8,128)(2,1)S(1)}, u32[]{:S(2)}, u32[]{:S(2)}) collective-permute-start(bf16[2,2,256,256]{3,2,1,0:T(8,128)(2,1)S(1)} %get-tuple-element.36.refs_0_), channel_id=1, source_target_pairs={{0,2},{1,3},{2,0},{3,1},{4,6},{5,7},{6,4},{7,5},{8,10},{9,11},{10,... | collective-permute-start | bytes 1572872 | tf_op jit(solution)/shard_map/ppermute | solution.py:62
  21.8 13.9 %collective-permute-done.1.refs_2_ = bf16[2,2,128,256]{3,2,1,0:T(8,128)(2,1)S(1)} collective-permute-done((bf16[2,2,128,256]{3,2,1,0:T(8,128)(2,1)S(1)}, bf16[2,2,128,256]{3,2,1,0:T(8,128)(2,1)S(1)}, u32[]{:S(2)}, u32[]{:S(2)}) %collective-permute-start.1) | collective-permute-done | bytes 262176 | tf_op jit(solution)/shard_map/ppermute | solution.py:62
  37.0 1.7 %collective-permute-start.8 = (bf16[8,128,128]{2,1,0:T(8,128)(2,1)S(1)}, bf16[8,128,128]{2,1,0:T(8,128)(2,1)S(1)}, u32[]{:S(2)}, u32[]{:S(2)}) collective-permute-start(bf16[8,128,128]{2,1,0:T(8,128)(2,1)S(1)} %get-tuple-element.40.refs_0_), channel_id=1, source_target_pairs={{0,8},{8,0},{16,24},{24,16},{1,9},{9,1},{17,25},{25,17},{2,10},{10... | collective-permute-start | bytes 786440 | tf_op jit(solution)/shard_map/ppermute | solution.py:62
  39.4 2.7 %collective-permute-start.6 = (bf16[1,2,256,256]{3,2,1,0:T(8,128)(2,1)S(1)}, bf16[1,2,256,256]{3,2,1,0:T(8,128)(2,1)S(1)}, u32[]{:S(2)}, u32[]{:S(2)}) collective-permute-start(bf16[1,2,256,256]{3,2,1,0:T(8,128)(2,1)S(1)} %get-tuple-element.42.refs_0_), channel_id=1, source_target_pairs={{0,4},{1,5},{2,6},{3,7},{4,0},{5,1},{6,2},{7,3},{8,12},{9,13},{10,... | collective-permute-start | bytes 786440 | tf_op jit(solution)/shard_map/ppermute | solution.py:62
  42.0 1.5 %collective-permute-start.5 = (bf16[1,2,128,256]{3,2,1,0:T(8,128)(2,1)S(1)}, bf16[1,2,128,256]{3,2,1,0:T(8,128)(2,1)S(1)}, u32[]{:S(2)}, u32[]{:S(2)}) collective-permute-start(bf16[1,2,128,256]{3,2,1,0:T(8,128)(2,1)S(1)} %get-tuple-element.38.refs_0_), channel_id=1, source_target_pairs={{0,16},{8,24},{16,0},{24,8},{1,17},{9,25},{17,1},{25,9},{2,18},{10... | collective-permute-start | bytes 393224 | tf_op jit(solution)/shard_map/ppermute | solution.py:62
  43.5 3.6 %collective-permute-done.5.refs_2_ = bf16[1,2,128,256]{3,2,1,0:T(8,128)(2,1)S(1)} collective-permute-done((bf16[1,2,128,256]{3,2,1,0:T(8,128)(2,1)S(1)}, bf16[1,2,128,256]{3,2,1,0:T(8,128)(2,1)S(1)}, u32[]{:S(2)}, u32[]{:S(2)}) %collective-permute-start.5) | collective-permute-done | bytes 131104 | tf_op jit(solution)/shard_map/ppermute | solution.py:62
  47.1 5.8 %collective-permute-done.6.refs_1_.refs_9_ = bf16[1,2,256,256]{3,2,1,0:T(8,128)(2,1)S(1)} collective-permute-done((bf16[1,2,256,256]{3,2,1,0:T(8,128)(2,1)S(1)}, bf16[1,2,256,256]{3,2,1,0:T(8,128)(2,1)S(1)}, u32[]{:S(2)}, u32[]{:S(2)}) %collective-permute-start.6) | collective-permute-done | bytes 262176 | tf_op jit(solution)/shard_map/ppermute | solution.py:62
  54.1 1.8 %collective-permute-done.9.refs_3_ = bf16[4,256,256]{2,1,0:T(8,128)(2,1)S(1)} collective-permute-done((bf16[4,256,256]{2,1,0:T(8,128)(2,1)S(1)}, bf16[4,256,256]{2,1,0:T(8,128)(2,1)S(1)}, u32[]{:S(2)}, u32[]{:S(2)}) %collective-permute-start.9) | collective-permute-done | bytes 524320 | tf_op jit(solution)/shard_map/ppermute | solution.py:62
  56.6 7.1 %collective-permute-done.10.refs_2_ = bf16[2,128,256]{2,1,0:T(8,128)(2,1)S(1)} collective-permute-done((bf16[2,128,256]{2,1,0:T(8,128)(2,1)S(1)}, bf16[2,128,256]{2,1,0:T(8,128)(2,1)S(1)}, u32[]{:S(2)}, u32[]{:S(2)}) %collective-permute-start.10) | collective-permute-done | bytes 131104 | tf_op jit(solution)/shard_map/ppermute | solution.py:62
  63.8 2.0 %collective-permute-start.11 = (bf16[256,256]{1,0:T(8,128)(2,1)S(1)}, bf16[256,256]{1,0:T(8,128)(2,1)S(1)}, u32[]{:S(2)}, u32[]{:S(2)}) collective-permute-start(bf16[256,256]{1,0:T(8,128)(2,1)S(1)} %get-tuple-element.51), channel_id=1, source_target_pairs={{0,2},{1,3},{2,0},{3,1},{4,6},{5,7},{6,4},{7,5},{8,10},{9,11},{10,... | collective-permute-start | bytes 393224 | tf_op jit(solution)/shard_map/ppermute | solution.py:62
  65.8 2.4 %collective-permute-start.13 = (bf16[256,256]{1,0:T(8,128)(2,1)S(1)}, bf16[256,256]{1,0:T(8,128)(2,1)S(1)}, u32[]{:S(2)}, u32[]{:S(2)}) collective-permute-start(bf16[256,256]{1,0:T(8,128)(2,1)S(1)} %get-tuple-element.49.refs_0_), channel_id=1, source_target_pairs={{0,6},{1,7},{2,4},{3,5},{4,2},{5,3},{6,0},{7,1},{8,14},{9,15},{10,... | collective-permute-start | bytes 393224 | tf_op jit(solution)/shard_map/ppermute | solution.py:62
  68.2 11.8 %collective-permute-done.11.refs_5_ = bf16[256,256]{1,0:T(8,128)(2,1)S(1)} collective-permute-done((bf16[256,256]{1,0:T(8,128)(2,1)S(1)}, bf16[256,256]{1,0:T(8,128)(2,1)S(1)}, u32[]{:S(2)}, u32[]{:S(2)}) %collective-permute-start.11) | collective-permute-done | bytes 131104 | tf_op jit(solution)/shard_map/ppermute | solution.py:62
  81.5 2.1 %collective-permute-start.18 = (bf16[256,256]{1,0:T(8,128)(2,1)S(1)}, bf16[256,256]{1,0:T(8,128)(2,1)S(1)}, u32[]{:S(2)}, u32[]{:S(2)}) collective-permute-start(bf16[256,256]{1,0:T(8,128)(2,1)S(1)} %get-tuple-element.55.refs_1_), channel_id=1, source_target_pairs={{0,6},{1,7},{2,4},{3,5},{4,2},{5,3},{6,0},{7,1},{8,14},{9,15},{10,... | collective-permute-start | bytes 393224 | tf_op jit(solution)/shard_map/ppermute | solution.py:62
  83.6 2.3 %collective-permute-start.16 = (bf16[256,256]{1,0:T(8,128)(2,1)S(1)}, bf16[256,256]{1,0:T(8,128)(2,1)S(1)}, u32[]{:S(2)}, u32[]{:S(2)}) collective-permute-start(bf16[256,256]{1,0:T(8,128)(2,1)S(1)} %get-tuple-element.55.refs_1_), channel_id=1, source_target_pairs={{0,2},{1,3},{2,0},{3,1},{4,6},{5,7},{6,4},{7,5},{8,10},{9,11},{10,... | collective-permute-start | bytes 393224 | tf_op jit(solution)/shard_map/ppermute | solution.py:62
  85.9 4.4 %shard_map.124.refs_0_.refs_1_ = f32[2,256,512]{2,1,0:T(8,128)S(1)} custom-call(f32[2,256,256]{2,1,0:T(8,128)S(1)} %shard_map.123.refs_0_.refs_1_, f32[2,256,256]{2,1,0:T(8,128)S(1)} %shard_map.123.refs_0_.refs_1_, f32[2,256,256]{2,1,0:T(8,128)S(1)} %collective-permute-done.15.refs_2_), custom_call_target="tpu_custom_call" | custom-call | bytes 20000 | tf_op jit(solution)/shard_map/pallas_call | solution.py:45
  90.4 4.5 %collective-permute-done.17.refs_3_ = bf16[256,256]{1,0:T(8,128)(2,1)S(1)} collective-permute-done((bf16[256,256]{1,0:T(8,128)(2,1)S(1)}, bf16[256,256]{1,0:T(8,128)(2,1)S(1)}, u32[]{:S(2)}, u32[]{:S(2)}) %collective-permute-start.17) | collective-permute-done | bytes 131104 | tf_op jit(solution)/shard_map/ppermute | solution.py:62
  95.0 1.9 %collective-permute-done.19.refs_3_ = bf16[4,256,256]{2,1,0:T(8,128)(2,1)S(1)} collective-permute-done((bf16[4,256,256]{2,1,0:T(8,128)(2,1)S(1)}, bf16[4,256,256]{2,1,0:T(8,128)(2,1)S(1)}, u32[]{:S(2)}, u32[]{:S(2)}) %collective-permute-start.19) | collective-permute-done | bytes 524320 | tf_op jit(solution)/shard_map/ppermute | solution.py:62
  98.3 1.5 %collective-permute-start.22 = (bf16[8,128,256]{2,1,0:T(8,128)(2,1)S(1)}, bf16[8,128,256]{2,1,0:T(8,128)(2,1)S(1)}, u32[]{:S(2)}, u32[]{:S(2)}) collective-permute-start(bf16[8,128,256]{2,1,0:T(8,128)(2,1)S(1)} %get-tuple-element.57.refs_3_), channel_id=1, source_target_pairs={{0,24},{8,16},{16,8},{24,0},{1,25},{9,17},{17,9},{25,1},{2,26},{10... | collective-permute-start | bytes 1572872 | tf_op jit(solution)/shard_map/ppermute | solution.py:62
  100.4 1.5 %collective-permute-start.20 = (bf16[8,128,256]{2,1,0:T(8,128)(2,1)S(1)}, bf16[8,128,256]{2,1,0:T(8,128)(2,1)S(1)}, u32[]{:S(2)}, u32[]{:S(2)}) collective-permute-start(bf16[8,128,256]{2,1,0:T(8,128)(2,1)S(1)} %get-tuple-element.57.refs_3_), channel_id=1, source_target_pairs={{0,8},{8,0},{16,24},{24,16},{1,9},{9,1},{17,25},{25,17},{2,10},{10... | collective-permute-start | bytes 1572872 | tf_op jit(solution)/shard_map/ppermute | solution.py:62
  101.9 4.5 %shard_map.127.refs_0_.refs_1_ = f32[2,256,512]{2,1,0:T(8,128)S(1)} custom-call(bf16[256,256]{1,0:T(8,128)(2,1)} %get-tuple-element.56.refs_0_, f32[2,256,512]{2,1,0:T(8,128)S(1)} %shard_map.124.refs_0_.refs_1_), custom_call_target="tpu_custom_call" | custom-call | bytes 20000 | tf_op jit(solution)/shard_map/pallas_call | solution.py:45
  106.5 4.6 %shard_map.128.refs_0_.refs_1_ = f32[2,256,512]{2,1,0:T(8,128)S(1)} custom-call(f32[2,256,512]{2,1,0:T(8,128)S(1)} %shard_map.127.refs_0_.refs_1_, f32[2,256,512]{2,1,0:T(8,128)S(1)} %shard_map.127.refs_0_.refs_1_), custom_call_target="tpu_custom_call" | custom-call | bytes 20000 | tf_op jit(solution)/shard_map/pallas_call | solution.py:45
  111.0 3.4 %shard_map.129.refs_0_.refs_2_ = bf16[2,128,256]{2,1,0:T(8,128)(2,1)S(1)} custom-call(f32[2,256,512]{2,1,0:T(8,128)S(1)} %shard_map.128.refs_0_.refs_1_, f32[2,256,512]{2,1,0:T(8,128)S(1)} %shard_map.128.refs_0_.refs_1_, bf16[2,128,256]{2,1,0:T(8,128)(2,1)S(1)} %bitcast.7), custom_call_target="tpu_custom_call" | custom-call | bytes 20000 | tf_op jit(solution)/shard_map/pallas_call | solution.py:45
  114.5 1.5 %collective-permute-start.25 = (bf16[2,128,256]{2,1,0:T(8,128)(2,1)S(1)}, bf16[2,128,256]{2,1,0:T(8,128)(2,1)S(1)}, u32[]{:S(2)}, u32[]{:S(2)}) collective-permute-start(bf16[2,128,256]{2,1,0:T(8,128)(2,1)S(1)} %shard_map.129.refs_0_.refs_2_), channel_id=1, source_target_pairs={{0,24},{8,16},{16,8},{24,0},{1,25},{9,17},{17,9},{25,1},{2,26},{10... | collective-permute-start | bytes 393224 | tf_op jit(solution)/shard_map/ppermute | solution.py:62
  116.5 1.5 %collective-permute-start.23 = (bf16[2,128,256]{2,1,0:T(8,128)(2,1)S(1)}, bf16[2,128,256]{2,1,0:T(8,128)(2,1)S(1)}, u32[]{:S(2)}, u32[]{:S(2)}) collective-permute-start(bf16[2,128,256]{2,1,0:T(8,128)(2,1)S(1)} %shard_map.129.refs_0_.refs_2_), channel_id=1, source_target_pairs={{0,8},{8,0},{16,24},{24,16},{1,9},{9,1},{17,25},{25,17},{2,10},{10... | collective-permute-start | bytes 393224 | tf_op jit(solution)/shard_map/ppermute | solution.py:62
  118.0 7.4 %collective-permute-done.21.refs_5_ = bf16[8,128,256]{2,1,0:T(8,128)(2,1)S(1)} collective-permute-done((bf16[8,128,256]{2,1,0:T(8,128)(2,1)S(1)}, bf16[8,128,256]{2,1,0:T(8,128)(2,1)S(1)}, u32[]{:S(2)}, u32[]{:S(2)}) %collective-permute-start.21) | collective-permute-done | bytes 524320 | tf_op jit(solution)/shard_map/ppermute | solution.py:62
  125.4 2.5 %shard_map.130.refs_0_ = bf16[8,128,1024]{2,1,0:T(8,128)(2,1)} custom-call(bf16[2,128,256]{2,1,0:T(8,128)(2,1)S(1)} %shard_map.129.refs_0_.refs_2_, s32[3]{0:T(128)S(1)} %pad_add_fusion.place.refs_1_.refs_2_, bf16[8,128,1024]{2,1,0:T(8,128)(2,1)S(1)} %copy-done.8, bf16[8,128,256]{2,1,0:T(8,128)(2,1)S(1)} %get-tuple-element.57.refs_3_, ...), custom_call_target="tpu_custom_call" | custom-call | bytes 20000 | tf_op jit(solution)/shard_map/pallas_call | solution.py:45
  127.9 1.6 %copy-done.2 = bf16[8,128,1024]{2,1,0:T(8,128)(2,1)S(1)} copy-done((bf16[8,128,1024]{2,1,0:T(8,128)(2,1)S(1)}, bf16[8,128,1024]{2,1,0:T(8,128)(2,1)}, u32[]{:S(2)}) %copy-start.2) | copy-done | bytes 2097176
  130.7 2.2 %shard_map.131 = (f32[4,256,256]{2,1,0:T(8,128)}, f32[4,256,256]{2,1,0:T(8,128)}) custom-call(bf16[8,128,1024]{2,1,0:T(8,128)(2,1)S(1)} %copy-done.2, s32[3]{0:T(128)S(1)} %pad_add_fusion.place.refs_1_.refs_2_, s32[8]{0:T(128)S(1)} %copy-done.12, bf16[8,256,256]{2,1,0:T(8,128)(2,1)S(1)} %bitcast.8, f32[4,256,256]{2,1,0:T(8,128)S(1)} %copy-done.5, ...), custom_call_target="tpu_custom_call" | custom-call | bytes 20000 | tf_op jit(solution)/shard_map/pallas_call | solution.py:45
  134.2 1.6 %shard_map.132 = f32[8,128,256]{2,1,0:T(8,128)} custom-call(f32[4,256,256]{2,1,0:T(8,128)S(1)} %copy-done.9, s32[3]{0:T(128)S(1)} %pad_add_fusion.place.refs_1_.refs_2_, bf16[2,128,256]{2,1,0:T(8,128)(2,1)S(1)} %shard_map.129.refs_0_.refs_2_, bf16[2,128,256]{2,1,0:T(8,128)(2,1)S(1)} %collective-permute-done.23.refs_3_, ...), custom_call_target="tpu_custom_call" | custom-call | bytes 20000 | tf_op jit(solution)/shard_map/pallas_call | solution.py:45
  (74 shorter events, 17.5 us)
Async XLA Ops:
  7.2 120.7 %all-gather.3.cloned.1.call-start = ((), (), s32[]{:S(2)}) async-start(), calls=%async_computation | async-start | bytes 1179648 | tf_op jit(solution)/shard_map/all_gather | solution.py:474
  13.0 5.9 %collective-permute-start = (bf16[4,2,256,256]{3,2,1,0:T(8,128)(2,1)S(1)}, bf16[4,2,256,256]{3,2,1,0:T(8,128)(2,1)S(1)}, u32[]{:S(2)}, u32[]{:S(2)}) collective-permute-start(bf16[4,2,256,256]{3,2,1,0:T(8,128)(2,1)S(1)} %get-tuple-element.33.refs_0_), channel_id=1, source_target_pairs={{0,1},{1,0},{2,3},{3,2},{4,5},{5,4},{6,7},{7,6},{8,9},{9,8},{10,11... | collective-permute-start | bytes 3145736 | tf_op jit(solution)/shard_map/ppermute | solution.py:62
  13.5 22.3 %collective-permute-start.3 = (bf16[2,8,128,128]{3,2,1,0:T(8,128)(2,1)S(1)}, bf16[2,8,128,128]{3,2,1,0:T(8,128)(2,1)S(1)}, u32[]{:S(2)}, u32[]{:S(2)}) collective-permute-start(bf16[2,8,128,128]{3,2,1,0:T(8,128)(2,1)S(1)} %get-tuple-element.32.refs_0_), channel_id=1, source_target_pairs={{0,16},{8,24},{16,0},{24,8},{1,17},{9,25},{17,1},{25,9},{2,18},{10... | collective-permute-start | bytes 1572872 | tf_op jit(solution)/shard_map/ppermute | solution.py:62
  16.1 19.7 %collective-permute-start.2 = (bf16[2,8,128,128]{3,2,1,0:T(8,128)(2,1)S(1)}, bf16[2,8,128,128]{3,2,1,0:T(8,128)(2,1)S(1)}, u32[]{:S(2)}, u32[]{:S(2)}) collective-permute-start(bf16[2,8,128,128]{3,2,1,0:T(8,128)(2,1)S(1)} %get-tuple-element.39), channel_id=1, source_target_pairs={{0,8},{8,0},{16,24},{24,16},{1,9},{9,1},{17,25},{25,17},{2,10},{10... | collective-permute-start | bytes 1572872 | tf_op jit(solution)/shard_map/ppermute | solution.py:62
  19.6 19.2 %collective-permute-start.4 = (bf16[2,2,256,256]{3,2,1,0:T(8,128)(2,1)S(1)}, bf16[2,2,256,256]{3,2,1,0:T(8,128)(2,1)S(1)}, u32[]{:S(2)}, u32[]{:S(2)}) collective-permute-start(bf16[2,2,256,256]{3,2,1,0:T(8,128)(2,1)S(1)} %get-tuple-element.36.refs_0_), channel_id=1, source_target_pairs={{0,2},{1,3},{2,0},{3,1},{4,6},{5,7},{6,4},{7,5},{8,10},{9,11},{10,... | collective-permute-start | bytes 1572872 | tf_op jit(solution)/shard_map/ppermute | solution.py:62
  21.2 14.5 %collective-permute-start.1 = (bf16[2,2,128,256]{3,2,1,0:T(8,128)(2,1)S(1)}, bf16[2,2,128,256]{3,2,1,0:T(8,128)(2,1)S(1)}, u32[]{:S(2)}, u32[]{:S(2)}) collective-permute-start(bf16[2,2,128,256]{3,2,1,0:T(8,128)(2,1)S(1)} %get-tuple-element.34.refs_0_), channel_id=1, source_target_pairs={{0,8},{8,0},{16,24},{24,16},{1,9},{9,1},{17,25},{25,17},{2,10},{10... | collective-permute-start | bytes 786440 | tf_op jit(solution)/shard_map/ppermute | solution.py:62
  35.8 17.1 %copy-start.3 = (f32[8,128,256]{2,1,0:T(8,128)S(1)}, f32[8,128,256]{2,1,0:T(8,128)}, u32[]{:S(2)}) copy-start(f32[8,128,256]{2,1,0:T(8,128)} %refs_4_.4) | copy-start | bytes 3145732
  36.7 10.5 %collective-permute-start.7 = (bf16[8,128,128]{2,1,0:T(8,128)(2,1)S(1)}, bf16[8,128,128]{2,1,0:T(8,128)(2,1)S(1)}, u32[]{:S(2)}, u32[]{:S(2)}) collective-permute-start(bf16[8,128,128]{2,1,0:T(8,128)(2,1)S(1)} %get-tuple-element.46), channel_id=1, source_target_pairs={{0,16},{8,24},{16,0},{24,8},{1,17},{9,25},{17,1},{25,9},{2,18},{10... | collective-permute-start | bytes 786440 | tf_op jit(solution)/shard_map/ppermute | solution.py:62
  37.0 10.1 %collective-permute-start.8 = (bf16[8,128,128]{2,1,0:T(8,128)(2,1)S(1)}, bf16[8,128,128]{2,1,0:T(8,128)(2,1)S(1)}, u32[]{:S(2)}, u32[]{:S(2)}) collective-permute-start(bf16[8,128,128]{2,1,0:T(8,128)(2,1)S(1)} %get-tuple-element.40.refs_0_), channel_id=1, source_target_pairs={{0,8},{8,0},{16,24},{24,16},{1,9},{9,1},{17,25},{25,17},{2,10},{10... | collective-permute-start | bytes 786440 | tf_op jit(solution)/shard_map/ppermute | solution.py:62
  39.4 13.6 %collective-permute-start.6 = (bf16[1,2,256,256]{3,2,1,0:T(8,128)(2,1)S(1)}, bf16[1,2,256,256]{3,2,1,0:T(8,128)(2,1)S(1)}, u32[]{:S(2)}, u32[]{:S(2)}) collective-permute-start(bf16[1,2,256,256]{3,2,1,0:T(8,128)(2,1)S(1)} %get-tuple-element.42.refs_0_), channel_id=1, source_target_pairs={{0,4},{1,5},{2,6},{3,7},{4,0},{5,1},{6,2},{7,3},{8,12},{9,13},{10,... | collective-permute-start | bytes 786440 | tf_op jit(solution)/shard_map/ppermute | solution.py:62
  42.0 5.1 %collective-permute-start.5 = (bf16[1,2,128,256]{3,2,1,0:T(8,128)(2,1)S(1)}, bf16[1,2,128,256]{3,2,1,0:T(8,128)(2,1)S(1)}, u32[]{:S(2)}, u32[]{:S(2)}) collective-permute-start(bf16[1,2,128,256]{3,2,1,0:T(8,128)(2,1)S(1)} %get-tuple-element.38.refs_0_), channel_id=1, source_target_pairs={{0,16},{8,24},{16,0},{24,8},{1,17},{9,25},{17,1},{25,9},{2,18},{10... | collective-permute-start | bytes 393224 | tf_op jit(solution)/shard_map/ppermute | solution.py:62
  54.0 26.1 %copy-start.13 = (s32[8]{0:T(128)S(1)}, s32[8]{0:T(128)}, u32[]{:S(2)}) copy-start(s32[8]{0:T(128)} %refs_3_.5) | copy-start | bytes 100
  54.0 2.0 %collective-permute-start.9 = (bf16[4,256,256]{2,1,0:T(8,128)(2,1)S(1)}, bf16[4,256,256]{2,1,0:T(8,128)(2,1)S(1)}, u32[]{:S(2)}, u32[]{:S(2)}) collective-permute-start(bf16[4,256,256]{2,1,0:T(8,128)(2,1)S(1)} %get-tuple-element.47.refs_0_), channel_id=1, source_target_pairs={{0,1},{1,0},{2,3},{3,2},{4,5},{5,4},{6,7},{7,6},{8,9},{9,8},{10,11... | collective-permute-start | bytes 1572872 | tf_op jit(solution)/shard_map/ppermute | solution.py:62
  54.1 9.6 %collective-permute-start.10 = (bf16[2,128,256]{2,1,0:T(8,128)(2,1)S(1)}, bf16[2,128,256]{2,1,0:T(8,128)(2,1)S(1)}, u32[]{:S(2)}, u32[]{:S(2)}) collective-permute-start(bf16[2,128,256]{2,1,0:T(8,128)(2,1)S(1)} %bitcast.5), channel_id=1, source_target_pairs={{0,4},{1,5},{2,6},{3,7},{4,0},{5,1},{6,2},{7,3},{8,12},{9,13},{10,... | collective-permute-start | bytes 393224 | tf_op jit(solution)/shard_map/ppermute | solution.py:62
  63.7 17.2 %collective-permute-start.14 = (bf16[4,128,256]{2,1,0:T(8,128)(2,1)S(1)}, bf16[4,128,256]{2,1,0:T(8,128)(2,1)S(1)}, u32[]{:S(2)}, u32[]{:S(2)}) collective-permute-start(bf16[4,128,256]{2,1,0:T(8,128)(2,1)S(1)} %shard_map.121.refs_0_.refs_1_), channel_id=1, source_target_pairs={{0,2},{1,3},{2,0},{3,1},{4,6},{5,7},{6,4},{7,5},{8,10},{9,11},{10,... | collective-permute-start | bytes 786440 | tf_op jit(solution)/shard_map/ppermute | solution.py:62
  63.8 16.3 %collective-permute-start.11 = (bf16[256,256]{1,0:T(8,128)(2,1)S(1)}, bf16[256,256]{1,0:T(8,128)(2,1)S(1)}, u32[]{:S(2)}, u32[]{:S(2)}) collective-permute-start(bf16[256,256]{1,0:T(8,128)(2,1)S(1)} %get-tuple-element.51), channel_id=1, source_target_pairs={{0,2},{1,3},{2,0},{3,1},{4,6},{5,7},{6,4},{7,5},{8,10},{9,11},{10,... | collective-permute-start | bytes 393224 | tf_op jit(solution)/shard_map/ppermute | solution.py:62
  65.8 14.3 %collective-permute-start.12 = (bf16[256,256]{1,0:T(8,128)(2,1)S(1)}, bf16[256,256]{1,0:T(8,128)(2,1)S(1)}, u32[]{:S(2)}, u32[]{:S(2)}) collective-permute-start(bf16[256,256]{1,0:T(8,128)(2,1)S(1)} %get-tuple-element.52), channel_id=1, source_target_pairs={{0,4},{1,5},{2,6},{3,7},{4,0},{5,1},{6,2},{7,3},{8,12},{9,13},{10,... | collective-permute-start | bytes 393224 | tf_op jit(solution)/shard_map/ppermute | solution.py:62
  65.8 14.3 %collective-permute-start.13 = (bf16[256,256]{1,0:T(8,128)(2,1)S(1)}, bf16[256,256]{1,0:T(8,128)(2,1)S(1)}, u32[]{:S(2)}, u32[]{:S(2)}) collective-permute-start(bf16[256,256]{1,0:T(8,128)(2,1)S(1)} %get-tuple-element.49.refs_0_), channel_id=1, source_target_pairs={{0,6},{1,7},{2,4},{3,5},{4,2},{5,3},{6,0},{7,1},{8,14},{9,15},{10,... | collective-permute-start | bytes 393224 | tf_op jit(solution)/shard_map/ppermute | solution.py:62
  81.4 4.5 %collective-permute-start.15 = (f32[2,256,256]{2,1,0:T(8,128)S(1)}, f32[2,256,256]{2,1,0:T(8,128)S(1)}, u32[]{:S(2)}, u32[]{:S(2)}) collective-permute-start(f32[2,256,256]{2,1,0:T(8,128)S(1)} %shard_map.123.refs_0_.refs_1_), channel_id=1, source_target_pairs={{0,1},{1,0},{2,3},{3,2},{4,5},{5,4},{6,7},{7,6},{8,9},{9,8},{10,11... | collective-permute-start | bytes 1572872 | tf_op jit(solution)/shard_map/ppermute | solution.py:62
  81.5 8.9 %collective-permute-start.18 = (bf16[256,256]{1,0:T(8,128)(2,1)S(1)}, bf16[256,256]{1,0:T(8,128)(2,1)S(1)}, u32[]{:S(2)}, u32[]{:S(2)}) collective-permute-start(bf16[256,256]{1,0:T(8,128)(2,1)S(1)} %get-tuple-element.55.refs_1_), channel_id=1, source_target_pairs={{0,6},{1,7},{2,4},{3,5},{4,2},{5,3},{6,0},{7,1},{8,14},{9,15},{10,... | collective-permute-start | bytes 393224 | tf_op jit(solution)/shard_map/ppermute | solution.py:62
  83.6 11.2 %collective-permute-start.17 = (bf16[256,256]{1,0:T(8,128)(2,1)S(1)}, bf16[256,256]{1,0:T(8,128)(2,1)S(1)}, u32[]{:S(2)}, u32[]{:S(2)}) collective-permute-start(bf16[256,256]{1,0:T(8,128)(2,1)S(1)} %get-tuple-element.55.refs_1_), channel_id=1, source_target_pairs={{0,4},{1,5},{2,6},{3,7},{4,0},{5,1},{6,2},{7,3},{8,12},{9,13},{10,... | collective-permute-start | bytes 393224 | tf_op jit(solution)/shard_map/ppermute | solution.py:62
  83.6 11.2 %collective-permute-start.16 = (bf16[256,256]{1,0:T(8,128)(2,1)S(1)}, bf16[256,256]{1,0:T(8,128)(2,1)S(1)}, u32[]{:S(2)}, u32[]{:S(2)}) collective-permute-start(bf16[256,256]{1,0:T(8,128)(2,1)S(1)} %get-tuple-element.55.refs_1_), channel_id=1, source_target_pairs={{0,2},{1,3},{2,0},{3,1},{4,6},{5,7},{6,4},{7,5},{8,10},{9,11},{10,... | collective-permute-start | bytes 393224 | tf_op jit(solution)/shard_map/ppermute | solution.py:62
  94.9 2.0 %collective-permute-start.19 = (bf16[4,256,256]{2,1,0:T(8,128)(2,1)S(1)}, bf16[4,256,256]{2,1,0:T(8,128)(2,1)S(1)}, u32[]{:S(2)}, u32[]{:S(2)}) collective-permute-start(bf16[4,256,256]{2,1,0:T(8,128)(2,1)S(1)} %shard_map.125.refs_0_.refs_2_), channel_id=1, source_target_pairs={{0,1},{1,0},{2,3},{3,2},{4,5},{5,4},{6,7},{7,6},{8,9},{9,8},{10,11... | collective-permute-start | bytes 1572872 | tf_op jit(solution)/shard_map/ppermute | solution.py:62
  98.3 18.2 %collective-permute-start.22 = (bf16[8,128,256]{2,1,0:T(8,128)(2,1)S(1)}, bf16[8,128,256]{2,1,0:T(8,128)(2,1)S(1)}, u32[]{:S(2)}, u32[]{:S(2)}) collective-permute-start(bf16[8,128,256]{2,1,0:T(8,128)(2,1)S(1)} %get-tuple-element.57.refs_3_), channel_id=1, source_target_pairs={{0,24},{8,16},{16,8},{24,0},{1,25},{9,17},{17,9},{25,1},{2,26},{10... | collective-permute-start | bytes 1572872 | tf_op jit(solution)/shard_map/ppermute | solution.py:62
  99.9 25.5 %collective-permute-start.21 = (bf16[8,128,256]{2,1,0:T(8,128)(2,1)S(1)}, bf16[8,128,256]{2,1,0:T(8,128)(2,1)S(1)}, u32[]{:S(2)}, u32[]{:S(2)}) collective-permute-start(bf16[8,128,256]{2,1,0:T(8,128)(2,1)S(1)} %get-tuple-element.57.refs_3_), channel_id=1, source_target_pairs={{0,16},{8,24},{16,0},{24,8},{1,17},{9,25},{17,1},{25,9},{2,18},{10... | collective-permute-start | bytes 1572872 | tf_op jit(solution)/shard_map/ppermute | solution.py:62
  100.4 25.1 %collective-permute-start.20 = (bf16[8,128,256]{2,1,0:T(8,128)(2,1)S(1)}, bf16[8,128,256]{2,1,0:T(8,128)(2,1)S(1)}, u32[]{:S(2)}, u32[]{:S(2)}) collective-permute-start(bf16[8,128,256]{2,1,0:T(8,128)(2,1)S(1)} %get-tuple-element.57.refs_3_), channel_id=1, source_target_pairs={{0,8},{8,0},{16,24},{24,16},{1,9},{9,1},{17,25},{25,17},{2,10},{10... | collective-permute-start | bytes 1572872 | tf_op jit(solution)/shard_map/ppermute | solution.py:62
  106.4 19.0 %copy-start.8 = (bf16[8,128,1024]{2,1,0:T(8,128)(2,1)S(1)}, bf16[8,128,1024]{2,1,0:T(8,128)(2,1)}, u32[]{:S(2)}) copy-start(bf16[8,128,1024]{2,1,0:T(8,128)(2,1)} %refs_2_.14) | copy-start | bytes 6291460
  114.4 13.5 %copy-start.5 = (f32[4,256,256]{2,1,0:T(8,128)S(1)}, f32[4,256,256]{2,1,0:T(8,128)}, u32[]{:S(2)}) copy-start(f32[4,256,256]{2,1,0:T(8,128)} %refs_4_.5) | copy-start | bytes 3145732
  114.4 13.5 %copy-start.7 = (f32[4,256,256]{2,1,0:T(8,128)S(1)}, f32[4,256,256]{2,1,0:T(8,128)}, u32[]{:S(2)}) copy-start(f32[4,256,256]{2,1,0:T(8,128)} %refs_5_.1) | copy-start | bytes 3145732
  114.5 18.5 %collective-permute-start.25 = (bf16[2,128,256]{2,1,0:T(8,128)(2,1)S(1)}, bf16[2,128,256]{2,1,0:T(8,128)(2,1)S(1)}, u32[]{:S(2)}, u32[]{:S(2)}) collective-permute-start(bf16[2,128,256]{2,1,0:T(8,128)(2,1)S(1)} %shard_map.129.refs_0_.refs_2_), channel_id=1, source_target_pairs={{0,24},{8,16},{16,8},{24,0},{1,25},{9,17},{17,9},{25,1},{2,26},{10... | collective-permute-start | bytes 393224 | tf_op jit(solution)/shard_map/ppermute | solution.py:62
  116.0 17.0 %collective-permute-start.24 = (bf16[2,128,256]{2,1,0:T(8,128)(2,1)S(1)}, bf16[2,128,256]{2,1,0:T(8,128)(2,1)S(1)}, u32[]{:S(2)}, u32[]{:S(2)}) collective-permute-start(bf16[2,128,256]{2,1,0:T(8,128)(2,1)S(1)} %shard_map.129.refs_0_.refs_2_), channel_id=1, source_target_pairs={{0,16},{8,24},{16,0},{24,8},{1,17},{9,25},{17,1},{25,9},{2,18},{10... | collective-permute-start | bytes 393224 | tf_op jit(solution)/shard_map/ppermute | solution.py:62
  116.5 16.5 %collective-permute-start.23 = (bf16[2,128,256]{2,1,0:T(8,128)(2,1)S(1)}, bf16[2,128,256]{2,1,0:T(8,128)(2,1)S(1)}, u32[]{:S(2)}, u32[]{:S(2)}) collective-permute-start(bf16[2,128,256]{2,1,0:T(8,128)(2,1)S(1)} %shard_map.129.refs_0_.refs_2_), channel_id=1, source_target_pairs={{0,8},{8,0},{16,24},{24,16},{1,9},{9,1},{17,25},{25,17},{2,10},{10... | collective-permute-start | bytes 393224 | tf_op jit(solution)/shard_map/ppermute | solution.py:62
  (9 other events, 24.7 us)
Sparse Core Ops, SparseCore 0:
  98.5 20.5 all-gather.2

commit v6 on v5

--- a/solution.py
+++ b/solution.py
@@ -62,43 +62,42 @@
     return lax.ppermute(x, axis, [(i, i ^ mask) for i in range(size)])
 
 
-def split_kernel(place, grad_ref, *outs):
+def front_kernel(place, grad_ref, sketch_ref, keep_ref, relay_ref, *outs):
     half = outs[0].shape[3]
+    count, each = grad_ref.shape[1], keep_ref.shape[0]
     for side, out in enumerate(outs):
         for i, k in enumerate((1 << side, 3)):
             start = (place[0] ^ k) * 2 + side
             columns = pl.ds(pl.multiple_of(start * half, half), half)
-            out[i] = grad_ref[0, :, :, columns]
-
-
-def add_kernel(place, grad_ref, *refs):
-    sides = len(refs) // 3
-    arrived, sums, sends = refs[:sides], refs[sides : 2 * sides], refs[2 * sides :]
-    half = sums[0].shape[2]
-    for side in range(sides):
+            out[i, :count] = grad_ref[0, :, :, columns]
+    for k in range(4):
+        for i in range(each):
+            m = (place[0] ^ k) * each + i
+            part = jnp.dot(grad_ref[0, m], sketch_ref[...], preferred_element_type=f32)
+            if k == 0:
+                keep_ref[i] = part
+                continue
+            for side, out in enumerate(outs):
+                piece = part[:, side * half : (side + 1) * half]
+                if k == 2 >> side:
+                    relay_ref[side, i] = piece
+                else:
+                    out[k // 3, count + i] = piece.astype(bf16)
+
+
+def add_kernel(place, grad_ref, relay_ref, *refs):
+    arrived, sums, sends = refs[:2], refs[2:4], refs[4:]
+    count, _, half = sums[0].shape
+    for side in range(2):
         for i, (k, out) in enumerate(((0, sums[side]), (2 >> side, sends[side]))):
             start = (place[0] ^ k) * 2 + side
             columns = pl.ds(pl.multiple_of(start * half, half), half)
-            for m in range(out.shape[0]):
+            for m in range(count):
                 total = grad_ref[0, m, :, columns].astype(f32) + arrived[side][i, m].astype(f32)
                 out[m] = total.astype(out.dtype)
-
-
-def sample_kernel(place, grad_ref, sketch_ref, keep_ref, send_ref):
-    half, each = keep_ref.shape[0], keep_ref.shape[1]
-    for k in range(2 * half):
-        out = (keep_ref, send_ref)[k % 2]
-        for i in range(each):
-            m = (place[0] ^ k) * each + i
-            product = jnp.dot(grad_ref[0, m], sketch_ref[...], preferred_element_type=f32)
-            out[k // 2, i] = product.astype(out.dtype)
-
-
-def halve_kernel(keep_ref, other_ref, *outs):
-    for k in range(keep_ref.shape[0]):
-        total = keep_ref[k] + other_ref[k].astype(f32)
-        out = outs[k % len(outs)]
-        out[k // len(outs)] = total.astype(out.dtype)
+        for i in range(relay_ref.shape[1]):
+            total = relay_ref[side, i] + arrived[side][1, count + i].astype(f32)
+            sends[side][count + i] = total.astype(bf16)
 
 
 def stack_kernel(own_ref, other_ref, out_ref):
@@ -244,15 +243,16 @@
 
 
 def project_kernel(place, *refs, scale):
-    *sums, basis_ref, mine_ref, other_ref = refs
+    sums, relayed, arrived = refs[:2], refs[2:4], refs[4:6]
+    keep_ref, basis_ref, mine_ref, sample_ref, other_ref = refs[6:]
     core = place[2]
-    half = sums[0].shape[2]
+    count, _, half = sums[0].shape
     for i in range(mine_ref.shape[0]):
         for out, want in ((other_ref, 1 - core), (mine_ref, core)):
             m = 2 * i + want
             scaled = (basis_ref[m] * scale).astype(bf16)
             for side in range(2):
-                total = sums[side][m] + sums[2 + side][m].astype(f32)
+                total = sums[side][m] + relayed[side][m].astype(f32)
                 product = lax.dot_general(
                     scaled,
                     total.astype(bf16),
@@ -260,6 +260,12 @@
                     preferred_element_type=f32,
                 )
                 out[i, :, side * half : (side + 1) * half] = product.astype(out.dtype)
+    for i in range(keep_ref.shape[0]):
+        for side in range(2):
+            columns = slice(side * half, (side + 1) * half)
+            total = keep_ref[i, :, columns] + arrived[side][0, count + i].astype(f32)
+            total = total + relayed[side][count + i].astype(f32)
+            sample_ref[i, :, columns] = total.astype(bf16)
 
 
 def pair_kernel(place, mine_ref, other_ref, *outs):
@@ -365,70 +371,50 @@
     struct = jax.ShapeDtypeStruct
 
     call = Sequence()
-    halved = struct((2, count, shard, quarter // 2), bf16)
-    sides = call(split_kernel, [halved] * 2, (place, grads), scalars=1)
-    half = chips
+    half = quarter // 2
+    keep, relay, *sides = call(
+        front_kernel,
+        [struct((each, shard, rank_full), f32), struct((2, each, shard, half), f32)]
+        + [struct((2, count + each, shard, half), bf16)] * 2,
+        (place, grads, sketch),
+        scalars=1,
+    )
+    sides = [swap(sides[i], "dp", 1 << i) for i in range(2)]
+    left = chips
     moments, lent = call(
         pick_kernel,
-        [struct((half, 2, rank_full, quarter), bf16)] * 2,
+        [struct((left, 2, rank_full, quarter), bf16)] * 2,
         (place, owner, first_moment, second_moment),
         scalars=2,
     )
     lent = swap(lent, "rows", 1)
-    keep, send = call(
-        sample_kernel,
-        [struct((groups // 2, each, shard, rank_full), kind) for kind in (f32, bf16)],
-        (place, grads, sketch),
-        scalars=1,
-    )
-    half //= 2
-    moments, lent = call(
-        functools.partial(merge_kernel, bit=-1),
-        [struct((half, 2, rank_full, quarter), bf16)] * 2,
-        (place, owner, moments, lent),
-        scalars=2,
-    )
-    lent = swap(lent, "rows", 2)
-    sides = [swap(sides[i], "dp", 1 << i) for i in range(2)]
-    send = swap(send, "dp", 1)
-    part = groups // 2
-    mask = 1
-    while part > 1:
-        part //= 2
-        keep, send = call(
-            halve_kernel,
-            [struct((part, each, shard, rank_full), kind) for kind in (f32, bf16)],
-            (keep, send),
-        )
-        mask *= 2
-        send = swap(send, "dp", mask)
-    *sums, left, right = call(
-        add_kernel,
-        [struct((count, shard, quarter // 2), kind) for kind in (f32, f32, bf16, bf16)],
-        (place, grads, *sides),
-        scalars=1,
-    )
-    left, right = swap(left, "dp", 2), swap(right, "dp", 1)
-    bit = 0
-    while half > 1:
-        half //= 2
+    bit = -1
+    while left > 1:
+        left //= 2
         moments, lent = call(
             functools.partial(merge_kernel, bit=bit),
-            [struct((half, 2, rank_full, quarter), bf16)] * 2,
+            [struct((left, 2, rank_full, quarter), bf16)] * 2,
             (place, owner, moments, lent),
             scalars=2,
         )
         bit += 1
         lent = swap(lent, "rows", 2 << bit)
-    sample = call(
-        halve_kernel,
-        [struct((1, each, shard, rank_full), bf16)],
-        (keep, send),
-    )[0].reshape(each, shard, rank_full)
-    mine, other = call(
+    *sums, first_send, second_send = call(
+        add_kernel,
+        [struct((count, shard, half), f32)] * 2
+        + [struct((count + each, shard, half), bf16)] * 2,
+        (place, grads, relay, *sides),
+        scalars=1,
+    )
+    relayed = [swap(first_send, "dp", 2), swap(second_send, "dp", 1)]
+    mine, sample, other = call(
         functools.partial(project_kernel, scale=inverse_root),
-        [struct((chips, rank_full, quarter), f32), struct((chips, rank_full, quarter), bf16)],
-        (place, *sums, left, right, basis),
+        [
+            struct((chips, rank_full, quarter), f32),
+            struct((each, shard, rank_full), bf16),
+            struct((chips, rank_full, quarter), bf16),
+        ],
+        (place, *sums, *relayed, *sides, keep, basis),
         scalars=1,
         after=(lent,),
     )
@@ -442,12 +428,6 @@
         scalars=1,
     )
     terms = [terms[0]] + [swap(terms[k], "rows", 2 * k) for k in range(1, chips)]
-    stacked = sample
-    while mask > 1:
-        both = struct((2 * stacked.shape[0], shard, rank_full), bf16)
-        stacked = call(stack_kernel, both, (stacked, arrived))
-        mask //= 2
-        arrived = swap(stacked, "rows", 2 * mask)
     work_shape = struct((each, rank_full, 2 * rank_full), f32)
     last = rank_full // BLOCK - 1
     update, projected = call(
@@ -457,21 +437,33 @@
         scalars=3,
     )
     near = [update] + [swap(update, "rows", 2 * k) for k in range(1, chips)]
+    stacked = sample
+    while mask > 1:
+        both = struct((2 * stacked.shape[0], shard, rank_full), bf16)
+        stacked = call(stack_kernel, both, (stacked, arrived))
+        mask //= 2
+        arrived = swap(stacked, "rows", 2 * mask)
+    near = call(
+        gather_kernel,
+        struct((chips, rank_full, quarter), bf16),
+        tuple(near),
+        after=(arrived,),
+    )
+    far = swap(near, "rows", 1)
     gram = call(
         gram_kernel, struct((each, rank_full, rank_full), f32), (stacked, arrived)
     )
     other_gram = swap(gram, "rows", 1)
-    work = call(start_kernel, work_shape, (gram, other_gram))
-    near = call(gather_kernel, struct((chips, rank_full, quarter), bf16), tuple(near))
-    far = swap(near, "rows", 1)
     delta, projected = call(
         functools.partial(delta_kernel, chips=chips, scale=inverse_root),
         [struct((count, shard, quarter), bf16), struct((rank_full, quarter), bf16)],
         (place, near, far, basis, projected),
         scalars=1,
+        after=(other_gram,),
     )
     deltas = [delta] + [swap(delta, "dp", k) for k in range(1, groups)]
     gathered = lax.all_gather(projected, "rows", axis=0)
+    work = call(start_kernel, work_shape, (gram, other_gram))
     for j in range(1, last):
         work = call(functools.partial(middle_kernel, j=j), work_shape, (work,))
     rows_basis = call(
@@ -481,17 +473,17 @@
         scratch=[pltpu.VMEM(work_shape.shape, f32)],
     )
     shared = [rows_basis] + [swap(rows_basis, "dp", k) for k in range(1, groups)]
+    first_out, second_out = call(
+        functools.partial(moment_kernel, chunks=1),
+        [struct(first_moment.shape, f32)] * 2,
+        (place, owner, gathered, first_moment, second_moment),
+        scalars=2,
+    )
     new_weight = call(
         functools.partial(weight_kernel, groups=groups, chunks=1),
         struct(weight.shape, bf16),
         (place, weight, *deltas),
         scalars=1,
-    )
-    first_out, second_out = call(
-        functools.partial(moment_kernel, chunks=1),
-        [struct(first_moment.shape, f32)] * 2,
-        (place, owner, gathered, first_moment, second_moment),
-        scalars=2,
     )
     new_basis = call(basis_kernel, struct(basis.shape, f32), (place, *shared), scalars=1)
     return (new_weight, new_basis, first_out, second_out)

time: 143 us -> 140 us (0.979)
  waiting for transfers between devices: 57.8 us -> 52.6 us
    ppermute x26 -> x24, waiting for transfers between devices: 57.8 us -> 52.6 us  [swap(): return lax.ppermute(x, axis, [(i, i ^ mask) for i in range(size)])]
    ppermute x26 -> x24, starting transfers between devices: 29.4 us -> 30.3 us  [swap(): return lax.ppermute(x, axis, [(i, i ^ mask) for i in range(size)])]
    pallas_call x22 -> x19, Pallas kernels: 32.8 us -> 33.5 us  [__call__(): pl.pallas_call(body, out_shape=out_shape, in_specs=specs, out_specs=[VMEM...]
    unnamed x28 -> x32, local copies, waits for them, and re-layouts: 8.11 us -> 8.44 us
  transfers between devices with their start and end apart: 27 -> 25, of which waited for: 9 -> 12; matrix products, arithmetic and copies ran while one was open for 0% -> 0% of each run, Pallas kernels for 19% -> 18%
where the time goes in v6:
time: 140 us; the launch traced here: 139 us
  waiting for transfers between devices  52.6 us (38%)
  Pallas kernels  33.5 us (24%)
  starting transfers between devices  30.3 us (22%)
  between operations  14.3 us (10%)
  local copies, waits for them, and re-layouts  8.44 us (6%)
    ppermute x24, waiting for transfers between devices, swap(): return lax.ppermute(x, axis, [(i, i ^ mask) for i in range(size)])  52.6 us
    pallas_call x19, Pallas kernels, __call__(): pl.pallas_call(body, out_shape=out_shape, in_specs=specs, out_specs=[VMEM...  33.5 us
    ppermute x24, starting transfers between devices, swap(): return lax.ppermute(x, axis, [(i, i ^ mask) for i in range(size)])  30.3 us
    unnamed x32, local copies, waits for them, and re-layouts  8.44 us
  transfers between devices with their start and end apart: 25, of which 12 were waited for; matrix products, arithmetic and copies ran while one was open for 0% of the time, Pallas kernels for 18%

profile of v6, /device:TPU:0, one launch (start us, length us, event | category | flops | bytes accessed | tf_op | source)
XLA Modules:
  0.0 139.2 jit_solution(10931463518766510620)
XLA Ops:
  7.3 1.6 %copy-done = bf16[1,8,128,1024]{3,2,1,0:T(8,128)(2,1)S(1)} copy-done((bf16[1,8,128,1024]{3,2,1,0:T(8,128)(2,1)S(1)}, bf16[1,8,128,1024]{3,2,1,0:T(8,128)(2,1)}, u32[]{:S(2)}) %copy-start) | copy-done | bytes 2097176
  10.0 1.5 %shard_map.111 = (f32[2,128,256]{2,1,0:T(8,128)S(1)}, f32[2,2,128,128]{3,2,1,0:T(8,128)S(1)}, bf16[2,10,128,128]{3,2,1,0:T(8,128)(2,1)S(1)}, bf16[2,10,128,128]{3,2,1,0:T(8,128)(2,1)S(1)}) custom-call(s32[3]{0:T(128)S(1)} %pad_add_fusion.place.refs_1_.refs_2_, bf16[1,8,128,1024]{3,2,1,0:T(8,128)(2,1)S(1)} %copy-done, bf16[1024,256]{1,0:T(8,128)(2,1)S(1)} %copy-done.9), custom_call_target="tpu_custom_call" | custom-call | bytes 20000 | tf_op jit(solution)/shard_map/pallas_call | solution.py:45
  12.8 2.6 %collective-permute-start.2 = (bf16[2,10,128,128]{3,2,1,0:T(8,128)(2,1)S(1)}, bf16[2,10,128,128]{3,2,1,0:T(8,128)(2,1)S(1)}, u32[]{:S(2)}, u32[]{:S(2)}) collective-permute-start(bf16[2,10,128,128]{3,2,1,0:T(8,128)(2,1)S(1)} %get-tuple-element.38), channel_id=1, source_target_pairs={{0,8},{8,0},{16,24},{24,16},{1,9},{9,1},{17,25},{25,17},{2,10},{10... | collective-permute-start | bytes 1966088 | tf_op jit(solution)/shard_map/ppermute | solution.py:62
  15.4 1.5 %collective-permute-start.3 = (bf16[2,10,128,128]{3,2,1,0:T(8,128)(2,1)S(1)}, bf16[2,10,128,128]{3,2,1,0:T(8,128)(2,1)S(1)}, u32[]{:S(2)}, u32[]{:S(2)}) collective-permute-start(bf16[2,10,128,128]{3,2,1,0:T(8,128)(2,1)S(1)} %get-tuple-element.31.refs_0_), channel_id=1, source_target_pairs={{0,16},{8,24},{16,0},{24,8},{1,17},{9,25},{17,1},{25,9},{2,18},{10... | collective-permute-start | bytes 1966088 | tf_op jit(solution)/shard_map/ppermute | solution.py:62
  17.6 1.6 %collective-permute-start.1 = (bf16[2,2,256,256]{3,2,1,0:T(8,128)(2,1)S(1)}, bf16[2,2,256,256]{3,2,1,0:T(8,128)(2,1)S(1)}, u32[]{:S(2)}, u32[]{:S(2)}) collective-permute-start(bf16[2,2,256,256]{3,2,1,0:T(8,128)(2,1)S(1)} %get-tuple-element.34.refs_0_), channel_id=1, source_target_pairs={{0,2},{1,3},{2,0},{3,1},{4,6},{5,7},{6,4},{7,5},{8,10},{9,11},{10,... | collective-permute-start | bytes 1572872 | tf_op jit(solution)/shard_map/ppermute | solution.py:62
  19.2 12.1 %collective-permute-done.1.refs_4_ = bf16[2,2,256,256]{3,2,1,0:T(8,128)(2,1)S(1)} collective-permute-done((bf16[2,2,256,256]{3,2,1,0:T(8,128)(2,1)S(1)}, bf16[2,2,256,256]{3,2,1,0:T(8,128)(2,1)S(1)}, u32[]{:S(2)}, u32[]{:S(2)}) %collective-permute-start.1) | collective-permute-done | bytes 524320 | tf_op jit(solution)/shard_map/ppermute | solution.py:62
  33.1 1.6 %collective-permute-start.5 = (bf16[10,128,128]{2,1,0:T(8,128)(2,1)S(1)}, bf16[10,128,128]{2,1,0:T(8,128)(2,1)S(1)}, u32[]{:S(2)}, u32[]{:S(2)}) collective-permute-start(bf16[10,128,128]{2,1,0:T(8,128)(2,1)S(1)} %get-tuple-element.42), channel_id=1, source_target_pairs={{0,16},{8,24},{16,0},{24,8},{1,17},{9,25},{17,1},{25,9},{2,18},{10... | collective-permute-start | bytes 983048 | tf_op jit(solution)/shard_map/ppermute | solution.py:62
  35.8 2.6 %collective-permute-start.4 = (bf16[1,2,256,256]{3,2,1,0:T(8,128)(2,1)S(1)}, bf16[1,2,256,256]{3,2,1,0:T(8,128)(2,1)S(1)}, u32[]{:S(2)}, u32[]{:S(2)}) collective-permute-start(bf16[1,2,256,256]{3,2,1,0:T(8,128)(2,1)S(1)} %get-tuple-element.36.refs_0_), channel_id=1, source_target_pairs={{0,4},{1,5},{2,6},{3,7},{4,0},{5,1},{6,2},{7,3},{8,12},{9,13},{10,... | collective-permute-start | bytes 786440 | tf_op jit(solution)/shard_map/ppermute | solution.py:62
  38.4 10.9 %collective-permute-done.4.refs_1_.refs_9_ = bf16[1,2,256,256]{3,2,1,0:T(8,128)(2,1)S(1)} collective-permute-done((bf16[1,2,256,256]{3,2,1,0:T(8,128)(2,1)S(1)}, bf16[1,2,256,256]{3,2,1,0:T(8,128)(2,1)S(1)}, u32[]{:S(2)}, u32[]{:S(2)}) %collective-permute-start.4) | collective-permute-done | bytes 262176 | tf_op jit(solution)/shard_map/ppermute | solution.py:62
  49.3 1.7 %shard_map.116 = (f32[4,256,256]{2,1,0:T(8,128)S(1)}, bf16[2,128,256]{2,1,0:T(8,128)(2,1)S(1)}, bf16[4,256,256]{2,1,0:T(8,128)(2,1)S(1)}) custom-call(bf16[10,128,128]{2,1,0:T(8,128)(2,1)S(1)} %get-tuple-element.39.refs_0_, bf16[1,2,256,256]{3,2,1,0:T(8,128)(2,1)S(1)} %collective-permute-done.4.refs_1_.refs_9_, s32[3]{0:T(128)S(1)} %pad_add_fusion.place.refs_1_.refs_2_, ...), custom_call_target="tpu_custom_call" | custom-call | bytes 20000 | tf_op jit(solution)/shard_map/pallas_call | solution.py:45
  51.1 1.9 %collective-permute-done.7.refs_3_ = bf16[4,256,256]{2,1,0:T(8,128)(2,1)S(1)} collective-permute-done((bf16[4,256,256]{2,1,0:T(8,128)(2,1)S(1)}, bf16[4,256,256]{2,1,0:T(8,128)(2,1)S(1)}, u32[]{:S(2)}, u32[]{:S(2)}) %collective-permute-start.7) | collective-permute-done | bytes 524320 | tf_op jit(solution)/shard_map/ppermute | solution.py:62
  53.6 3.5 %collective-permute-start.10 = (bf16[256,256]{1,0:T(8,128)(2,1)S(1)}, bf16[256,256]{1,0:T(8,128)(2,1)S(1)}, u32[]{:S(2)}, u32[]{:S(2)}) collective-permute-start(bf16[256,256]{1,0:T(8,128)(2,1)S(1)} %get-tuple-element.46.refs_0_), channel_id=1, source_target_pairs={{0,6},{1,7},{2,4},{3,5},{4,2},{5,3},{6,0},{7,1},{8,14},{9,15},{10,... | collective-permute-start | bytes 393224 | tf_op jit(solution)/shard_map/ppermute | solution.py:62
  58.1 2.0 %collective-permute-start.11 = (bf16[2,128,256]{2,1,0:T(8,128)(2,1)S(1)}, bf16[2,128,256]{2,1,0:T(8,128)(2,1)S(1)}, u32[]{:S(2)}, u32[]{:S(2)}) collective-permute-start(bf16[2,128,256]{2,1,0:T(8,128)(2,1)S(1)} %get-tuple-element.52.refs_1_.refs_2_), channel_id=1, source_target_pairs={{0,4},{1,5},{2,6},{3,7},{4,0},{5,1},{6,2},{7,3},{8,12},{9,13},{10,... | collective-permute-start | bytes 393224 | tf_op jit(solution)/shard_map/ppermute | solution.py:62
  60.1 1.8 %collective-permute-done.10.refs_7_ = bf16[256,256]{1,0:T(8,128)(2,1)S(1)} collective-permute-done((bf16[256,256]{1,0:T(8,128)(2,1)S(1)}, bf16[256,256]{1,0:T(8,128)(2,1)S(1)}, u32[]{:S(2)}, u32[]{:S(2)}) %collective-permute-start.10) | collective-permute-done | bytes 131104 | tf_op jit(solution)/shard_map/ppermute | solution.py:62
  61.9 3.9 %collective-permute-done.8.refs_5_ = bf16[256,256]{1,0:T(8,128)(2,1)S(1)} collective-permute-done((bf16[256,256]{1,0:T(8,128)(2,1)S(1)}, bf16[256,256]{1,0:T(8,128)(2,1)S(1)}, u32[]{:S(2)}, u32[]{:S(2)}) %collective-permute-start.8) | collective-permute-done | bytes 131104 | tf_op jit(solution)/shard_map/ppermute | solution.py:62
  65.8 5.6 %collective-permute-done.9.refs_6_ = bf16[256,256]{1,0:T(8,128)(2,1)S(1)} collective-permute-done((bf16[256,256]{1,0:T(8,128)(2,1)S(1)}, bf16[256,256]{1,0:T(8,128)(2,1)S(1)}, u32[]{:S(2)}, u32[]{:S(2)}) %collective-permute-start.9) | collective-permute-done | bytes 131104 | tf_op jit(solution)/shard_map/ppermute | solution.py:62
  73.5 2.0 %collective-permute-start.13 = (bf16[256,256]{1,0:T(8,128)(2,1)S(1)}, bf16[256,256]{1,0:T(8,128)(2,1)S(1)}, u32[]{:S(2)}, u32[]{:S(2)}) collective-permute-start(bf16[256,256]{1,0:T(8,128)(2,1)S(1)} %get-tuple-element.53.refs_2_), channel_id=1, source_target_pairs={{0,2},{1,3},{2,0},{3,1},{4,6},{5,7},{6,4},{7,5},{8,10},{9,11},{10,... | collective-permute-start | bytes 393224 | tf_op jit(solution)/shard_map/ppermute | solution.py:62
  76.5 1.4 %collective-permute-start.15 = (bf16[256,256]{1,0:T(8,128)(2,1)S(1)}, bf16[256,256]{1,0:T(8,128)(2,1)S(1)}, u32[]{:S(2)}, u32[]{:S(2)}) collective-permute-start(bf16[256,256]{1,0:T(8,128)(2,1)S(1)} %get-tuple-element.53.refs_2_), channel_id=1, source_target_pairs={{0,6},{1,7},{2,4},{3,5},{4,2},{5,3},{6,0},{7,1},{8,14},{9,15},{10,... | collective-permute-start | bytes 393224 | tf_op jit(solution)/shard_map/ppermute | solution.py:62
  77.9 8.7 %collective-permute-done.13.refs_3_ = bf16[256,256]{1,0:T(8,128)(2,1)S(1)} collective-permute-done((bf16[256,256]{1,0:T(8,128)(2,1)S(1)}, bf16[256,256]{1,0:T(8,128)(2,1)S(1)}, u32[]{:S(2)}, u32[]{:S(2)}) %collective-permute-start.13) | collective-permute-done | bytes 131104 | tf_op jit(solution)/shard_map/ppermute | solution.py:62
  86.6 4.2 %collective-permute-done.15.refs_5_ = bf16[256,256]{1,0:T(8,128)(2,1)S(1)} collective-permute-done((bf16[256,256]{1,0:T(8,128)(2,1)S(1)}, bf16[256,256]{1,0:T(8,128)(2,1)S(1)}, u32[]{:S(2)}, u32[]{:S(2)}) %collective-permute-start.15) | collective-permute-done | bytes 131104 | tf_op jit(solution)/shard_map/ppermute | solution.py:62
  91.9 1.4 %collective-permute-done.16.refs_1_.refs_2_ = f32[2,256,256]{2,1,0:T(8,128)S(1)} collective-permute-done((f32[2,256,256]{2,1,0:T(8,128)S(1)}, f32[2,256,256]{2,1,0:T(8,128)S(1)}, u32[]{:S(2)}, u32[]{:S(2)}) %collective-permute-start.16) | collective-permute-done | bytes 524320 | tf_op jit(solution)/shard_map/ppermute | solution.py:62
  94.0 1.4 %shard_map.122 = (bf16[8,128,256]{2,1,0:T(8,128)(2,1)S(1)}, bf16[256,256]{1,0:T(8,128)(2,1)}) custom-call(f32[2,256,256]{2,1,0:T(8,128)S(1)} %shard_map.121.refs_0_.refs_1_, f32[2,256,256]{2,1,0:T(8,128)S(1)} %collective-permute-done.16.refs_1_.refs_2_, s32[3]{0:T(128)S(1)} %pad_add_fusion.place.refs_1_.refs_2_, ...), custom_call_target="tpu_custom_call" | custom-call | bytes 20000 | tf_op jit(solution)/shard_map/pallas_call | solution.py:45
  97.8 2.1 %collective-permute-start.20 = (bf16[8,128,256]{2,1,0:T(8,128)(2,1)}, bf16[8,128,256]{2,1,0:T(8,128)(2,1)}, u32[]{:S(2)}, u32[]{:S(2)}) collective-permute-start(bf16[8,128,256]{2,1,0:T(8,128)(2,1)} %copy-done.10), channel_id=1, source_target_pairs={{0,24},{8,16},{16,8},{24,0},{1,25},{9,17},{17,9},{25,1},{2,26},{10... | collective-permute-start | bytes 1572872 | tf_op jit(solution)/shard_map/ppermute | solution.py:62
  99.8 4.4 %shard_map.123.refs_0_.refs_1_ = f32[2,256,512]{2,1,0:T(8,128)S(1)} custom-call(bf16[256,256]{1,0:T(8,128)(2,1)} %get-tuple-element.54.refs_0_, f32[2,256,256]{2,1,0:T(8,128)S(1)} %shard_map.121.refs_0_.refs_1_, f32[2,256,256]{2,1,0:T(8,128)S(1)} %collective-permute-done.16.refs_1_.refs_2_), custom_call_target="tpu_custom_call" | custom-call | bytes 20000 | tf_op jit(solution)/shard_map/pallas_call | solution.py:45
  104.2 4.6 %shard_map.124.refs_0_.refs_1_ = f32[2,256,512]{2,1,0:T(8,128)S(1)} custom-call(f32[2,256,512]{2,1,0:T(8,128)S(1)} %shard_map.123.refs_0_.refs_1_, f32[2,256,512]{2,1,0:T(8,128)S(1)} %shard_map.123.refs_0_.refs_1_), custom_call_target="tpu_custom_call" | custom-call | bytes 20000 | tf_op jit(solution)/shard_map/pallas_call | solution.py:45
  108.8 4.6 %shard_map.125.refs_0_.refs_1_ = f32[2,256,512]{2,1,0:T(8,128)S(1)} custom-call(f32[2,256,512]{2,1,0:T(8,128)S(1)} %shard_map.124.refs_0_.refs_1_, f32[2,256,512]{2,1,0:T(8,128)S(1)} %shard_map.124.refs_0_.refs_1_), custom_call_target="tpu_custom_call" | custom-call | bytes 20000 | tf_op jit(solution)/shard_map/pallas_call | solution.py:45
  113.4 3.4 %shard_map.126.refs_0_.refs_2_ = bf16[2,128,256]{2,1,0:T(8,128)(2,1)S(1)} custom-call(f32[2,256,512]{2,1,0:T(8,128)S(1)} %shard_map.125.refs_0_.refs_1_, f32[2,256,512]{2,1,0:T(8,128)S(1)} %shard_map.125.refs_0_.refs_1_, bf16[2,128,256]{2,1,0:T(8,128)(2,1)S(1)} %get-tuple-element.52.refs_1_.refs_2_), custom_call_target="tpu_custom_call" | custom-call | bytes 20000 | tf_op jit(solution)/shard_map/pallas_call | solution.py:45
  119.1 2.1 %collective-permute-start.23 = (bf16[2,128,256]{2,1,0:T(8,128)(2,1)S(1)}, bf16[2,128,256]{2,1,0:T(8,128)(2,1)S(1)}, u32[]{:S(2)}, u32[]{:S(2)}) collective-permute-start(bf16[2,128,256]{2,1,0:T(8,128)(2,1)S(1)} %shard_map.126.refs_0_.refs_2_), channel_id=1, source_target_pairs={{0,24},{8,16},{16,8},{24,0},{1,25},{9,17},{17,9},{25,1},{2,26},{10... | collective-permute-start | bytes 393224 | tf_op jit(solution)/shard_map/ppermute | solution.py:62
  122.6 2.2 %shard_map.127 = (f32[4,256,256]{2,1,0:T(8,128)}, f32[4,256,256]{2,1,0:T(8,128)}) custom-call(bf16[2,128,256]{2,1,0:T(8,128)(2,1)S(1)} %shard_map.126.refs_0_.refs_2_, s32[3]{0:T(128)S(1)} %pad_add_fusion.place.refs_1_.refs_2_, s32[8]{0:T(128)S(1)} %copy-done.14, bf16[8,256,256]{2,1,0:T(8,128)(2,1)S(1)} %bitcast.4, f32[4,256,256]{2,1,0:T(8,128)S(1)} %copy-done.4, ...), custom_call_target="tpu_custom_call" | custom-call | bytes 20000 | tf_op jit(solution)/shard_map/pallas_call | solution.py:45
  126.0 3.2 %shard_map.128.refs_0_ = bf16[8,128,1024]{2,1,0:T(8,128)(2,1)} custom-call(f32[4,256,256]{2,1,0:T(8,128)S(1)} %copy-done.8, s32[3]{0:T(128)S(1)} %pad_add_fusion.place.refs_1_.refs_2_, bf16[8,128,1024]{2,1,0:T(8,128)(2,1)S(1)} %copy-done.6, bf16[8,128,256]{2,1,0:T(8,128)(2,1)S(1)} %copy-done.11, bf16[8,128,256]{2,1,0:T(8,128)(2,1)S(1)} %copy-done.13, ...), custom_call_target="tpu_custom_call" | custom-call | bytes 20000 | tf_op jit(solution)/shard_map/pallas_call | solution.py:45
  129.2 1.6 %copy-done.2 = bf16[8,128,1024]{2,1,0:T(8,128)(2,1)S(1)} copy-done((bf16[8,128,1024]{2,1,0:T(8,128)(2,1)S(1)}, bf16[8,128,1024]{2,1,0:T(8,128)(2,1)}, u32[]{:S(2)}) %copy-start.2) | copy-done | bytes 2097176
  130.8 1.6 %shard_map.129 = f32[8,128,256]{2,1,0:T(8,128)} custom-call(bf16[8,128,1024]{2,1,0:T(8,128)(2,1)S(1)} %copy-done.2, s32[3]{0:T(128)S(1)} %pad_add_fusion.place.refs_1_.refs_2_, bf16[2,128,256]{2,1,0:T(8,128)(2,1)S(1)} %shard_map.126.refs_0_.refs_2_, bf16[2,128,256]{2,1,0:T(8,128)(2,1)S(1)} %collective-permute-done.21.refs_3_, ...), custom_call_target="tpu_custom_call" | custom-call | bytes 20000 | tf_op jit(solution)/shard_map/pallas_call | solution.py:45
  (71 shorter events, 19.7 us)
Async XLA Ops:
  7.2 4.3 %copy-start.14 = (s32[8]{0:T(128)S(1)}, s32[8]{0:T(128)}, u32[]{:S(2)}) copy-start(s32[8]{0:T(128)} %refs_2_.12) | copy-start | bytes 100
  7.2 114.0 %all-gather.3.cloned.1.call-start = ((), (), s32[]{:S(2)}) async-start(), calls=%async_computation | async-start | bytes 1179648 | tf_op jit(solution)/shard_map/all_gather | solution.py:465
  12.3 4.6 %collective-permute-start = (bf16[4,2,256,256]{3,2,1,0:T(8,128)(2,1)S(1)}, bf16[4,2,256,256]{3,2,1,0:T(8,128)(2,1)S(1)}, u32[]{:S(2)}, u32[]{:S(2)}) collective-permute-start(bf16[4,2,256,256]{3,2,1,0:T(8,128)(2,1)S(1)} %get-tuple-element.32.refs_0_), channel_id=1, source_target_pairs={{0,1},{1,0},{2,3},{3,2},{4,5},{5,4},{6,7},{7,6},{8,9},{9,8},{10,11... | collective-permute-start | bytes 3145736 | tf_op jit(solution)/shard_map/ppermute | solution.py:62
  12.8 19.1 %collective-permute-start.2 = (bf16[2,10,128,128]{3,2,1,0:T(8,128)(2,1)S(1)}, bf16[2,10,128,128]{3,2,1,0:T(8,128)(2,1)S(1)}, u32[]{:S(2)}, u32[]{:S(2)}) collective-permute-start(bf16[2,10,128,128]{3,2,1,0:T(8,128)(2,1)S(1)} %get-tuple-element.38), channel_id=1, source_target_pairs={{0,8},{8,0},{16,24},{24,16},{1,9},{9,1},{17,25},{25,17},{2,10},{10... | collective-permute-start | bytes 1966088 | tf_op jit(solution)/shard_map/ppermute | solution.py:62
  15.4 16.8 %collective-permute-start.3 = (bf16[2,10,128,128]{3,2,1,0:T(8,128)(2,1)S(1)}, bf16[2,10,128,128]{3,2,1,0:T(8,128)(2,1)S(1)}, u32[]{:S(2)}, u32[]{:S(2)}) collective-permute-start(bf16[2,10,128,128]{3,2,1,0:T(8,128)(2,1)S(1)} %get-tuple-element.31.refs_0_), channel_id=1, source_target_pairs={{0,16},{8,24},{16,0},{24,8},{1,17},{9,25},{17,1},{25,9},{2,18},{10... | collective-permute-start | bytes 1966088 | tf_op jit(solution)/shard_map/ppermute | solution.py:62
  16.9 15.3 %copy-start.1 = (bf16[1,8,128,1024]{3,2,1,0:T(8,128)(2,1)S(1)}, bf16[1,8,128,1024]{3,2,1,0:T(8,128)(2,1)}, u32[]{:S(2)}) copy-start(bf16[1,8,128,1024]{3,2,1,0:T(8,128)(2,1)} %refs_2_.10) | copy-start | bytes 6291460
  17.6 13.8 %collective-permute-start.1 = (bf16[2,2,256,256]{3,2,1,0:T(8,128)(2,1)S(1)}, bf16[2,2,256,256]{3,2,1,0:T(8,128)(2,1)S(1)}, u32[]{:S(2)}, u32[]{:S(2)}) collective-permute-start(bf16[2,2,256,256]{3,2,1,0:T(8,128)(2,1)S(1)} %get-tuple-element.34.refs_0_), channel_id=1, source_target_pairs={{0,2},{1,3},{2,0},{3,1},{4,6},{5,7},{6,4},{7,5},{8,10},{9,11},{10,... | collective-permute-start | bytes 1572872 | tf_op jit(solution)/shard_map/ppermute | solution.py:62
  33.1 16.2 %collective-permute-start.5 = (bf16[10,128,128]{2,1,0:T(8,128)(2,1)S(1)}, bf16[10,128,128]{2,1,0:T(8,128)(2,1)S(1)}, u32[]{:S(2)}, u32[]{:S(2)}) collective-permute-start(bf16[10,128,128]{2,1,0:T(8,128)(2,1)S(1)} %get-tuple-element.42), channel_id=1, source_target_pairs={{0,16},{8,24},{16,0},{24,8},{1,17},{9,25},{17,1},{25,9},{2,18},{10... | collective-permute-start | bytes 983048 | tf_op jit(solution)/shard_map/ppermute | solution.py:62
  34.7 14.6 %collective-permute-start.6 = (bf16[10,128,128]{2,1,0:T(8,128)(2,1)S(1)}, bf16[10,128,128]{2,1,0:T(8,128)(2,1)S(1)}, u32[]{:S(2)}, u32[]{:S(2)}) collective-permute-start(bf16[10,128,128]{2,1,0:T(8,128)(2,1)S(1)} %get-tuple-element.39.refs_0_), channel_id=1, source_target_pairs={{0,8},{8,0},{16,24},{24,16},{1,9},{9,1},{17,25},{25,17},{2,10},{10... | collective-permute-start | bytes 983048 | tf_op jit(solution)/shard_map/ppermute | solution.py:62
  35.8 13.5 %collective-permute-start.4 = (bf16[1,2,256,256]{3,2,1,0:T(8,128)(2,1)S(1)}, bf16[1,2,256,256]{3,2,1,0:T(8,128)(2,1)S(1)}, u32[]{:S(2)}, u32[]{:S(2)}) collective-permute-start(bf16[1,2,256,256]{3,2,1,0:T(8,128)(2,1)S(1)} %get-tuple-element.36.refs_0_), channel_id=1, source_target_pairs={{0,4},{1,5},{2,6},{3,7},{4,0},{5,1},{6,2},{7,3},{8,12},{9,13},{10,... | collective-permute-start | bytes 786440 | tf_op jit(solution)/shard_map/ppermute | solution.py:62
  51.0 20.4 %copy-start.15 = (s32[8]{0:T(128)S(1)}, s32[8]{0:T(128)}, u32[]{:S(2)}) copy-start(s32[8]{0:T(128)} %refs_3_.3) | copy-start | bytes 100
  51.0 2.0 %collective-permute-start.7 = (bf16[4,256,256]{2,1,0:T(8,128)(2,1)S(1)}, bf16[4,256,256]{2,1,0:T(8,128)(2,1)S(1)}, u32[]{:S(2)}, u32[]{:S(2)}) collective-permute-start(bf16[4,256,256]{2,1,0:T(8,128)(2,1)S(1)} %get-tuple-element.44.refs_0_), channel_id=1, source_target_pairs={{0,1},{1,0},{2,3},{3,2},{4,5},{5,4},{6,7},{7,6},{8,9},{9,8},{10,11... | collective-permute-start | bytes 1572872 | tf_op jit(solution)/shard_map/ppermute | solution.py:62
  53.6 8.3 %collective-permute-start.10 = (bf16[256,256]{1,0:T(8,128)(2,1)S(1)}, bf16[256,256]{1,0:T(8,128)(2,1)S(1)}, u32[]{:S(2)}, u32[]{:S(2)}) collective-permute-start(bf16[256,256]{1,0:T(8,128)(2,1)S(1)} %get-tuple-element.46.refs_0_), channel_id=1, source_target_pairs={{0,6},{1,7},{2,4},{3,5},{4,2},{5,3},{6,0},{7,1},{8,14},{9,15},{10,... | collective-permute-start | bytes 393224 | tf_op jit(solution)/shard_map/ppermute | solution.py:62
  57.2 8.6 %collective-permute-start.8 = (bf16[256,256]{1,0:T(8,128)(2,1)S(1)}, bf16[256,256]{1,0:T(8,128)(2,1)S(1)}, u32[]{:S(2)}, u32[]{:S(2)}) collective-permute-start(bf16[256,256]{1,0:T(8,128)(2,1)S(1)} %get-tuple-element.48), channel_id=1, source_target_pairs={{0,2},{1,3},{2,0},{3,1},{4,6},{5,7},{6,4},{7,5},{8,10},{9,11},{10,... | collective-permute-start | bytes 393224 | tf_op jit(solution)/shard_map/ppermute | solution.py:62
  57.2 14.2 %collective-permute-start.9 = (bf16[256,256]{1,0:T(8,128)(2,1)S(1)}, bf16[256,256]{1,0:T(8,128)(2,1)S(1)}, u32[]{:S(2)}, u32[]{:S(2)}) collective-permute-start(bf16[256,256]{1,0:T(8,128)(2,1)S(1)} %get-tuple-element.49), channel_id=1, source_target_pairs={{0,4},{1,5},{2,6},{3,7},{4,0},{5,1},{6,2},{7,3},{8,12},{9,13},{10,... | collective-permute-start | bytes 393224 | tf_op jit(solution)/shard_map/ppermute | solution.py:62
  58.1 15.3 %collective-permute-start.11 = (bf16[2,128,256]{2,1,0:T(8,128)(2,1)S(1)}, bf16[2,128,256]{2,1,0:T(8,128)(2,1)S(1)}, u32[]{:S(2)}, u32[]{:S(2)}) collective-permute-start(bf16[2,128,256]{2,1,0:T(8,128)(2,1)S(1)} %get-tuple-element.52.refs_1_.refs_2_), channel_id=1, source_target_pairs={{0,4},{1,5},{2,6},{3,7},{4,0},{5,1},{6,2},{7,3},{8,12},{9,13},{10,... | collective-permute-start | bytes 393224 | tf_op jit(solution)/shard_map/ppermute | solution.py:62
  72.2 21.8 %copy-start.3 = (f32[8,128,256]{2,1,0:T(8,128)S(1)}, f32[8,128,256]{2,1,0:T(8,128)}, u32[]{:S(2)}) copy-start(f32[8,128,256]{2,1,0:T(8,128)} %refs_5_.2) | copy-start | bytes 3145732
  73.4 17.4 %collective-permute-start.12 = (bf16[4,128,256]{2,1,0:T(8,128)(2,1)S(1)}, bf16[4,128,256]{2,1,0:T(8,128)(2,1)S(1)}, u32[]{:S(2)}, u32[]{:S(2)}) collective-permute-start(bf16[4,128,256]{2,1,0:T(8,128)(2,1)S(1)} %shard_map.119.refs_0_.refs_1_), channel_id=1, source_target_pairs={{0,2},{1,3},{2,0},{3,1},{4,6},{5,7},{6,4},{7,5},{8,10},{9,11},{10,... | collective-permute-start | bytes 786440 | tf_op jit(solution)/shard_map/ppermute | solution.py:62
  73.5 13.1 %collective-permute-start.13 = (bf16[256,256]{1,0:T(8,128)(2,1)S(1)}, bf16[256,256]{1,0:T(8,128)(2,1)S(1)}, u32[]{:S(2)}, u32[]{:S(2)}) collective-permute-start(bf16[256,256]{1,0:T(8,128)(2,1)S(1)} %get-tuple-element.53.refs_2_), channel_id=1, source_target_pairs={{0,2},{1,3},{2,0},{3,1},{4,6},{5,7},{6,4},{7,5},{8,10},{9,11},{10,... | collective-permute-start | bytes 393224 | tf_op jit(solution)/shard_map/ppermute | solution.py:62
  75.5 11.1 %collective-permute-start.14 = (bf16[256,256]{1,0:T(8,128)(2,1)S(1)}, bf16[256,256]{1,0:T(8,128)(2,1)S(1)}, u32[]{:S(2)}, u32[]{:S(2)}) collective-permute-start(bf16[256,256]{1,0:T(8,128)(2,1)S(1)} %get-tuple-element.53.refs_2_), channel_id=1, source_target_pairs={{0,4},{1,5},{2,6},{3,7},{4,0},{5,1},{6,2},{7,3},{8,12},{9,13},{10,... | collective-permute-start | bytes 393224 | tf_op jit(solution)/shard_map/ppermute | solution.py:62
  76.5 14.3 %collective-permute-start.15 = (bf16[256,256]{1,0:T(8,128)(2,1)S(1)}, bf16[256,256]{1,0:T(8,128)(2,1)S(1)}, u32[]{:S(2)}, u32[]{:S(2)}) collective-permute-start(bf16[256,256]{1,0:T(8,128)(2,1)S(1)} %get-tuple-element.53.refs_2_), channel_id=1, source_target_pairs={{0,6},{1,7},{2,4},{3,5},{4,2},{5,3},{6,0},{7,1},{8,14},{9,15},{10,... | collective-permute-start | bytes 393224 | tf_op jit(solution)/shard_map/ppermute | solution.py:62
  91.3 2.0 %collective-permute-start.16 = (f32[2,256,256]{2,1,0:T(8,128)S(1)}, f32[2,256,256]{2,1,0:T(8,128)S(1)}, u32[]{:S(2)}, u32[]{:S(2)}) collective-permute-start(f32[2,256,256]{2,1,0:T(8,128)S(1)} %shard_map.121.refs_0_.refs_1_), channel_id=1, source_target_pairs={{0,1},{1,0},{2,3},{3,2},{4,5},{5,4},{6,7},{7,6},{8,9},{9,8},{10,11... | collective-permute-start | bytes 1572872 | tf_op jit(solution)/shard_map/ppermute | solution.py:62
  91.4 2.6 %collective-permute-start.17 = (bf16[4,256,256]{2,1,0:T(8,128)(2,1)S(1)}, bf16[4,256,256]{2,1,0:T(8,128)(2,1)S(1)}, u32[]{:S(2)}, u32[]{:S(2)}) collective-permute-start(bf16[4,256,256]{2,1,0:T(8,128)(2,1)S(1)} %shard_map.120.refs_0_.refs_3_), channel_id=1, source_target_pairs={{0,1},{1,0},{2,3},{3,2},{4,5},{5,4},{6,7},{7,6},{8,9},{9,8},{10,11... | collective-permute-start | bytes 1572872 | tf_op jit(solution)/shard_map/ppermute | solution.py:62
  96.3 22.0 %collective-permute-start.18 = (bf16[8,128,256]{2,1,0:T(8,128)(2,1)}, bf16[8,128,256]{2,1,0:T(8,128)(2,1)S(1)}, u32[]{:S(2)}, u32[]{:S(2)}) collective-permute-start(bf16[8,128,256]{2,1,0:T(8,128)(2,1)} %copy-done.10), channel_id=1, source_target_pairs={{0,8},{8,0},{16,24},{24,16},{1,9},{9,1},{17,25},{25,17},{2,10},{10... | collective-permute-start | bytes 1572872 | tf_op jit(solution)/shard_map/ppermute | solution.py:62
  97.3 27.5 %collective-permute-start.19 = (bf16[8,128,256]{2,1,0:T(8,128)(2,1)}, bf16[8,128,256]{2,1,0:T(8,128)(2,1)}, u32[]{:S(2)}, u32[]{:S(2)}) collective-permute-start(bf16[8,128,256]{2,1,0:T(8,128)(2,1)} %copy-done.10), channel_id=1, source_target_pairs={{0,16},{8,24},{16,0},{24,8},{1,17},{9,25},{17,1},{25,9},{2,18},{10... | collective-permute-start | bytes 1572872 | tf_op jit(solution)/shard_map/ppermute | solution.py:62
  97.8 27.0 %collective-permute-start.20 = (bf16[8,128,256]{2,1,0:T(8,128)(2,1)}, bf16[8,128,256]{2,1,0:T(8,128)(2,1)}, u32[]{:S(2)}, u32[]{:S(2)}) collective-permute-start(bf16[8,128,256]{2,1,0:T(8,128)(2,1)} %copy-done.10), channel_id=1, source_target_pairs={{0,24},{8,16},{16,8},{24,0},{1,25},{9,17},{17,9},{25,1},{2,26},{10... | collective-permute-start | bytes 1572872 | tf_op jit(solution)/shard_map/ppermute | solution.py:62
  113.4 11.3 %copy-start.11 = (bf16[8,128,256]{2,1,0:T(8,128)(2,1)S(1)}, bf16[8,128,256]{2,1,0:T(8,128)(2,1)}, u32[]{:S(2)}) copy-start(bf16[8,128,256]{2,1,0:T(8,128)(2,1)} %copy-done.10) | copy-start | bytes 1572868
  116.8 12.3 %collective-permute-start.21 = (bf16[2,128,256]{2,1,0:T(8,128)(2,1)S(1)}, bf16[2,128,256]{2,1,0:T(8,128)(2,1)S(1)}, u32[]{:S(2)}, u32[]{:S(2)}) collective-permute-start(bf16[2,128,256]{2,1,0:T(8,128)(2,1)S(1)} %shard_map.126.refs_0_.refs_2_), channel_id=1, source_target_pairs={{0,8},{8,0},{16,24},{24,16},{1,9},{9,1},{17,25},{25,17},{2,10},{10... | collective-permute-start | bytes 393224 | tf_op jit(solution)/shard_map/ppermute | solution.py:62
  117.8 11.3 %collective-permute-start.22 = (bf16[2,128,256]{2,1,0:T(8,128)(2,1)S(1)}, bf16[2,128,256]{2,1,0:T(8,128)(2,1)S(1)}, u32[]{:S(2)}, u32[]{:S(2)}) collective-permute-start(bf16[2,128,256]{2,1,0:T(8,128)(2,1)S(1)} %shard_map.126.refs_0_.refs_2_), channel_id=1, source_target_pairs={{0,16},{8,24},{16,0},{24,8},{1,17},{9,25},{17,1},{25,9},{2,18},{10... | collective-permute-start | bytes 393224 | tf_op jit(solution)/shard_map/ppermute | solution.py:62
  119.1 10.1 %collective-permute-start.23 = (bf16[2,128,256]{2,1,0:T(8,128)(2,1)S(1)}, bf16[2,128,256]{2,1,0:T(8,128)(2,1)S(1)}, u32[]{:S(2)}, u32[]{:S(2)}) collective-permute-start(bf16[2,128,256]{2,1,0:T(8,128)(2,1)S(1)} %shard_map.126.refs_0_.refs_2_), channel_id=1, source_target_pairs={{0,24},{8,16},{16,8},{24,0},{1,25},{9,17},{17,9},{25,1},{2,26},{10... | collective-permute-start | bytes 393224 | tf_op jit(solution)/shard_map/ppermute | solution.py:62
  121.2 3.6 %copy-start.6 = (bf16[8,128,1024]{2,1,0:T(8,128)(2,1)S(1)}, bf16[8,128,1024]{2,1,0:T(8,128)(2,1)}, u32[]{:S(2)}) copy-start(bf16[8,128,1024]{2,1,0:T(8,128)(2,1)} %refs_2_.13) | copy-start | bytes 6291460
  122.6 2.2 %copy-start.13 = (bf16[8,128,256]{2,1,0:T(8,128)(2,1)S(1)}, bf16[8,128,256]{2,1,0:T(8,128)(2,1)}, u32[]{:S(2)}) copy-start(bf16[8,128,256]{2,1,0:T(8,128)(2,1)} %copy-done.12) | copy-start | bytes 1572868
  (9 other events, 11.5 us)
Sparse Core Ops, SparseCore 0:
  96.4 20.0 all-gather.2

commit v7 on v6

--- a/solution.py
+++ b/solution.py
@@ -229,17 +229,31 @@
             out[i, 1] = second_ref[slot].astype(bf16)
 
 
-def merge_kernel(place, owner, mine_ref, other_ref, *outs, bit):
+def near_half(place, owner, rel, bit):
     z, core = place[1], place[2]
-    stride = 1 if bit < 0 else 2 << bit
-    split = len(outs)
-    for i in range(mine_ref.shape[0]):
-        source = owner[2 * (z ^ (i * stride)) + core]
-        if bit < 0:
-            local = (source & 1) == core
-        else:
-            local = (((source >> 1) ^ z) >> bit) & 1 == 0
-        outs[i % split][i // split] = jnp.where(local, mine_ref[i], other_ref[i])
+    source = owner[2 * (z ^ rel) + core]
+    if bit < 0:
+        return (source & 1) == core
+    return (((source >> 1) ^ z) >> bit) & 1 == 0
+
+
+def divide(rels, bit):
+    keep = [i for i, rel in enumerate(rels) if not rel >> bit & 1]
+    send = [rels.index(rels[i] ^ (1 << bit)) for i in keep]
+    return keep, send
+
+
+def merge_kernel(place, owner, *refs, rels, bits, cuts):
+    inputs, outs = refs[:-4], refs[-4:]
+    for t in range(2):
+        for where, out in zip(divide(rels[t], cuts[t]), outs[2 * t : 2 * t + 2]):
+            for j, i in enumerate(where):
+                local = near_half(place, owner, rels[t][i], bits[t])
+                if len(inputs) == 2:
+                    own, lent = inputs[0][i, t], inputs[1][i, t]
+                else:
+                    own, lent = inputs[2 * t][i], inputs[2 * t + 1][i]
+                out[j] = jnp.where(local, own, lent)
 
 
 def project_kernel(place, *refs, scale):
@@ -274,9 +288,9 @@
         out[...] = (mine_ref[i] + other_ref[i].astype(f32)).astype(out.dtype)
 
 
-def update_kernel(place, owner, rank, *refs, chips, bit, start):
+def update_kernel(place, owner, rank, *refs, chips, bits, start):
     terms = refs[:chips]
-    moment_ref, lent_ref, update_ref, projected_ref = refs[chips:]
+    first_ref, first_lent, second_ref, second_lent, update_ref, projected_ref = refs[chips:]
     z, core = place[1], place[2]
     m = 2 * z + core
     projected = terms[0][...].astype(f32)
@@ -284,9 +298,10 @@
         projected = projected + ref[...].astype(f32)
     width = projected.shape[1]
     columns = slice(start, start + width)
-    local = (((owner[m] >> 1) ^ z) >> bit) & 1 == 0
-    first = jnp.where(local, moment_ref[0, 0, :, columns], lent_ref[0, 0, :, columns])
-    second = jnp.where(local, moment_ref[0, 1, :, columns], lent_ref[0, 1, :, columns])
+    near = near_half(place, owner, 0, bits[0])
+    first = jnp.where(near, first_ref[0, :, columns], first_lent[0, :, columns])
+    near = near_half(place, owner, 0, bits[1])
+    second = jnp.where(near, second_ref[0, :, columns], second_lent[0, :, columns])
     first_new = beta_one * first.astype(f32) + (1.0 - beta_one) * projected
     second_new = beta_two * second.astype(f32) + (1.0 - beta_two) * projected * projected
     update = (first_new / bias_one) / (jnp.sqrt(second_new / bias_two) + epsilon)
@@ -380,25 +395,29 @@
         scalars=1,
     )
     sides = [swap(sides[i], "dp", 1 << i) for i in range(2)]
-    left = chips
-    moments, lent = call(
+    picked, lent = call(
         pick_kernel,
-        [struct((left, 2, rank_full, quarter), bf16)] * 2,
+        [struct((chips, 2, rank_full, quarter), bf16)] * 2,
         (place, owner, first_moment, second_moment),
         scalars=2,
     )
-    lent = swap(lent, "rows", 1)
-    bit = -1
-    while left > 1:
-        left //= 2
-        moments, lent = call(
-            functools.partial(merge_kernel, bit=bit),
-            [struct((left, 2, rank_full, quarter), bf16)] * 2,
-            (place, owner, moments, lent),
+    inputs = [picked, swap(lent, "rows", 1)]
+    rels = [list(range(chips)), list(range(chips))]
+    bits = (-1, -1)
+    levels = chips.bit_length() - 1
+    for level in range(levels):
+        cuts = (level, levels - 1 - level)
+        merged = call(
+            functools.partial(merge_kernel, rels=rels, bits=bits, cuts=cuts),
+            [struct((len(rels[0]) // 2, rank_full, quarter), bf16)] * 4,
+            (place, owner, *inputs),
             scalars=2,
         )
-        bit += 1
-        lent = swap(lent, "rows", 2 << bit)
+        rels = [[rels[t][i] for i in divide(rels[t], cuts[t])[0]] for t in range(2)]
+        bits = cuts
+        inputs = []
+        for t in range(2):
+            inputs += [merged[2 * t], swap(merged[2 * t + 1], "rows", 2 << cuts[t])]
     *sums, first_send, second_send = call(
         add_kernel,
         [struct((count, shard, half), f32)] * 2
@@ -416,7 +435,7 @@
         ],
         (place, *sums, *relayed, *sides, keep, basis),
         scalars=1,
-        after=(lent,),
+        after=(inputs[1], inputs[3]),
     )
     other = swap(other, "rows", 1)
     mask = chips // 2
@@ -431,9 +450,9 @@
     work_shape = struct((each, rank_full, 2 * rank_full), f32)
     last = rank_full // BLOCK - 1
     update, projected = call(
-        functools.partial(update_kernel, chips=chips, bit=bit, start=0),
+        functools.partial(update_kernel, chips=chips, bits=bits, start=0),
         [struct((rank_full, quarter), bf16)] * 2,
-        (place, owner, rank, *terms, moments, lent),
+        (place, owner, rank, *terms, *inputs),
         scalars=3,
     )
     near = [update] + [swap(update, "rows", 2 * k) for k in range(1, chips)]

time: 140 us -> 135 us (0.964)
  waiting for transfers between devices: 52.6 us -> 47.2 us
    ppermute x24 -> x26, waiting for transfers between devices: 52.6 us -> 47.2 us  [swap(): return lax.ppermute(x, axis, [(i, i ^ mask) for i in range(size)])]
    ppermute x24 -> x26, starting transfers between devices: 30.3 us -> 31.5 us  [swap(): return lax.ppermute(x, axis, [(i, i ^ mask) for i in range(size)])]
  transfers between devices with their start and end apart: 25 -> 27, of which waited for: 12 -> 11; matrix products, arithmetic and copies ran while one was open for 0% -> 0% of each run, Pallas kernels for 18% -> 18%
where the time goes in v7:
time: 135 us
  waiting for transfers between devices  47.2 us (35%)
  Pallas kernels  33.4 us (25%)
  starting transfers between devices  31.5 us (23%)
  between operations  14.3 us (11%)
  local copies, waits for them, and re-layouts  8.44 us (6%)
    ppermute x26, waiting for transfers between devices, swap(): return lax.ppermute(x, axis, [(i, i ^ mask) for i in range(size)])  47.2 us
    pallas_call x19, Pallas kernels, __call__(): pl.pallas_call(body, out_shape=out_shape, in_specs=specs, out_specs=[VMEM...  33.4 us
    ppermute x26, starting transfers between devices, swap(): return lax.ppermute(x, axis, [(i, i ^ mask) for i in range(size)])  31.5 us
    unnamed x32, local copies, waits for them, and re-layouts  8.44 us
  transfers between devices with their start and end apart: 27, of which 11 were waited for; matrix products, arithmetic and copies ran while one was open for 0% of the time, Pallas kernels for 18%

profile of v7, /device:TPU:0, one launch (start us, length us, event | category | flops | bytes accessed | tf_op | source)
XLA Modules:
  0.0 135.0 jit_solution(270528642691889441)
XLA Ops:
  7.3 1.6 %copy-done = bf16[1,8,128,1024]{3,2,1,0:T(8,128)(2,1)S(1)} copy-done((bf16[1,8,128,1024]{3,2,1,0:T(8,128)(2,1)S(1)}, bf16[1,8,128,1024]{3,2,1,0:T(8,128)(2,1)}, u32[]{:S(2)}) %copy-start) | copy-done | bytes 2097176
  10.0 1.5 %shard_map.111 = (f32[2,128,256]{2,1,0:T(8,128)S(1)}, f32[2,2,128,128]{3,2,1,0:T(8,128)S(1)}, bf16[2,10,128,128]{3,2,1,0:T(8,128)(2,1)S(1)}, bf16[2,10,128,128]{3,2,1,0:T(8,128)(2,1)S(1)}) custom-call(s32[3]{0:T(128)S(1)} %pad_add_fusion.place.refs_1_.refs_3_.refs_2_, bf16[1,8,128,1024]{3,2,1,0:T(8,128)(2,1)S(1)} %copy-done, bf16[1024,256]{1,0:T(8,128)(2,1)S(1)} %copy-done.9), custom_call_target="tpu_custom_call" | custom-call | bytes 20000 | tf_op jit(solution)/shard_map/pallas_call | solution.py:45
  12.8 2.6 %collective-permute-start.3 = (bf16[2,10,128,128]{3,2,1,0:T(8,128)(2,1)S(1)}, bf16[2,10,128,128]{3,2,1,0:T(8,128)(2,1)S(1)}, u32[]{:S(2)}, u32[]{:S(2)}) collective-permute-start(bf16[2,10,128,128]{3,2,1,0:T(8,128)(2,1)S(1)} %get-tuple-element.44), channel_id=1, source_target_pairs={{0,8},{8,0},{16,24},{24,16},{1,9},{9,1},{17,25},{25,17},{2,10},{10... | collective-permute-start | bytes 1966088 | tf_op jit(solution)/shard_map/ppermute | solution.py:62
  15.4 1.5 %collective-permute-start.4 = (bf16[2,10,128,128]{3,2,1,0:T(8,128)(2,1)S(1)}, bf16[2,10,128,128]{3,2,1,0:T(8,128)(2,1)S(1)}, u32[]{:S(2)}, u32[]{:S(2)}) collective-permute-start(bf16[2,10,128,128]{3,2,1,0:T(8,128)(2,1)S(1)} %get-tuple-element.35.refs_0_), channel_id=1, source_target_pairs={{0,16},{8,24},{16,0},{24,8},{1,17},{9,25},{17,1},{25,9},{2,18},{10... | collective-permute-start | bytes 1966088 | tf_op jit(solution)/shard_map/ppermute | solution.py:62
  17.6 1.6 %collective-permute-start.1 = (bf16[2,256,256]{2,1,0:T(8,128)(2,1)S(1)}, bf16[2,256,256]{2,1,0:T(8,128)(2,1)S(1)}, u32[]{:S(2)}, u32[]{:S(2)}) collective-permute-start(bf16[2,256,256]{2,1,0:T(8,128)(2,1)S(1)} %get-tuple-element.40), channel_id=1, source_target_pairs={{0,2},{1,3},{2,0},{3,1},{4,6},{5,7},{6,4},{7,5},{8,10},{9,11},{10,... | collective-permute-start | bytes 786440 | tf_op jit(solution)/shard_map/ppermute | solution.py:62
  19.2 2.6 %collective-permute-start.2 = (bf16[2,256,256]{2,1,0:T(8,128)(2,1)S(1)}, bf16[2,256,256]{2,1,0:T(8,128)(2,1)S(1)}, u32[]{:S(2)}, u32[]{:S(2)}) collective-permute-start(bf16[2,256,256]{2,1,0:T(8,128)(2,1)S(1)} %get-tuple-element.38.refs_0_), channel_id=1, source_target_pairs={{0,4},{1,5},{2,6},{3,7},{4,0},{5,1},{6,2},{7,3},{8,12},{9,13},{10,... | collective-permute-start | bytes 786440 | tf_op jit(solution)/shard_map/ppermute | solution.py:62
  21.8 9.4 %collective-permute-done.1.refs_4_ = bf16[2,256,256]{2,1,0:T(8,128)(2,1)S(1)} collective-permute-done((bf16[2,256,256]{2,1,0:T(8,128)(2,1)S(1)}, bf16[2,256,256]{2,1,0:T(8,128)(2,1)S(1)}, u32[]{:S(2)}, u32[]{:S(2)}) %collective-permute-start.1) | collective-permute-done | bytes 262176 | tf_op jit(solution)/shard_map/ppermute | solution.py:62
  31.2 2.4 %collective-permute-done.2.refs_6_ = bf16[2,256,256]{2,1,0:T(8,128)(2,1)S(1)} collective-permute-done((bf16[2,256,256]{2,1,0:T(8,128)(2,1)S(1)}, bf16[2,256,256]{2,1,0:T(8,128)(2,1)S(1)}, u32[]{:S(2)}, u32[]{:S(2)}) %collective-permute-start.2) | collective-permute-done | bytes 262176 | tf_op jit(solution)/shard_map/ppermute | solution.py:62
  36.5 1.5 %collective-permute-start.8 = (bf16[10,128,128]{2,1,0:T(8,128)(2,1)S(1)}, bf16[10,128,128]{2,1,0:T(8,128)(2,1)S(1)}, u32[]{:S(2)}, u32[]{:S(2)}) collective-permute-start(bf16[10,128,128]{2,1,0:T(8,128)(2,1)S(1)} %get-tuple-element.45.refs_0_), channel_id=1, source_target_pairs={{0,8},{8,0},{16,24},{24,16},{1,9},{9,1},{17,25},{25,17},{2,10},{10... | collective-permute-start | bytes 983048 | tf_op jit(solution)/shard_map/ppermute | solution.py:62
  38.4 2.7 %collective-permute-start.6 = (bf16[1,256,256]{2,1,0:T(8,128)(2,1)S(1)}, bf16[1,256,256]{2,1,0:T(8,128)(2,1)S(1)}, u32[]{:S(2)}, u32[]{:S(2)}) collective-permute-start(bf16[1,256,256]{2,1,0:T(8,128)(2,1)S(1)} %get-tuple-element.42.refs_0_), channel_id=1, source_target_pairs={{0,2},{1,3},{2,0},{3,1},{4,6},{5,7},{6,4},{7,5},{8,10},{9,11},{10,... | collective-permute-start | bytes 393224 | tf_op jit(solution)/shard_map/ppermute | solution.py:62
  41.1 4.3 %collective-permute-done.5.refs_1_.refs_9_ = bf16[1,256,256]{2,1,0:T(8,128)(2,1)S(1)} collective-permute-done((bf16[1,256,256]{2,1,0:T(8,128)(2,1)S(1)}, bf16[1,256,256]{2,1,0:T(8,128)(2,1)S(1)}, u32[]{:S(2)}, u32[]{:S(2)}) %collective-permute-start.5) | collective-permute-done | bytes 131104 | tf_op jit(solution)/shard_map/ppermute | solution.py:62
  45.4 1.7 %shard_map.116 = (f32[4,256,256]{2,1,0:T(8,128)S(1)}, bf16[2,128,256]{2,1,0:T(8,128)(2,1)S(1)}, bf16[4,256,256]{2,1,0:T(8,128)(2,1)S(1)}) custom-call(bf16[10,128,128]{2,1,0:T(8,128)(2,1)S(1)} %get-tuple-element.45.refs_0_, bf16[1,256,256]{2,1,0:T(8,128)(2,1)S(1)} %collective-permute-done.5.refs_1_.refs_9_, ...), custom_call_target="tpu_custom_call" | custom-call | bytes 20000 | tf_op jit(solution)/shard_map/pallas_call | solution.py:45
  47.2 1.9 %collective-permute-done.9.refs_3_ = bf16[4,256,256]{2,1,0:T(8,128)(2,1)S(1)} collective-permute-done((bf16[4,256,256]{2,1,0:T(8,128)(2,1)S(1)}, bf16[4,256,256]{2,1,0:T(8,128)(2,1)S(1)}, u32[]{:S(2)}, u32[]{:S(2)}) %collective-permute-start.9) | collective-permute-done | bytes 524320 | tf_op jit(solution)/shard_map/ppermute | solution.py:62
  50.5 1.9 %collective-permute-start.11 = (bf16[256,256]{1,0:T(8,128)(2,1)S(1)}, bf16[256,256]{1,0:T(8,128)(2,1)S(1)}, u32[]{:S(2)}, u32[]{:S(2)}) collective-permute-start(bf16[256,256]{1,0:T(8,128)(2,1)S(1)} %get-tuple-element.56), channel_id=1, source_target_pairs={{0,4},{1,5},{2,6},{3,7},{4,0},{5,1},{6,2},{7,3},{8,12},{9,13},{10,... | collective-permute-start | bytes 393224 | tf_op jit(solution)/shard_map/ppermute | solution.py:62
  52.4 1.7 %collective-permute-start.12 = (bf16[256,256]{1,0:T(8,128)(2,1)S(1)}, bf16[256,256]{1,0:T(8,128)(2,1)S(1)}, u32[]{:S(2)}, u32[]{:S(2)}) collective-permute-start(bf16[256,256]{1,0:T(8,128)(2,1)S(1)} %get-tuple-element.53.refs_0_), channel_id=1, source_target_pairs={{0,6},{1,7},{2,4},{3,5},{4,2},{5,3},{6,0},{7,1},{8,14},{9,15},{10,... | collective-permute-start | bytes 393224 | tf_op jit(solution)/shard_map/ppermute | solution.py:62
  54.2 3.0 %collective-permute-done.10.refs_5_ = bf16[256,256]{1,0:T(8,128)(2,1)S(1)} collective-permute-done((bf16[256,256]{1,0:T(8,128)(2,1)S(1)}, bf16[256,256]{1,0:T(8,128)(2,1)S(1)}, u32[]{:S(2)}, u32[]{:S(2)}) %collective-permute-start.10) | collective-permute-done | bytes 131104 | tf_op jit(solution)/shard_map/ppermute | solution.py:62
  57.1 9.0 %collective-permute-done.11.refs_6_ = bf16[256,256]{1,0:T(8,128)(2,1)S(1)} collective-permute-done((bf16[256,256]{1,0:T(8,128)(2,1)S(1)}, bf16[256,256]{1,0:T(8,128)(2,1)S(1)}, u32[]{:S(2)}, u32[]{:S(2)}) %collective-permute-start.11) | collective-permute-done | bytes 131104 | tf_op jit(solution)/shard_map/ppermute | solution.py:62
  67.0 3.7 %collective-permute-done.13.refs_2_ = bf16[2,128,256]{2,1,0:T(8,128)(2,1)S(1)} collective-permute-done((bf16[2,128,256]{2,1,0:T(8,128)(2,1)S(1)}, bf16[2,128,256]{2,1,0:T(8,128)(2,1)S(1)}, u32[]{:S(2)}, u32[]{:S(2)}) %collective-permute-start.13) | collective-permute-done | bytes 131104 | tf_op jit(solution)/shard_map/ppermute | solution.py:62
  70.8 2.0 %collective-permute-start.15 = (bf16[256,256]{1,0:T(8,128)(2,1)S(1)}, bf16[256,256]{1,0:T(8,128)(2,1)S(1)}, u32[]{:S(2)}, u32[]{:S(2)}) collective-permute-start(bf16[256,256]{1,0:T(8,128)(2,1)S(1)} %get-tuple-element.61.refs_2_), channel_id=1, source_target_pairs={{0,2},{1,3},{2,0},{3,1},{4,6},{5,7},{6,4},{7,5},{8,10},{9,11},{10,... | collective-permute-start | bytes 393224 | tf_op jit(solution)/shard_map/ppermute | solution.py:62
  73.2 2.1 %collective-permute-start.17 = (bf16[256,256]{1,0:T(8,128)(2,1)S(1)}, bf16[256,256]{1,0:T(8,128)(2,1)S(1)}, u32[]{:S(2)}, u32[]{:S(2)}) collective-permute-start(bf16[256,256]{1,0:T(8,128)(2,1)S(1)} %get-tuple-element.61.refs_2_), channel_id=1, source_target_pairs={{0,6},{1,7},{2,4},{3,5},{4,2},{5,3},{6,0},{7,1},{8,14},{9,15},{10,... | collective-permute-start | bytes 393224 | tf_op jit(solution)/shard_map/ppermute | solution.py:62
  75.3 9.8 %collective-permute-done.15.refs_3_ = bf16[256,256]{1,0:T(8,128)(2,1)S(1)} collective-permute-done((bf16[256,256]{1,0:T(8,128)(2,1)S(1)}, bf16[256,256]{1,0:T(8,128)(2,1)S(1)}, u32[]{:S(2)}, u32[]{:S(2)}) %collective-permute-start.15) | collective-permute-done | bytes 131104 | tf_op jit(solution)/shard_map/ppermute | solution.py:62
  89.8 1.4 %shard_map.122 = (bf16[8,128,256]{2,1,0:T(8,128)(2,1)S(1)}, bf16[256,256]{1,0:T(8,128)(2,1)}) custom-call(f32[2,256,256]{2,1,0:T(8,128)S(1)} %shard_map.121.refs_0_.refs_1_, f32[2,256,256]{2,1,0:T(8,128)S(1)} %collective-permute-done.18.refs_1_.refs_2_, s32[3]{0:T(128)S(1)} %pad_add_fusion.place.refs_1_.refs_3_.refs_2_, ...), custom_call_target="tpu_custom_call" | custom-call | bytes 20000 | tf_op jit(solution)/shard_map/pallas_call | solution.py:45
  92.1 1.6 %collective-permute-start.20 = (bf16[8,128,256]{2,1,0:T(8,128)(2,1)}, bf16[8,128,256]{2,1,0:T(8,128)(2,1)S(1)}, u32[]{:S(2)}, u32[]{:S(2)}) collective-permute-start(bf16[8,128,256]{2,1,0:T(8,128)(2,1)} %copy-done.10), channel_id=1, source_target_pairs={{0,8},{8,0},{16,24},{24,16},{1,9},{9,1},{17,25},{25,17},{2,10},{10... | collective-permute-start | bytes 1572872 | tf_op jit(solution)/shard_map/ppermute | solution.py:62
  95.6 4.4 %shard_map.123.refs_0_.refs_1_ = f32[2,256,512]{2,1,0:T(8,128)S(1)} custom-call(bf16[256,256]{1,0:T(8,128)(2,1)} %get-tuple-element.62.refs_0_, f32[2,256,256]{2,1,0:T(8,128)S(1)} %shard_map.121.refs_0_.refs_1_, f32[2,256,256]{2,1,0:T(8,128)S(1)} %collective-permute-done.18.refs_1_.refs_2_), custom_call_target="tpu_custom_call" | custom-call | bytes 20000 | tf_op jit(solution)/shard_map/pallas_call | solution.py:45
  100.1 4.6 %shard_map.124.refs_0_.refs_1_ = f32[2,256,512]{2,1,0:T(8,128)S(1)} custom-call(f32[2,256,512]{2,1,0:T(8,128)S(1)} %shard_map.123.refs_0_.refs_1_, f32[2,256,512]{2,1,0:T(8,128)S(1)} %shard_map.123.refs_0_.refs_1_), custom_call_target="tpu_custom_call" | custom-call | bytes 20000 | tf_op jit(solution)/shard_map/pallas_call | solution.py:45
  104.6 4.6 %shard_map.125.refs_0_.refs_1_ = f32[2,256,512]{2,1,0:T(8,128)S(1)} custom-call(f32[2,256,512]{2,1,0:T(8,128)S(1)} %shard_map.124.refs_0_.refs_1_, f32[2,256,512]{2,1,0:T(8,128)S(1)} %shard_map.124.refs_0_.refs_1_), custom_call_target="tpu_custom_call" | custom-call | bytes 20000 | tf_op jit(solution)/shard_map/pallas_call | solution.py:45
  109.2 3.4 %shard_map.126.refs_0_.refs_2_ = bf16[2,128,256]{2,1,0:T(8,128)(2,1)S(1)} custom-call(f32[2,256,512]{2,1,0:T(8,128)S(1)} %shard_map.125.refs_0_.refs_1_, f32[2,256,512]{2,1,0:T(8,128)S(1)} %shard_map.125.refs_0_.refs_1_, bf16[2,128,256]{2,1,0:T(8,128)(2,1)S(1)} %get-tuple-element.60.refs_1_.refs_2_), custom_call_target="tpu_custom_call" | custom-call | bytes 20000 | tf_op jit(solution)/shard_map/pallas_call | solution.py:45
  112.6 1.6 %collective-permute-start.23 = (bf16[2,128,256]{2,1,0:T(8,128)(2,1)S(1)}, bf16[2,128,256]{2,1,0:T(8,128)(2,1)S(1)}, u32[]{:S(2)}, u32[]{:S(2)}) collective-permute-start(bf16[2,128,256]{2,1,0:T(8,128)(2,1)S(1)} %shard_map.126.refs_0_.refs_2_), channel_id=1, source_target_pairs={{0,8},{8,0},{16,24},{24,16},{1,9},{9,1},{17,25},{25,17},{2,10},{10... | collective-permute-start | bytes 393224 | tf_op jit(solution)/shard_map/ppermute | solution.py:62
  118.4 2.2 %shard_map.127 = (f32[4,256,256]{2,1,0:T(8,128)}, f32[4,256,256]{2,1,0:T(8,128)}) custom-call(bf16[2,128,256]{2,1,0:T(8,128)(2,1)S(1)} %shard_map.126.refs_0_.refs_2_, s32[3]{0:T(128)S(1)} %pad_add_fusion.place.refs_1_.refs_3_.refs_2_, s32[8]{0:T(128)S(1)} %copy-done.14, bf16[8,256,256]{2,1,0:T(8,128)(2,1)S(1)} %bitcast.4, f32[4,256,256]{2,1,0:T(8,128)S(1)} %copy-done.4, ...), custom_call_target="tpu_custom_call" | custom-call | bytes 20000 | tf_op jit(solution)/shard_map/pallas_call | solution.py:45
  121.8 3.1 %shard_map.128.refs_0_ = bf16[8,128,1024]{2,1,0:T(8,128)(2,1)} custom-call(f32[4,256,256]{2,1,0:T(8,128)S(1)} %copy-done.8, s32[3]{0:T(128)S(1)} %pad_add_fusion.place.refs_1_.refs_3_.refs_2_, bf16[8,128,1024]{2,1,0:T(8,128)(2,1)S(1)} %copy-done.6, bf16[8,128,256]{2,1,0:T(8,128)(2,1)S(1)} %copy-done.11, bf16[8,128,256]{2,1,0:T(8,128)(2,1)S(1)} %copy-done.13, ...), custom_call_target="tpu_custom_call" | custom-call | bytes 20000 | tf_op jit(solution)/shard_map/pallas_call | solution.py:45
  125.0 1.6 %copy-done.2 = bf16[8,128,1024]{2,1,0:T(8,128)(2,1)S(1)} copy-done((bf16[8,128,1024]{2,1,0:T(8,128)(2,1)S(1)}, bf16[8,128,1024]{2,1,0:T(8,128)(2,1)}, u32[]{:S(2)}) %copy-start.2) | copy-done | bytes 2097176
  126.6 1.6 %shard_map.129 = f32[8,128,256]{2,1,0:T(8,128)} custom-call(bf16[8,128,1024]{2,1,0:T(8,128)(2,1)S(1)} %copy-done.2, s32[3]{0:T(128)S(1)} %pad_add_fusion.place.refs_1_.refs_3_.refs_2_, bf16[2,128,256]{2,1,0:T(8,128)(2,1)S(1)} %shard_map.126.refs_0_.refs_2_, bf16[2,128,256]{2,1,0:T(8,128)(2,1)S(1)} %collective-permute-done.23.refs_3_, ...), custom_call_target="tpu_custom_call" | custom-call | bytes 20000 | tf_op jit(solution)/shard_map/pallas_call | solution.py:45
  (75 shorter events, 21.9 us)
Async XLA Ops:
  7.2 4.3 %copy-start.14 = (s32[8]{0:T(128)S(1)}, s32[8]{0:T(128)}, u32[]{:S(2)}) copy-start(s32[8]{0:T(128)} %refs_2_.12) | copy-start | bytes 100
  7.2 109.8 %all-gather.3.cloned.1.call-start = ((), (), s32[]{:S(2)}) async-start(), calls=%async_computation | async-start | bytes 1179648 | tf_op jit(solution)/shard_map/all_gather | solution.py:484
  12.3 4.6 %collective-permute-start = (bf16[4,2,256,256]{3,2,1,0:T(8,128)(2,1)S(1)}, bf16[4,2,256,256]{3,2,1,0:T(8,128)(2,1)S(1)}, u32[]{:S(2)}, u32[]{:S(2)}) collective-permute-start(bf16[4,2,256,256]{3,2,1,0:T(8,128)(2,1)S(1)} %get-tuple-element.36.refs_0_), channel_id=1, source_target_pairs={{0,1},{1,0},{2,3},{3,2},{4,5},{5,4},{6,7},{7,6},{8,9},{9,8},{10,11... | collective-permute-start | bytes 3145736 | tf_op jit(solution)/shard_map/ppermute | solution.py:62
  12.8 21.4 %collective-permute-start.3 = (bf16[2,10,128,128]{3,2,1,0:T(8,128)(2,1)S(1)}, bf16[2,10,128,128]{3,2,1,0:T(8,128)(2,1)S(1)}, u32[]{:S(2)}, u32[]{:S(2)}) collective-permute-start(bf16[2,10,128,128]{3,2,1,0:T(8,128)(2,1)S(1)} %get-tuple-element.44), channel_id=1, source_target_pairs={{0,8},{8,0},{16,24},{24,16},{1,9},{9,1},{17,25},{25,17},{2,10},{10... | collective-permute-start | bytes 1966088 | tf_op jit(solution)/shard_map/ppermute | solution.py:62
  15.4 18.8 %collective-permute-start.4 = (bf16[2,10,128,128]{3,2,1,0:T(8,128)(2,1)S(1)}, bf16[2,10,128,128]{3,2,1,0:T(8,128)(2,1)S(1)}, u32[]{:S(2)}, u32[]{:S(2)}) collective-permute-start(bf16[2,10,128,128]{3,2,1,0:T(8,128)(2,1)S(1)} %get-tuple-element.35.refs_0_), channel_id=1, source_target_pairs={{0,16},{8,24},{16,0},{24,8},{1,17},{9,25},{17,1},{25,9},{2,18},{10... | collective-permute-start | bytes 1966088 | tf_op jit(solution)/shard_map/ppermute | solution.py:62
  16.9 17.3 %copy-start.1 = (bf16[1,8,128,1024]{3,2,1,0:T(8,128)(2,1)S(1)}, bf16[1,8,128,1024]{3,2,1,0:T(8,128)(2,1)}, u32[]{:S(2)}) copy-start(bf16[1,8,128,1024]{3,2,1,0:T(8,128)(2,1)} %refs_2_.10) | copy-start | bytes 6291460
  17.6 13.7 %collective-permute-start.1 = (bf16[2,256,256]{2,1,0:T(8,128)(2,1)S(1)}, bf16[2,256,256]{2,1,0:T(8,128)(2,1)S(1)}, u32[]{:S(2)}, u32[]{:S(2)}) collective-permute-start(bf16[2,256,256]{2,1,0:T(8,128)(2,1)S(1)} %get-tuple-element.40), channel_id=1, source_target_pairs={{0,2},{1,3},{2,0},{3,1},{4,6},{5,7},{6,4},{7,5},{8,10},{9,11},{10,... | collective-permute-start | bytes 786440 | tf_op jit(solution)/shard_map/ppermute | solution.py:62
  19.2 14.4 %collective-permute-start.2 = (bf16[2,256,256]{2,1,0:T(8,128)(2,1)S(1)}, bf16[2,256,256]{2,1,0:T(8,128)(2,1)S(1)}, u32[]{:S(2)}, u32[]{:S(2)}) collective-permute-start(bf16[2,256,256]{2,1,0:T(8,128)(2,1)S(1)} %get-tuple-element.38.refs_0_), channel_id=1, source_target_pairs={{0,4},{1,5},{2,6},{3,7},{4,0},{5,1},{6,2},{7,3},{8,12},{9,13},{10,... | collective-permute-start | bytes 786440 | tf_op jit(solution)/shard_map/ppermute | solution.py:62
  35.1 10.2 %collective-permute-start.7 = (bf16[10,128,128]{2,1,0:T(8,128)(2,1)S(1)}, bf16[10,128,128]{2,1,0:T(8,128)(2,1)S(1)}, u32[]{:S(2)}, u32[]{:S(2)}) collective-permute-start(bf16[10,128,128]{2,1,0:T(8,128)(2,1)S(1)} %get-tuple-element.49), channel_id=1, source_target_pairs={{0,16},{8,24},{16,0},{24,8},{1,17},{9,25},{17,1},{25,9},{2,18},{10... | collective-permute-start | bytes 983048 | tf_op jit(solution)/shard_map/ppermute | solution.py:62
  36.5 8.8 %collective-permute-start.8 = (bf16[10,128,128]{2,1,0:T(8,128)(2,1)S(1)}, bf16[10,128,128]{2,1,0:T(8,128)(2,1)S(1)}, u32[]{:S(2)}, u32[]{:S(2)}) collective-permute-start(bf16[10,128,128]{2,1,0:T(8,128)(2,1)S(1)} %get-tuple-element.45.refs_0_), channel_id=1, source_target_pairs={{0,8},{8,0},{16,24},{24,16},{1,9},{9,1},{17,25},{25,17},{2,10},{10... | collective-permute-start | bytes 983048 | tf_op jit(solution)/shard_map/ppermute | solution.py:62
  38.0 7.3 %collective-permute-start.5 = (bf16[1,256,256]{2,1,0:T(8,128)(2,1)S(1)}, bf16[1,256,256]{2,1,0:T(8,128)(2,1)S(1)}, u32[]{:S(2)}, u32[]{:S(2)}) collective-permute-start(bf16[1,256,256]{2,1,0:T(8,128)(2,1)S(1)} %get-tuple-element.46), channel_id=1, source_target_pairs={{0,4},{1,5},{2,6},{3,7},{4,0},{5,1},{6,2},{7,3},{8,12},{9,13},{10,... | collective-permute-start | bytes 393224 | tf_op jit(solution)/shard_map/ppermute | solution.py:62
  38.4 7.0 %collective-permute-start.6 = (bf16[1,256,256]{2,1,0:T(8,128)(2,1)S(1)}, bf16[1,256,256]{2,1,0:T(8,128)(2,1)S(1)}, u32[]{:S(2)}, u32[]{:S(2)}) collective-permute-start(bf16[1,256,256]{2,1,0:T(8,128)(2,1)S(1)} %get-tuple-element.42.refs_0_), channel_id=1, source_target_pairs={{0,2},{1,3},{2,0},{3,1},{4,6},{5,7},{6,4},{7,5},{8,10},{9,11},{10,... | collective-permute-start | bytes 393224 | tf_op jit(solution)/shard_map/ppermute | solution.py:62
  47.1 19.1 %copy-start.15 = (s32[8]{0:T(128)S(1)}, s32[8]{0:T(128)}, u32[]{:S(2)}) copy-start(s32[8]{0:T(128)} %refs_3_.3) | copy-start | bytes 100
  47.1 2.0 %collective-permute-start.9 = (bf16[4,256,256]{2,1,0:T(8,128)(2,1)S(1)}, bf16[4,256,256]{2,1,0:T(8,128)(2,1)S(1)}, u32[]{:S(2)}, u32[]{:S(2)}) collective-permute-start(bf16[4,256,256]{2,1,0:T(8,128)(2,1)S(1)} %get-tuple-element.51.refs_0_), channel_id=1, source_target_pairs={{0,1},{1,0},{2,3},{3,2},{4,5},{5,4},{6,7},{7,6},{8,9},{9,8},{10,11... | collective-permute-start | bytes 1572872 | tf_op jit(solution)/shard_map/ppermute | solution.py:62
  49.7 7.4 %collective-permute-start.10 = (bf16[256,256]{1,0:T(8,128)(2,1)S(1)}, bf16[256,256]{1,0:T(8,128)(2,1)S(1)}, u32[]{:S(2)}, u32[]{:S(2)}) collective-permute-start(bf16[256,256]{1,0:T(8,128)(2,1)S(1)} %get-tuple-element.55), channel_id=1, source_target_pairs={{0,2},{1,3},{2,0},{3,1},{4,6},{5,7},{6,4},{7,5},{8,10},{9,11},{10,... | collective-permute-start | bytes 393224 | tf_op jit(solution)/shard_map/ppermute | solution.py:62
  50.5 15.7 %collective-permute-start.11 = (bf16[256,256]{1,0:T(8,128)(2,1)S(1)}, bf16[256,256]{1,0:T(8,128)(2,1)S(1)}, u32[]{:S(2)}, u32[]{:S(2)}) collective-permute-start(bf16[256,256]{1,0:T(8,128)(2,1)S(1)} %get-tuple-element.56), channel_id=1, source_target_pairs={{0,4},{1,5},{2,6},{3,7},{4,0},{5,1},{6,2},{7,3},{8,12},{9,13},{10,... | collective-permute-start | bytes 393224 | tf_op jit(solution)/shard_map/ppermute | solution.py:62
  52.4 13.7 %collective-permute-start.12 = (bf16[256,256]{1,0:T(8,128)(2,1)S(1)}, bf16[256,256]{1,0:T(8,128)(2,1)S(1)}, u32[]{:S(2)}, u32[]{:S(2)}) collective-permute-start(bf16[256,256]{1,0:T(8,128)(2,1)S(1)} %get-tuple-element.53.refs_0_), channel_id=1, source_target_pairs={{0,6},{1,7},{2,4},{3,5},{4,2},{5,3},{6,0},{7,1},{8,14},{9,15},{10,... | collective-permute-start | bytes 393224 | tf_op jit(solution)/shard_map/ppermute | solution.py:62
  54.2 16.6 %collective-permute-start.13 = (bf16[2,128,256]{2,1,0:T(8,128)(2,1)S(1)}, bf16[2,128,256]{2,1,0:T(8,128)(2,1)S(1)}, u32[]{:S(2)}, u32[]{:S(2)}) collective-permute-start(bf16[2,128,256]{2,1,0:T(8,128)(2,1)S(1)} %get-tuple-element.60.refs_1_.refs_2_), channel_id=1, source_target_pairs={{0,4},{1,5},{2,6},{3,7},{4,0},{5,1},{6,2},{7,3},{8,12},{9,13},{10,... | collective-permute-start | bytes 393224 | tf_op jit(solution)/shard_map/ppermute | solution.py:62
  67.0 22.8 %copy-start.3 = (f32[8,128,256]{2,1,0:T(8,128)S(1)}, f32[8,128,256]{2,1,0:T(8,128)}, u32[]{:S(2)}) copy-start(f32[8,128,256]{2,1,0:T(8,128)} %refs_5_.2) | copy-start | bytes 3145732
  70.8 15.8 %collective-permute-start.14 = (bf16[4,128,256]{2,1,0:T(8,128)(2,1)S(1)}, bf16[4,128,256]{2,1,0:T(8,128)(2,1)S(1)}, u32[]{:S(2)}, u32[]{:S(2)}) collective-permute-start(bf16[4,128,256]{2,1,0:T(8,128)(2,1)S(1)} %shard_map.119.refs_0_.refs_1_), channel_id=1, source_target_pairs={{0,2},{1,3},{2,0},{3,1},{4,6},{5,7},{6,4},{7,5},{8,10},{9,11},{10,... | collective-permute-start | bytes 786440 | tf_op jit(solution)/shard_map/ppermute | solution.py:62
  70.8 14.3 %collective-permute-start.15 = (bf16[256,256]{1,0:T(8,128)(2,1)S(1)}, bf16[256,256]{1,0:T(8,128)(2,1)S(1)}, u32[]{:S(2)}, u32[]{:S(2)}) collective-permute-start(bf16[256,256]{1,0:T(8,128)(2,1)S(1)} %get-tuple-element.61.refs_2_), channel_id=1, source_target_pairs={{0,2},{1,3},{2,0},{3,1},{4,6},{5,7},{6,4},{7,5},{8,10},{9,11},{10,... | collective-permute-start | bytes 393224 | tf_op jit(solution)/shard_map/ppermute | solution.py:62
  72.9 12.3 %collective-permute-start.16 = (bf16[256,256]{1,0:T(8,128)(2,1)S(1)}, bf16[256,256]{1,0:T(8,128)(2,1)S(1)}, u32[]{:S(2)}, u32[]{:S(2)}) collective-permute-start(bf16[256,256]{1,0:T(8,128)(2,1)S(1)} %get-tuple-element.61.refs_2_), channel_id=1, source_target_pairs={{0,4},{1,5},{2,6},{3,7},{4,0},{5,1},{6,2},{7,3},{8,12},{9,13},{10,... | collective-permute-start | bytes 393224 | tf_op jit(solution)/shard_map/ppermute | solution.py:62
  73.2 13.4 %collective-permute-start.17 = (bf16[256,256]{1,0:T(8,128)(2,1)S(1)}, bf16[256,256]{1,0:T(8,128)(2,1)S(1)}, u32[]{:S(2)}, u32[]{:S(2)}) collective-permute-start(bf16[256,256]{1,0:T(8,128)(2,1)S(1)} %get-tuple-element.61.refs_2_), channel_id=1, source_target_pairs={{0,6},{1,7},{2,4},{3,5},{4,2},{5,3},{6,0},{7,1},{8,14},{9,15},{10,... | collective-permute-start | bytes 393224 | tf_op jit(solution)/shard_map/ppermute | solution.py:62
  87.1 2.0 %collective-permute-start.18 = (f32[2,256,256]{2,1,0:T(8,128)S(1)}, f32[2,256,256]{2,1,0:T(8,128)S(1)}, u32[]{:S(2)}, u32[]{:S(2)}) collective-permute-start(f32[2,256,256]{2,1,0:T(8,128)S(1)} %shard_map.121.refs_0_.refs_1_), channel_id=1, source_target_pairs={{0,1},{1,0},{2,3},{3,2},{4,5},{5,4},{6,7},{7,6},{8,9},{9,8},{10,11... | collective-permute-start | bytes 1572872 | tf_op jit(solution)/shard_map/ppermute | solution.py:62
  87.2 2.6 %collective-permute-start.19 = (bf16[4,256,256]{2,1,0:T(8,128)(2,1)S(1)}, bf16[4,256,256]{2,1,0:T(8,128)(2,1)S(1)}, u32[]{:S(2)}, u32[]{:S(2)}) collective-permute-start(bf16[4,256,256]{2,1,0:T(8,128)(2,1)S(1)} %shard_map.120.refs_0_.refs_3_), channel_id=1, source_target_pairs={{0,1},{1,0},{2,3},{3,2},{4,5},{5,4},{6,7},{7,6},{8,9},{9,8},{10,11... | collective-permute-start | bytes 1572872 | tf_op jit(solution)/shard_map/ppermute | solution.py:62
  92.1 22.7 %collective-permute-start.20 = (bf16[8,128,256]{2,1,0:T(8,128)(2,1)}, bf16[8,128,256]{2,1,0:T(8,128)(2,1)S(1)}, u32[]{:S(2)}, u32[]{:S(2)}) collective-permute-start(bf16[8,128,256]{2,1,0:T(8,128)(2,1)} %copy-done.10), channel_id=1, source_target_pairs={{0,8},{8,0},{16,24},{24,16},{1,9},{9,1},{17,25},{25,17},{2,10},{10... | collective-permute-start | bytes 1572872 | tf_op jit(solution)/shard_map/ppermute | solution.py:62
  93.7 26.8 %collective-permute-start.21 = (bf16[8,128,256]{2,1,0:T(8,128)(2,1)}, bf16[8,128,256]{2,1,0:T(8,128)(2,1)}, u32[]{:S(2)}, u32[]{:S(2)}) collective-permute-start(bf16[8,128,256]{2,1,0:T(8,128)(2,1)} %copy-done.10), channel_id=1, source_target_pairs={{0,16},{8,24},{16,0},{24,8},{1,17},{9,25},{17,1},{25,9},{2,18},{10... | collective-permute-start | bytes 1572872 | tf_op jit(solution)/shard_map/ppermute | solution.py:62
  94.2 26.3 %collective-permute-start.22 = (bf16[8,128,256]{2,1,0:T(8,128)(2,1)}, bf16[8,128,256]{2,1,0:T(8,128)(2,1)}, u32[]{:S(2)}, u32[]{:S(2)}) collective-permute-start(bf16[8,128,256]{2,1,0:T(8,128)(2,1)} %copy-done.10), channel_id=1, source_target_pairs={{0,24},{8,16},{16,8},{24,0},{1,25},{9,17},{17,9},{25,1},{2,26},{10... | collective-permute-start | bytes 1572872 | tf_op jit(solution)/shard_map/ppermute | solution.py:62
  109.2 11.4 %copy-start.11 = (bf16[8,128,256]{2,1,0:T(8,128)(2,1)S(1)}, bf16[8,128,256]{2,1,0:T(8,128)(2,1)}, u32[]{:S(2)}) copy-start(bf16[8,128,256]{2,1,0:T(8,128)(2,1)} %copy-done.10) | copy-start | bytes 1572868
  112.6 12.3 %collective-permute-start.23 = (bf16[2,128,256]{2,1,0:T(8,128)(2,1)S(1)}, bf16[2,128,256]{2,1,0:T(8,128)(2,1)S(1)}, u32[]{:S(2)}, u32[]{:S(2)}) collective-permute-start(bf16[2,128,256]{2,1,0:T(8,128)(2,1)S(1)} %shard_map.126.refs_0_.refs_2_), channel_id=1, source_target_pairs={{0,8},{8,0},{16,24},{24,16},{1,9},{9,1},{17,25},{25,17},{2,10},{10... | collective-permute-start | bytes 393224 | tf_op jit(solution)/shard_map/ppermute | solution.py:62
  114.3 10.7 %collective-permute-start.24 = (bf16[2,128,256]{2,1,0:T(8,128)(2,1)S(1)}, bf16[2,128,256]{2,1,0:T(8,128)(2,1)S(1)}, u32[]{:S(2)}, u32[]{:S(2)}) collective-permute-start(bf16[2,128,256]{2,1,0:T(8,128)(2,1)S(1)} %shard_map.126.refs_0_.refs_2_), channel_id=1, source_target_pairs={{0,16},{8,24},{16,0},{24,8},{1,17},{9,25},{17,1},{25,9},{2,18},{10... | collective-permute-start | bytes 393224 | tf_op jit(solution)/shard_map/ppermute | solution.py:62
  115.6 9.4 %collective-permute-start.25 = (bf16[2,128,256]{2,1,0:T(8,128)(2,1)S(1)}, bf16[2,128,256]{2,1,0:T(8,128)(2,1)S(1)}, u32[]{:S(2)}, u32[]{:S(2)}) collective-permute-start(bf16[2,128,256]{2,1,0:T(8,128)(2,1)S(1)} %shard_map.126.refs_0_.refs_2_), channel_id=1, source_target_pairs={{0,24},{8,16},{16,8},{24,0},{1,25},{9,17},{17,9},{25,1},{2,26},{10... | collective-permute-start | bytes 393224 | tf_op jit(solution)/shard_map/ppermute | solution.py:62
  (11 other events, 17.3 us)
Sparse Core Ops, SparseCore 0:
  92.2 20.5 all-gather.2

commit v8 on v7

--- a/solution.py
+++ b/solution.py
@@ -109,6 +109,12 @@
 def gather_kernel(*refs):
     for k, ref in enumerate(refs[:-1]):
         refs[-1][k] = ref[...]
+
+
+def pass_kernel(*refs):
+    half = len(refs) // 2
+    for ref, out in zip(refs[:half], refs[half:]):
+        out[...] = ref[...]
 
 
 def gram_kernel(*refs):
@@ -311,7 +317,8 @@
 
 
 def delta_kernel(place, *refs, chips, scale):
-    near, far, basis_ref, projected_ref, out_ref, passed_ref = refs
+    near, far, basis_ref, projected_ref, *outs, passed_ref = refs
+    half = outs[0].shape[2]
     z, core = place[1], place[2]
     passed_ref[...] = projected_ref[...]
     for k in range(chips):
@@ -320,7 +327,8 @@
             product = jnp.dot(
                 (basis_ref[m] * scale).astype(bf16), ref[k], preferred_element_type=f32
             )
-            out_ref[m] = product.astype(bf16)
+            for side, out in enumerate(outs):
+                out[m] = product[:, side * half : (side + 1) * half].astype(bf16)
 
 
 def weight_kernel(place, weight_ref, *refs, groups, chunks):
@@ -447,6 +455,12 @@
         scalars=1,
     )
     terms = [terms[0]] + [swap(terms[k], "rows", 2 * k) for k in range(1, chips)]
+    stacked = sample
+    while mask > 1:
+        both = struct((2 * stacked.shape[0], shard, rank_full), bf16)
+        stacked = call(stack_kernel, both, (stacked, arrived))
+        mask //= 2
+        arrived = swap(stacked, "rows", 2 * mask)
     work_shape = struct((each, rank_full, 2 * rank_full), f32)
     last = rank_full // BLOCK - 1
     update, projected = call(
@@ -454,37 +468,37 @@
         [struct((rank_full, quarter), bf16)] * 2,
         (place, owner, rank, *terms, *inputs),
         scalars=3,
+        after=(arrived,),
     )
     near = [update] + [swap(update, "rows", 2 * k) for k in range(1, chips)]
-    stacked = sample
-    while mask > 1:
-        both = struct((2 * stacked.shape[0], shard, rank_full), bf16)
-        stacked = call(stack_kernel, both, (stacked, arrived))
-        mask //= 2
-        arrived = swap(stacked, "rows", 2 * mask)
+    gram = call(
+        gram_kernel, struct((each, rank_full, rank_full), f32), (stacked, arrived)
+    )
+    other_gram = swap(gram, "rows", 1)
+    work = call(start_kernel, work_shape, (gram, other_gram))
+    early = last // 2 + 1
+    for j in range(1, early):
+        work = call(functools.partial(middle_kernel, j=j), work_shape, (work,))
     near = call(
         gather_kernel,
         struct((chips, rank_full, quarter), bf16),
         tuple(near),
-        after=(arrived,),
     )
     far = swap(near, "rows", 1)
-    gram = call(
-        gram_kernel, struct((each, rank_full, rank_full), f32), (stacked, arrived)
-    )
-    other_gram = swap(gram, "rows", 1)
-    delta, projected = call(
+    *own, projected = call(
         functools.partial(delta_kernel, chips=chips, scale=inverse_root),
-        [struct((count, shard, quarter), bf16), struct((rank_full, quarter), bf16)],
+        [struct((count, shard, half), bf16)] * 2 + [struct((rank_full, quarter), bf16)],
         (place, near, far, basis, projected),
         scalars=1,
-        after=(other_gram,),
-    )
-    deltas = [delta] + [swap(delta, "dp", k) for k in range(1, groups)]
+    )
+    beside = [swap(own[0], "dp", 1), swap(own[1], "dp", 2)]
+    later = [swap(own[1], "dp", 1), swap(own[0], "dp", 2)]
     gathered = lax.all_gather(projected, "rows", axis=0)
-    work = call(start_kernel, work_shape, (gram, other_gram))
-    for j in range(1, last):
+    for j in range(early, last):
         work = call(functools.partial(middle_kernel, j=j), work_shape, (work,))
+    passed = call(pass_kernel, [struct(own[0].shape, bf16)] * 2, tuple(beside))
+    across = [swap(passed[0], "dp", 2), swap(passed[1], "dp", 1)]
+    deltas = [own[0], beside[0], later[1], across[0], own[1], later[0], beside[1], across[1]]
     rows_basis = call(
         functools.partial(finish_kernel, j=last, scale=root),
         struct(sample.shape, bf16),
@@ -497,9 +511,10 @@
         [struct(first_moment.shape, f32)] * 2,
         (place, owner, gathered, first_moment, second_moment),
         scalars=2,
+        after=tuple(across),
     )
     new_weight = call(
-        functools.partial(weight_kernel, groups=groups, chunks=1),
+        functools.partial(weight_kernel, groups=groups, chunks=2),
         struct(weight.shape, bf16),
         (place, weight, *deltas),
         scalars=1,

time: 135 us -> 132 us (0.978)
  waiting for transfers between devices: 47.2 us -> 41.9 us
  starting transfers between devices: 31.5 us -> 34.6 us
  local copies, waits for them, and re-layouts: 8.44 us -> 6.85 us
    ppermute x26 -> x29, waiting for transfers between devices: 47.2 us -> 41.9 us  [swap(): return lax.ppermute(x, axis, [(i, i ^ mask) for i in range(size)])]
    ppermute x26 -> x29, starting transfers between devices: 31.5 us -> 34.6 us  [swap(): return lax.ppermute(x, axis, [(i, i ^ mask) for i in range(size)])]
    unnamed x32 -> x28, local copies, waits for them, and re-layouts: 8.44 us -> 6.85 us
    pallas_call x19 -> x20, Pallas kernels: 33.4 us -> 34.2 us  [__call__(): pl.pallas_call(body, out_shape=out_shape, in_specs=specs, out_specs=[VMEM...]
  transfers between devices with their start and end apart: 27 -> 30, of which waited for: 11 -> 11; matrix products, arithmetic and copies ran while one was open for 0% -> 0% of each run, Pallas kernels for 18% -> 18%
where the time goes in v8:
time: 132 us
  waiting for transfers between devices  41.9 us (32%)
  starting transfers between devices  34.6 us (26%)
  Pallas kernels  34.2 us (26%)
  between operations  14.4 us (11%)
  local copies, waits for them, and re-layouts  6.85 us (5%)
    ppermute x29, waiting for transfers between devices, swap(): return lax.ppermute(x, axis, [(i, i ^ mask) for i in range(size)])  41.9 us
    ppermute x29, starting transfers between devices, swap(): return lax.ppermute(x, axis, [(i, i ^ mask) for i in range(size)])  34.6 us
    pallas_call x20, Pallas kernels, __call__(): pl.pallas_call(body, out_shape=out_shape, in_specs=specs, out_specs=[VMEM...  34.2 us
    unnamed x28, local copies, waits for them, and re-layouts  6.85 us
  transfers between devices with their start and end apart: 30, of which 11 were waited for; matrix products, arithmetic and copies ran while one was open for 0% of the time, Pallas kernels for 18%

profile of v8, /device:TPU:0, one launch (start us, length us, event | category | flops | bytes accessed | tf_op | source)
XLA Modules:
  0.0 132.0 jit_solution(3346836165466305022)
XLA Ops:
  7.3 1.6 %copy-done = bf16[1,8,128,1024]{3,2,1,0:T(8,128)(2,1)S(1)} copy-done((bf16[1,8,128,1024]{3,2,1,0:T(8,128)(2,1)S(1)}, bf16[1,8,128,1024]{3,2,1,0:T(8,128)(2,1)}, u32[]{:S(2)}) %copy-start) | copy-done | bytes 2097176
  10.0 1.5 %shard_map.111 = (f32[2,128,256]{2,1,0:T(8,128)S(1)}, f32[2,2,128,128]{3,2,1,0:T(8,128)S(1)}, bf16[2,10,128,128]{3,2,1,0:T(8,128)(2,1)S(1)}, bf16[2,10,128,128]{3,2,1,0:T(8,128)(2,1)S(1)}) custom-call(s32[3]{0:T(128)S(1)} %pad_add_fusion.place.refs_1_.refs_3_.refs_2_, bf16[1,8,128,1024]{3,2,1,0:T(8,128)(2,1)S(1)} %copy-done, bf16[1024,256]{1,0:T(8,128)(2,1)S(1)} %copy-done.11), custom_call_target="tpu_custom_call" | custom-call | bytes 20000 | tf_op jit(solution)/shard_map/pallas_call | solution.py:45
  12.8 2.6 %collective-permute-start.3 = (bf16[2,10,128,128]{3,2,1,0:T(8,128)(2,1)S(1)}, bf16[2,10,128,128]{3,2,1,0:T(8,128)(2,1)S(1)}, u32[]{:S(2)}, u32[]{:S(2)}) collective-permute-start(bf16[2,10,128,128]{3,2,1,0:T(8,128)(2,1)S(1)} %get-tuple-element.47), channel_id=1, source_target_pairs={{0,8},{8,0},{16,24},{24,16},{1,9},{9,1},{17,25},{25,17},{2,10},{10... | collective-permute-start | bytes 1966088 | tf_op jit(solution)/shard_map/ppermute | solution.py:62
  15.4 1.5 %collective-permute-start.4 = (bf16[2,10,128,128]{3,2,1,0:T(8,128)(2,1)S(1)}, bf16[2,10,128,128]{3,2,1,0:T(8,128)(2,1)S(1)}, u32[]{:S(2)}, u32[]{:S(2)}) collective-permute-start(bf16[2,10,128,128]{3,2,1,0:T(8,128)(2,1)S(1)} %get-tuple-element.38.refs_0_), channel_id=1, source_target_pairs={{0,16},{8,24},{16,0},{24,8},{1,17},{9,25},{17,1},{25,9},{2,18},{10... | collective-permute-start | bytes 1966088 | tf_op jit(solution)/shard_map/ppermute | solution.py:62
  17.6 1.6 %collective-permute-start.1 = (bf16[2,256,256]{2,1,0:T(8,128)(2,1)S(1)}, bf16[2,256,256]{2,1,0:T(8,128)(2,1)S(1)}, u32[]{:S(2)}, u32[]{:S(2)}) collective-permute-start(bf16[2,256,256]{2,1,0:T(8,128)(2,1)S(1)} %get-tuple-element.43), channel_id=1, source_target_pairs={{0,2},{1,3},{2,0},{3,1},{4,6},{5,7},{6,4},{7,5},{8,10},{9,11},{10,... | collective-permute-start | bytes 786440 | tf_op jit(solution)/shard_map/ppermute | solution.py:62
  19.2 2.6 %collective-permute-start.2 = (bf16[2,256,256]{2,1,0:T(8,128)(2,1)S(1)}, bf16[2,256,256]{2,1,0:T(8,128)(2,1)S(1)}, u32[]{:S(2)}, u32[]{:S(2)}) collective-permute-start(bf16[2,256,256]{2,1,0:T(8,128)(2,1)S(1)} %get-tuple-element.41.refs_0_), channel_id=1, source_target_pairs={{0,4},{1,5},{2,6},{3,7},{4,0},{5,1},{6,2},{7,3},{8,12},{9,13},{10,... | collective-permute-start | bytes 786440 | tf_op jit(solution)/shard_map/ppermute | solution.py:62
  21.8 9.4 %collective-permute-done.1.refs_4_ = bf16[2,256,256]{2,1,0:T(8,128)(2,1)S(1)} collective-permute-done((bf16[2,256,256]{2,1,0:T(8,128)(2,1)S(1)}, bf16[2,256,256]{2,1,0:T(8,128)(2,1)S(1)}, u32[]{:S(2)}, u32[]{:S(2)}) %collective-permute-start.1) | collective-permute-done | bytes 262176 | tf_op jit(solution)/shard_map/ppermute | solution.py:62
  31.3 2.3 %collective-permute-done.2.refs_6_ = bf16[2,256,256]{2,1,0:T(8,128)(2,1)S(1)} collective-permute-done((bf16[2,256,256]{2,1,0:T(8,128)(2,1)S(1)}, bf16[2,256,256]{2,1,0:T(8,128)(2,1)S(1)}, u32[]{:S(2)}, u32[]{:S(2)}) %collective-permute-start.2) | collective-permute-done | bytes 262176 | tf_op jit(solution)/shard_map/ppermute | solution.py:62
  36.5 1.5 %collective-permute-start.8 = (bf16[10,128,128]{2,1,0:T(8,128)(2,1)S(1)}, bf16[10,128,128]{2,1,0:T(8,128)(2,1)S(1)}, u32[]{:S(2)}, u32[]{:S(2)}) collective-permute-start(bf16[10,128,128]{2,1,0:T(8,128)(2,1)S(1)} %get-tuple-element.48.refs_0_), channel_id=1, source_target_pairs={{0,8},{8,0},{16,24},{24,16},{1,9},{9,1},{17,25},{25,17},{2,10},{10... | collective-permute-start | bytes 983048 | tf_op jit(solution)/shard_map/ppermute | solution.py:62
  38.4 2.7 %collective-permute-start.6 = (bf16[1,256,256]{2,1,0:T(8,128)(2,1)S(1)}, bf16[1,256,256]{2,1,0:T(8,128)(2,1)S(1)}, u32[]{:S(2)}, u32[]{:S(2)}) collective-permute-start(bf16[1,256,256]{2,1,0:T(8,128)(2,1)S(1)} %get-tuple-element.45.refs_0_), channel_id=1, source_target_pairs={{0,2},{1,3},{2,0},{3,1},{4,6},{5,7},{6,4},{7,5},{8,10},{9,11},{10,... | collective-permute-start | bytes 393224 | tf_op jit(solution)/shard_map/ppermute | solution.py:62
  41.1 4.3 %collective-permute-done.5.refs_1_.refs_10_ = bf16[1,256,256]{2,1,0:T(8,128)(2,1)S(1)} collective-permute-done((bf16[1,256,256]{2,1,0:T(8,128)(2,1)S(1)}, bf16[1,256,256]{2,1,0:T(8,128)(2,1)S(1)}, u32[]{:S(2)}, u32[]{:S(2)}) %collective-permute-start.5) | collective-permute-done | bytes 131104 | tf_op jit(solution)/shard_map/ppermute | solution.py:62
  45.4 1.7 %shard_map.116 = (f32[4,256,256]{2,1,0:T(8,128)S(1)}, bf16[2,128,256]{2,1,0:T(8,128)(2,1)S(1)}, bf16[4,256,256]{2,1,0:T(8,128)(2,1)S(1)}) custom-call(bf16[10,128,128]{2,1,0:T(8,128)(2,1)S(1)} %get-tuple-element.48.refs_0_, bf16[1,256,256]{2,1,0:T(8,128)(2,1)S(1)} %collective-permute-done.5.refs_1_.refs_10_, ...), custom_call_target="tpu_custom_call" | custom-call | bytes 20000 | tf_op jit(solution)/shard_map/pallas_call | solution.py:45
  49.7 7.1 %collective-permute-done.10.refs_2_ = bf16[2,128,256]{2,1,0:T(8,128)(2,1)S(1)} collective-permute-done((bf16[2,128,256]{2,1,0:T(8,128)(2,1)S(1)}, bf16[2,128,256]{2,1,0:T(8,128)(2,1)S(1)}, u32[]{:S(2)}, u32[]{:S(2)}) %collective-permute-start.10) | collective-permute-done | bytes 131104 | tf_op jit(solution)/shard_map/ppermute | solution.py:62
  56.9 2.0 %collective-permute-start.12 = (bf16[256,256]{1,0:T(8,128)(2,1)S(1)}, bf16[256,256]{1,0:T(8,128)(2,1)S(1)}, u32[]{:S(2)}, u32[]{:S(2)}) collective-permute-start(bf16[256,256]{1,0:T(8,128)(2,1)S(1)} %get-tuple-element.59), channel_id=1, source_target_pairs={{0,2},{1,3},{2,0},{3,1},{4,6},{5,7},{6,4},{7,5},{8,10},{9,11},{10,... | collective-permute-start | bytes 393224 | tf_op jit(solution)/shard_map/ppermute | solution.py:62
  59.4 2.0 %collective-permute-start.14 = (bf16[256,256]{1,0:T(8,128)(2,1)S(1)}, bf16[256,256]{1,0:T(8,128)(2,1)S(1)}, u32[]{:S(2)}, u32[]{:S(2)}) collective-permute-start(bf16[256,256]{1,0:T(8,128)(2,1)S(1)} %get-tuple-element.56.refs_0_), channel_id=1, source_target_pairs={{0,6},{1,7},{2,4},{3,5},{4,2},{5,3},{6,0},{7,1},{8,14},{9,15},{10,... | collective-permute-start | bytes 393224 | tf_op jit(solution)/shard_map/ppermute | solution.py:62
  61.4 9.5 %collective-permute-done.12.refs_6_ = bf16[256,256]{1,0:T(8,128)(2,1)S(1)} collective-permute-done((bf16[256,256]{1,0:T(8,128)(2,1)S(1)}, bf16[256,256]{1,0:T(8,128)(2,1)S(1)}, u32[]{:S(2)}, u32[]{:S(2)}) %collective-permute-start.12) | collective-permute-done | bytes 131104 | tf_op jit(solution)/shard_map/ppermute | solution.py:62
  70.9 2.8 %collective-permute-done.14.refs_8_ = bf16[256,256]{1,0:T(8,128)(2,1)S(1)} collective-permute-done((bf16[256,256]{1,0:T(8,128)(2,1)S(1)}, bf16[256,256]{1,0:T(8,128)(2,1)S(1)}, u32[]{:S(2)}, u32[]{:S(2)}) %collective-permute-start.14) | collective-permute-done | bytes 131104 | tf_op jit(solution)/shard_map/ppermute | solution.py:62
  75.2 2.4 %collective-permute-start.17 = (bf16[256,256]{1,0:T(8,128)(2,1)S(1)}, bf16[256,256]{1,0:T(8,128)(2,1)S(1)}, u32[]{:S(2)}, u32[]{:S(2)}) collective-permute-start(bf16[256,256]{1,0:T(8,128)(2,1)S(1)} %get-tuple-element.64.refs_1_), channel_id=1, source_target_pairs={{0,4},{1,5},{2,6},{3,7},{4,0},{5,1},{6,2},{7,3},{8,12},{9,13},{10,... | collective-permute-start | bytes 393224 | tf_op jit(solution)/shard_map/ppermute | solution.py:62
  77.5 2.0 %collective-permute-start.18 = (bf16[256,256]{1,0:T(8,128)(2,1)S(1)}, bf16[256,256]{1,0:T(8,128)(2,1)S(1)}, u32[]{:S(2)}, u32[]{:S(2)}) collective-permute-start(bf16[256,256]{1,0:T(8,128)(2,1)S(1)} %get-tuple-element.64.refs_1_), channel_id=1, source_target_pairs={{0,6},{1,7},{2,4},{3,5},{4,2},{5,3},{6,0},{7,1},{8,14},{9,15},{10,... | collective-permute-start | bytes 393224 | tf_op jit(solution)/shard_map/ppermute | solution.py:62
  79.6 4.4 %shard_map.121.refs_0_.refs_1_ = f32[2,256,512]{2,1,0:T(8,128)S(1)} custom-call(f32[2,256,256]{2,1,0:T(8,128)S(1)} %shard_map.120.refs_0_.refs_1_, f32[2,256,256]{2,1,0:T(8,128)S(1)} %shard_map.120.refs_0_.refs_1_, f32[2,256,256]{2,1,0:T(8,128)S(1)} %collective-permute-done.15.refs_2_), custom_call_target="tpu_custom_call" | custom-call | bytes 20000 | tf_op jit(solution)/shard_map/pallas_call | solution.py:45
  84.0 4.6 %shard_map.122.refs_0_.refs_1_ = f32[2,256,512]{2,1,0:T(8,128)S(1)} custom-call(f32[2,256,512]{2,1,0:T(8,128)S(1)} %shard_map.121.refs_0_.refs_1_, f32[2,256,512]{2,1,0:T(8,128)S(1)} %shard_map.121.refs_0_.refs_1_), custom_call_target="tpu_custom_call" | custom-call | bytes 20000 | tf_op jit(solution)/shard_map/pallas_call | solution.py:45
  88.7 1.9 %collective-permute-done.19.refs_3_ = bf16[4,256,256]{2,1,0:T(8,128)(2,1)S(1)} collective-permute-done((bf16[4,256,256]{2,1,0:T(8,128)(2,1)S(1)}, bf16[4,256,256]{2,1,0:T(8,128)(2,1)S(1)}, u32[]{:S(2)}, u32[]{:S(2)}) %collective-permute-start.19) | collective-permute-done | bytes 524320 | tf_op jit(solution)/shard_map/ppermute | solution.py:62
  90.6 1.7 %shard_map.124 = (bf16[8,128,128]{2,1,0:T(8,128)(2,1)}, bf16[8,128,128]{2,1,0:T(8,128)(2,1)}, bf16[256,256]{1,0:T(8,128)(2,1)}) custom-call(bf16[4,256,256]{2,1,0:T(8,128)(2,1)S(1)} %shard_map.123.refs_0_.refs_2_, s32[3]{0:T(128)S(1)} %pad_add_fusion.place.refs_1_.refs_3_.refs_2_, bf16[4,256,256]{2,1,0:T(8,128)(2,1)S(1)} %shard_map.123.refs_0_.refs_2_, ...), custom_call_target="tpu_custom_call" | custom-call | bytes 20000 | tf_op jit(solution)/shard_map/pallas_call | solution.py:45
  93.5 4.6 %shard_map.125.refs_0_.refs_1_ = f32[2,256,512]{2,1,0:T(8,128)S(1)} custom-call(bf16[256,256]{1,0:T(8,128)(2,1)} %get-tuple-element.65.refs_0_, f32[2,256,512]{2,1,0:T(8,128)S(1)} %shard_map.122.refs_0_.refs_1_), custom_call_target="tpu_custom_call" | custom-call | bytes 20000 | tf_op jit(solution)/shard_map/pallas_call | solution.py:45
  98.1 2.8 %collective-permute-done.20.refs_1_.refs_4_ = bf16[8,128,128]{2,1,0:T(8,128)(2,1)S(1)} collective-permute-done((bf16[8,128,128]{2,1,0:T(8,128)(2,1)}, bf16[8,128,128]{2,1,0:T(8,128)(2,1)S(1)}, u32[]{:S(2)}, u32[]{:S(2)}) %collective-permute-start.20) | collective-permute-done | bytes 262176 | tf_op jit(solution)/shard_map/ppermute | solution.py:62
  103.3 1.5 %collective-permute-start.24 = (bf16[8,128,128]{2,1,0:T(8,128)(2,1)}, bf16[8,128,128]{2,1,0:T(8,128)(2,1)}, u32[]{:S(2)}, u32[]{:S(2)}) collective-permute-start(bf16[8,128,128]{2,1,0:T(8,128)(2,1)} %get-tuple-element.66.refs_3_), channel_id=1, source_target_pairs={{0,16},{8,24},{16,0},{24,8},{1,17},{9,25},{17,1},{25,9},{2,18},{10... | collective-permute-start | bytes 786440 | tf_op jit(solution)/shard_map/ppermute | solution.py:62
  105.5 3.4 %shard_map.127.refs_0_.refs_2_ = bf16[2,128,256]{2,1,0:T(8,128)(2,1)S(1)} custom-call(bf16[8,128,128]{2,1,0:T(8,128)(2,1)S(1)} %get-tuple-element.68.refs_0_, f32[2,256,512]{2,1,0:T(8,128)S(1)} %shard_map.125.refs_0_.refs_1_, bf16[2,128,256]{2,1,0:T(8,128)(2,1)S(1)} %get-tuple-element.57.refs_1_.refs_2_), custom_call_target="tpu_custom_call" | custom-call | bytes 20000 | tf_op jit(solution)/shard_map/pallas_call | solution.py:45
  111.2 2.3 %collective-permute-start.28 = (bf16[2,128,256]{2,1,0:T(8,128)(2,1)S(1)}, bf16[2,128,256]{2,1,0:T(8,128)(2,1)}, u32[]{:S(2)}, u32[]{:S(2)}) collective-permute-start(bf16[2,128,256]{2,1,0:T(8,128)(2,1)S(1)} %shard_map.127.refs_0_.refs_2_), channel_id=1, source_target_pairs={{0,24},{8,16},{16,8},{24,0},{1,25},{9,17},{17,9},{25,1},{2,26},{10... | collective-permute-start | bytes 393224 | tf_op jit(solution)/shard_map/ppermute | solution.py:62
  114.9 2.2 %shard_map.128 = (f32[4,256,256]{2,1,0:T(8,128)}, f32[4,256,256]{2,1,0:T(8,128)}) custom-call(bf16[2,128,256]{2,1,0:T(8,128)(2,1)S(1)} %shard_map.127.refs_0_.refs_2_, bf16[8,128,128]{2,1,0:T(8,128)(2,1)S(1)} %collective-permute-done.22.refs_1_.refs_6_, bf16[8,128,128]{2,1,0:T(8,128)(2,1)S(1)} %collective-permute-done.23.refs_2_.refs_10_, ...), custom_call_target="tpu_custom_call" | custom-call | bytes 20000 | tf_op jit(solution)/shard_map/pallas_call | solution.py:45
  118.3 3.2 %shard_map.129.refs_0_ = bf16[8,128,1024]{2,1,0:T(8,128)(2,1)} custom-call(f32[4,256,256]{2,1,0:T(8,128)S(1)} %copy-done.8, s32[3]{0:T(128)S(1)} %pad_add_fusion.place.refs_1_.refs_3_.refs_2_, bf16[8,128,1024]{2,1,0:T(8,128)(2,1)S(1)} %copy-done.6, bf16[8,128,128]{2,1,0:T(8,128)(2,1)} %get-tuple-element.66.refs_3_, ...), custom_call_target="tpu_custom_call" | custom-call | bytes 20000 | tf_op jit(solution)/shard_map/pallas_call | solution.py:45
  121.6 1.6 %copy-done.2 = bf16[8,128,1024]{2,1,0:T(8,128)(2,1)S(1)} copy-done((bf16[8,128,1024]{2,1,0:T(8,128)(2,1)S(1)}, bf16[8,128,1024]{2,1,0:T(8,128)(2,1)}, u32[]{:S(2)}) %copy-start.2) | copy-done | bytes 2097176
  123.2 2.0 %shard_map.130 = f32[8,128,256]{2,1,0:T(8,128)} custom-call(bf16[8,128,1024]{2,1,0:T(8,128)(2,1)S(1)} %copy-done.2, s32[3]{0:T(128)S(1)} %pad_add_fusion.place.refs_1_.refs_3_.refs_2_, bf16[2,128,256]{2,1,0:T(8,128)(2,1)S(1)} %shard_map.127.refs_0_.refs_2_, bf16[2,128,256]{2,1,0:T(8,128)(2,1)S(1)} %collective-permute-done.26.refs_3_, ...), custom_call_target="tpu_custom_call" | custom-call | bytes 20000 | tf_op jit(solution)/shard_map/pallas_call | solution.py:45
  (78 shorter events, 20.3 us)
Async XLA Ops:
  7.2 106.3 %all-gather.3.cloned.1.call-start = ((), (), s32[]{:S(2)}) async-start(), calls=%async_computation | async-start | bytes 1179648 | tf_op jit(solution)/shard_map/all_gather | solution.py:496
  12.3 4.6 %collective-permute-start = (bf16[4,2,256,256]{3,2,1,0:T(8,128)(2,1)S(1)}, bf16[4,2,256,256]{3,2,1,0:T(8,128)(2,1)S(1)}, u32[]{:S(2)}, u32[]{:S(2)}) collective-permute-start(bf16[4,2,256,256]{3,2,1,0:T(8,128)(2,1)S(1)} %get-tuple-element.39.refs_0_), channel_id=1, source_target_pairs={{0,1},{1,0},{2,3},{3,2},{4,5},{5,4},{6,7},{7,6},{8,9},{9,8},{10,11... | collective-permute-start | bytes 3145736 | tf_op jit(solution)/shard_map/ppermute | solution.py:62
  12.8 21.4 %collective-permute-start.3 = (bf16[2,10,128,128]{3,2,1,0:T(8,128)(2,1)S(1)}, bf16[2,10,128,128]{3,2,1,0:T(8,128)(2,1)S(1)}, u32[]{:S(2)}, u32[]{:S(2)}) collective-permute-start(bf16[2,10,128,128]{3,2,1,0:T(8,128)(2,1)S(1)} %get-tuple-element.47), channel_id=1, source_target_pairs={{0,8},{8,0},{16,24},{24,16},{1,9},{9,1},{17,25},{25,17},{2,10},{10... | collective-permute-start | bytes 1966088 | tf_op jit(solution)/shard_map/ppermute | solution.py:62
  15.4 18.8 %collective-permute-start.4 = (bf16[2,10,128,128]{3,2,1,0:T(8,128)(2,1)S(1)}, bf16[2,10,128,128]{3,2,1,0:T(8,128)(2,1)S(1)}, u32[]{:S(2)}, u32[]{:S(2)}) collective-permute-start(bf16[2,10,128,128]{3,2,1,0:T(8,128)(2,1)S(1)} %get-tuple-element.38.refs_0_), channel_id=1, source_target_pairs={{0,16},{8,24},{16,0},{24,8},{1,17},{9,25},{17,1},{25,9},{2,18},{10... | collective-permute-start | bytes 1966088 | tf_op jit(solution)/shard_map/ppermute | solution.py:62
  16.9 17.3 %copy-start.1 = (bf16[1,8,128,1024]{3,2,1,0:T(8,128)(2,1)S(1)}, bf16[1,8,128,1024]{3,2,1,0:T(8,128)(2,1)}, u32[]{:S(2)}) copy-start(bf16[1,8,128,1024]{3,2,1,0:T(8,128)(2,1)} %refs_2_.8) | copy-start | bytes 6291460
  17.6 13.7 %collective-permute-start.1 = (bf16[2,256,256]{2,1,0:T(8,128)(2,1)S(1)}, bf16[2,256,256]{2,1,0:T(8,128)(2,1)S(1)}, u32[]{:S(2)}, u32[]{:S(2)}) collective-permute-start(bf16[2,256,256]{2,1,0:T(8,128)(2,1)S(1)} %get-tuple-element.43), channel_id=1, source_target_pairs={{0,2},{1,3},{2,0},{3,1},{4,6},{5,7},{6,4},{7,5},{8,10},{9,11},{10,... | collective-permute-start | bytes 786440 | tf_op jit(solution)/shard_map/ppermute | solution.py:62
  19.2 14.4 %collective-permute-start.2 = (bf16[2,256,256]{2,1,0:T(8,128)(2,1)S(1)}, bf16[2,256,256]{2,1,0:T(8,128)(2,1)S(1)}, u32[]{:S(2)}, u32[]{:S(2)}) collective-permute-start(bf16[2,256,256]{2,1,0:T(8,128)(2,1)S(1)} %get-tuple-element.41.refs_0_), channel_id=1, source_target_pairs={{0,4},{1,5},{2,6},{3,7},{4,0},{5,1},{6,2},{7,3},{8,12},{9,13},{10,... | collective-permute-start | bytes 786440 | tf_op jit(solution)/shard_map/ppermute | solution.py:62
  35.1 10.2 %collective-permute-start.7 = (bf16[10,128,128]{2,1,0:T(8,128)(2,1)S(1)}, bf16[10,128,128]{2,1,0:T(8,128)(2,1)S(1)}, u32[]{:S(2)}, u32[]{:S(2)}) collective-permute-start(bf16[10,128,128]{2,1,0:T(8,128)(2,1)S(1)} %get-tuple-element.52), channel_id=1, source_target_pairs={{0,16},{8,24},{16,0},{24,8},{1,17},{9,25},{17,1},{25,9},{2,18},{10... | collective-permute-start | bytes 983048 | tf_op jit(solution)/shard_map/ppermute | solution.py:62
  36.5 8.8 %collective-permute-start.8 = (bf16[10,128,128]{2,1,0:T(8,128)(2,1)S(1)}, bf16[10,128,128]{2,1,0:T(8,128)(2,1)S(1)}, u32[]{:S(2)}, u32[]{:S(2)}) collective-permute-start(bf16[10,128,128]{2,1,0:T(8,128)(2,1)S(1)} %get-tuple-element.48.refs_0_), channel_id=1, source_target_pairs={{0,8},{8,0},{16,24},{24,16},{1,9},{9,1},{17,25},{25,17},{2,10},{10... | collective-permute-start | bytes 983048 | tf_op jit(solution)/shard_map/ppermute | solution.py:62
  38.0 7.3 %collective-permute-start.5 = (bf16[1,256,256]{2,1,0:T(8,128)(2,1)S(1)}, bf16[1,256,256]{2,1,0:T(8,128)(2,1)S(1)}, u32[]{:S(2)}, u32[]{:S(2)}) collective-permute-start(bf16[1,256,256]{2,1,0:T(8,128)(2,1)S(1)} %get-tuple-element.49), channel_id=1, source_target_pairs={{0,4},{1,5},{2,6},{3,7},{4,0},{5,1},{6,2},{7,3},{8,12},{9,13},{10,... | collective-permute-start | bytes 393224 | tf_op jit(solution)/shard_map/ppermute | solution.py:62
  38.4 7.0 %collective-permute-start.6 = (bf16[1,256,256]{2,1,0:T(8,128)(2,1)S(1)}, bf16[1,256,256]{2,1,0:T(8,128)(2,1)S(1)}, u32[]{:S(2)}, u32[]{:S(2)}) collective-permute-start(bf16[1,256,256]{2,1,0:T(8,128)(2,1)S(1)} %get-tuple-element.45.refs_0_), channel_id=1, source_target_pairs={{0,2},{1,3},{2,0},{3,1},{4,6},{5,7},{6,4},{7,5},{8,10},{9,11},{10,... | collective-permute-start | bytes 393224 | tf_op jit(solution)/shard_map/ppermute | solution.py:62
  47.1 26.6 %copy-start.13 = (s32[8]{0:T(128)S(1)}, s32[8]{0:T(128)}, u32[]{:S(2)}) copy-start(s32[8]{0:T(128)} %refs_4_.5) | copy-start | bytes 100
  47.1 2.0 %collective-permute-start.9 = (bf16[4,256,256]{2,1,0:T(8,128)(2,1)S(1)}, bf16[4,256,256]{2,1,0:T(8,128)(2,1)S(1)}, u32[]{:S(2)}, u32[]{:S(2)}) collective-permute-start(bf16[4,256,256]{2,1,0:T(8,128)(2,1)S(1)} %get-tuple-element.54.refs_0_), channel_id=1, source_target_pairs={{0,1},{1,0},{2,3},{3,2},{4,5},{5,4},{6,7},{7,6},{8,9},{9,8},{10,11... | collective-permute-start | bytes 1572872 | tf_op jit(solution)/shard_map/ppermute | solution.py:62
  47.2 9.6 %collective-permute-start.10 = (bf16[2,128,256]{2,1,0:T(8,128)(2,1)S(1)}, bf16[2,128,256]{2,1,0:T(8,128)(2,1)S(1)}, u32[]{:S(2)}, u32[]{:S(2)}) collective-permute-start(bf16[2,128,256]{2,1,0:T(8,128)(2,1)S(1)} %get-tuple-element.57.refs_1_.refs_2_), channel_id=1, source_target_pairs={{0,4},{1,5},{2,6},{3,7},{4,0},{5,1},{6,2},{7,3},{8,12},{9,13},{10,... | collective-permute-start | bytes 393224 | tf_op jit(solution)/shard_map/ppermute | solution.py:62
  56.9 16.9 %collective-permute-start.11 = (bf16[4,128,256]{2,1,0:T(8,128)(2,1)S(1)}, bf16[4,128,256]{2,1,0:T(8,128)(2,1)S(1)}, u32[]{:S(2)}, u32[]{:S(2)}) collective-permute-start(bf16[4,128,256]{2,1,0:T(8,128)(2,1)S(1)} %shard_map.118.refs_0_.refs_1_), channel_id=1, source_target_pairs={{0,2},{1,3},{2,0},{3,1},{4,6},{5,7},{6,4},{7,5},{8,10},{9,11},{10,... | collective-permute-start | bytes 786440 | tf_op jit(solution)/shard_map/ppermute | solution.py:62
  56.9 14.0 %collective-permute-start.12 = (bf16[256,256]{1,0:T(8,128)(2,1)S(1)}, bf16[256,256]{1,0:T(8,128)(2,1)S(1)}, u32[]{:S(2)}, u32[]{:S(2)}) collective-permute-start(bf16[256,256]{1,0:T(8,128)(2,1)S(1)} %get-tuple-element.59), channel_id=1, source_target_pairs={{0,2},{1,3},{2,0},{3,1},{4,6},{5,7},{6,4},{7,5},{8,10},{9,11},{10,... | collective-permute-start | bytes 393224 | tf_op jit(solution)/shard_map/ppermute | solution.py:62
  58.9 12.0 %collective-permute-start.13 = (bf16[256,256]{1,0:T(8,128)(2,1)S(1)}, bf16[256,256]{1,0:T(8,128)(2,1)S(1)}, u32[]{:S(2)}, u32[]{:S(2)}) collective-permute-start(bf16[256,256]{1,0:T(8,128)(2,1)S(1)} %get-tuple-element.60), channel_id=1, source_target_pairs={{0,4},{1,5},{2,6},{3,7},{4,0},{5,1},{6,2},{7,3},{8,12},{9,13},{10,... | collective-permute-start | bytes 393224 | tf_op jit(solution)/shard_map/ppermute | solution.py:62
  59.4 14.3 %collective-permute-start.14 = (bf16[256,256]{1,0:T(8,128)(2,1)S(1)}, bf16[256,256]{1,0:T(8,128)(2,1)S(1)}, u32[]{:S(2)}, u32[]{:S(2)}) collective-permute-start(bf16[256,256]{1,0:T(8,128)(2,1)S(1)} %get-tuple-element.56.refs_0_), channel_id=1, source_target_pairs={{0,6},{1,7},{2,4},{3,5},{4,2},{5,3},{6,0},{7,1},{8,14},{9,15},{10,... | collective-permute-start | bytes 393224 | tf_op jit(solution)/shard_map/ppermute | solution.py:62
  75.0 4.5 %collective-permute-start.15 = (f32[2,256,256]{2,1,0:T(8,128)S(1)}, f32[2,256,256]{2,1,0:T(8,128)S(1)}, u32[]{:S(2)}, u32[]{:S(2)}) collective-permute-start(f32[2,256,256]{2,1,0:T(8,128)S(1)} %shard_map.120.refs_0_.refs_1_), channel_id=1, source_target_pairs={{0,1},{1,0},{2,3},{3,2},{4,5},{5,4},{6,7},{7,6},{8,9},{9,8},{10,11... | collective-permute-start | bytes 1572872 | tf_op jit(solution)/shard_map/ppermute | solution.py:62
  75.1 13.4 %collective-permute-start.16 = (bf16[256,256]{1,0:T(8,128)(2,1)S(1)}, bf16[256,256]{1,0:T(8,128)(2,1)S(1)}, u32[]{:S(2)}, u32[]{:S(2)}) collective-permute-start(bf16[256,256]{1,0:T(8,128)(2,1)S(1)} %get-tuple-element.64.refs_1_), channel_id=1, source_target_pairs={{0,2},{1,3},{2,0},{3,1},{4,6},{5,7},{6,4},{7,5},{8,10},{9,11},{10,... | collective-permute-start | bytes 393224 | tf_op jit(solution)/shard_map/ppermute | solution.py:62
  75.2 13.4 %collective-permute-start.17 = (bf16[256,256]{1,0:T(8,128)(2,1)S(1)}, bf16[256,256]{1,0:T(8,128)(2,1)S(1)}, u32[]{:S(2)}, u32[]{:S(2)}) collective-permute-start(bf16[256,256]{1,0:T(8,128)(2,1)S(1)} %get-tuple-element.64.refs_1_), channel_id=1, source_target_pairs={{0,4},{1,5},{2,6},{3,7},{4,0},{5,1},{6,2},{7,3},{8,12},{9,13},{10,... | collective-permute-start | bytes 393224 | tf_op jit(solution)/shard_map/ppermute | solution.py:62
  77.5 11.0 %collective-permute-start.18 = (bf16[256,256]{1,0:T(8,128)(2,1)S(1)}, bf16[256,256]{1,0:T(8,128)(2,1)S(1)}, u32[]{:S(2)}, u32[]{:S(2)}) collective-permute-start(bf16[256,256]{1,0:T(8,128)(2,1)S(1)} %get-tuple-element.64.refs_1_), channel_id=1, source_target_pairs={{0,6},{1,7},{2,4},{3,5},{4,2},{5,3},{6,0},{7,1},{8,14},{9,15},{10,... | collective-permute-start | bytes 393224 | tf_op jit(solution)/shard_map/ppermute | solution.py:62
  88.6 2.0 %collective-permute-start.19 = (bf16[4,256,256]{2,1,0:T(8,128)(2,1)S(1)}, bf16[4,256,256]{2,1,0:T(8,128)(2,1)S(1)}, u32[]{:S(2)}, u32[]{:S(2)}) collective-permute-start(bf16[4,256,256]{2,1,0:T(8,128)(2,1)S(1)} %shard_map.123.refs_0_.refs_2_), channel_id=1, source_target_pairs={{0,1},{1,0},{2,3},{3,2},{4,5},{5,4},{6,7},{7,6},{8,9},{9,8},{10,11... | collective-permute-start | bytes 1572872 | tf_op jit(solution)/shard_map/ppermute | solution.py:62
  92.3 8.6 %collective-permute-start.20 = (bf16[8,128,128]{2,1,0:T(8,128)(2,1)}, bf16[8,128,128]{2,1,0:T(8,128)(2,1)S(1)}, u32[]{:S(2)}, u32[]{:S(2)}) collective-permute-start(bf16[8,128,128]{2,1,0:T(8,128)(2,1)} %get-tuple-element.66.refs_3_), channel_id=1, source_target_pairs={{0,8},{8,0},{16,24},{24,16},{1,9},{9,1},{17,25},{25,17},{2,10},{10... | collective-permute-start | bytes 786440 | tf_op jit(solution)/shard_map/ppermute | solution.py:62
  93.0 8.3 %collective-permute-start.21 = (bf16[8,128,128]{2,1,0:T(8,128)(2,1)}, bf16[8,128,128]{2,1,0:T(8,128)(2,1)S(1)}, u32[]{:S(2)}, u32[]{:S(2)}) collective-permute-start(bf16[8,128,128]{2,1,0:T(8,128)(2,1)} %get-tuple-element.67.refs_7_), channel_id=1, source_target_pairs={{0,16},{8,24},{16,0},{24,8},{1,17},{9,25},{17,1},{25,9},{2,18},{10... | collective-permute-start | bytes 786440 | tf_op jit(solution)/shard_map/ppermute | solution.py:62
  101.3 9.3 %collective-permute-start.22 = (bf16[8,128,128]{2,1,0:T(8,128)(2,1)S(1)}, bf16[8,128,128]{2,1,0:T(8,128)(2,1)S(1)}, u32[]{:S(2)}, u32[]{:S(2)}) collective-permute-start(bf16[8,128,128]{2,1,0:T(8,128)(2,1)S(1)} %get-tuple-element.69), channel_id=1, source_target_pairs={{0,16},{8,24},{16,0},{24,8},{1,17},{9,25},{17,1},{25,9},{2,18},{10... | collective-permute-start | bytes 786440 | tf_op jit(solution)/shard_map/ppermute | solution.py:62
  101.9 9.2 %collective-permute-start.23 = (bf16[8,128,128]{2,1,0:T(8,128)(2,1)S(1)}, bf16[8,128,128]{2,1,0:T(8,128)(2,1)S(1)}, u32[]{:S(2)}, u32[]{:S(2)}) collective-permute-start(bf16[8,128,128]{2,1,0:T(8,128)(2,1)S(1)} %get-tuple-element.68.refs_0_), channel_id=1, source_target_pairs={{0,8},{8,0},{16,24},{24,16},{1,9},{9,1},{17,25},{25,17},{2,10},{10... | collective-permute-start | bytes 786440 | tf_op jit(solution)/shard_map/ppermute | solution.py:62
  103.3 13.8 %collective-permute-start.24 = (bf16[8,128,128]{2,1,0:T(8,128)(2,1)}, bf16[8,128,128]{2,1,0:T(8,128)(2,1)}, u32[]{:S(2)}, u32[]{:S(2)}) collective-permute-start(bf16[8,128,128]{2,1,0:T(8,128)(2,1)} %get-tuple-element.66.refs_3_), channel_id=1, source_target_pairs={{0,16},{8,24},{16,0},{24,8},{1,17},{9,25},{17,1},{25,9},{2,18},{10... | collective-permute-start | bytes 786440 | tf_op jit(solution)/shard_map/ppermute | solution.py:62
  104.8 12.3 %collective-permute-start.25 = (bf16[8,128,128]{2,1,0:T(8,128)(2,1)}, bf16[8,128,128]{2,1,0:T(8,128)(2,1)}, u32[]{:S(2)}, u32[]{:S(2)}) collective-permute-start(bf16[8,128,128]{2,1,0:T(8,128)(2,1)} %get-tuple-element.67.refs_7_), channel_id=1, source_target_pairs={{0,8},{8,0},{16,24},{24,16},{1,9},{9,1},{17,25},{25,17},{2,10},{10... | collective-permute-start | bytes 786440 | tf_op jit(solution)/shard_map/ppermute | solution.py:62
  108.9 12.7 %collective-permute-start.26 = (bf16[2,128,256]{2,1,0:T(8,128)(2,1)S(1)}, bf16[2,128,256]{2,1,0:T(8,128)(2,1)S(1)}, u32[]{:S(2)}, u32[]{:S(2)}) collective-permute-start(bf16[2,128,256]{2,1,0:T(8,128)(2,1)S(1)} %shard_map.127.refs_0_.refs_2_), channel_id=1, source_target_pairs={{0,8},{8,0},{16,24},{24,16},{1,9},{9,1},{17,25},{25,17},{2,10},{10... | collective-permute-start | bytes 393224 | tf_op jit(solution)/shard_map/ppermute | solution.py:62
  110.7 10.9 %collective-permute-start.27 = (bf16[2,128,256]{2,1,0:T(8,128)(2,1)S(1)}, bf16[2,128,256]{2,1,0:T(8,128)(2,1)S(1)}, u32[]{:S(2)}, u32[]{:S(2)}) collective-permute-start(bf16[2,128,256]{2,1,0:T(8,128)(2,1)S(1)} %shard_map.127.refs_0_.refs_2_), channel_id=1, source_target_pairs={{0,16},{8,24},{16,0},{24,8},{1,17},{9,25},{17,1},{25,9},{2,18},{10... | collective-permute-start | bytes 393224 | tf_op jit(solution)/shard_map/ppermute | solution.py:62
  111.2 10.4 %collective-permute-start.28 = (bf16[2,128,256]{2,1,0:T(8,128)(2,1)S(1)}, bf16[2,128,256]{2,1,0:T(8,128)(2,1)}, u32[]{:S(2)}, u32[]{:S(2)}) collective-permute-start(bf16[2,128,256]{2,1,0:T(8,128)(2,1)S(1)} %shard_map.127.refs_0_.refs_2_), channel_id=1, source_target_pairs={{0,24},{8,16},{16,8},{24,0},{1,25},{9,17},{17,9},{25,1},{2,26},{10... | collective-permute-start | bytes 393224 | tf_op jit(solution)/shard_map/ppermute | solution.py:62
  (12 other events, 39.6 us)
Sparse Core Ops, SparseCore 0:
  92.4 20.6 all-gather.2

commit v9 on v8

--- a/solution.py
+++ b/solution.py
@@ -19,6 +19,7 @@
 HIGHEST = lax.Precision.HIGHEST
 VMEM_LIMIT = 48 * 1024 * 1024
 VMEM = pl.BlockSpec(memory_space=pltpu.VMEM)
+ANY = pl.BlockSpec(memory_space=pl.ANY)
 SMEM = pl.BlockSpec(memory_space=pltpu.SMEM)
 f32 = jnp.float32
 bf16 = jnp.bfloat16
@@ -28,15 +29,16 @@
     def __init__(self):
         self.last = None
 
-    def __call__(self, kernel, out_shape, args, scalars=0, us=2.0, scratch=(), after=()):
+    def __call__(self, kernel, out_shape, args, scalars=0, us=2.0, scratch=(), after=(), hbm=0, direct=False):
         many = isinstance(out_shape, (tuple, list))
-        specs = [SMEM] * scalars + [VMEM] * (len(args) - scalars)
+        specs = [SMEM] * scalars + [ANY] * hbm + [VMEM] * (len(args) - scalars - hbm)
+        place_out = ANY if direct else VMEM
         body = kernel
         if self.last is not None:
             after = (self.last, *after)
         unread = len(after)
         if unread:
-            specs = [pl.BlockSpec(memory_space=pl.ANY)] * unread + specs
+            specs = [ANY] * unread + specs
             args = (*after, *args)
 
             def body(*refs):
@@ -46,7 +48,7 @@
             body,
             out_shape=out_shape,
             in_specs=specs,
-            out_specs=[VMEM] * len(out_shape) if many else VMEM,
+            out_specs=[place_out] * len(out_shape) if many else place_out,
             scratch_shapes=list(scratch),
             compiler_params=pltpu.CompilerParams(vmem_limit_bytes=VMEM_LIMIT),
             cost_estimate=pl.CostEstimate(
@@ -100,12 +102,6 @@
             sends[side][count + i] = total.astype(bf16)
 
 
-def stack_kernel(own_ref, other_ref, out_ref):
-    half = own_ref.shape[0]
-    out_ref[:half] = own_ref[...]
-    out_ref[half:] = other_ref[...]
-
-
 def gather_kernel(*refs):
     for k, ref in enumerate(refs[:-1]):
         refs[-1][k] = ref[...]
@@ -117,18 +113,19 @@
         out[...] = ref[...]
 
 
-def gram_kernel(*refs):
+def gram_kernel(mixed_ref, *refs):
     out = refs[-1]
-    each = out.shape[0]
+    each, size, _ = out.shape
+    shard = refs[0].shape[1]
     for i in range(each):
+        first = size + i * shard
+        blocks = [mixed_ref[first : first + shard]] + [ref[i] for ref in refs[:-1]]
         total = None
-        for ref in refs[:-1]:
-            for j in range(i, ref.shape[0], each):
-                block = ref[j]
-                term = lax.dot_general(
-                    block, block, (((0,), (0,)), ((), ())), preferred_element_type=f32
-                )
-                total = term if total is None else total + term
+        for block in blocks:
+            term = lax.dot_general(
+                block, block, (((0,), (0,)), ((), ())), preferred_element_type=f32
+            )
+            total = term if total is None else total + term
         out[i] = total
 
 
@@ -288,10 +285,15 @@
             sample_ref[i, :, columns] = total.astype(bf16)
 
 
-def pair_kernel(place, mine_ref, other_ref, *outs):
+def pair_kernel(place, mine_ref, other_ref, sample_ref, *outs):
+    rank_full = mine_ref.shape[1]
+    each, shard, _ = sample_ref.shape
     for k, out in enumerate(outs):
         i = place[1] ^ k
-        out[...] = (mine_ref[i] + other_ref[i].astype(f32)).astype(out.dtype)
+        out[:rank_full] = (mine_ref[i] + other_ref[i].astype(f32)).astype(out.dtype)
+    for i in range(each):
+        first = rank_full + i * shard
+        outs[1][first : first + shard] = sample_ref[i]
 
 
 def update_kernel(place, owner, rank, *refs, chips, bits, start):
@@ -301,7 +303,7 @@
     m = 2 * z + core
     projected = terms[0][...].astype(f32)
     for ref in terms[1:]:
-        projected = projected + ref[...].astype(f32)
+        projected = projected + ref[: projected.shape[0]].astype(f32)
     width = projected.shape[1]
     columns = slice(start, start + width)
     near = near_half(place, owner, 0, bits[0])
@@ -332,16 +334,21 @@
 
 
 def weight_kernel(place, weight_ref, *refs, groups, chunks):
-    out_ref = refs[-1]
-    width = refs[0].shape[2]
-    for h in range(chunks):
-        for k in range(groups):
-            start = ((place[0] ^ k) * chunks + h) * width
-            columns = pl.ds(pl.multiple_of(start, 128), width)
-            for m in range(out_ref.shape[0]):
-                delta = refs[h * groups + k][m].astype(f32)
+    *deltas, out_hbm, out_ref, sems = refs
+    width = deltas[0].shape[2]
+    copies = []
+    for m in range(out_ref.shape[0]):
+        for h in range(chunks):
+            for k in range(groups):
+                start = ((place[0] ^ k) * chunks + h) * width
+                columns = pl.ds(pl.multiple_of(start, 128), width)
+                delta = deltas[h * groups + k][m].astype(f32)
                 old = weight_ref[m, :, columns].astype(f32)
                 out_ref[m, :, columns] = (old - step_size * delta).astype(bf16)
+        copies.append(pltpu.make_async_copy(out_ref.at[m], out_hbm.at[m], sems.at[m]))
+        copies[-1].start()
+    for copy in copies:
+        copy.wait()
 
 
 def basis_kernel(place, *refs):
@@ -352,12 +359,10 @@
             out_ref[(place[0] ^ k) * each + i] = ref[i].astype(f32)
 
 
-def moment_kernel(place, owner, *refs, chunks):
-    projected_refs = refs[:chunks]
-    first_ref, second_ref, first_out, second_out = refs[chunks:]
+def moment_kernel(place, owner, projected_hbm, first_ref, second_ref, *refs):
+    first_hbm, second_hbm, projected_ref, first_out, second_out, sems = refs
     here = place[1] * 2 + place[2]
-    capacity, rank_full, _ = first_out.shape
-    width = projected_refs[0].shape[2]
+    capacity = first_out.shape[0]
     seen = jnp.int32(0)
     index = [jnp.int32(0)] * capacity
     for m in range(owner.shape[0]):
@@ -365,17 +370,29 @@
         for s in range(capacity):
             index[s] = jnp.where(hit & (seen == s), m, index[s])
         seen = seen + hit.astype(jnp.int32)
+    fetches = [
+        pltpu.make_async_copy(projected_hbm.at[index[s]], projected_ref.at[s], sems.at[0, s])
+        for s in range(capacity)
+    ]
+    for fetch in fetches:
+        fetch.start()
+    copies = []
     for s in range(capacity):
+        fetches[s].wait()
         keep = seen > s
-        for h in range(chunks):
-            columns = slice(h * width, (h + 1) * width)
-            projected = projected_refs[h][index[s]].astype(f32)
-            first_new = beta_one * first_ref[s, :, columns] + (1.0 - beta_one) * projected
-            second_new = (
-                beta_two * second_ref[s, :, columns] + (1.0 - beta_two) * projected * projected
+        projected = projected_ref[s].astype(f32)
+        first_new = beta_one * first_ref[s] + (1.0 - beta_one) * projected
+        second_new = beta_two * second_ref[s] + (1.0 - beta_two) * projected * projected
+        first_out[s] = jnp.where(keep, first_new, 0.0)
+        second_out[s] = jnp.where(keep, second_new, 0.0)
+        pairs = ((first_out, first_hbm), (second_out, second_hbm))
+        for t, (source, target) in enumerate(pairs):
+            copies.append(
+                pltpu.make_async_copy(source.at[s], target.at[s], sems.at[1 + t, s])
             )
-            first_out[s, :, columns] = jnp.where(keep, first_new, 0.0)
-            second_out[s, :, columns] = jnp.where(keep, second_new, 0.0)
+            copies[-1].start()
+    for copy in copies:
+        copy.wait()
 
 
 def per_device(grads, weight, basis, first_moment, second_moment, sketch, owner, rank):
@@ -446,21 +463,23 @@
         after=(inputs[1], inputs[3]),
     )
     other = swap(other, "rows", 1)
+    samples = [sample]
     mask = chips // 2
-    arrived = swap(sample, "rows", 2 * mask)
+    while mask > 1:
+        samples += [swap(x, "rows", 2 * mask) for x in samples]
+        mask //= 2
     terms = call(
         pair_kernel,
-        [struct((rank_full, quarter), f32)] + [struct((rank_full, quarter), bf16)] * (chips - 1),
-        (place, mine, other),
+        [
+            struct((rank_full, quarter), f32),
+            struct((rank_full + each * shard, quarter), bf16),
+        ]
+        + [struct((rank_full, quarter), bf16)] * (chips - 2),
+        (place, mine, other, sample),
         scalars=1,
     )
+    samples += [swap(x, "rows", 2) for x in samples[1:]]
     terms = [terms[0]] + [swap(terms[k], "rows", 2 * k) for k in range(1, chips)]
-    stacked = sample
-    while mask > 1:
-        both = struct((2 * stacked.shape[0], shard, rank_full), bf16)
-        stacked = call(stack_kernel, both, (stacked, arrived))
-        mask //= 2
-        arrived = swap(stacked, "rows", 2 * mask)
     work_shape = struct((each, rank_full, 2 * rank_full), f32)
     last = rank_full // BLOCK - 1
     update, projected = call(
@@ -468,11 +487,11 @@
         [struct((rank_full, quarter), bf16)] * 2,
         (place, owner, rank, *terms, *inputs),
         scalars=3,
-        after=(arrived,),
+        after=tuple(samples[1:]),
     )
     near = [update] + [swap(update, "rows", 2 * k) for k in range(1, chips)]
     gram = call(
-        gram_kernel, struct((each, rank_full, rank_full), f32), (stacked, arrived)
+        gram_kernel, struct((each, rank_full, rank_full), f32), (terms[1], *samples)
     )
     other_gram = swap(gram, "rows", 1)
     work = call(start_kernel, work_shape, (gram, other_gram))
@@ -507,17 +526,27 @@
     )
     shared = [rows_basis] + [swap(rows_basis, "dp", k) for k in range(1, groups)]
     first_out, second_out = call(
-        functools.partial(moment_kernel, chunks=1),
+        moment_kernel,
         [struct(first_moment.shape, f32)] * 2,
         (place, owner, gathered, first_moment, second_moment),
         scalars=2,
         after=tuple(across),
+        hbm=1,
+        direct=True,
+        scratch=[
+            pltpu.VMEM(first_moment.shape, bf16),
+            pltpu.VMEM(first_moment.shape, f32),
+            pltpu.VMEM(first_moment.shape, f32),
+            pltpu.SemaphoreType.DMA((3, capacity)),
+        ],
     )
     new_weight = call(
         functools.partial(weight_kernel, groups=groups, chunks=2),
         struct(weight.shape, bf16),
         (place, weight, *deltas),
         scalars=1,
+        direct=True,
+        scratch=[pltpu.VMEM(weight.shape, bf16), pltpu.SemaphoreType.DMA((count,))],
     )
     new_basis = call(basis_kernel, struct(basis.shape, f32), (place, *shared), scalars=1)
     return (new_weight, new_basis, first_out, second_out)

time: 132 us -> 130 us (0.985)
  waiting for transfers between devices: 41.9 us -> 38.4 us
  starting transfers between devices: 34.6 us -> 36.1 us
    ppermute x29, waiting for transfers between devices: 41.9 us -> 38.3 us  [swap(): return lax.ppermute(x, axis, [(i, i ^ mask) for i in range(size)])]
    ppermute x29, starting transfers between devices: 34.6 us -> 36.1 us  [swap(): return lax.ppermute(x, axis, [(i, i ^ mask) for i in range(size)])]
    pallas_call x20 -> x19, Pallas kernels: 34.2 us -> 34.3 us  [__call__(): pl.pallas_call(body, out_shape=out_shape, in_specs=specs, out_specs=[plac...]
  transfers between devices with their start and end apart: 30 -> 30, of which waited for: 11 -> 13; matrix products, arithmetic and copies ran while one was open for 0% -> 0% of each run, Pallas kernels for 18% -> 19%
where the time goes in v9:
time: 130 us
  waiting for transfers between devices  38.4 us (30%)
  starting transfers between devices  36.1 us (28%)
  Pallas kernels  34.3 us (26%)
  between operations  14.4 us (11%)
  local copies, waits for them, and re-layouts  6.85 us (5%)
    ppermute x29, waiting for transfers between devices, swap(): return lax.ppermute(x, axis, [(i, i ^ mask) for i in range(size)])  38.3 us
    ppermute x29, starting transfers between devices, swap(): return lax.ppermute(x, axis, [(i, i ^ mask) for i in range(size)])  36.1 us
    pallas_call x19, Pallas kernels, __call__(): pl.pallas_call(body, out_shape=out_shape, in_specs=specs, out_specs=[plac...  34.3 us
    unnamed x28, local copies, waits for them, and re-layouts  6.85 us
  transfers between devices with their start and end apart: 30, of which 13 were waited for; matrix products, arithmetic and copies ran while one was open for 0% of the time, Pallas kernels for 19%

profile of v9, /device:TPU:0, one launch (start us, length us, event | category | flops | bytes accessed | tf_op | source)
XLA Modules:
  0.0 130.1 jit_solution(11291023628989895436)
XLA Ops:
  7.3 1.6 %copy-done = bf16[1,8,128,1024]{3,2,1,0:T(8,128)(2,1)S(1)} copy-done((bf16[1,8,128,1024]{3,2,1,0:T(8,128)(2,1)S(1)}, bf16[1,8,128,1024]{3,2,1,0:T(8,128)(2,1)}, u32[]{:S(2)}) %copy-start) | copy-done | bytes 2097176
  10.0 1.5 %shard_map.111 = (f32[2,128,256]{2,1,0:T(8,128)S(1)}, f32[2,2,128,128]{3,2,1,0:T(8,128)S(1)}, bf16[2,10,128,128]{3,2,1,0:T(8,128)(2,1)S(1)}, bf16[2,10,128,128]{3,2,1,0:T(8,128)(2,1)S(1)}) custom-call(s32[3]{0:T(128)S(1)} %pad_add_fusion.place.refs_1_.refs_3_, bf16[1,8,128,1024]{3,2,1,0:T(8,128)(2,1)S(1)} %copy-done, bf16[1024,256]{1,0:T(8,128)(2,1)S(1)} %copy-done.11), custom_call_target="tpu_custom_call" | custom-call | bytes 20000 | tf_op jit(solution)/shard_map/pallas_call | solution.py:47
  12.8 2.6 %collective-permute-start.3 = (bf16[2,10,128,128]{3,2,1,0:T(8,128)(2,1)S(1)}, bf16[2,10,128,128]{3,2,1,0:T(8,128)(2,1)S(1)}, u32[]{:S(2)}, u32[]{:S(2)}) collective-permute-start(bf16[2,10,128,128]{3,2,1,0:T(8,128)(2,1)S(1)} %get-tuple-element.47), channel_id=1, source_target_pairs={{0,8},{8,0},{16,24},{24,16},{1,9},{9,1},{17,25},{25,17},{2,10},{10... | collective-permute-start | bytes 1966088 | tf_op jit(solution)/shard_map/ppermute | solution.py:64
  15.4 1.5 %collective-permute-start.4 = (bf16[2,10,128,128]{3,2,1,0:T(8,128)(2,1)S(1)}, bf16[2,10,128,128]{3,2,1,0:T(8,128)(2,1)S(1)}, u32[]{:S(2)}, u32[]{:S(2)}) collective-permute-start(bf16[2,10,128,128]{3,2,1,0:T(8,128)(2,1)S(1)} %get-tuple-element.38.refs_0_), channel_id=1, source_target_pairs={{0,16},{8,24},{16,0},{24,8},{1,17},{9,25},{17,1},{25,9},{2,18},{10... | collective-permute-start | bytes 1966088 | tf_op jit(solution)/shard_map/ppermute | solution.py:64
  17.6 1.6 %collective-permute-start.1 = (bf16[2,256,256]{2,1,0:T(8,128)(2,1)S(1)}, bf16[2,256,256]{2,1,0:T(8,128)(2,1)S(1)}, u32[]{:S(2)}, u32[]{:S(2)}) collective-permute-start(bf16[2,256,256]{2,1,0:T(8,128)(2,1)S(1)} %get-tuple-element.43), channel_id=1, source_target_pairs={{0,2},{1,3},{2,0},{3,1},{4,6},{5,7},{6,4},{7,5},{8,10},{9,11},{10,... | collective-permute-start | bytes 786440 | tf_op jit(solution)/shard_map/ppermute | solution.py:64
  19.2 2.6 %collective-permute-start.2 = (bf16[2,256,256]{2,1,0:T(8,128)(2,1)S(1)}, bf16[2,256,256]{2,1,0:T(8,128)(2,1)S(1)}, u32[]{:S(2)}, u32[]{:S(2)}) collective-permute-start(bf16[2,256,256]{2,1,0:T(8,128)(2,1)S(1)} %get-tuple-element.41.refs_0_), channel_id=1, source_target_pairs={{0,4},{1,5},{2,6},{3,7},{4,0},{5,1},{6,2},{7,3},{8,12},{9,13},{10,... | collective-permute-start | bytes 786440 | tf_op jit(solution)/shard_map/ppermute | solution.py:64
  21.8 9.4 %collective-permute-done.1.refs_4_ = bf16[2,256,256]{2,1,0:T(8,128)(2,1)S(1)} collective-permute-done((bf16[2,256,256]{2,1,0:T(8,128)(2,1)S(1)}, bf16[2,256,256]{2,1,0:T(8,128)(2,1)S(1)}, u32[]{:S(2)}, u32[]{:S(2)}) %collective-permute-start.1) | collective-permute-done | bytes 262176 | tf_op jit(solution)/shard_map/ppermute | solution.py:64
  31.3 2.3 %collective-permute-done.2.refs_6_ = bf16[2,256,256]{2,1,0:T(8,128)(2,1)S(1)} collective-permute-done((bf16[2,256,256]{2,1,0:T(8,128)(2,1)S(1)}, bf16[2,256,256]{2,1,0:T(8,128)(2,1)S(1)}, u32[]{:S(2)}, u32[]{:S(2)}) %collective-permute-start.2) | collective-permute-done | bytes 262176 | tf_op jit(solution)/shard_map/ppermute | solution.py:64
  38.4 2.7 %collective-permute-start.6 = (bf16[1,256,256]{2,1,0:T(8,128)(2,1)S(1)}, bf16[1,256,256]{2,1,0:T(8,128)(2,1)S(1)}, u32[]{:S(2)}, u32[]{:S(2)}) collective-permute-start(bf16[1,256,256]{2,1,0:T(8,128)(2,1)S(1)} %get-tuple-element.45.refs_0_), channel_id=1, source_target_pairs={{0,2},{1,3},{2,0},{3,1},{4,6},{5,7},{6,4},{7,5},{8,10},{9,11},{10,... | collective-permute-start | bytes 393224 | tf_op jit(solution)/shard_map/ppermute | solution.py:64
  41.1 4.3 %collective-permute-done.5.refs_1_.refs_11_ = bf16[1,256,256]{2,1,0:T(8,128)(2,1)S(1)} collective-permute-done((bf16[1,256,256]{2,1,0:T(8,128)(2,1)S(1)}, bf16[1,256,256]{2,1,0:T(8,128)(2,1)S(1)}, u32[]{:S(2)}, u32[]{:S(2)}) %collective-permute-start.5) | collective-permute-done | bytes 131104 | tf_op jit(solution)/shard_map/ppermute | solution.py:64
  45.4 1.7 %shard_map.116 = (f32[4,256,256]{2,1,0:T(8,128)S(1)}, bf16[2,128,256]{2,1,0:T(8,128)(2,1)S(1)}, bf16[4,256,256]{2,1,0:T(8,128)(2,1)S(1)}) custom-call(bf16[10,128,128]{2,1,0:T(8,128)(2,1)S(1)} %get-tuple-element.48.refs_0_, bf16[1,256,256]{2,1,0:T(8,128)(2,1)S(1)} %collective-permute-done.5.refs_1_.refs_11_, ...), custom_call_target="tpu_custom_call" | custom-call | bytes 20000 | tf_op jit(solution)/shard_map/pallas_call | solution.py:47
  50.7 6.3 %collective-permute-done.10.refs_1_.refs_3_ = bf16[2,128,256]{2,1,0:T(8,128)(2,1)S(1)} collective-permute-done((bf16[2,128,256]{2,1,0:T(8,128)(2,1)S(1)}, bf16[2,128,256]{2,1,0:T(8,128)(2,1)S(1)}, u32[]{:S(2)}, u32[]{:S(2)}) %collective-permute-start.10) | collective-permute-done | bytes 131104 | tf_op jit(solution)/shard_map/ppermute | solution.py:64
  56.9 2.4 %collective-permute-start.13 = (bf16[256,256]{1,0:T(8,128)(2,1)S(1)}, bf16[256,256]{1,0:T(8,128)(2,1)S(1)}, u32[]{:S(2)}, u32[]{:S(2)}) collective-permute-start(bf16[256,256]{1,0:T(8,128)(2,1)S(1)} %get-tuple-element.60), channel_id=1, source_target_pairs={{0,4},{1,5},{2,6},{3,7},{4,0},{5,1},{6,2},{7,3},{8,12},{9,13},{10,... | collective-permute-start | bytes 393224 | tf_op jit(solution)/shard_map/ppermute | solution.py:64
  59.3 2.0 %collective-permute-start.14 = (bf16[256,256]{1,0:T(8,128)(2,1)S(1)}, bf16[256,256]{1,0:T(8,128)(2,1)S(1)}, u32[]{:S(2)}, u32[]{:S(2)}) collective-permute-start(bf16[256,256]{1,0:T(8,128)(2,1)S(1)} %get-tuple-element.57.refs_0_), channel_id=1, source_target_pairs={{0,6},{1,7},{2,4},{3,5},{4,2},{5,3},{6,0},{7,1},{8,14},{9,15},{10,... | collective-permute-start | bytes 393224 | tf_op jit(solution)/shard_map/ppermute | solution.py:64
  61.3 4.7 %collective-permute-done.11.refs_2_.refs_4_ = bf16[2,128,256]{2,1,0:T(8,128)(2,1)S(1)} collective-permute-done((bf16[2,128,256]{2,1,0:T(8,128)(2,1)S(1)}, bf16[2,128,256]{2,1,0:T(8,128)(2,1)S(1)}, u32[]{:S(2)}, u32[]{:S(2)}) %collective-permute-start.11) | collective-permute-done | bytes 131104 | tf_op jit(solution)/shard_map/ppermute | solution.py:64
  66.0 3.8 %collective-permute-done.13.refs_8_ = bf16[256,256]{1,0:T(8,128)(2,1)S(1)} collective-permute-done((bf16[256,256]{1,0:T(8,128)(2,1)S(1)}, bf16[256,256]{1,0:T(8,128)(2,1)S(1)}, u32[]{:S(2)}, u32[]{:S(2)}) %collective-permute-start.13) | collective-permute-done | bytes 131104 | tf_op jit(solution)/shard_map/ppermute | solution.py:64
  71.2 2.3 %collective-permute-start.16 = (bf16[256,256]{1,0:T(8,128)(2,1)S(1)}, bf16[256,256]{1,0:T(8,128)(2,1)S(1)}, u32[]{:S(2)}, u32[]{:S(2)}) collective-permute-start(bf16[256,256]{1,0:T(8,128)(2,1)S(1)} %get-tuple-element.64.refs_1_), channel_id=1, source_target_pairs={{0,2},{1,3},{2,0},{3,1},{4,6},{5,7},{6,4},{7,5},{8,10},{9,11},{10,... | collective-permute-start | bytes 393224 | tf_op jit(solution)/shard_map/ppermute | solution.py:64
  74.2 1.8 %collective-permute-start.18 = (bf16[256,256]{1,0:T(8,128)(2,1)S(1)}, bf16[256,256]{1,0:T(8,128)(2,1)S(1)}, u32[]{:S(2)}, u32[]{:S(2)}) collective-permute-start(bf16[256,256]{1,0:T(8,128)(2,1)S(1)} %get-tuple-element.64.refs_1_), channel_id=1, source_target_pairs={{0,6},{1,7},{2,4},{3,5},{4,2},{5,3},{6,0},{7,1},{8,14},{9,15},{10,... | collective-permute-start | bytes 393224 | tf_op jit(solution)/shard_map/ppermute | solution.py:64
  76.0 4.4 %shard_map.120.refs_0_.refs_1_ = f32[2,256,512]{2,1,0:T(8,128)S(1)} custom-call(f32[2,256,256]{2,1,0:T(8,128)S(1)} %shard_map.119.refs_0_.refs_1_, f32[2,256,256]{2,1,0:T(8,128)S(1)} %shard_map.119.refs_0_.refs_1_, f32[2,256,256]{2,1,0:T(8,128)S(1)} %collective-permute-done.15.refs_2_), custom_call_target="tpu_custom_call" | custom-call | bytes 20000 | tf_op jit(solution)/shard_map/pallas_call | solution.py:47
  80.4 4.6 %shard_map.121.refs_0_.refs_1_ = f32[2,256,512]{2,1,0:T(8,128)S(1)} custom-call(f32[2,256,512]{2,1,0:T(8,128)S(1)} %shard_map.120.refs_0_.refs_1_, f32[2,256,512]{2,1,0:T(8,128)S(1)} %shard_map.120.refs_0_.refs_1_), custom_call_target="tpu_custom_call" | custom-call | bytes 20000 | tf_op jit(solution)/shard_map/pallas_call | solution.py:47
  86.6 1.9 %collective-permute-done.19.refs_3_ = bf16[4,256,256]{2,1,0:T(8,128)(2,1)S(1)} collective-permute-done((bf16[4,256,256]{2,1,0:T(8,128)(2,1)S(1)}, bf16[4,256,256]{2,1,0:T(8,128)(2,1)S(1)}, u32[]{:S(2)}, u32[]{:S(2)}) %collective-permute-start.19) | collective-permute-done | bytes 524320 | tf_op jit(solution)/shard_map/ppermute | solution.py:64
  88.5 1.7 %shard_map.123 = (bf16[8,128,128]{2,1,0:T(8,128)(2,1)}, bf16[8,128,128]{2,1,0:T(8,128)(2,1)}, bf16[256,256]{1,0:T(8,128)(2,1)}) custom-call(bf16[4,256,256]{2,1,0:T(8,128)(2,1)S(1)} %shard_map.122.refs_0_.refs_2_, s32[3]{0:T(128)S(1)} %pad_add_fusion.place.refs_1_.refs_3_, bf16[4,256,256]{2,1,0:T(8,128)(2,1)S(1)} %shard_map.122.refs_0_.refs_2_, ...), custom_call_target="tpu_custom_call" | custom-call | bytes 20000 | tf_op jit(solution)/shard_map/pallas_call | solution.py:47
  91.3 4.5 %shard_map.124.refs_0_.refs_1_ = f32[2,256,512]{2,1,0:T(8,128)S(1)} custom-call(bf16[256,256]{1,0:T(8,128)(2,1)} %get-tuple-element.65.refs_0_, f32[2,256,512]{2,1,0:T(8,128)S(1)} %shard_map.121.refs_0_.refs_1_), custom_call_target="tpu_custom_call" | custom-call | bytes 20000 | tf_op jit(solution)/shard_map/pallas_call | solution.py:47
  95.8 3.0 %collective-permute-done.20.refs_1_.refs_4_ = bf16[8,128,128]{2,1,0:T(8,128)(2,1)S(1)} collective-permute-done((bf16[8,128,128]{2,1,0:T(8,128)(2,1)}, bf16[8,128,128]{2,1,0:T(8,128)(2,1)S(1)}, u32[]{:S(2)}, u32[]{:S(2)}) %collective-permute-start.20) | collective-permute-done | bytes 262176 | tf_op jit(solution)/shard_map/ppermute | solution.py:64
  99.7 1.5 %collective-permute-start.23 = (bf16[8,128,128]{2,1,0:T(8,128)(2,1)S(1)}, bf16[8,128,128]{2,1,0:T(8,128)(2,1)S(1)}, u32[]{:S(2)}, u32[]{:S(2)}) collective-permute-start(bf16[8,128,128]{2,1,0:T(8,128)(2,1)S(1)} %get-tuple-element.68.refs_0_), channel_id=1, source_target_pairs={{0,8},{8,0},{16,24},{24,16},{1,9},{9,1},{17,25},{25,17},{2,10},{10... | collective-permute-start | bytes 786440 | tf_op jit(solution)/shard_map/ppermute | solution.py:64
  103.0 3.4 %shard_map.126.refs_0_.refs_2_ = bf16[2,128,256]{2,1,0:T(8,128)(2,1)S(1)} custom-call(bf16[8,128,128]{2,1,0:T(8,128)(2,1)S(1)} %get-tuple-element.68.refs_0_, f32[2,256,512]{2,1,0:T(8,128)S(1)} %shard_map.124.refs_0_.refs_1_, bf16[2,128,256]{2,1,0:T(8,128)(2,1)S(1)} %get-tuple-element.56.refs_4_.refs_2_), custom_call_target="tpu_custom_call" | custom-call | bytes 20000 | tf_op jit(solution)/shard_map/pallas_call | solution.py:47
  106.4 1.7 %collective-permute-start.26 = (bf16[2,128,256]{2,1,0:T(8,128)(2,1)S(1)}, bf16[2,128,256]{2,1,0:T(8,128)(2,1)S(1)}, u32[]{:S(2)}, u32[]{:S(2)}) collective-permute-start(bf16[2,128,256]{2,1,0:T(8,128)(2,1)S(1)} %shard_map.126.refs_0_.refs_2_), channel_id=1, source_target_pairs={{0,8},{8,0},{16,24},{24,16},{1,9},{9,1},{17,25},{25,17},{2,10},{10... | collective-permute-start | bytes 393224 | tf_op jit(solution)/shard_map/ppermute | solution.py:64
  108.9 2.5 %collective-permute-start.28 = (bf16[2,128,256]{2,1,0:T(8,128)(2,1)S(1)}, bf16[2,128,256]{2,1,0:T(8,128)(2,1)}, u32[]{:S(2)}, u32[]{:S(2)}) collective-permute-start(bf16[2,128,256]{2,1,0:T(8,128)(2,1)S(1)} %shard_map.126.refs_0_.refs_2_), channel_id=1, source_target_pairs={{0,24},{8,16},{16,8},{24,0},{1,25},{9,17},{17,9},{25,1},{2,26},{10... | collective-permute-start | bytes 393224 | tf_op jit(solution)/shard_map/ppermute | solution.py:64
  112.9 2.7 %shard_map.127 = (f32[4,256,256]{2,1,0:T(8,128)}, f32[4,256,256]{2,1,0:T(8,128)}) custom-call(bf16[2,128,256]{2,1,0:T(8,128)(2,1)S(1)} %shard_map.126.refs_0_.refs_2_, bf16[8,128,128]{2,1,0:T(8,128)(2,1)S(1)} %collective-permute-done.22.refs_1_.refs_6_, bf16[8,128,128]{2,1,0:T(8,128)(2,1)S(1)} %collective-permute-done.23.refs_2_.refs_10_, ...), custom_call_target="tpu_custom_call" | custom-call | bytes 20000 | tf_op jit(solution)/shard_map/pallas_call | solution.py:47
  116.9 2.8 %shard_map.128.refs_0_ = bf16[8,128,1024]{2,1,0:T(8,128)(2,1)} custom-call(f32[4,256,256]{2,1,0:T(8,128)S(1)} %copy-done.8, s32[3]{0:T(128)S(1)} %pad_add_fusion.place.refs_1_.refs_3_, bf16[8,128,1024]{2,1,0:T(8,128)(2,1)S(1)} %copy-done.6, bf16[8,128,128]{2,1,0:T(8,128)(2,1)} %get-tuple-element.66.refs_3_, ...), custom_call_target="tpu_custom_call" | custom-call | bytes 20000 | tf_op jit(solution)/shard_map/pallas_call | solution.py:47
  119.7 1.6 %copy-done.2 = bf16[8,128,1024]{2,1,0:T(8,128)(2,1)S(1)} copy-done((bf16[8,128,1024]{2,1,0:T(8,128)(2,1)S(1)}, bf16[8,128,1024]{2,1,0:T(8,128)(2,1)}, u32[]{:S(2)}) %copy-start.2) | copy-done | bytes 2097176
  121.3 2.0 %shard_map.129 = f32[8,128,256]{2,1,0:T(8,128)} custom-call(bf16[8,128,1024]{2,1,0:T(8,128)(2,1)S(1)} %copy-done.2, s32[3]{0:T(128)S(1)} %pad_add_fusion.place.refs_1_.refs_3_, bf16[2,128,256]{2,1,0:T(8,128)(2,1)S(1)} %shard_map.126.refs_0_.refs_2_, bf16[2,128,256]{2,1,0:T(8,128)(2,1)S(1)} %collective-permute-done.26.refs_3_, ...), custom_call_target="tpu_custom_call" | custom-call | bytes 20000 | tf_op jit(solution)/shard_map/pallas_call | solution.py:47
  (77 shorter events, 22.3 us)
Async XLA Ops:
  7.2 104.3 %all-gather.3.cloned.1.call-start = ((), (), s32[]{:S(2)}) async-start(), calls=%async_computation | async-start | bytes 1179648 | tf_op jit(solution)/shard_map/all_gather | solution.py:515
  12.3 4.6 %collective-permute-start = (bf16[4,2,256,256]{3,2,1,0:T(8,128)(2,1)S(1)}, bf16[4,2,256,256]{3,2,1,0:T(8,128)(2,1)S(1)}, u32[]{:S(2)}, u32[]{:S(2)}) collective-permute-start(bf16[4,2,256,256]{3,2,1,0:T(8,128)(2,1)S(1)} %get-tuple-element.39.refs_0_), channel_id=1, source_target_pairs={{0,1},{1,0},{2,3},{3,2},{4,5},{5,4},{6,7},{7,6},{8,9},{9,8},{10,11... | collective-permute-start | bytes 3145736 | tf_op jit(solution)/shard_map/ppermute | solution.py:64
  12.8 21.4 %collective-permute-start.3 = (bf16[2,10,128,128]{3,2,1,0:T(8,128)(2,1)S(1)}, bf16[2,10,128,128]{3,2,1,0:T(8,128)(2,1)S(1)}, u32[]{:S(2)}, u32[]{:S(2)}) collective-permute-start(bf16[2,10,128,128]{3,2,1,0:T(8,128)(2,1)S(1)} %get-tuple-element.47), channel_id=1, source_target_pairs={{0,8},{8,0},{16,24},{24,16},{1,9},{9,1},{17,25},{25,17},{2,10},{10... | collective-permute-start | bytes 1966088 | tf_op jit(solution)/shard_map/ppermute | solution.py:64
  15.4 18.8 %collective-permute-start.4 = (bf16[2,10,128,128]{3,2,1,0:T(8,128)(2,1)S(1)}, bf16[2,10,128,128]{3,2,1,0:T(8,128)(2,1)S(1)}, u32[]{:S(2)}, u32[]{:S(2)}) collective-permute-start(bf16[2,10,128,128]{3,2,1,0:T(8,128)(2,1)S(1)} %get-tuple-element.38.refs_0_), channel_id=1, source_target_pairs={{0,16},{8,24},{16,0},{24,8},{1,17},{9,25},{17,1},{25,9},{2,18},{10... | collective-permute-start | bytes 1966088 | tf_op jit(solution)/shard_map/ppermute | solution.py:64
  16.9 17.3 %copy-start.1 = (bf16[1,8,128,1024]{3,2,1,0:T(8,128)(2,1)S(1)}, bf16[1,8,128,1024]{3,2,1,0:T(8,128)(2,1)}, u32[]{:S(2)}) copy-start(bf16[1,8,128,1024]{3,2,1,0:T(8,128)(2,1)} %refs_2_.8) | copy-start | bytes 6291460
  17.6 13.7 %collective-permute-start.1 = (bf16[2,256,256]{2,1,0:T(8,128)(2,1)S(1)}, bf16[2,256,256]{2,1,0:T(8,128)(2,1)S(1)}, u32[]{:S(2)}, u32[]{:S(2)}) collective-permute-start(bf16[2,256,256]{2,1,0:T(8,128)(2,1)S(1)} %get-tuple-element.43), channel_id=1, source_target_pairs={{0,2},{1,3},{2,0},{3,1},{4,6},{5,7},{6,4},{7,5},{8,10},{9,11},{10,... | collective-permute-start | bytes 786440 | tf_op jit(solution)/shard_map/ppermute | solution.py:64
  19.2 14.4 %collective-permute-start.2 = (bf16[2,256,256]{2,1,0:T(8,128)(2,1)S(1)}, bf16[2,256,256]{2,1,0:T(8,128)(2,1)S(1)}, u32[]{:S(2)}, u32[]{:S(2)}) collective-permute-start(bf16[2,256,256]{2,1,0:T(8,128)(2,1)S(1)} %get-tuple-element.41.refs_0_), channel_id=1, source_target_pairs={{0,4},{1,5},{2,6},{3,7},{4,0},{5,1},{6,2},{7,3},{8,12},{9,13},{10,... | collective-permute-start | bytes 786440 | tf_op jit(solution)/shard_map/ppermute | solution.py:64
  35.1 10.2 %collective-permute-start.7 = (bf16[10,128,128]{2,1,0:T(8,128)(2,1)S(1)}, bf16[10,128,128]{2,1,0:T(8,128)(2,1)S(1)}, u32[]{:S(2)}, u32[]{:S(2)}) collective-permute-start(bf16[10,128,128]{2,1,0:T(8,128)(2,1)S(1)} %get-tuple-element.52), channel_id=1, source_target_pairs={{0,16},{8,24},{16,0},{24,8},{1,17},{9,25},{17,1},{25,9},{2,18},{10... | collective-permute-start | bytes 983048 | tf_op jit(solution)/shard_map/ppermute | solution.py:64
  36.5 8.8 %collective-permute-start.8 = (bf16[10,128,128]{2,1,0:T(8,128)(2,1)S(1)}, bf16[10,128,128]{2,1,0:T(8,128)(2,1)S(1)}, u32[]{:S(2)}, u32[]{:S(2)}) collective-permute-start(bf16[10,128,128]{2,1,0:T(8,128)(2,1)S(1)} %get-tuple-element.48.refs_0_), channel_id=1, source_target_pairs={{0,8},{8,0},{16,24},{24,16},{1,9},{9,1},{17,25},{25,17},{2,10},{10... | collective-permute-start | bytes 983048 | tf_op jit(solution)/shard_map/ppermute | solution.py:64
  38.0 7.3 %collective-permute-start.5 = (bf16[1,256,256]{2,1,0:T(8,128)(2,1)S(1)}, bf16[1,256,256]{2,1,0:T(8,128)(2,1)S(1)}, u32[]{:S(2)}, u32[]{:S(2)}) collective-permute-start(bf16[1,256,256]{2,1,0:T(8,128)(2,1)S(1)} %get-tuple-element.49), channel_id=1, source_target_pairs={{0,4},{1,5},{2,6},{3,7},{4,0},{5,1},{6,2},{7,3},{8,12},{9,13},{10,... | collective-permute-start | bytes 393224 | tf_op jit(solution)/shard_map/ppermute | solution.py:64
  38.4 7.0 %collective-permute-start.6 = (bf16[1,256,256]{2,1,0:T(8,128)(2,1)S(1)}, bf16[1,256,256]{2,1,0:T(8,128)(2,1)S(1)}, u32[]{:S(2)}, u32[]{:S(2)}) collective-permute-start(bf16[1,256,256]{2,1,0:T(8,128)(2,1)S(1)} %get-tuple-element.45.refs_0_), channel_id=1, source_target_pairs={{0,2},{1,3},{2,0},{3,1},{4,6},{5,7},{6,4},{7,5},{8,10},{9,11},{10,... | collective-permute-start | bytes 393224 | tf_op jit(solution)/shard_map/ppermute | solution.py:64
  47.1 22.7 %copy-start.13 = (s32[8]{0:T(128)S(1)}, s32[8]{0:T(128)}, u32[]{:S(2)}) copy-start(s32[8]{0:T(128)} %refs_5_.1) | copy-start | bytes 100
  47.1 2.0 %collective-permute-start.9 = (bf16[4,256,256]{2,1,0:T(8,128)(2,1)S(1)}, bf16[4,256,256]{2,1,0:T(8,128)(2,1)S(1)}, u32[]{:S(2)}, u32[]{:S(2)}) collective-permute-start(bf16[4,256,256]{2,1,0:T(8,128)(2,1)S(1)} %get-tuple-element.54.refs_0_), channel_id=1, source_target_pairs={{0,1},{1,0},{2,3},{3,2},{4,5},{5,4},{6,7},{7,6},{8,9},{9,8},{10,11... | collective-permute-start | bytes 1572872 | tf_op jit(solution)/shard_map/ppermute | solution.py:64
  47.2 9.7 %collective-permute-start.10 = (bf16[2,128,256]{2,1,0:T(8,128)(2,1)S(1)}, bf16[2,128,256]{2,1,0:T(8,128)(2,1)S(1)}, u32[]{:S(2)}, u32[]{:S(2)}) collective-permute-start(bf16[2,128,256]{2,1,0:T(8,128)(2,1)S(1)} %get-tuple-element.56.refs_4_.refs_2_), channel_id=1, source_target_pairs={{0,4},{1,5},{2,6},{3,7},{4,0},{5,1},{6,2},{7,3},{8,12},{9,13},{10,... | collective-permute-start | bytes 393224 | tf_op jit(solution)/shard_map/ppermute | solution.py:64
  49.7 20.1 %collective-permute-start.12 = (bf16[512,256]{1,0:T(8,128)(2,1)S(1)}, bf16[512,256]{1,0:T(8,128)(2,1)S(1)}, u32[]{:S(2)}, u32[]{:S(2)}) collective-permute-start(bf16[512,256]{1,0:T(8,128)(2,1)S(1)} %get-tuple-element.59), channel_id=1, source_target_pairs={{0,2},{1,3},{2,0},{3,1},{4,6},{5,7},{6,4},{7,5},{8,10},{9,11},{10,... | collective-permute-start | bytes 786440 | tf_op jit(solution)/shard_map/ppermute | solution.py:64
  56.9 9.1 %collective-permute-start.11 = (bf16[2,128,256]{2,1,0:T(8,128)(2,1)S(1)}, bf16[2,128,256]{2,1,0:T(8,128)(2,1)S(1)}, u32[]{:S(2)}, u32[]{:S(2)}) collective-permute-start(bf16[2,128,256]{2,1,0:T(8,128)(2,1)S(1)} %collective-permute-done.10.refs_1_.refs_3_), channel_id=1, source_target_pairs={{0,2},{1,3},{2,0},{3,1},{4,6},{5,7},{6,4},{7,5},{8,10},{9,11},{10,... | collective-permute-start | bytes 393224 | tf_op jit(solution)/shard_map/ppermute | solution.py:64
  56.9 12.9 %collective-permute-start.13 = (bf16[256,256]{1,0:T(8,128)(2,1)S(1)}, bf16[256,256]{1,0:T(8,128)(2,1)S(1)}, u32[]{:S(2)}, u32[]{:S(2)}) collective-permute-start(bf16[256,256]{1,0:T(8,128)(2,1)S(1)} %get-tuple-element.60), channel_id=1, source_target_pairs={{0,4},{1,5},{2,6},{3,7},{4,0},{5,1},{6,2},{7,3},{8,12},{9,13},{10,... | collective-permute-start | bytes 393224 | tf_op jit(solution)/shard_map/ppermute | solution.py:64
  59.3 10.5 %collective-permute-start.14 = (bf16[256,256]{1,0:T(8,128)(2,1)S(1)}, bf16[256,256]{1,0:T(8,128)(2,1)S(1)}, u32[]{:S(2)}, u32[]{:S(2)}) collective-permute-start(bf16[256,256]{1,0:T(8,128)(2,1)S(1)} %get-tuple-element.57.refs_0_), channel_id=1, source_target_pairs={{0,6},{1,7},{2,4},{3,5},{4,2},{5,3},{6,0},{7,1},{8,14},{9,15},{10,... | collective-permute-start | bytes 393224 | tf_op jit(solution)/shard_map/ppermute | solution.py:64
  71.2 4.8 %collective-permute-start.15 = (f32[2,256,256]{2,1,0:T(8,128)S(1)}, f32[2,256,256]{2,1,0:T(8,128)S(1)}, u32[]{:S(2)}, u32[]{:S(2)}) collective-permute-start(f32[2,256,256]{2,1,0:T(8,128)S(1)} %shard_map.119.refs_0_.refs_1_), channel_id=1, source_target_pairs={{0,1},{1,0},{2,3},{3,2},{4,5},{5,4},{6,7},{7,6},{8,9},{9,8},{10,11... | collective-permute-start | bytes 1572872 | tf_op jit(solution)/shard_map/ppermute | solution.py:64
  71.2 13.7 %collective-permute-start.16 = (bf16[256,256]{1,0:T(8,128)(2,1)S(1)}, bf16[256,256]{1,0:T(8,128)(2,1)S(1)}, u32[]{:S(2)}, u32[]{:S(2)}) collective-permute-start(bf16[256,256]{1,0:T(8,128)(2,1)S(1)} %get-tuple-element.64.refs_1_), channel_id=1, source_target_pairs={{0,2},{1,3},{2,0},{3,1},{4,6},{5,7},{6,4},{7,5},{8,10},{9,11},{10,... | collective-permute-start | bytes 393224 | tf_op jit(solution)/shard_map/ppermute | solution.py:64
  73.5 12.9 %collective-permute-start.17 = (bf16[256,256]{1,0:T(8,128)(2,1)S(1)}, bf16[256,256]{1,0:T(8,128)(2,1)S(1)}, u32[]{:S(2)}, u32[]{:S(2)}) collective-permute-start(bf16[256,256]{1,0:T(8,128)(2,1)S(1)} %get-tuple-element.64.refs_1_), channel_id=1, source_target_pairs={{0,4},{1,5},{2,6},{3,7},{4,0},{5,1},{6,2},{7,3},{8,12},{9,13},{10,... | collective-permute-start | bytes 393224 | tf_op jit(solution)/shard_map/ppermute | solution.py:64
  74.2 12.2 %collective-permute-start.18 = (bf16[256,256]{1,0:T(8,128)(2,1)S(1)}, bf16[256,256]{1,0:T(8,128)(2,1)S(1)}, u32[]{:S(2)}, u32[]{:S(2)}) collective-permute-start(bf16[256,256]{1,0:T(8,128)(2,1)S(1)} %get-tuple-element.64.refs_1_), channel_id=1, source_target_pairs={{0,6},{1,7},{2,4},{3,5},{4,2},{5,3},{6,0},{7,1},{8,14},{9,15},{10,... | collective-permute-start | bytes 393224 | tf_op jit(solution)/shard_map/ppermute | solution.py:64
  86.5 2.0 %collective-permute-start.19 = (bf16[4,256,256]{2,1,0:T(8,128)(2,1)S(1)}, bf16[4,256,256]{2,1,0:T(8,128)(2,1)S(1)}, u32[]{:S(2)}, u32[]{:S(2)}) collective-permute-start(bf16[4,256,256]{2,1,0:T(8,128)(2,1)S(1)} %shard_map.122.refs_0_.refs_2_), channel_id=1, source_target_pairs={{0,1},{1,0},{2,3},{3,2},{4,5},{5,4},{6,7},{7,6},{8,9},{9,8},{10,11... | collective-permute-start | bytes 1572872 | tf_op jit(solution)/shard_map/ppermute | solution.py:64
  90.2 8.6 %collective-permute-start.20 = (bf16[8,128,128]{2,1,0:T(8,128)(2,1)}, bf16[8,128,128]{2,1,0:T(8,128)(2,1)S(1)}, u32[]{:S(2)}, u32[]{:S(2)}) collective-permute-start(bf16[8,128,128]{2,1,0:T(8,128)(2,1)} %get-tuple-element.66.refs_3_), channel_id=1, source_target_pairs={{0,8},{8,0},{16,24},{24,16},{1,9},{9,1},{17,25},{25,17},{2,10},{10... | collective-permute-start | bytes 786440 | tf_op jit(solution)/shard_map/ppermute | solution.py:64
  90.6 8.3 %collective-permute-start.21 = (bf16[8,128,128]{2,1,0:T(8,128)(2,1)}, bf16[8,128,128]{2,1,0:T(8,128)(2,1)S(1)}, u32[]{:S(2)}, u32[]{:S(2)}) collective-permute-start(bf16[8,128,128]{2,1,0:T(8,128)(2,1)} %get-tuple-element.67.refs_7_), channel_id=1, source_target_pairs={{0,16},{8,24},{16,0},{24,8},{1,17},{9,25},{17,1},{25,9},{2,18},{10... | collective-permute-start | bytes 786440 | tf_op jit(solution)/shard_map/ppermute | solution.py:64
  98.9 9.3 %collective-permute-start.22 = (bf16[8,128,128]{2,1,0:T(8,128)(2,1)S(1)}, bf16[8,128,128]{2,1,0:T(8,128)(2,1)S(1)}, u32[]{:S(2)}, u32[]{:S(2)}) collective-permute-start(bf16[8,128,128]{2,1,0:T(8,128)(2,1)S(1)} %get-tuple-element.69), channel_id=1, source_target_pairs={{0,16},{8,24},{16,0},{24,8},{1,17},{9,25},{17,1},{25,9},{2,18},{10... | collective-permute-start | bytes 786440 | tf_op jit(solution)/shard_map/ppermute | solution.py:64
  99.7 9.2 %collective-permute-start.23 = (bf16[8,128,128]{2,1,0:T(8,128)(2,1)S(1)}, bf16[8,128,128]{2,1,0:T(8,128)(2,1)S(1)}, u32[]{:S(2)}, u32[]{:S(2)}) collective-permute-start(bf16[8,128,128]{2,1,0:T(8,128)(2,1)S(1)} %get-tuple-element.68.refs_0_), channel_id=1, source_target_pairs={{0,8},{8,0},{16,24},{24,16},{1,9},{9,1},{17,25},{25,17},{2,10},{10... | collective-permute-start | bytes 786440 | tf_op jit(solution)/shard_map/ppermute | solution.py:64
  101.2 14.4 %collective-permute-start.24 = (bf16[8,128,128]{2,1,0:T(8,128)(2,1)}, bf16[8,128,128]{2,1,0:T(8,128)(2,1)}, u32[]{:S(2)}, u32[]{:S(2)}) collective-permute-start(bf16[8,128,128]{2,1,0:T(8,128)(2,1)} %get-tuple-element.66.refs_3_), channel_id=1, source_target_pairs={{0,16},{8,24},{16,0},{24,8},{1,17},{9,25},{17,1},{25,9},{2,18},{10... | collective-permute-start | bytes 786440 | tf_op jit(solution)/shard_map/ppermute | solution.py:64
  102.7 12.9 %collective-permute-start.25 = (bf16[8,128,128]{2,1,0:T(8,128)(2,1)}, bf16[8,128,128]{2,1,0:T(8,128)(2,1)}, u32[]{:S(2)}, u32[]{:S(2)}) collective-permute-start(bf16[8,128,128]{2,1,0:T(8,128)(2,1)} %get-tuple-element.67.refs_7_), channel_id=1, source_target_pairs={{0,8},{8,0},{16,24},{24,16},{1,9},{9,1},{17,25},{25,17},{2,10},{10... | collective-permute-start | bytes 786440 | tf_op jit(solution)/shard_map/ppermute | solution.py:64
  106.4 13.2 %collective-permute-start.26 = (bf16[2,128,256]{2,1,0:T(8,128)(2,1)S(1)}, bf16[2,128,256]{2,1,0:T(8,128)(2,1)S(1)}, u32[]{:S(2)}, u32[]{:S(2)}) collective-permute-start(bf16[2,128,256]{2,1,0:T(8,128)(2,1)S(1)} %shard_map.126.refs_0_.refs_2_), channel_id=1, source_target_pairs={{0,8},{8,0},{16,24},{24,16},{1,9},{9,1},{17,25},{25,17},{2,10},{10... | collective-permute-start | bytes 393224 | tf_op jit(solution)/shard_map/ppermute | solution.py:64
  108.2 11.4 %collective-permute-start.27 = (bf16[2,128,256]{2,1,0:T(8,128)(2,1)S(1)}, bf16[2,128,256]{2,1,0:T(8,128)(2,1)S(1)}, u32[]{:S(2)}, u32[]{:S(2)}) collective-permute-start(bf16[2,128,256]{2,1,0:T(8,128)(2,1)S(1)} %shard_map.126.refs_0_.refs_2_), channel_id=1, source_target_pairs={{0,16},{8,24},{16,0},{24,8},{1,17},{9,25},{17,1},{25,9},{2,18},{10... | collective-permute-start | bytes 393224 | tf_op jit(solution)/shard_map/ppermute | solution.py:64
  108.9 10.8 %collective-permute-start.28 = (bf16[2,128,256]{2,1,0:T(8,128)(2,1)S(1)}, bf16[2,128,256]{2,1,0:T(8,128)(2,1)}, u32[]{:S(2)}, u32[]{:S(2)}) collective-permute-start(bf16[2,128,256]{2,1,0:T(8,128)(2,1)S(1)} %shard_map.126.refs_0_.refs_2_), channel_id=1, source_target_pairs={{0,24},{8,16},{16,8},{24,0},{1,25},{9,17},{17,9},{25,1},{2,26},{10... | collective-permute-start | bytes 393224 | tf_op jit(solution)/shard_map/ppermute | solution.py:64
  (12 other events, 39.2 us)
Sparse Core Ops, SparseCore 0:
  90.3 21.1 all-gather.2

commit v10 on v9

--- a/solution.py
+++ b/solution.py
@@ -20,6 +20,7 @@
 VMEM_LIMIT = 48 * 1024 * 1024
 VMEM = pl.BlockSpec(memory_space=pltpu.VMEM)
 ANY = pl.BlockSpec(memory_space=pl.ANY)
+HBM = pl.BlockSpec(memory_space=pltpu.HBM)
 SMEM = pl.BlockSpec(memory_space=pltpu.SMEM)
 f32 = jnp.float32
 bf16 = jnp.bfloat16
@@ -31,8 +32,8 @@
 
     def __call__(self, kernel, out_shape, args, scalars=0, us=2.0, scratch=(), after=(), hbm=0, direct=False):
         many = isinstance(out_shape, (tuple, list))
-        specs = [SMEM] * scalars + [ANY] * hbm + [VMEM] * (len(args) - scalars - hbm)
-        place_out = ANY if direct else VMEM
+        specs = [SMEM] * scalars + [HBM] * hbm + [VMEM] * (len(args) - scalars - hbm)
+        place_out = HBM if direct else VMEM
         body = kernel
         if self.last is not None:
             after = (self.last, *after)
@@ -487,7 +488,6 @@
         [struct((rank_full, quarter), bf16)] * 2,
         (place, owner, rank, *terms, *inputs),
         scalars=3,
-        after=tuple(samples[1:]),
     )
     near = [update] + [swap(update, "rows", 2 * k) for k in range(1, chips)]
     gram = call(

time: 130 us -> 130 us (level)
    ppermute x29, waiting for transfers between devices: 38.3 us -> 36.5 us  [swap(): return lax.ppermute(x, axis, [(i, i ^ mask) for i in range(size)])]
  transfers between devices with their start and end apart: 30 -> 30, of which waited for: 13 -> 12; matrix products, arithmetic and copies ran while one was open for 0% -> 0% of each run, Pallas kernels for 19% -> 19%
where the time goes in v10:
time: 130 us
  starting transfers between devices  37.3 us (29%)
  waiting for transfers between devices  37.2 us (29%)
  Pallas kernels  34.3 us (26%)
  between operations  14.4 us (11%)
  local copies, waits for them, and re-layouts  6.85 us (5%)
    ppermute x29, starting transfers between devices, swap(): return lax.ppermute(x, axis, [(i, i ^ mask) for i in range(size)])  37.2 us
    ppermute x29, waiting for transfers between devices, swap(): return lax.ppermute(x, axis, [(i, i ^ mask) for i in range(size)])  36.5 us
    pallas_call x19, Pallas kernels, __call__(): pl.pallas_call(body, out_shape=out_shape, in_specs=specs, out_specs=[plac...  34.3 us
    unnamed x28, local copies, waits for them, and re-layouts  6.85 us
  transfers between devices with their start and end apart: 30, of which 12 were waited for; matrix products, arithmetic and copies ran while one was open for 0% of the time, Pallas kernels for 19%

profile of v10, /device:TPU:0, one launch (start us, length us, event | category | flops | bytes accessed | tf_op | source)
XLA Modules:
  0.0 130.0 jit_solution(6315797137749792155)
XLA Ops:
  7.3 1.6 %copy-done = bf16[1,8,128,1024]{3,2,1,0:T(8,128)(2,1)S(1)} copy-done((bf16[1,8,128,1024]{3,2,1,0:T(8,128)(2,1)S(1)}, bf16[1,8,128,1024]{3,2,1,0:T(8,128)(2,1)}, u32[]{:S(2)}) %copy-start) | copy-done | bytes 2097176
  10.0 1.5 %shard_map.111 = (f32[2,128,256]{2,1,0:T(8,128)S(1)}, f32[2,2,128,128]{3,2,1,0:T(8,128)S(1)}, bf16[2,10,128,128]{3,2,1,0:T(8,128)(2,1)S(1)}, bf16[2,10,128,128]{3,2,1,0:T(8,128)(2,1)S(1)}) custom-call(s32[3]{0:T(128)S(1)} %pad_add_fusion.place.refs_1_.refs_3_, bf16[1,8,128,1024]{3,2,1,0:T(8,128)(2,1)S(1)} %copy-done, bf16[1024,256]{1,0:T(8,128)(2,1)S(1)} %copy-done.11), custom_call_target="tpu_custom_call" | custom-call | bytes 20000 | tf_op jit(solution)/shard_map/pallas_call | solution.py:48
  12.8 2.6 %collective-permute-start.3 = (bf16[2,10,128,128]{3,2,1,0:T(8,128)(2,1)S(1)}, bf16[2,10,128,128]{3,2,1,0:T(8,128)(2,1)S(1)}, u32[]{:S(2)}, u32[]{:S(2)}) collective-permute-start(bf16[2,10,128,128]{3,2,1,0:T(8,128)(2,1)S(1)} %get-tuple-element.47), channel_id=1, source_target_pairs={{0,8},{8,0},{16,24},{24,16},{1,9},{9,1},{17,25},{25,17},{2,10},{10... | collective-permute-start | bytes 1966088 | tf_op jit(solution)/shard_map/ppermute | solution.py:65
  15.4 1.5 %collective-permute-start.4 = (bf16[2,10,128,128]{3,2,1,0:T(8,128)(2,1)S(1)}, bf16[2,10,128,128]{3,2,1,0:T(8,128)(2,1)S(1)}, u32[]{:S(2)}, u32[]{:S(2)}) collective-permute-start(bf16[2,10,128,128]{3,2,1,0:T(8,128)(2,1)S(1)} %get-tuple-element.38.refs_0_), channel_id=1, source_target_pairs={{0,16},{8,24},{16,0},{24,8},{1,17},{9,25},{17,1},{25,9},{2,18},{10... | collective-permute-start | bytes 1966088 | tf_op jit(solution)/shard_map/ppermute | solution.py:65
  17.6 1.6 %collective-permute-start.1 = (bf16[2,256,256]{2,1,0:T(8,128)(2,1)S(1)}, bf16[2,256,256]{2,1,0:T(8,128)(2,1)S(1)}, u32[]{:S(2)}, u32[]{:S(2)}) collective-permute-start(bf16[2,256,256]{2,1,0:T(8,128)(2,1)S(1)} %get-tuple-element.43), channel_id=1, source_target_pairs={{0,2},{1,3},{2,0},{3,1},{4,6},{5,7},{6,4},{7,5},{8,10},{9,11},{10,... | collective-permute-start | bytes 786440 | tf_op jit(solution)/shard_map/ppermute | solution.py:65
  19.2 2.6 %collective-permute-start.2 = (bf16[2,256,256]{2,1,0:T(8,128)(2,1)S(1)}, bf16[2,256,256]{2,1,0:T(8,128)(2,1)S(1)}, u32[]{:S(2)}, u32[]{:S(2)}) collective-permute-start(bf16[2,256,256]{2,1,0:T(8,128)(2,1)S(1)} %get-tuple-element.41.refs_0_), channel_id=1, source_target_pairs={{0,4},{1,5},{2,6},{3,7},{4,0},{5,1},{6,2},{7,3},{8,12},{9,13},{10,... | collective-permute-start | bytes 786440 | tf_op jit(solution)/shard_map/ppermute | solution.py:65
  21.8 9.4 %collective-permute-done.1.refs_4_ = bf16[2,256,256]{2,1,0:T(8,128)(2,1)S(1)} collective-permute-done((bf16[2,256,256]{2,1,0:T(8,128)(2,1)S(1)}, bf16[2,256,256]{2,1,0:T(8,128)(2,1)S(1)}, u32[]{:S(2)}, u32[]{:S(2)}) %collective-permute-start.1) | collective-permute-done | bytes 262176 | tf_op jit(solution)/shard_map/ppermute | solution.py:65
  31.3 2.3 %collective-permute-done.2.refs_6_ = bf16[2,256,256]{2,1,0:T(8,128)(2,1)S(1)} collective-permute-done((bf16[2,256,256]{2,1,0:T(8,128)(2,1)S(1)}, bf16[2,256,256]{2,1,0:T(8,128)(2,1)S(1)}, u32[]{:S(2)}, u32[]{:S(2)}) %collective-permute-start.2) | collective-permute-done | bytes 262176 | tf_op jit(solution)/shard_map/ppermute | solution.py:65
  38.4 2.7 %collective-permute-start.6 = (bf16[1,256,256]{2,1,0:T(8,128)(2,1)S(1)}, bf16[1,256,256]{2,1,0:T(8,128)(2,1)S(1)}, u32[]{:S(2)}, u32[]{:S(2)}) collective-permute-start(bf16[1,256,256]{2,1,0:T(8,128)(2,1)S(1)} %get-tuple-element.45.refs_0_), channel_id=1, source_target_pairs={{0,2},{1,3},{2,0},{3,1},{4,6},{5,7},{6,4},{7,5},{8,10},{9,11},{10,... | collective-permute-start | bytes 393224 | tf_op jit(solution)/shard_map/ppermute | solution.py:65
  41.1 4.3 %collective-permute-done.5.refs_1_.refs_9_ = bf16[1,256,256]{2,1,0:T(8,128)(2,1)S(1)} collective-permute-done((bf16[1,256,256]{2,1,0:T(8,128)(2,1)S(1)}, bf16[1,256,256]{2,1,0:T(8,128)(2,1)S(1)}, u32[]{:S(2)}, u32[]{:S(2)}) %collective-permute-start.5) | collective-permute-done | bytes 131104 | tf_op jit(solution)/shard_map/ppermute | solution.py:65
  45.4 1.7 %shard_map.116 = (f32[4,256,256]{2,1,0:T(8,128)S(1)}, bf16[2,128,256]{2,1,0:T(8,128)(2,1)S(1)}, bf16[4,256,256]{2,1,0:T(8,128)(2,1)S(1)}) custom-call(bf16[10,128,128]{2,1,0:T(8,128)(2,1)S(1)} %get-tuple-element.48.refs_0_, bf16[1,256,256]{2,1,0:T(8,128)(2,1)S(1)} %collective-permute-done.5.refs_1_.refs_9_, ...), custom_call_target="tpu_custom_call" | custom-call | bytes 20000 | tf_op jit(solution)/shard_map/pallas_call | solution.py:48
  47.2 1.9 %collective-permute-done.9.refs_3_ = bf16[4,256,256]{2,1,0:T(8,128)(2,1)S(1)} collective-permute-done((bf16[4,256,256]{2,1,0:T(8,128)(2,1)S(1)}, bf16[4,256,256]{2,1,0:T(8,128)(2,1)S(1)}, u32[]{:S(2)}, u32[]{:S(2)}) %collective-permute-start.9) | collective-permute-done | bytes 524320 | tf_op jit(solution)/shard_map/ppermute | solution.py:65
  50.5 2.0 %collective-permute-start.13 = (bf16[2,128,256]{2,1,0:T(8,128)(2,1)S(1)}, bf16[2,128,256]{2,1,0:T(8,128)(2,1)S(1)}, u32[]{:S(2)}, u32[]{:S(2)}) collective-permute-start(bf16[2,128,256]{2,1,0:T(8,128)(2,1)S(1)} %get-tuple-element.56.refs_4_.refs_2_), channel_id=1, source_target_pairs={{0,4},{1,5},{2,6},{3,7},{4,0},{5,1},{6,2},{7,3},{8,12},{9,13},{10,... | collective-permute-start | bytes 393224 | tf_op jit(solution)/shard_map/ppermute | solution.py:65
  53.5 1.7 %collective-permute-start.12 = (bf16[256,256]{1,0:T(8,128)(2,1)S(1)}, bf16[256,256]{1,0:T(8,128)(2,1)S(1)}, u32[]{:S(2)}, u32[]{:S(2)}) collective-permute-start(bf16[256,256]{1,0:T(8,128)(2,1)S(1)} %get-tuple-element.57.refs_0_), channel_id=1, source_target_pairs={{0,6},{1,7},{2,4},{3,5},{4,2},{5,3},{6,0},{7,1},{8,14},{9,15},{10,... | collective-permute-start | bytes 393224 | tf_op jit(solution)/shard_map/ppermute | solution.py:65
  55.1 4.9 %collective-permute-done.13.refs_3_ = bf16[2,128,256]{2,1,0:T(8,128)(2,1)S(1)} collective-permute-done((bf16[2,128,256]{2,1,0:T(8,128)(2,1)S(1)}, bf16[2,128,256]{2,1,0:T(8,128)(2,1)S(1)}, u32[]{:S(2)}, u32[]{:S(2)}) %collective-permute-start.13) | collective-permute-done | bytes 131104 | tf_op jit(solution)/shard_map/ppermute | solution.py:65
  60.0 2.7 %collective-permute-start.14 = (bf16[2,128,256]{2,1,0:T(8,128)(2,1)S(1)}, bf16[2,128,256]{2,1,0:T(8,128)(2,1)S(1)}, u32[]{:S(2)}, u32[]{:S(2)}) collective-permute-start(bf16[2,128,256]{2,1,0:T(8,128)(2,1)S(1)} %collective-permute-done.13.refs_3_), channel_id=1, source_target_pairs={{0,2},{1,3},{2,0},{3,1},{4,6},{5,7},{6,4},{7,5},{8,10},{9,11},{10,... | collective-permute-start | bytes 393224 | tf_op jit(solution)/shard_map/ppermute | solution.py:65
  62.8 6.3 %collective-permute-done.11.refs_6_ = bf16[256,256]{1,0:T(8,128)(2,1)S(1)} collective-permute-done((bf16[256,256]{1,0:T(8,128)(2,1)S(1)}, bf16[256,256]{1,0:T(8,128)(2,1)S(1)}, u32[]{:S(2)}, u32[]{:S(2)}) %collective-permute-start.11) | collective-permute-done | bytes 131104 | tf_op jit(solution)/shard_map/ppermute | solution.py:65
  70.5 2.4 %collective-permute-start.16 = (bf16[256,256]{1,0:T(8,128)(2,1)S(1)}, bf16[256,256]{1,0:T(8,128)(2,1)S(1)}, u32[]{:S(2)}, u32[]{:S(2)}) collective-permute-start(bf16[256,256]{1,0:T(8,128)(2,1)S(1)} %get-tuple-element.64.refs_1_), channel_id=1, source_target_pairs={{0,2},{1,3},{2,0},{3,1},{4,6},{5,7},{6,4},{7,5},{8,10},{9,11},{10,... | collective-permute-start | bytes 393224 | tf_op jit(solution)/shard_map/ppermute | solution.py:65
  73.2 2.1 %collective-permute-start.18 = (bf16[256,256]{1,0:T(8,128)(2,1)S(1)}, bf16[256,256]{1,0:T(8,128)(2,1)S(1)}, u32[]{:S(2)}, u32[]{:S(2)}) collective-permute-start(bf16[256,256]{1,0:T(8,128)(2,1)S(1)} %get-tuple-element.64.refs_1_), channel_id=1, source_target_pairs={{0,6},{1,7},{2,4},{3,5},{4,2},{5,3},{6,0},{7,1},{8,14},{9,15},{10,... | collective-permute-start | bytes 393224 | tf_op jit(solution)/shard_map/ppermute | solution.py:65
  75.3 4.4 %shard_map.120.refs_0_.refs_1_ = f32[2,256,512]{2,1,0:T(8,128)S(1)} custom-call(f32[2,256,256]{2,1,0:T(8,128)S(1)} %shard_map.119.refs_0_.refs_1_, f32[2,256,256]{2,1,0:T(8,128)S(1)} %shard_map.119.refs_0_.refs_1_, f32[2,256,256]{2,1,0:T(8,128)S(1)} %collective-permute-done.15.refs_2_), custom_call_target="tpu_custom_call" | custom-call | bytes 20000 | tf_op jit(solution)/shard_map/pallas_call | solution.py:48
  79.7 4.6 %shard_map.121.refs_0_.refs_1_ = f32[2,256,512]{2,1,0:T(8,128)S(1)} custom-call(f32[2,256,512]{2,1,0:T(8,128)S(1)} %shard_map.120.refs_0_.refs_1_, f32[2,256,512]{2,1,0:T(8,128)S(1)} %shard_map.120.refs_0_.refs_1_), custom_call_target="tpu_custom_call" | custom-call | bytes 20000 | tf_op jit(solution)/shard_map/pallas_call | solution.py:48
  85.9 1.9 %collective-permute-done.19.refs_3_ = bf16[4,256,256]{2,1,0:T(8,128)(2,1)S(1)} collective-permute-done((bf16[4,256,256]{2,1,0:T(8,128)(2,1)S(1)}, bf16[4,256,256]{2,1,0:T(8,128)(2,1)S(1)}, u32[]{:S(2)}, u32[]{:S(2)}) %collective-permute-start.19) | collective-permute-done | bytes 524320 | tf_op jit(solution)/shard_map/ppermute | solution.py:65
  87.8 1.7 %shard_map.123 = (bf16[8,128,128]{2,1,0:T(8,128)(2,1)}, bf16[8,128,128]{2,1,0:T(8,128)(2,1)}, bf16[256,256]{1,0:T(8,128)(2,1)}) custom-call(bf16[4,256,256]{2,1,0:T(8,128)(2,1)S(1)} %shard_map.122.refs_0_.refs_2_, s32[3]{0:T(128)S(1)} %pad_add_fusion.place.refs_1_.refs_3_, bf16[4,256,256]{2,1,0:T(8,128)(2,1)S(1)} %shard_map.122.refs_0_.refs_2_, ...), custom_call_target="tpu_custom_call" | custom-call | bytes 20000 | tf_op jit(solution)/shard_map/pallas_call | solution.py:48
  91.1 4.6 %shard_map.124.refs_0_.refs_1_ = f32[2,256,512]{2,1,0:T(8,128)S(1)} custom-call(bf16[256,256]{1,0:T(8,128)(2,1)} %get-tuple-element.65.refs_0_, f32[2,256,512]{2,1,0:T(8,128)S(1)} %shard_map.121.refs_0_.refs_1_), custom_call_target="tpu_custom_call" | custom-call | bytes 20000 | tf_op jit(solution)/shard_map/pallas_call | solution.py:48
  95.6 2.5 %collective-permute-done.20.refs_1_.refs_4_ = bf16[8,128,128]{2,1,0:T(8,128)(2,1)S(1)} collective-permute-done((bf16[8,128,128]{2,1,0:T(8,128)(2,1)}, bf16[8,128,128]{2,1,0:T(8,128)(2,1)S(1)}, u32[]{:S(2)}, u32[]{:S(2)}) %collective-permute-start.20) | collective-permute-done | bytes 262176 | tf_op jit(solution)/shard_map/ppermute | solution.py:65
  100.5 1.5 %collective-permute-start.24 = (bf16[8,128,128]{2,1,0:T(8,128)(2,1)}, bf16[8,128,128]{2,1,0:T(8,128)(2,1)}, u32[]{:S(2)}, u32[]{:S(2)}) collective-permute-start(bf16[8,128,128]{2,1,0:T(8,128)(2,1)} %get-tuple-element.66.refs_3_), channel_id=1, source_target_pairs={{0,16},{8,24},{16,0},{24,8},{1,17},{9,25},{17,1},{25,9},{2,18},{10... | collective-permute-start | bytes 786440 | tf_op jit(solution)/shard_map/ppermute | solution.py:65
  103.0 3.4 %shard_map.126.refs_0_.refs_2_ = bf16[2,128,256]{2,1,0:T(8,128)(2,1)S(1)} custom-call(bf16[8,128,128]{2,1,0:T(8,128)(2,1)S(1)} %get-tuple-element.68.refs_0_, f32[2,256,512]{2,1,0:T(8,128)S(1)} %shard_map.124.refs_0_.refs_1_, bf16[2,128,256]{2,1,0:T(8,128)(2,1)S(1)} %get-tuple-element.56.refs_4_.refs_2_), custom_call_target="tpu_custom_call" | custom-call | bytes 20000 | tf_op jit(solution)/shard_map/pallas_call | solution.py:48
  108.7 2.0 %collective-permute-start.28 = (bf16[2,128,256]{2,1,0:T(8,128)(2,1)S(1)}, bf16[2,128,256]{2,1,0:T(8,128)(2,1)}, u32[]{:S(2)}, u32[]{:S(2)}) collective-permute-start(bf16[2,128,256]{2,1,0:T(8,128)(2,1)S(1)} %shard_map.126.refs_0_.refs_2_), channel_id=1, source_target_pairs={{0,24},{8,16},{16,8},{24,0},{1,25},{9,17},{17,9},{25,1},{2,26},{10... | collective-permute-start | bytes 393224 | tf_op jit(solution)/shard_map/ppermute | solution.py:65
  112.7 2.7 %shard_map.127 = (f32[4,256,256]{2,1,0:T(8,128)}, f32[4,256,256]{2,1,0:T(8,128)}) custom-call(bf16[2,128,256]{2,1,0:T(8,128)(2,1)S(1)} %shard_map.126.refs_0_.refs_2_, bf16[8,128,128]{2,1,0:T(8,128)(2,1)S(1)} %collective-permute-done.22.refs_1_.refs_6_, bf16[8,128,128]{2,1,0:T(8,128)(2,1)S(1)} %collective-permute-done.23.refs_2_.refs_10_, ...), custom_call_target="tpu_custom_call" | custom-call | bytes 20000 | tf_op jit(solution)/shard_map/pallas_call | solution.py:48
  116.7 2.8 %shard_map.128.refs_0_ = bf16[8,128,1024]{2,1,0:T(8,128)(2,1)} custom-call(f32[4,256,256]{2,1,0:T(8,128)S(1)} %copy-done.8, s32[3]{0:T(128)S(1)} %pad_add_fusion.place.refs_1_.refs_3_, bf16[8,128,1024]{2,1,0:T(8,128)(2,1)S(1)} %copy-done.6, bf16[8,128,128]{2,1,0:T(8,128)(2,1)} %get-tuple-element.66.refs_3_, ...), custom_call_target="tpu_custom_call" | custom-call | bytes 20000 | tf_op jit(solution)/shard_map/pallas_call | solution.py:48
  119.6 1.6 %copy-done.2 = bf16[8,128,1024]{2,1,0:T(8,128)(2,1)S(1)} copy-done((bf16[8,128,1024]{2,1,0:T(8,128)(2,1)S(1)}, bf16[8,128,1024]{2,1,0:T(8,128)(2,1)}, u32[]{:S(2)}) %copy-start.2) | copy-done | bytes 2097176
  121.2 2.0 %shard_map.129 = f32[8,128,256]{2,1,0:T(8,128)} custom-call(bf16[8,128,1024]{2,1,0:T(8,128)(2,1)S(1)} %copy-done.2, s32[3]{0:T(128)S(1)} %pad_add_fusion.place.refs_1_.refs_3_, bf16[2,128,256]{2,1,0:T(8,128)(2,1)S(1)} %shard_map.126.refs_0_.refs_2_, bf16[2,128,256]{2,1,0:T(8,128)(2,1)S(1)} %collective-permute-done.26.refs_3_, ...), custom_call_target="tpu_custom_call" | custom-call | bytes 20000 | tf_op jit(solution)/shard_map/pallas_call | solution.py:48
  (77 shorter events, 24.2 us)
Async XLA Ops:
  7.2 104.2 %all-gather.3.cloned.1.call-start = ((), (), s32[]{:S(2)}) async-start(), calls=%async_computation | async-start | bytes 1179648 | tf_op jit(solution)/shard_map/all_gather | solution.py:515
  12.3 4.6 %collective-permute-start = (bf16[4,2,256,256]{3,2,1,0:T(8,128)(2,1)S(1)}, bf16[4,2,256,256]{3,2,1,0:T(8,128)(2,1)S(1)}, u32[]{:S(2)}, u32[]{:S(2)}) collective-permute-start(bf16[4,2,256,256]{3,2,1,0:T(8,128)(2,1)S(1)} %get-tuple-element.39.refs_0_), channel_id=1, source_target_pairs={{0,1},{1,0},{2,3},{3,2},{4,5},{5,4},{6,7},{7,6},{8,9},{9,8},{10,11... | collective-permute-start | bytes 3145736 | tf_op jit(solution)/shard_map/ppermute | solution.py:65
  12.8 21.4 %collective-permute-start.3 = (bf16[2,10,128,128]{3,2,1,0:T(8,128)(2,1)S(1)}, bf16[2,10,128,128]{3,2,1,0:T(8,128)(2,1)S(1)}, u32[]{:S(2)}, u32[]{:S(2)}) collective-permute-start(bf16[2,10,128,128]{3,2,1,0:T(8,128)(2,1)S(1)} %get-tuple-element.47), channel_id=1, source_target_pairs={{0,8},{8,0},{16,24},{24,16},{1,9},{9,1},{17,25},{25,17},{2,10},{10... | collective-permute-start | bytes 1966088 | tf_op jit(solution)/shard_map/ppermute | solution.py:65
  15.4 18.8 %collective-permute-start.4 = (bf16[2,10,128,128]{3,2,1,0:T(8,128)(2,1)S(1)}, bf16[2,10,128,128]{3,2,1,0:T(8,128)(2,1)S(1)}, u32[]{:S(2)}, u32[]{:S(2)}) collective-permute-start(bf16[2,10,128,128]{3,2,1,0:T(8,128)(2,1)S(1)} %get-tuple-element.38.refs_0_), channel_id=1, source_target_pairs={{0,16},{8,24},{16,0},{24,8},{1,17},{9,25},{17,1},{25,9},{2,18},{10... | collective-permute-start | bytes 1966088 | tf_op jit(solution)/shard_map/ppermute | solution.py:65
  16.9 17.3 %copy-start.1 = (bf16[1,8,128,1024]{3,2,1,0:T(8,128)(2,1)S(1)}, bf16[1,8,128,1024]{3,2,1,0:T(8,128)(2,1)}, u32[]{:S(2)}) copy-start(bf16[1,8,128,1024]{3,2,1,0:T(8,128)(2,1)} %refs_2_.9) | copy-start | bytes 6291460
  17.6 13.7 %collective-permute-start.1 = (bf16[2,256,256]{2,1,0:T(8,128)(2,1)S(1)}, bf16[2,256,256]{2,1,0:T(8,128)(2,1)S(1)}, u32[]{:S(2)}, u32[]{:S(2)}) collective-permute-start(bf16[2,256,256]{2,1,0:T(8,128)(2,1)S(1)} %get-tuple-element.43), channel_id=1, source_target_pairs={{0,2},{1,3},{2,0},{3,1},{4,6},{5,7},{6,4},{7,5},{8,10},{9,11},{10,... | collective-permute-start | bytes 786440 | tf_op jit(solution)/shard_map/ppermute | solution.py:65
  19.2 14.4 %collective-permute-start.2 = (bf16[2,256,256]{2,1,0:T(8,128)(2,1)S(1)}, bf16[2,256,256]{2,1,0:T(8,128)(2,1)S(1)}, u32[]{:S(2)}, u32[]{:S(2)}) collective-permute-start(bf16[2,256,256]{2,1,0:T(8,128)(2,1)S(1)} %get-tuple-element.41.refs_0_), channel_id=1, source_target_pairs={{0,4},{1,5},{2,6},{3,7},{4,0},{5,1},{6,2},{7,3},{8,12},{9,13},{10,... | collective-permute-start | bytes 786440 | tf_op jit(solution)/shard_map/ppermute | solution.py:65
  35.1 10.2 %collective-permute-start.7 = (bf16[10,128,128]{2,1,0:T(8,128)(2,1)S(1)}, bf16[10,128,128]{2,1,0:T(8,128)(2,1)S(1)}, u32[]{:S(2)}, u32[]{:S(2)}) collective-permute-start(bf16[10,128,128]{2,1,0:T(8,128)(2,1)S(1)} %get-tuple-element.52), channel_id=1, source_target_pairs={{0,16},{8,24},{16,0},{24,8},{1,17},{9,25},{17,1},{25,9},{2,18},{10... | collective-permute-start | bytes 983048 | tf_op jit(solution)/shard_map/ppermute | solution.py:65
  36.5 8.8 %collective-permute-start.8 = (bf16[10,128,128]{2,1,0:T(8,128)(2,1)S(1)}, bf16[10,128,128]{2,1,0:T(8,128)(2,1)S(1)}, u32[]{:S(2)}, u32[]{:S(2)}) collective-permute-start(bf16[10,128,128]{2,1,0:T(8,128)(2,1)S(1)} %get-tuple-element.48.refs_0_), channel_id=1, source_target_pairs={{0,8},{8,0},{16,24},{24,16},{1,9},{9,1},{17,25},{25,17},{2,10},{10... | collective-permute-start | bytes 983048 | tf_op jit(solution)/shard_map/ppermute | solution.py:65
  38.0 7.3 %collective-permute-start.5 = (bf16[1,256,256]{2,1,0:T(8,128)(2,1)S(1)}, bf16[1,256,256]{2,1,0:T(8,128)(2,1)S(1)}, u32[]{:S(2)}, u32[]{:S(2)}) collective-permute-start(bf16[1,256,256]{2,1,0:T(8,128)(2,1)S(1)} %get-tuple-element.49), channel_id=1, source_target_pairs={{0,4},{1,5},{2,6},{3,7},{4,0},{5,1},{6,2},{7,3},{8,12},{9,13},{10,... | collective-permute-start | bytes 393224 | tf_op jit(solution)/shard_map/ppermute | solution.py:65
  38.4 7.0 %collective-permute-start.6 = (bf16[1,256,256]{2,1,0:T(8,128)(2,1)S(1)}, bf16[1,256,256]{2,1,0:T(8,128)(2,1)S(1)}, u32[]{:S(2)}, u32[]{:S(2)}) collective-permute-start(bf16[1,256,256]{2,1,0:T(8,128)(2,1)S(1)} %get-tuple-element.45.refs_0_), channel_id=1, source_target_pairs={{0,2},{1,3},{2,0},{3,1},{4,6},{5,7},{6,4},{7,5},{8,10},{9,11},{10,... | collective-permute-start | bytes 393224 | tf_op jit(solution)/shard_map/ppermute | solution.py:65
  47.1 22.0 %copy-start.13 = (s32[8]{0:T(128)S(1)}, s32[8]{0:T(128)}, u32[]{:S(2)}) copy-start(s32[8]{0:T(128)} %refs_3_.3) | copy-start | bytes 100
  47.1 2.0 %collective-permute-start.9 = (bf16[4,256,256]{2,1,0:T(8,128)(2,1)S(1)}, bf16[4,256,256]{2,1,0:T(8,128)(2,1)S(1)}, u32[]{:S(2)}, u32[]{:S(2)}) collective-permute-start(bf16[4,256,256]{2,1,0:T(8,128)(2,1)S(1)} %get-tuple-element.54.refs_0_), channel_id=1, source_target_pairs={{0,1},{1,0},{2,3},{3,2},{4,5},{5,4},{6,7},{7,6},{8,9},{9,8},{10,11... | collective-permute-start | bytes 1572872 | tf_op jit(solution)/shard_map/ppermute | solution.py:65
  49.8 19.3 %collective-permute-start.10 = (bf16[512,256]{1,0:T(8,128)(2,1)S(1)}, bf16[512,256]{1,0:T(8,128)(2,1)S(1)}, u32[]{:S(2)}, u32[]{:S(2)}) collective-permute-start(bf16[512,256]{1,0:T(8,128)(2,1)S(1)} %get-tuple-element.59), channel_id=1, source_target_pairs={{0,2},{1,3},{2,0},{3,1},{4,6},{5,7},{6,4},{7,5},{8,10},{9,11},{10,... | collective-permute-start | bytes 786440 | tf_op jit(solution)/shard_map/ppermute | solution.py:65
  50.5 9.5 %collective-permute-start.13 = (bf16[2,128,256]{2,1,0:T(8,128)(2,1)S(1)}, bf16[2,128,256]{2,1,0:T(8,128)(2,1)S(1)}, u32[]{:S(2)}, u32[]{:S(2)}) collective-permute-start(bf16[2,128,256]{2,1,0:T(8,128)(2,1)S(1)} %get-tuple-element.56.refs_4_.refs_2_), channel_id=1, source_target_pairs={{0,4},{1,5},{2,6},{3,7},{4,0},{5,1},{6,2},{7,3},{8,12},{9,13},{10,... | collective-permute-start | bytes 393224 | tf_op jit(solution)/shard_map/ppermute | solution.py:65
  52.5 16.6 %collective-permute-start.11 = (bf16[256,256]{1,0:T(8,128)(2,1)S(1)}, bf16[256,256]{1,0:T(8,128)(2,1)S(1)}, u32[]{:S(2)}, u32[]{:S(2)}) collective-permute-start(bf16[256,256]{1,0:T(8,128)(2,1)S(1)} %get-tuple-element.60), channel_id=1, source_target_pairs={{0,4},{1,5},{2,6},{3,7},{4,0},{5,1},{6,2},{7,3},{8,12},{9,13},{10,... | collective-permute-start | bytes 393224 | tf_op jit(solution)/shard_map/ppermute | solution.py:65
  53.5 15.6 %collective-permute-start.12 = (bf16[256,256]{1,0:T(8,128)(2,1)S(1)}, bf16[256,256]{1,0:T(8,128)(2,1)S(1)}, u32[]{:S(2)}, u32[]{:S(2)}) collective-permute-start(bf16[256,256]{1,0:T(8,128)(2,1)S(1)} %get-tuple-element.57.refs_0_), channel_id=1, source_target_pairs={{0,6},{1,7},{2,4},{3,5},{4,2},{5,3},{6,0},{7,1},{8,14},{9,15},{10,... | collective-permute-start | bytes 393224 | tf_op jit(solution)/shard_map/ppermute | solution.py:65
  60.0 9.9 %collective-permute-start.14 = (bf16[2,128,256]{2,1,0:T(8,128)(2,1)S(1)}, bf16[2,128,256]{2,1,0:T(8,128)(2,1)S(1)}, u32[]{:S(2)}, u32[]{:S(2)}) collective-permute-start(bf16[2,128,256]{2,1,0:T(8,128)(2,1)S(1)} %collective-permute-done.13.refs_3_), channel_id=1, source_target_pairs={{0,2},{1,3},{2,0},{3,1},{4,6},{5,7},{6,4},{7,5},{8,10},{9,11},{10,... | collective-permute-start | bytes 393224 | tf_op jit(solution)/shard_map/ppermute | solution.py:65
  70.4 4.9 %collective-permute-start.15 = (f32[2,256,256]{2,1,0:T(8,128)S(1)}, f32[2,256,256]{2,1,0:T(8,128)S(1)}, u32[]{:S(2)}, u32[]{:S(2)}) collective-permute-start(f32[2,256,256]{2,1,0:T(8,128)S(1)} %shard_map.119.refs_0_.refs_1_), channel_id=1, source_target_pairs={{0,1},{1,0},{2,3},{3,2},{4,5},{5,4},{6,7},{7,6},{8,9},{9,8},{10,11... | collective-permute-start | bytes 1572872 | tf_op jit(solution)/shard_map/ppermute | solution.py:65
  70.5 13.8 %collective-permute-start.16 = (bf16[256,256]{1,0:T(8,128)(2,1)S(1)}, bf16[256,256]{1,0:T(8,128)(2,1)S(1)}, u32[]{:S(2)}, u32[]{:S(2)}) collective-permute-start(bf16[256,256]{1,0:T(8,128)(2,1)S(1)} %get-tuple-element.64.refs_1_), channel_id=1, source_target_pairs={{0,2},{1,3},{2,0},{3,1},{4,6},{5,7},{6,4},{7,5},{8,10},{9,11},{10,... | collective-permute-start | bytes 393224 | tf_op jit(solution)/shard_map/ppermute | solution.py:65
  72.8 12.9 %collective-permute-start.17 = (bf16[256,256]{1,0:T(8,128)(2,1)S(1)}, bf16[256,256]{1,0:T(8,128)(2,1)S(1)}, u32[]{:S(2)}, u32[]{:S(2)}) collective-permute-start(bf16[256,256]{1,0:T(8,128)(2,1)S(1)} %get-tuple-element.64.refs_1_), channel_id=1, source_target_pairs={{0,4},{1,5},{2,6},{3,7},{4,0},{5,1},{6,2},{7,3},{8,12},{9,13},{10,... | collective-permute-start | bytes 393224 | tf_op jit(solution)/shard_map/ppermute | solution.py:65
  73.2 12.5 %collective-permute-start.18 = (bf16[256,256]{1,0:T(8,128)(2,1)S(1)}, bf16[256,256]{1,0:T(8,128)(2,1)S(1)}, u32[]{:S(2)}, u32[]{:S(2)}) collective-permute-start(bf16[256,256]{1,0:T(8,128)(2,1)S(1)} %get-tuple-element.64.refs_1_), channel_id=1, source_target_pairs={{0,6},{1,7},{2,4},{3,5},{4,2},{5,3},{6,0},{7,1},{8,14},{9,15},{10,... | collective-permute-start | bytes 393224 | tf_op jit(solution)/shard_map/ppermute | solution.py:65
  85.8 2.0 %collective-permute-start.19 = (bf16[4,256,256]{2,1,0:T(8,128)(2,1)S(1)}, bf16[4,256,256]{2,1,0:T(8,128)(2,1)S(1)}, u32[]{:S(2)}, u32[]{:S(2)}) collective-permute-start(bf16[4,256,256]{2,1,0:T(8,128)(2,1)S(1)} %shard_map.122.refs_0_.refs_2_), channel_id=1, source_target_pairs={{0,1},{1,0},{2,3},{3,2},{4,5},{5,4},{6,7},{7,6},{8,9},{9,8},{10,11... | collective-permute-start | bytes 1572872 | tf_op jit(solution)/shard_map/ppermute | solution.py:65
  89.5 8.6 %collective-permute-start.20 = (bf16[8,128,128]{2,1,0:T(8,128)(2,1)}, bf16[8,128,128]{2,1,0:T(8,128)(2,1)S(1)}, u32[]{:S(2)}, u32[]{:S(2)}) collective-permute-start(bf16[8,128,128]{2,1,0:T(8,128)(2,1)} %get-tuple-element.66.refs_3_), channel_id=1, source_target_pairs={{0,8},{8,0},{16,24},{24,16},{1,9},{9,1},{17,25},{25,17},{2,10},{10... | collective-permute-start | bytes 786440 | tf_op jit(solution)/shard_map/ppermute | solution.py:65
  90.5 8.3 %collective-permute-start.21 = (bf16[8,128,128]{2,1,0:T(8,128)(2,1)}, bf16[8,128,128]{2,1,0:T(8,128)(2,1)S(1)}, u32[]{:S(2)}, u32[]{:S(2)}) collective-permute-start(bf16[8,128,128]{2,1,0:T(8,128)(2,1)} %get-tuple-element.67.refs_7_), channel_id=1, source_target_pairs={{0,16},{8,24},{16,0},{24,8},{1,17},{9,25},{17,1},{25,9},{2,18},{10... | collective-permute-start | bytes 786440 | tf_op jit(solution)/shard_map/ppermute | solution.py:65
  98.8 9.3 %collective-permute-start.22 = (bf16[8,128,128]{2,1,0:T(8,128)(2,1)S(1)}, bf16[8,128,128]{2,1,0:T(8,128)(2,1)S(1)}, u32[]{:S(2)}, u32[]{:S(2)}) collective-permute-start(bf16[8,128,128]{2,1,0:T(8,128)(2,1)S(1)} %get-tuple-element.69), channel_id=1, source_target_pairs={{0,16},{8,24},{16,0},{24,8},{1,17},{9,25},{17,1},{25,9},{2,18},{10... | collective-permute-start | bytes 786440 | tf_op jit(solution)/shard_map/ppermute | solution.py:65
  99.4 9.2 %collective-permute-start.23 = (bf16[8,128,128]{2,1,0:T(8,128)(2,1)S(1)}, bf16[8,128,128]{2,1,0:T(8,128)(2,1)S(1)}, u32[]{:S(2)}, u32[]{:S(2)}) collective-permute-start(bf16[8,128,128]{2,1,0:T(8,128)(2,1)S(1)} %get-tuple-element.68.refs_0_), channel_id=1, source_target_pairs={{0,8},{8,0},{16,24},{24,16},{1,9},{9,1},{17,25},{25,17},{2,10},{10... | collective-permute-start | bytes 786440 | tf_op jit(solution)/shard_map/ppermute | solution.py:65
  100.5 15.0 %collective-permute-start.24 = (bf16[8,128,128]{2,1,0:T(8,128)(2,1)}, bf16[8,128,128]{2,1,0:T(8,128)(2,1)}, u32[]{:S(2)}, u32[]{:S(2)}) collective-permute-start(bf16[8,128,128]{2,1,0:T(8,128)(2,1)} %get-tuple-element.66.refs_3_), channel_id=1, source_target_pairs={{0,16},{8,24},{16,0},{24,8},{1,17},{9,25},{17,1},{25,9},{2,18},{10... | collective-permute-start | bytes 786440 | tf_op jit(solution)/shard_map/ppermute | solution.py:65
  102.0 13.5 %collective-permute-start.25 = (bf16[8,128,128]{2,1,0:T(8,128)(2,1)}, bf16[8,128,128]{2,1,0:T(8,128)(2,1)}, u32[]{:S(2)}, u32[]{:S(2)}) collective-permute-start(bf16[8,128,128]{2,1,0:T(8,128)(2,1)} %get-tuple-element.67.refs_7_), channel_id=1, source_target_pairs={{0,8},{8,0},{16,24},{24,16},{1,9},{9,1},{17,25},{25,17},{2,10},{10... | collective-permute-start | bytes 786440 | tf_op jit(solution)/shard_map/ppermute | solution.py:65
  106.4 13.2 %collective-permute-start.26 = (bf16[2,128,256]{2,1,0:T(8,128)(2,1)S(1)}, bf16[2,128,256]{2,1,0:T(8,128)(2,1)S(1)}, u32[]{:S(2)}, u32[]{:S(2)}) collective-permute-start(bf16[2,128,256]{2,1,0:T(8,128)(2,1)S(1)} %shard_map.126.refs_0_.refs_2_), channel_id=1, source_target_pairs={{0,8},{8,0},{16,24},{24,16},{1,9},{9,1},{17,25},{25,17},{2,10},{10... | collective-permute-start | bytes 393224 | tf_op jit(solution)/shard_map/ppermute | solution.py:65
  108.2 11.4 %collective-permute-start.27 = (bf16[2,128,256]{2,1,0:T(8,128)(2,1)S(1)}, bf16[2,128,256]{2,1,0:T(8,128)(2,1)S(1)}, u32[]{:S(2)}, u32[]{:S(2)}) collective-permute-start(bf16[2,128,256]{2,1,0:T(8,128)(2,1)S(1)} %shard_map.126.refs_0_.refs_2_), channel_id=1, source_target_pairs={{0,16},{8,24},{16,0},{24,8},{1,17},{9,25},{17,1},{25,9},{2,18},{10... | collective-permute-start | bytes 393224 | tf_op jit(solution)/shard_map/ppermute | solution.py:65
  108.7 10.9 %collective-permute-start.28 = (bf16[2,128,256]{2,1,0:T(8,128)(2,1)S(1)}, bf16[2,128,256]{2,1,0:T(8,128)(2,1)}, u32[]{:S(2)}, u32[]{:S(2)}) collective-permute-start(bf16[2,128,256]{2,1,0:T(8,128)(2,1)S(1)} %shard_map.126.refs_0_.refs_2_), channel_id=1, source_target_pairs={{0,24},{8,16},{16,8},{24,0},{1,25},{9,17},{17,9},{25,1},{2,26},{10... | collective-permute-start | bytes 393224 | tf_op jit(solution)/shard_map/ppermute | solution.py:65
  (12 other events, 39.1 us)
Sparse Core Ops, SparseCore 0:
  89.6 21.7 all-gather.2

commit v11 on v10

--- a/solution.py
+++ b/solution.py
@@ -30,10 +30,11 @@
     def __init__(self):
         self.last = None
 
-    def __call__(self, kernel, out_shape, args, scalars=0, us=2.0, scratch=(), after=(), hbm=0, direct=False):
+    def __call__(self, kernel, out_shape, args, scalars=0, us=2.0, scratch=(), after=(), hbm=0, direct=0):
         many = isinstance(out_shape, (tuple, list))
         specs = [SMEM] * scalars + [HBM] * hbm + [VMEM] * (len(args) - scalars - hbm)
-        place_out = HBM if direct else VMEM
+        outs = len(out_shape) if many else 1
+        out_specs = [HBM] * direct + [VMEM] * (outs - direct)
         body = kernel
         if self.last is not None:
             after = (self.last, *after)
@@ -49,14 +50,14 @@
             body,
             out_shape=out_shape,
             in_specs=specs,
-            out_specs=[place_out] * len(out_shape) if many else place_out,
+            out_specs=out_specs if many else out_specs[0],
             scratch_shapes=list(scratch),
             compiler_params=pltpu.CompilerParams(vmem_limit_bytes=VMEM_LIMIT),
             cost_estimate=pl.CostEstimate(
                 flops=0, bytes_accessed=int(us * COST), transcendentals=0
             ),
         )(*args)
-        self.last = result[-1] if many else result
+        self.last = min(result, key=lambda x: x.size) if many else result
         return result
 
 
@@ -335,7 +336,8 @@
 
 
 def weight_kernel(place, weight_ref, *refs, groups, chunks):
-    *deltas, out_hbm, out_ref, sems = refs
+    *deltas, out_hbm, done_ref, out_ref, sems = refs
+    done_ref[...] = jnp.zeros(done_ref.shape, f32)
     width = deltas[0].shape[2]
     copies = []
     for m in range(out_ref.shape[0]):
@@ -361,7 +363,8 @@
 
 
 def moment_kernel(place, owner, projected_hbm, first_ref, second_ref, *refs):
-    first_hbm, second_hbm, projected_ref, first_out, second_out, sems = refs
+    first_hbm, second_hbm, done_ref, projected_ref, first_out, second_out, sems = refs
+    done_ref[...] = jnp.zeros(done_ref.shape, f32)
     here = place[1] * 2 + place[2]
     capacity = first_out.shape[0]
     seen = jnp.int32(0)
@@ -525,14 +528,14 @@
         scratch=[pltpu.VMEM(work_shape.shape, f32)],
     )
     shared = [rows_basis] + [swap(rows_basis, "dp", k) for k in range(1, groups)]
-    first_out, second_out = call(
+    first_out, second_out, _ = call(
         moment_kernel,
-        [struct(first_moment.shape, f32)] * 2,
+        [struct(first_moment.shape, f32)] * 2 + [struct((8, 128), f32)],
         (place, owner, gathered, first_moment, second_moment),
         scalars=2,
         after=tuple(across),
         hbm=1,
-        direct=True,
+        direct=2,
         scratch=[
             pltpu.VMEM(first_moment.shape, bf16),
             pltpu.VMEM(first_moment.shape, f32),
@@ -540,12 +543,12 @@
             pltpu.SemaphoreType.DMA((3, capacity)),
         ],
     )
-    new_weight = call(
+    new_weight, _ = call(
         functools.partial(weight_kernel, groups=groups, chunks=2),
-        struct(weight.shape, bf16),
+        [struct(weight.shape, bf16), struct((8, 128), f32)],
         (place, weight, *deltas),
         scalars=1,
-        direct=True,
+        direct=1,
         scratch=[pltpu.VMEM(weight.shape, bf16), pltpu.SemaphoreType.DMA((count,))],
     )
     new_basis = call(basis_kernel, struct(basis.shape, f32), (place, *shared), scalars=1)

time: 130 us -> 128 us (0.985)
  local copies, waits for them, and re-layouts: 6.85 us -> 4.05 us
    unnamed x28 -> x24, local copies, waits for them, and re-layouts: 6.85 us -> 4.05 us
  transfers between devices with their start and end apart: 30 -> 30, of which waited for: 12 -> 13; matrix products, arithmetic and copies ran while one was open for 0% -> 0% of each run, Pallas kernels for 19% -> 19%
where the time goes in v11:
time: 128 us; the launch traced here: 127 us
  waiting for transfers between devices  37.5 us (29%)
  starting transfers between devices  37.2 us (29%)
  Pallas kernels  34.3 us (27%)
  between operations  14.3 us (11%)
  local copies, waits for them, and re-layouts  4.05 us (3%)
    ppermute x29, starting transfers between devices, swap(): return lax.ppermute(x, axis, [(i, i ^ mask) for i in range(size)])  37.2 us
    ppermute x29, waiting for transfers between devices, swap(): return lax.ppermute(x, axis, [(i, i ^ mask) for i in range(size)])  36.8 us
    pallas_call x19, Pallas kernels, __call__(): pl.pallas_call(body, out_shape=out_shape, in_specs=specs, out_specs=out_s...  34.3 us
    unnamed x24, local copies, waits for them, and re-layouts  4.05 us
  transfers between devices with their start and end apart: 30, of which 13 were waited for; matrix products, arithmetic and copies ran while one was open for 0% of the time, Pallas kernels for 19%

profile of v11, /device:TPU:0, one launch (start us, length us, event | category | flops | bytes accessed | tf_op | source)
XLA Modules:
  0.0 127.4 jit_solution(5811128292177606768)
XLA Ops:
  7.3 1.6 %copy-done = bf16[1,8,128,1024]{3,2,1,0:T(8,128)(2,1)S(1)} copy-done((bf16[1,8,128,1024]{3,2,1,0:T(8,128)(2,1)S(1)}, bf16[1,8,128,1024]{3,2,1,0:T(8,128)(2,1)}, u32[]{:S(2)}) %copy-start) | copy-done | bytes 2097176
  10.0 1.5 %shard_map.111 = (f32[2,128,256]{2,1,0:T(8,128)S(1)}, f32[2,2,128,128]{3,2,1,0:T(8,128)S(1)}, bf16[2,10,128,128]{3,2,1,0:T(8,128)(2,1)S(1)}, bf16[2,10,128,128]{3,2,1,0:T(8,128)(2,1)S(1)}) custom-call(s32[3]{0:T(128)S(1)} %pad_add_fusion.place.refs_1_.refs_3_, bf16[1,8,128,1024]{3,2,1,0:T(8,128)(2,1)S(1)} %copy-done, bf16[1024,256]{1,0:T(8,128)(2,1)S(1)} %copy-done.9), custom_call_target="tpu_custom_call" | custom-call | bytes 20000 | tf_op jit(solution)/shard_map/pallas_call | solution.py:49
  12.8 2.6 %collective-permute-start.3 = (bf16[2,10,128,128]{3,2,1,0:T(8,128)(2,1)S(1)}, bf16[2,10,128,128]{3,2,1,0:T(8,128)(2,1)S(1)}, u32[]{:S(2)}, u32[]{:S(2)}) collective-permute-start(bf16[2,10,128,128]{3,2,1,0:T(8,128)(2,1)S(1)} %get-tuple-element.50), channel_id=1, source_target_pairs={{0,8},{8,0},{16,24},{24,16},{1,9},{9,1},{17,25},{25,17},{2,10},{10... | collective-permute-start | bytes 1966088 | tf_op jit(solution)/shard_map/ppermute | solution.py:66
  15.4 1.5 %collective-permute-start.4 = (bf16[2,10,128,128]{3,2,1,0:T(8,128)(2,1)S(1)}, bf16[2,10,128,128]{3,2,1,0:T(8,128)(2,1)S(1)}, u32[]{:S(2)}, u32[]{:S(2)}) collective-permute-start(bf16[2,10,128,128]{3,2,1,0:T(8,128)(2,1)S(1)} %get-tuple-element.51), channel_id=1, source_target_pairs={{0,16},{8,24},{16,0},{24,8},{1,17},{9,25},{17,1},{25,9},{2,18},{10... | collective-permute-start | bytes 1966088 | tf_op jit(solution)/shard_map/ppermute | solution.py:66
  17.6 1.6 %collective-permute-start.1 = (bf16[2,256,256]{2,1,0:T(8,128)(2,1)S(1)}, bf16[2,256,256]{2,1,0:T(8,128)(2,1)S(1)}, u32[]{:S(2)}, u32[]{:S(2)}) collective-permute-start(bf16[2,256,256]{2,1,0:T(8,128)(2,1)S(1)} %get-tuple-element.45), channel_id=1, source_target_pairs={{0,2},{1,3},{2,0},{3,1},{4,6},{5,7},{6,4},{7,5},{8,10},{9,11},{10,... | collective-permute-start | bytes 786440 | tf_op jit(solution)/shard_map/ppermute | solution.py:66
  19.2 2.6 %collective-permute-start.2 = (bf16[2,256,256]{2,1,0:T(8,128)(2,1)S(1)}, bf16[2,256,256]{2,1,0:T(8,128)(2,1)S(1)}, u32[]{:S(2)}, u32[]{:S(2)}) collective-permute-start(bf16[2,256,256]{2,1,0:T(8,128)(2,1)S(1)} %get-tuple-element.47), channel_id=1, source_target_pairs={{0,4},{1,5},{2,6},{3,7},{4,0},{5,1},{6,2},{7,3},{8,12},{9,13},{10,... | collective-permute-start | bytes 786440 | tf_op jit(solution)/shard_map/ppermute | solution.py:66
  21.8 9.4 %collective-permute-done.1.refs_4_ = bf16[2,256,256]{2,1,0:T(8,128)(2,1)S(1)} collective-permute-done((bf16[2,256,256]{2,1,0:T(8,128)(2,1)S(1)}, bf16[2,256,256]{2,1,0:T(8,128)(2,1)S(1)}, u32[]{:S(2)}, u32[]{:S(2)}) %collective-permute-start.1) | collective-permute-done | bytes 262176 | tf_op jit(solution)/shard_map/ppermute | solution.py:66
  31.3 2.3 %collective-permute-done.2.refs_6_ = bf16[2,256,256]{2,1,0:T(8,128)(2,1)S(1)} collective-permute-done((bf16[2,256,256]{2,1,0:T(8,128)(2,1)S(1)}, bf16[2,256,256]{2,1,0:T(8,128)(2,1)S(1)}, u32[]{:S(2)}, u32[]{:S(2)}) %collective-permute-start.2) | collective-permute-done | bytes 262176 | tf_op jit(solution)/shard_map/ppermute | solution.py:66
  36.5 1.5 %collective-permute-start.8 = (bf16[10,128,128]{2,1,0:T(8,128)(2,1)S(1)}, bf16[10,128,128]{2,1,0:T(8,128)(2,1)S(1)}, u32[]{:S(2)}, u32[]{:S(2)}) collective-permute-start(bf16[10,128,128]{2,1,0:T(8,128)(2,1)S(1)} %get-tuple-element.57), channel_id=1, source_target_pairs={{0,8},{8,0},{16,24},{24,16},{1,9},{9,1},{17,25},{25,17},{2,10},{10... | collective-permute-start | bytes 983048 | tf_op jit(solution)/shard_map/ppermute | solution.py:66
  38.4 2.7 %collective-permute-start.6 = (bf16[1,256,256]{2,1,0:T(8,128)(2,1)S(1)}, bf16[1,256,256]{2,1,0:T(8,128)(2,1)S(1)}, u32[]{:S(2)}, u32[]{:S(2)}) collective-permute-start(bf16[1,256,256]{2,1,0:T(8,128)(2,1)S(1)} %get-tuple-element.54), channel_id=1, source_target_pairs={{0,2},{1,3},{2,0},{3,1},{4,6},{5,7},{6,4},{7,5},{8,10},{9,11},{10,... | collective-permute-start | bytes 393224 | tf_op jit(solution)/shard_map/ppermute | solution.py:66
  41.1 4.3 %collective-permute-done.5.refs_1_.refs_9_ = bf16[1,256,256]{2,1,0:T(8,128)(2,1)S(1)} collective-permute-done((bf16[1,256,256]{2,1,0:T(8,128)(2,1)S(1)}, bf16[1,256,256]{2,1,0:T(8,128)(2,1)S(1)}, u32[]{:S(2)}, u32[]{:S(2)}) %collective-permute-start.5) | collective-permute-done | bytes 131104 | tf_op jit(solution)/shard_map/ppermute | solution.py:66
  45.4 1.7 %shard_map.116 = (f32[4,256,256]{2,1,0:T(8,128)S(1)}, bf16[2,128,256]{2,1,0:T(8,128)(2,1)S(1)}, bf16[4,256,256]{2,1,0:T(8,128)(2,1)S(1)}) custom-call(f32[8,128,128]{2,1,0:T(8,128)S(1)} %get-tuple-element.52.refs_0_.refs_4_, bf16[1,256,256]{2,1,0:T(8,128)(2,1)S(1)} %collective-permute-done.5.refs_1_.refs_9_, ...), custom_call_target="tpu_custom_call" | custom-call | bytes 20000 | tf_op jit(solution)/shard_map/pallas_call | solution.py:49
  47.2 1.9 %collective-permute-done.9.refs_3_ = bf16[4,256,256]{2,1,0:T(8,128)(2,1)S(1)} collective-permute-done((bf16[4,256,256]{2,1,0:T(8,128)(2,1)S(1)}, bf16[4,256,256]{2,1,0:T(8,128)(2,1)S(1)}, u32[]{:S(2)}, u32[]{:S(2)}) %collective-permute-start.9) | collective-permute-done | bytes 524320 | tf_op jit(solution)/shard_map/ppermute | solution.py:66
  50.5 2.0 %collective-permute-start.13 = (bf16[2,128,256]{2,1,0:T(8,128)(2,1)S(1)}, bf16[2,128,256]{2,1,0:T(8,128)(2,1)S(1)}, u32[]{:S(2)}, u32[]{:S(2)}) collective-permute-start(bf16[2,128,256]{2,1,0:T(8,128)(2,1)S(1)} %get-tuple-element.58.refs_0_.refs_4_.refs_2_), channel_id=1, source_target_pairs={{0,4},{1,5},{2,6},{3,7},{4,0},{5,1},{6,2},{7,3},{8,12},{9,13},{10,... | collective-permute-start | bytes 393224 | tf_op jit(solution)/shard_map/ppermute | solution.py:66
  53.4 1.7 %collective-permute-start.12 = (bf16[256,256]{1,0:T(8,128)(2,1)S(1)}, bf16[256,256]{1,0:T(8,128)(2,1)S(1)}, u32[]{:S(2)}, u32[]{:S(2)}) collective-permute-start(bf16[256,256]{1,0:T(8,128)(2,1)S(1)} %get-tuple-element.64), channel_id=1, source_target_pairs={{0,6},{1,7},{2,4},{3,5},{4,2},{5,3},{6,0},{7,1},{8,14},{9,15},{10,... | collective-permute-start | bytes 393224 | tf_op jit(solution)/shard_map/ppermute | solution.py:66
  55.1 4.9 %collective-permute-done.13.refs_3_ = bf16[2,128,256]{2,1,0:T(8,128)(2,1)S(1)} collective-permute-done((bf16[2,128,256]{2,1,0:T(8,128)(2,1)S(1)}, bf16[2,128,256]{2,1,0:T(8,128)(2,1)S(1)}, u32[]{:S(2)}, u32[]{:S(2)}) %collective-permute-start.13) | collective-permute-done | bytes 131104 | tf_op jit(solution)/shard_map/ppermute | solution.py:66
  60.0 2.8 %collective-permute-start.14 = (bf16[2,128,256]{2,1,0:T(8,128)(2,1)S(1)}, bf16[2,128,256]{2,1,0:T(8,128)(2,1)S(1)}, u32[]{:S(2)}, u32[]{:S(2)}) collective-permute-start(bf16[2,128,256]{2,1,0:T(8,128)(2,1)S(1)} %collective-permute-done.13.refs_3_), channel_id=1, source_target_pairs={{0,2},{1,3},{2,0},{3,1},{4,6},{5,7},{6,4},{7,5},{8,10},{9,11},{10,... | collective-permute-start | bytes 393224 | tf_op jit(solution)/shard_map/ppermute | solution.py:66
  62.8 6.3 %collective-permute-done.11.refs_6_ = bf16[256,256]{1,0:T(8,128)(2,1)S(1)} collective-permute-done((bf16[256,256]{1,0:T(8,128)(2,1)S(1)}, bf16[256,256]{1,0:T(8,128)(2,1)S(1)}, u32[]{:S(2)}, u32[]{:S(2)}) %collective-permute-start.11) | collective-permute-done | bytes 131104 | tf_op jit(solution)/shard_map/ppermute | solution.py:66
  70.5 2.4 %collective-permute-start.16 = (bf16[256,256]{1,0:T(8,128)(2,1)S(1)}, bf16[256,256]{1,0:T(8,128)(2,1)S(1)}, u32[]{:S(2)}, u32[]{:S(2)}) collective-permute-start(bf16[256,256]{1,0:T(8,128)(2,1)S(1)} %get-tuple-element.66.refs_0_.refs_1_), channel_id=1, source_target_pairs={{0,2},{1,3},{2,0},{3,1},{4,6},{5,7},{6,4},{7,5},{8,10},{9,11},{10,... | collective-permute-start | bytes 393224 | tf_op jit(solution)/shard_map/ppermute | solution.py:66
  73.2 2.1 %collective-permute-start.18 = (bf16[256,256]{1,0:T(8,128)(2,1)S(1)}, bf16[256,256]{1,0:T(8,128)(2,1)S(1)}, u32[]{:S(2)}, u32[]{:S(2)}) collective-permute-start(bf16[256,256]{1,0:T(8,128)(2,1)S(1)} %get-tuple-element.66.refs_0_.refs_1_), channel_id=1, source_target_pairs={{0,6},{1,7},{2,4},{3,5},{4,2},{5,3},{6,0},{7,1},{8,14},{9,15},{10,... | collective-permute-start | bytes 393224 | tf_op jit(solution)/shard_map/ppermute | solution.py:66
  75.3 4.4 %shard_map.120.refs_0_.refs_1_ = f32[2,256,512]{2,1,0:T(8,128)S(1)} custom-call(f32[2,256,256]{2,1,0:T(8,128)S(1)} %shard_map.119.refs_0_.refs_1_, f32[2,256,256]{2,1,0:T(8,128)S(1)} %shard_map.119.refs_0_.refs_1_, f32[2,256,256]{2,1,0:T(8,128)S(1)} %collective-permute-done.15.refs_2_), custom_call_target="tpu_custom_call" | custom-call | bytes 20000 | tf_op jit(solution)/shard_map/pallas_call | solution.py:49
  79.7 4.6 %shard_map.121.refs_0_.refs_1_ = f32[2,256,512]{2,1,0:T(8,128)S(1)} custom-call(f32[2,256,512]{2,1,0:T(8,128)S(1)} %shard_map.120.refs_0_.refs_1_, f32[2,256,512]{2,1,0:T(8,128)S(1)} %shard_map.120.refs_0_.refs_1_), custom_call_target="tpu_custom_call" | custom-call | bytes 20000 | tf_op jit(solution)/shard_map/pallas_call | solution.py:49
  85.9 1.9 %collective-permute-done.19.refs_3_ = bf16[4,256,256]{2,1,0:T(8,128)(2,1)S(1)} collective-permute-done((bf16[4,256,256]{2,1,0:T(8,128)(2,1)S(1)}, bf16[4,256,256]{2,1,0:T(8,128)(2,1)S(1)}, u32[]{:S(2)}, u32[]{:S(2)}) %collective-permute-start.19) | collective-permute-done | bytes 524320 | tf_op jit(solution)/shard_map/ppermute | solution.py:66
  87.8 1.7 %shard_map.123 = (bf16[8,128,128]{2,1,0:T(8,128)(2,1)}, bf16[8,128,128]{2,1,0:T(8,128)(2,1)}, bf16[256,256]{1,0:T(8,128)(2,1)}) custom-call(bf16[4,256,256]{2,1,0:T(8,128)(2,1)S(1)} %shard_map.122.refs_0_.refs_2_, s32[3]{0:T(128)S(1)} %pad_add_fusion.place.refs_1_.refs_3_, bf16[4,256,256]{2,1,0:T(8,128)(2,1)S(1)} %shard_map.122.refs_0_.refs_2_, ...), custom_call_target="tpu_custom_call" | custom-call | bytes 20000 | tf_op jit(solution)/shard_map/pallas_call | solution.py:49
  91.1 4.6 %shard_map.124.refs_0_.refs_1_ = f32[2,256,512]{2,1,0:T(8,128)S(1)} custom-call(bf16[256,256]{1,0:T(8,128)(2,1)} %get-tuple-element.68.refs_0_, f32[2,256,512]{2,1,0:T(8,128)S(1)} %shard_map.121.refs_0_.refs_1_), custom_call_target="tpu_custom_call" | custom-call | bytes 20000 | tf_op jit(solution)/shard_map/pallas_call | solution.py:49
  95.6 2.5 %collective-permute-done.20.refs_1_.refs_4_ = bf16[8,128,128]{2,1,0:T(8,128)(2,1)S(1)} collective-permute-done((bf16[8,128,128]{2,1,0:T(8,128)(2,1)}, bf16[8,128,128]{2,1,0:T(8,128)(2,1)S(1)}, u32[]{:S(2)}, u32[]{:S(2)}) %collective-permute-start.20) | collective-permute-done | bytes 262176 | tf_op jit(solution)/shard_map/ppermute | solution.py:66
  100.4 1.5 %collective-permute-start.24 = (bf16[8,128,128]{2,1,0:T(8,128)(2,1)}, bf16[8,128,128]{2,1,0:T(8,128)(2,1)}, u32[]{:S(2)}, u32[]{:S(2)}) collective-permute-start(bf16[8,128,128]{2,1,0:T(8,128)(2,1)} %get-tuple-element.69.refs_3_), channel_id=1, source_target_pairs={{0,16},{8,24},{16,0},{24,8},{1,17},{9,25},{17,1},{25,9},{2,18},{10... | collective-permute-start | bytes 786440 | tf_op jit(solution)/shard_map/ppermute | solution.py:66
  103.0 3.4 %shard_map.126.refs_0_.refs_2_ = bf16[2,128,256]{2,1,0:T(8,128)(2,1)S(1)} custom-call(bf16[8,128,128]{2,1,0:T(8,128)(2,1)S(1)} %get-tuple-element.71.refs_0_, f32[2,256,512]{2,1,0:T(8,128)S(1)} %shard_map.124.refs_0_.refs_1_, bf16[2,128,256]{2,1,0:T(8,128)(2,1)S(1)} %get-tuple-element.58.refs_0_.refs_4_.refs_2_), custom_call_target="tpu_custom_call" | custom-call | bytes 20000 | tf_op jit(solution)/shard_map/pallas_call | solution.py:49
  108.7 2.0 %collective-permute-start.28 = (bf16[2,128,256]{2,1,0:T(8,128)(2,1)S(1)}, bf16[2,128,256]{2,1,0:T(8,128)(2,1)}, u32[]{:S(2)}, u32[]{:S(2)}) collective-permute-start(bf16[2,128,256]{2,1,0:T(8,128)(2,1)S(1)} %shard_map.126.refs_0_.refs_2_), channel_id=1, source_target_pairs={{0,24},{8,16},{16,8},{24,0},{1,25},{9,17},{17,9},{25,1},{2,26},{10... | collective-permute-start | bytes 393224 | tf_op jit(solution)/shard_map/ppermute | solution.py:66
  112.7 2.7 %shard_map.127 = (f32[4,256,256]{2,1,0:T(8,128)}, f32[4,256,256]{2,1,0:T(8,128)}, f32[8,128]{1,0:T(8,128)S(1)}) custom-call(bf16[2,128,256]{2,1,0:T(8,128)(2,1)S(1)} %shard_map.126.refs_0_.refs_2_, bf16[8,128,128]{2,1,0:T(8,128)(2,1)S(1)} %collective-permute-done.22.refs_1_.refs_6_, bf16[8,128,128]{2,1,0:T(8,128)(2,1)S(1)} %collective-permute-done.23.refs_2_.refs_10_, ...), custom_call_target="tpu_custom_call" | custom-call | bytes 20000 | tf_op jit(solution)/shard_map/pallas_call | solution.py:49
  115.4 2.8 %shard_map.128 = (bf16[8,128,1024]{2,1,0:T(8,128)(2,1)}, f32[8,128]{1,0:T(8,128)S(1)}) custom-call(f32[8,128]{1,0:T(8,128)S(1)} %get-tuple-element.73.refs_0_, s32[3]{0:T(128)S(1)} %pad_add_fusion.place.refs_1_.refs_3_, bf16[8,128,1024]{2,1,0:T(8,128)(2,1)S(1)} %copy-done.5, bf16[8,128,128]{2,1,0:T(8,128)(2,1)} %get-tuple-element.69.refs_3_, ...), custom_call_target="tpu_custom_call" | custom-call | bytes 20000 | tf_op jit(solution)/shard_map/pallas_call | solution.py:49
  118.6 2.0 %shard_map.129 = f32[8,128,256]{2,1,0:T(8,128)} custom-call(f32[8,128]{1,0:T(8,128)S(1)} %get-tuple-element.75.refs_0_, s32[3]{0:T(128)S(1)} %pad_add_fusion.place.refs_1_.refs_3_, bf16[2,128,256]{2,1,0:T(8,128)(2,1)S(1)} %shard_map.126.refs_0_.refs_2_, bf16[2,128,256]{2,1,0:T(8,128)(2,1)S(1)} %collective-permute-done.26.refs_3_, ...), custom_call_target="tpu_custom_call" | custom-call | bytes 20000 | tf_op jit(solution)/shard_map/pallas_call | solution.py:49
  (73 shorter events, 21.8 us)
Async XLA Ops:
  7.2 104.1 %all-gather.3.cloned.1.call-start = ((), (), s32[]{:S(2)}) async-start(), calls=%async_computation | async-start | bytes 1179648 | tf_op jit(solution)/shard_map/all_gather | solution.py:518
  12.3 4.6 %collective-permute-start = (bf16[4,2,256,256]{3,2,1,0:T(8,128)(2,1)S(1)}, bf16[4,2,256,256]{3,2,1,0:T(8,128)(2,1)S(1)}, u32[]{:S(2)}, u32[]{:S(2)}) collective-permute-start(bf16[4,2,256,256]{3,2,1,0:T(8,128)(2,1)S(1)} %get-tuple-element.43), channel_id=1, source_target_pairs={{0,1},{1,0},{2,3},{3,2},{4,5},{5,4},{6,7},{7,6},{8,9},{9,8},{10,11... | collective-permute-start | bytes 3145736 | tf_op jit(solution)/shard_map/ppermute | solution.py:66
  12.8 21.4 %collective-permute-start.3 = (bf16[2,10,128,128]{3,2,1,0:T(8,128)(2,1)S(1)}, bf16[2,10,128,128]{3,2,1,0:T(8,128)(2,1)S(1)}, u32[]{:S(2)}, u32[]{:S(2)}) collective-permute-start(bf16[2,10,128,128]{3,2,1,0:T(8,128)(2,1)S(1)} %get-tuple-element.50), channel_id=1, source_target_pairs={{0,8},{8,0},{16,24},{24,16},{1,9},{9,1},{17,25},{25,17},{2,10},{10... | collective-permute-start | bytes 1966088 | tf_op jit(solution)/shard_map/ppermute | solution.py:66
  15.4 18.8 %collective-permute-start.4 = (bf16[2,10,128,128]{3,2,1,0:T(8,128)(2,1)S(1)}, bf16[2,10,128,128]{3,2,1,0:T(8,128)(2,1)S(1)}, u32[]{:S(2)}, u32[]{:S(2)}) collective-permute-start(bf16[2,10,128,128]{3,2,1,0:T(8,128)(2,1)S(1)} %get-tuple-element.51), channel_id=1, source_target_pairs={{0,16},{8,24},{16,0},{24,8},{1,17},{9,25},{17,1},{25,9},{2,18},{10... | collective-permute-start | bytes 1966088 | tf_op jit(solution)/shard_map/ppermute | solution.py:66
  16.9 17.3 %copy-start.1 = (bf16[1,8,128,1024]{3,2,1,0:T(8,128)(2,1)S(1)}, bf16[1,8,128,1024]{3,2,1,0:T(8,128)(2,1)}, u32[]{:S(2)}) copy-start(bf16[1,8,128,1024]{3,2,1,0:T(8,128)(2,1)} %refs_2_.9) | copy-start | bytes 6291460
  17.6 13.7 %collective-permute-start.1 = (bf16[2,256,256]{2,1,0:T(8,128)(2,1)S(1)}, bf16[2,256,256]{2,1,0:T(8,128)(2,1)S(1)}, u32[]{:S(2)}, u32[]{:S(2)}) collective-permute-start(bf16[2,256,256]{2,1,0:T(8,128)(2,1)S(1)} %get-tuple-element.45), channel_id=1, source_target_pairs={{0,2},{1,3},{2,0},{3,1},{4,6},{5,7},{6,4},{7,5},{8,10},{9,11},{10,... | collective-permute-start | bytes 786440 | tf_op jit(solution)/shard_map/ppermute | solution.py:66
  19.2 14.4 %collective-permute-start.2 = (bf16[2,256,256]{2,1,0:T(8,128)(2,1)S(1)}, bf16[2,256,256]{2,1,0:T(8,128)(2,1)S(1)}, u32[]{:S(2)}, u32[]{:S(2)}) collective-permute-start(bf16[2,256,256]{2,1,0:T(8,128)(2,1)S(1)} %get-tuple-element.47), channel_id=1, source_target_pairs={{0,4},{1,5},{2,6},{3,7},{4,0},{5,1},{6,2},{7,3},{8,12},{9,13},{10,... | collective-permute-start | bytes 786440 | tf_op jit(solution)/shard_map/ppermute | solution.py:66
  35.1 10.2 %collective-permute-start.7 = (bf16[10,128,128]{2,1,0:T(8,128)(2,1)S(1)}, bf16[10,128,128]{2,1,0:T(8,128)(2,1)S(1)}, u32[]{:S(2)}, u32[]{:S(2)}) collective-permute-start(bf16[10,128,128]{2,1,0:T(8,128)(2,1)S(1)} %get-tuple-element.56), channel_id=1, source_target_pairs={{0,16},{8,24},{16,0},{24,8},{1,17},{9,25},{17,1},{25,9},{2,18},{10... | collective-permute-start | bytes 983048 | tf_op jit(solution)/shard_map/ppermute | solution.py:66
  36.5 8.8 %collective-permute-start.8 = (bf16[10,128,128]{2,1,0:T(8,128)(2,1)S(1)}, bf16[10,128,128]{2,1,0:T(8,128)(2,1)S(1)}, u32[]{:S(2)}, u32[]{:S(2)}) collective-permute-start(bf16[10,128,128]{2,1,0:T(8,128)(2,1)S(1)} %get-tuple-element.57), channel_id=1, source_target_pairs={{0,8},{8,0},{16,24},{24,16},{1,9},{9,1},{17,25},{25,17},{2,10},{10... | collective-permute-start | bytes 983048 | tf_op jit(solution)/shard_map/ppermute | solution.py:66
  38.0 7.3 %collective-permute-start.5 = (bf16[1,256,256]{2,1,0:T(8,128)(2,1)S(1)}, bf16[1,256,256]{2,1,0:T(8,128)(2,1)S(1)}, u32[]{:S(2)}, u32[]{:S(2)}) collective-permute-start(bf16[1,256,256]{2,1,0:T(8,128)(2,1)S(1)} %get-tuple-element.53), channel_id=1, source_target_pairs={{0,4},{1,5},{2,6},{3,7},{4,0},{5,1},{6,2},{7,3},{8,12},{9,13},{10,... | collective-permute-start | bytes 393224 | tf_op jit(solution)/shard_map/ppermute | solution.py:66
  38.4 7.0 %collective-permute-start.6 = (bf16[1,256,256]{2,1,0:T(8,128)(2,1)S(1)}, bf16[1,256,256]{2,1,0:T(8,128)(2,1)S(1)}, u32[]{:S(2)}, u32[]{:S(2)}) collective-permute-start(bf16[1,256,256]{2,1,0:T(8,128)(2,1)S(1)} %get-tuple-element.54), channel_id=1, source_target_pairs={{0,2},{1,3},{2,0},{3,1},{4,6},{5,7},{6,4},{7,5},{8,10},{9,11},{10,... | collective-permute-start | bytes 393224 | tf_op jit(solution)/shard_map/ppermute | solution.py:66
  45.4 23.7 %copy-start.11 = (s32[8]{0:T(128)S(1)}, s32[8]{0:T(128)}, u32[]{:S(2)}) copy-start(s32[8]{0:T(128)} %refs_3_.3) | copy-start | bytes 100
  47.1 2.0 %collective-permute-start.9 = (bf16[4,256,256]{2,1,0:T(8,128)(2,1)S(1)}, bf16[4,256,256]{2,1,0:T(8,128)(2,1)S(1)}, u32[]{:S(2)}, u32[]{:S(2)}) collective-permute-start(bf16[4,256,256]{2,1,0:T(8,128)(2,1)S(1)} %get-tuple-element.60), channel_id=1, source_target_pairs={{0,1},{1,0},{2,3},{3,2},{4,5},{5,4},{6,7},{7,6},{8,9},{9,8},{10,11... | collective-permute-start | bytes 1572872 | tf_op jit(solution)/shard_map/ppermute | solution.py:66
  49.7 19.3 %collective-permute-start.10 = (bf16[512,256]{1,0:T(8,128)(2,1)S(1)}, bf16[512,256]{1,0:T(8,128)(2,1)S(1)}, u32[]{:S(2)}, u32[]{:S(2)}) collective-permute-start(bf16[512,256]{1,0:T(8,128)(2,1)S(1)} %get-tuple-element.62), channel_id=1, source_target_pairs={{0,2},{1,3},{2,0},{3,1},{4,6},{5,7},{6,4},{7,5},{8,10},{9,11},{10,... | collective-permute-start | bytes 786440 | tf_op jit(solution)/shard_map/ppermute | solution.py:66
  50.5 9.5 %collective-permute-start.13 = (bf16[2,128,256]{2,1,0:T(8,128)(2,1)S(1)}, bf16[2,128,256]{2,1,0:T(8,128)(2,1)S(1)}, u32[]{:S(2)}, u32[]{:S(2)}) collective-permute-start(bf16[2,128,256]{2,1,0:T(8,128)(2,1)S(1)} %get-tuple-element.58.refs_0_.refs_4_.refs_2_), channel_id=1, source_target_pairs={{0,4},{1,5},{2,6},{3,7},{4,0},{5,1},{6,2},{7,3},{8,12},{9,13},{10,... | collective-permute-start | bytes 393224 | tf_op jit(solution)/shard_map/ppermute | solution.py:66
  52.5 16.6 %collective-permute-start.11 = (bf16[256,256]{1,0:T(8,128)(2,1)S(1)}, bf16[256,256]{1,0:T(8,128)(2,1)S(1)}, u32[]{:S(2)}, u32[]{:S(2)}) collective-permute-start(bf16[256,256]{1,0:T(8,128)(2,1)S(1)} %get-tuple-element.63), channel_id=1, source_target_pairs={{0,4},{1,5},{2,6},{3,7},{4,0},{5,1},{6,2},{7,3},{8,12},{9,13},{10,... | collective-permute-start | bytes 393224 | tf_op jit(solution)/shard_map/ppermute | solution.py:66
  53.4 15.6 %collective-permute-start.12 = (bf16[256,256]{1,0:T(8,128)(2,1)S(1)}, bf16[256,256]{1,0:T(8,128)(2,1)S(1)}, u32[]{:S(2)}, u32[]{:S(2)}) collective-permute-start(bf16[256,256]{1,0:T(8,128)(2,1)S(1)} %get-tuple-element.64), channel_id=1, source_target_pairs={{0,6},{1,7},{2,4},{3,5},{4,2},{5,3},{6,0},{7,1},{8,14},{9,15},{10,... | collective-permute-start | bytes 393224 | tf_op jit(solution)/shard_map/ppermute | solution.py:66
  60.0 9.9 %collective-permute-start.14 = (bf16[2,128,256]{2,1,0:T(8,128)(2,1)S(1)}, bf16[2,128,256]{2,1,0:T(8,128)(2,1)S(1)}, u32[]{:S(2)}, u32[]{:S(2)}) collective-permute-start(bf16[2,128,256]{2,1,0:T(8,128)(2,1)S(1)} %collective-permute-done.13.refs_3_), channel_id=1, source_target_pairs={{0,2},{1,3},{2,0},{3,1},{4,6},{5,7},{6,4},{7,5},{8,10},{9,11},{10,... | collective-permute-start | bytes 393224 | tf_op jit(solution)/shard_map/ppermute | solution.py:66
  70.4 4.9 %collective-permute-start.15 = (f32[2,256,256]{2,1,0:T(8,128)S(1)}, f32[2,256,256]{2,1,0:T(8,128)S(1)}, u32[]{:S(2)}, u32[]{:S(2)}) collective-permute-start(f32[2,256,256]{2,1,0:T(8,128)S(1)} %shard_map.119.refs_0_.refs_1_), channel_id=1, source_target_pairs={{0,1},{1,0},{2,3},{3,2},{4,5},{5,4},{6,7},{7,6},{8,9},{9,8},{10,11... | collective-permute-start | bytes 1572872 | tf_op jit(solution)/shard_map/ppermute | solution.py:66
  70.5 13.8 %collective-permute-start.16 = (bf16[256,256]{1,0:T(8,128)(2,1)S(1)}, bf16[256,256]{1,0:T(8,128)(2,1)S(1)}, u32[]{:S(2)}, u32[]{:S(2)}) collective-permute-start(bf16[256,256]{1,0:T(8,128)(2,1)S(1)} %get-tuple-element.66.refs_0_.refs_1_), channel_id=1, source_target_pairs={{0,2},{1,3},{2,0},{3,1},{4,6},{5,7},{6,4},{7,5},{8,10},{9,11},{10,... | collective-permute-start | bytes 393224 | tf_op jit(solution)/shard_map/ppermute | solution.py:66
  72.8 12.9 %collective-permute-start.17 = (bf16[256,256]{1,0:T(8,128)(2,1)S(1)}, bf16[256,256]{1,0:T(8,128)(2,1)S(1)}, u32[]{:S(2)}, u32[]{:S(2)}) collective-permute-start(bf16[256,256]{1,0:T(8,128)(2,1)S(1)} %get-tuple-element.66.refs_0_.refs_1_), channel_id=1, source_target_pairs={{0,4},{1,5},{2,6},{3,7},{4,0},{5,1},{6,2},{7,3},{8,12},{9,13},{10,... | collective-permute-start | bytes 393224 | tf_op jit(solution)/shard_map/ppermute | solution.py:66
  73.2 12.5 %collective-permute-start.18 = (bf16[256,256]{1,0:T(8,128)(2,1)S(1)}, bf16[256,256]{1,0:T(8,128)(2,1)S(1)}, u32[]{:S(2)}, u32[]{:S(2)}) collective-permute-start(bf16[256,256]{1,0:T(8,128)(2,1)S(1)} %get-tuple-element.66.refs_0_.refs_1_), channel_id=1, source_target_pairs={{0,6},{1,7},{2,4},{3,5},{4,2},{5,3},{6,0},{7,1},{8,14},{9,15},{10,... | collective-permute-start | bytes 393224 | tf_op jit(solution)/shard_map/ppermute | solution.py:66
  85.8 2.0 %collective-permute-start.19 = (bf16[4,256,256]{2,1,0:T(8,128)(2,1)S(1)}, bf16[4,256,256]{2,1,0:T(8,128)(2,1)S(1)}, u32[]{:S(2)}, u32[]{:S(2)}) collective-permute-start(bf16[4,256,256]{2,1,0:T(8,128)(2,1)S(1)} %shard_map.122.refs_0_.refs_2_), channel_id=1, source_target_pairs={{0,1},{1,0},{2,3},{3,2},{4,5},{5,4},{6,7},{7,6},{8,9},{9,8},{10,11... | collective-permute-start | bytes 1572872 | tf_op jit(solution)/shard_map/ppermute | solution.py:66
  89.5 8.6 %collective-permute-start.20 = (bf16[8,128,128]{2,1,0:T(8,128)(2,1)}, bf16[8,128,128]{2,1,0:T(8,128)(2,1)S(1)}, u32[]{:S(2)}, u32[]{:S(2)}) collective-permute-start(bf16[8,128,128]{2,1,0:T(8,128)(2,1)} %get-tuple-element.69.refs_3_), channel_id=1, source_target_pairs={{0,8},{8,0},{16,24},{24,16},{1,9},{9,1},{17,25},{25,17},{2,10},{10... | collective-permute-start | bytes 786440 | tf_op jit(solution)/shard_map/ppermute | solution.py:66
  90.5 8.3 %collective-permute-start.21 = (bf16[8,128,128]{2,1,0:T(8,128)(2,1)}, bf16[8,128,128]{2,1,0:T(8,128)(2,1)S(1)}, u32[]{:S(2)}, u32[]{:S(2)}) collective-permute-start(bf16[8,128,128]{2,1,0:T(8,128)(2,1)} %get-tuple-element.70.refs_7_), channel_id=1, source_target_pairs={{0,16},{8,24},{16,0},{24,8},{1,17},{9,25},{17,1},{25,9},{2,18},{10... | collective-permute-start | bytes 786440 | tf_op jit(solution)/shard_map/ppermute | solution.py:66
  98.8 9.3 %collective-permute-start.22 = (bf16[8,128,128]{2,1,0:T(8,128)(2,1)S(1)}, bf16[8,128,128]{2,1,0:T(8,128)(2,1)S(1)}, u32[]{:S(2)}, u32[]{:S(2)}) collective-permute-start(bf16[8,128,128]{2,1,0:T(8,128)(2,1)S(1)} %get-tuple-element.71.refs_0_), channel_id=1, source_target_pairs={{0,16},{8,24},{16,0},{24,8},{1,17},{9,25},{17,1},{25,9},{2,18},{10... | collective-permute-start | bytes 786440 | tf_op jit(solution)/shard_map/ppermute | solution.py:66
  99.4 9.2 %collective-permute-start.23 = (bf16[8,128,128]{2,1,0:T(8,128)(2,1)S(1)}, bf16[8,128,128]{2,1,0:T(8,128)(2,1)S(1)}, u32[]{:S(2)}, u32[]{:S(2)}) collective-permute-start(bf16[8,128,128]{2,1,0:T(8,128)(2,1)S(1)} %get-tuple-element.72), channel_id=1, source_target_pairs={{0,8},{8,0},{16,24},{24,16},{1,9},{9,1},{17,25},{25,17},{2,10},{10... | collective-permute-start | bytes 786440 | tf_op jit(solution)/shard_map/ppermute | solution.py:66
  100.4 15.0 %collective-permute-start.24 = (bf16[8,128,128]{2,1,0:T(8,128)(2,1)}, bf16[8,128,128]{2,1,0:T(8,128)(2,1)}, u32[]{:S(2)}, u32[]{:S(2)}) collective-permute-start(bf16[8,128,128]{2,1,0:T(8,128)(2,1)} %get-tuple-element.69.refs_3_), channel_id=1, source_target_pairs={{0,16},{8,24},{16,0},{24,8},{1,17},{9,25},{17,1},{25,9},{2,18},{10... | collective-permute-start | bytes 786440 | tf_op jit(solution)/shard_map/ppermute | solution.py:66
  102.0 13.4 %collective-permute-start.25 = (bf16[8,128,128]{2,1,0:T(8,128)(2,1)}, bf16[8,128,128]{2,1,0:T(8,128)(2,1)}, u32[]{:S(2)}, u32[]{:S(2)}) collective-permute-start(bf16[8,128,128]{2,1,0:T(8,128)(2,1)} %get-tuple-element.70.refs_7_), channel_id=1, source_target_pairs={{0,8},{8,0},{16,24},{24,16},{1,9},{9,1},{17,25},{25,17},{2,10},{10... | collective-permute-start | bytes 786440 | tf_op jit(solution)/shard_map/ppermute | solution.py:66
  106.4 11.9 %collective-permute-start.26 = (bf16[2,128,256]{2,1,0:T(8,128)(2,1)S(1)}, bf16[2,128,256]{2,1,0:T(8,128)(2,1)S(1)}, u32[]{:S(2)}, u32[]{:S(2)}) collective-permute-start(bf16[2,128,256]{2,1,0:T(8,128)(2,1)S(1)} %shard_map.126.refs_0_.refs_2_), channel_id=1, source_target_pairs={{0,8},{8,0},{16,24},{24,16},{1,9},{9,1},{17,25},{25,17},{2,10},{10... | collective-permute-start | bytes 393224 | tf_op jit(solution)/shard_map/ppermute | solution.py:66
  108.2 10.1 %collective-permute-start.27 = (bf16[2,128,256]{2,1,0:T(8,128)(2,1)S(1)}, bf16[2,128,256]{2,1,0:T(8,128)(2,1)S(1)}, u32[]{:S(2)}, u32[]{:S(2)}) collective-permute-start(bf16[2,128,256]{2,1,0:T(8,128)(2,1)S(1)} %shard_map.126.refs_0_.refs_2_), channel_id=1, source_target_pairs={{0,16},{8,24},{16,0},{24,8},{1,17},{9,25},{17,1},{25,9},{2,18},{10... | collective-permute-start | bytes 393224 | tf_op jit(solution)/shard_map/ppermute | solution.py:66
  108.7 10.0 %collective-permute-start.28 = (bf16[2,128,256]{2,1,0:T(8,128)(2,1)S(1)}, bf16[2,128,256]{2,1,0:T(8,128)(2,1)}, u32[]{:S(2)}, u32[]{:S(2)}) collective-permute-start(bf16[2,128,256]{2,1,0:T(8,128)(2,1)S(1)} %shard_map.126.refs_0_.refs_2_), channel_id=1, source_target_pairs={{0,24},{8,16},{16,8},{24,0},{1,25},{9,17},{17,9},{25,1},{2,26},{10... | collective-permute-start | bytes 393224 | tf_op jit(solution)/shard_map/ppermute | solution.py:66
  (10 other events, 38.3 us)
Sparse Core Ops, SparseCore 0:
  89.6 21.6 all-gather.2

commit v12 on v11

--- a/solution.py
+++ b/solution.py
@@ -14,7 +14,7 @@
 step_size = 0.5
 epsilon = 1e-08
 BLOCK = 64
-GROUP = 4
+GROUP = 8
 COST = 10_000
 HIGHEST = lax.Precision.HIGHEST
 VMEM_LIMIT = 48 * 1024 * 1024

time: 128 us -> 128 us (level)
  waiting for transfers between devices: 37.5 us -> 39.7 us
  Pallas kernels: 34.3 us -> 32.1 us
    ppermute x29, waiting for transfers between devices: 36.8 us -> 39.1 us  [swap(): return lax.ppermute(x, axis, [(i, i ^ mask) for i in range(size)])]
    pallas_call x19, Pallas kernels: 34.3 us -> 32.1 us  [__call__(): pl.pallas_call(body, out_shape=out_shape, in_specs=specs, out_specs=out_s...]
  transfers between devices with their start and end apart: 30 -> 30, of which waited for: 13 -> 13; matrix products, arithmetic and copies ran while one was open for 0% -> 0% of each run, Pallas kernels for 19% -> 18%
where the time goes in v12:
time: 128 us; the launch traced here: 127 us
  waiting for transfers between devices  39.7 us (31%)
  starting transfers between devices  37.2 us (29%)
  Pallas kernels  32.1 us (25%)
  between operations  14.3 us (11%)
  local copies, waits for them, and re-layouts  4.05 us (3%)
    ppermute x29, waiting for transfers between devices, swap(): return lax.ppermute(x, axis, [(i, i ^ mask) for i in range(size)])  39.1 us
    ppermute x29, starting transfers between devices, swap(): return lax.ppermute(x, axis, [(i, i ^ mask) for i in range(size)])  37.2 us
    pallas_call x19, Pallas kernels, __call__(): pl.pallas_call(body, out_shape=out_shape, in_specs=specs, out_specs=out_s...  32.1 us
    unnamed x24, local copies, waits for them, and re-layouts  4.05 us
  transfers between devices with their start and end apart: 30, of which 13 were waited for; matrix products, arithmetic and copies ran while one was open for 0% of the time, Pallas kernels for 18%

profile of v12, /device:TPU:0, one launch (start us, length us, event | category | flops | bytes accessed | tf_op | source)
XLA Modules:
  0.0 127.4 jit_solution(6302693199105570161)
XLA Ops:
  7.3 1.6 %copy-done = bf16[1,8,128,1024]{3,2,1,0:T(8,128)(2,1)S(1)} copy-done((bf16[1,8,128,1024]{3,2,1,0:T(8,128)(2,1)S(1)}, bf16[1,8,128,1024]{3,2,1,0:T(8,128)(2,1)}, u32[]{:S(2)}) %copy-start) | copy-done | bytes 2097176
  10.0 1.5 %shard_map.111 = (f32[2,128,256]{2,1,0:T(8,128)S(1)}, f32[2,2,128,128]{3,2,1,0:T(8,128)S(1)}, bf16[2,10,128,128]{3,2,1,0:T(8,128)(2,1)S(1)}, bf16[2,10,128,128]{3,2,1,0:T(8,128)(2,1)S(1)}) custom-call(s32[3]{0:T(128)S(1)} %pad_add_fusion.place.refs_1_.refs_3_, bf16[1,8,128,1024]{3,2,1,0:T(8,128)(2,1)S(1)} %copy-done, bf16[1024,256]{1,0:T(8,128)(2,1)S(1)} %copy-done.9), custom_call_target="tpu_custom_call" | custom-call | bytes 20000 | tf_op jit(solution)/shard_map/pallas_call | solution.py:49
  12.8 2.6 %collective-permute-start.3 = (bf16[2,10,128,128]{3,2,1,0:T(8,128)(2,1)S(1)}, bf16[2,10,128,128]{3,2,1,0:T(8,128)(2,1)S(1)}, u32[]{:S(2)}, u32[]{:S(2)}) collective-permute-start(bf16[2,10,128,128]{3,2,1,0:T(8,128)(2,1)S(1)} %get-tuple-element.50), channel_id=1, source_target_pairs={{0,8},{8,0},{16,24},{24,16},{1,9},{9,1},{17,25},{25,17},{2,10},{10... | collective-permute-start | bytes 1966088 | tf_op jit(solution)/shard_map/ppermute | solution.py:66
  15.4 1.5 %collective-permute-start.4 = (bf16[2,10,128,128]{3,2,1,0:T(8,128)(2,1)S(1)}, bf16[2,10,128,128]{3,2,1,0:T(8,128)(2,1)S(1)}, u32[]{:S(2)}, u32[]{:S(2)}) collective-permute-start(bf16[2,10,128,128]{3,2,1,0:T(8,128)(2,1)S(1)} %get-tuple-element.51), channel_id=1, source_target_pairs={{0,16},{8,24},{16,0},{24,8},{1,17},{9,25},{17,1},{25,9},{2,18},{10... | collective-permute-start | bytes 1966088 | tf_op jit(solution)/shard_map/ppermute | solution.py:66
  17.6 1.6 %collective-permute-start.1 = (bf16[2,256,256]{2,1,0:T(8,128)(2,1)S(1)}, bf16[2,256,256]{2,1,0:T(8,128)(2,1)S(1)}, u32[]{:S(2)}, u32[]{:S(2)}) collective-permute-start(bf16[2,256,256]{2,1,0:T(8,128)(2,1)S(1)} %get-tuple-element.45), channel_id=1, source_target_pairs={{0,2},{1,3},{2,0},{3,1},{4,6},{5,7},{6,4},{7,5},{8,10},{9,11},{10,... | collective-permute-start | bytes 786440 | tf_op jit(solution)/shard_map/ppermute | solution.py:66
  19.2 2.6 %collective-permute-start.2 = (bf16[2,256,256]{2,1,0:T(8,128)(2,1)S(1)}, bf16[2,256,256]{2,1,0:T(8,128)(2,1)S(1)}, u32[]{:S(2)}, u32[]{:S(2)}) collective-permute-start(bf16[2,256,256]{2,1,0:T(8,128)(2,1)S(1)} %get-tuple-element.47), channel_id=1, source_target_pairs={{0,4},{1,5},{2,6},{3,7},{4,0},{5,1},{6,2},{7,3},{8,12},{9,13},{10,... | collective-permute-start | bytes 786440 | tf_op jit(solution)/shard_map/ppermute | solution.py:66
  21.8 9.4 %collective-permute-done.1.refs_4_ = bf16[2,256,256]{2,1,0:T(8,128)(2,1)S(1)} collective-permute-done((bf16[2,256,256]{2,1,0:T(8,128)(2,1)S(1)}, bf16[2,256,256]{2,1,0:T(8,128)(2,1)S(1)}, u32[]{:S(2)}, u32[]{:S(2)}) %collective-permute-start.1) | collective-permute-done | bytes 262176 | tf_op jit(solution)/shard_map/ppermute | solution.py:66
  31.3 2.3 %collective-permute-done.2.refs_6_ = bf16[2,256,256]{2,1,0:T(8,128)(2,1)S(1)} collective-permute-done((bf16[2,256,256]{2,1,0:T(8,128)(2,1)S(1)}, bf16[2,256,256]{2,1,0:T(8,128)(2,1)S(1)}, u32[]{:S(2)}, u32[]{:S(2)}) %collective-permute-start.2) | collective-permute-done | bytes 262176 | tf_op jit(solution)/shard_map/ppermute | solution.py:66
  38.4 2.7 %collective-permute-start.6 = (bf16[1,256,256]{2,1,0:T(8,128)(2,1)S(1)}, bf16[1,256,256]{2,1,0:T(8,128)(2,1)S(1)}, u32[]{:S(2)}, u32[]{:S(2)}) collective-permute-start(bf16[1,256,256]{2,1,0:T(8,128)(2,1)S(1)} %get-tuple-element.54), channel_id=1, source_target_pairs={{0,2},{1,3},{2,0},{3,1},{4,6},{5,7},{6,4},{7,5},{8,10},{9,11},{10,... | collective-permute-start | bytes 393224 | tf_op jit(solution)/shard_map/ppermute | solution.py:66
  41.1 4.3 %collective-permute-done.5.refs_1_.refs_9_ = bf16[1,256,256]{2,1,0:T(8,128)(2,1)S(1)} collective-permute-done((bf16[1,256,256]{2,1,0:T(8,128)(2,1)S(1)}, bf16[1,256,256]{2,1,0:T(8,128)(2,1)S(1)}, u32[]{:S(2)}, u32[]{:S(2)}) %collective-permute-start.5) | collective-permute-done | bytes 131104 | tf_op jit(solution)/shard_map/ppermute | solution.py:66
  45.4 1.7 %shard_map.116 = (f32[4,256,256]{2,1,0:T(8,128)S(1)}, bf16[2,128,256]{2,1,0:T(8,128)(2,1)S(1)}, bf16[4,256,256]{2,1,0:T(8,128)(2,1)S(1)}) custom-call(f32[8,128,128]{2,1,0:T(8,128)S(1)} %get-tuple-element.52.refs_0_.refs_4_, bf16[1,256,256]{2,1,0:T(8,128)(2,1)S(1)} %collective-permute-done.5.refs_1_.refs_9_, ...), custom_call_target="tpu_custom_call" | custom-call | bytes 20000 | tf_op jit(solution)/shard_map/pallas_call | solution.py:49
  47.2 1.9 %collective-permute-done.9.refs_3_ = bf16[4,256,256]{2,1,0:T(8,128)(2,1)S(1)} collective-permute-done((bf16[4,256,256]{2,1,0:T(8,128)(2,1)S(1)}, bf16[4,256,256]{2,1,0:T(8,128)(2,1)S(1)}, u32[]{:S(2)}, u32[]{:S(2)}) %collective-permute-start.9) | collective-permute-done | bytes 524320 | tf_op jit(solution)/shard_map/ppermute | solution.py:66
  50.5 2.0 %collective-permute-start.13 = (bf16[2,128,256]{2,1,0:T(8,128)(2,1)S(1)}, bf16[2,128,256]{2,1,0:T(8,128)(2,1)S(1)}, u32[]{:S(2)}, u32[]{:S(2)}) collective-permute-start(bf16[2,128,256]{2,1,0:T(8,128)(2,1)S(1)} %get-tuple-element.58.refs_0_.refs_4_.refs_2_), channel_id=1, source_target_pairs={{0,4},{1,5},{2,6},{3,7},{4,0},{5,1},{6,2},{7,3},{8,12},{9,13},{10,... | collective-permute-start | bytes 393224 | tf_op jit(solution)/shard_map/ppermute | solution.py:66
  53.4 1.7 %collective-permute-start.12 = (bf16[256,256]{1,0:T(8,128)(2,1)S(1)}, bf16[256,256]{1,0:T(8,128)(2,1)S(1)}, u32[]{:S(2)}, u32[]{:S(2)}) collective-permute-start(bf16[256,256]{1,0:T(8,128)(2,1)S(1)} %get-tuple-element.64), channel_id=1, source_target_pairs={{0,6},{1,7},{2,4},{3,5},{4,2},{5,3},{6,0},{7,1},{8,14},{9,15},{10,... | collective-permute-start | bytes 393224 | tf_op jit(solution)/shard_map/ppermute | solution.py:66
  55.1 4.9 %collective-permute-done.13.refs_3_ = bf16[2,128,256]{2,1,0:T(8,128)(2,1)S(1)} collective-permute-done((bf16[2,128,256]{2,1,0:T(8,128)(2,1)S(1)}, bf16[2,128,256]{2,1,0:T(8,128)(2,1)S(1)}, u32[]{:S(2)}, u32[]{:S(2)}) %collective-permute-start.13) | collective-permute-done | bytes 131104 | tf_op jit(solution)/shard_map/ppermute | solution.py:66
  60.0 2.8 %collective-permute-start.14 = (bf16[2,128,256]{2,1,0:T(8,128)(2,1)S(1)}, bf16[2,128,256]{2,1,0:T(8,128)(2,1)S(1)}, u32[]{:S(2)}, u32[]{:S(2)}) collective-permute-start(bf16[2,128,256]{2,1,0:T(8,128)(2,1)S(1)} %collective-permute-done.13.refs_3_), channel_id=1, source_target_pairs={{0,2},{1,3},{2,0},{3,1},{4,6},{5,7},{6,4},{7,5},{8,10},{9,11},{10,... | collective-permute-start | bytes 393224 | tf_op jit(solution)/shard_map/ppermute | solution.py:66
  62.8 6.3 %collective-permute-done.11.refs_6_ = bf16[256,256]{1,0:T(8,128)(2,1)S(1)} collective-permute-done((bf16[256,256]{1,0:T(8,128)(2,1)S(1)}, bf16[256,256]{1,0:T(8,128)(2,1)S(1)}, u32[]{:S(2)}, u32[]{:S(2)}) %collective-permute-start.11) | collective-permute-done | bytes 131104 | tf_op jit(solution)/shard_map/ppermute | solution.py:66
  70.5 2.4 %collective-permute-start.16 = (bf16[256,256]{1,0:T(8,128)(2,1)S(1)}, bf16[256,256]{1,0:T(8,128)(2,1)S(1)}, u32[]{:S(2)}, u32[]{:S(2)}) collective-permute-start(bf16[256,256]{1,0:T(8,128)(2,1)S(1)} %get-tuple-element.66.refs_0_.refs_1_), channel_id=1, source_target_pairs={{0,2},{1,3},{2,0},{3,1},{4,6},{5,7},{6,4},{7,5},{8,10},{9,11},{10,... | collective-permute-start | bytes 393224 | tf_op jit(solution)/shard_map/ppermute | solution.py:66
  73.2 2.1 %collective-permute-start.18 = (bf16[256,256]{1,0:T(8,128)(2,1)S(1)}, bf16[256,256]{1,0:T(8,128)(2,1)S(1)}, u32[]{:S(2)}, u32[]{:S(2)}) collective-permute-start(bf16[256,256]{1,0:T(8,128)(2,1)S(1)} %get-tuple-element.66.refs_0_.refs_1_), channel_id=1, source_target_pairs={{0,6},{1,7},{2,4},{3,5},{4,2},{5,3},{6,0},{7,1},{8,14},{9,15},{10,... | collective-permute-start | bytes 393224 | tf_op jit(solution)/shard_map/ppermute | solution.py:66
  75.3 3.8 %shard_map.120.refs_0_.refs_1_ = f32[2,256,512]{2,1,0:T(8,128)S(1)} custom-call(f32[2,256,256]{2,1,0:T(8,128)S(1)} %shard_map.119.refs_0_.refs_1_, f32[2,256,256]{2,1,0:T(8,128)S(1)} %shard_map.119.refs_0_.refs_1_, f32[2,256,256]{2,1,0:T(8,128)S(1)} %collective-permute-done.15.refs_2_), custom_call_target="tpu_custom_call" | custom-call | bytes 20000 | tf_op jit(solution)/shard_map/pallas_call | solution.py:49
  79.1 3.9 %shard_map.121.refs_0_.refs_1_ = f32[2,256,512]{2,1,0:T(8,128)S(1)} custom-call(f32[2,256,512]{2,1,0:T(8,128)S(1)} %shard_map.120.refs_0_.refs_1_, f32[2,256,512]{2,1,0:T(8,128)S(1)} %shard_map.120.refs_0_.refs_1_), custom_call_target="tpu_custom_call" | custom-call | bytes 20000 | tf_op jit(solution)/shard_map/pallas_call | solution.py:49
  83.1 2.7 %collective-permute-done.17.refs_3_ = bf16[256,256]{1,0:T(8,128)(2,1)S(1)} collective-permute-done((bf16[256,256]{1,0:T(8,128)(2,1)S(1)}, bf16[256,256]{1,0:T(8,128)(2,1)S(1)}, u32[]{:S(2)}, u32[]{:S(2)}) %collective-permute-start.17) | collective-permute-done | bytes 131104 | tf_op jit(solution)/shard_map/ppermute | solution.py:66
  85.9 1.9 %collective-permute-done.19.refs_3_ = bf16[4,256,256]{2,1,0:T(8,128)(2,1)S(1)} collective-permute-done((bf16[4,256,256]{2,1,0:T(8,128)(2,1)S(1)}, bf16[4,256,256]{2,1,0:T(8,128)(2,1)S(1)}, u32[]{:S(2)}, u32[]{:S(2)}) %collective-permute-start.19) | collective-permute-done | bytes 524320 | tf_op jit(solution)/shard_map/ppermute | solution.py:66
  87.8 1.7 %shard_map.123 = (bf16[8,128,128]{2,1,0:T(8,128)(2,1)}, bf16[8,128,128]{2,1,0:T(8,128)(2,1)}, bf16[256,256]{1,0:T(8,128)(2,1)}) custom-call(bf16[4,256,256]{2,1,0:T(8,128)(2,1)S(1)} %shard_map.122.refs_0_.refs_2_, s32[3]{0:T(128)S(1)} %pad_add_fusion.place.refs_1_.refs_3_, bf16[4,256,256]{2,1,0:T(8,128)(2,1)S(1)} %shard_map.122.refs_0_.refs_2_, ...), custom_call_target="tpu_custom_call" | custom-call | bytes 20000 | tf_op jit(solution)/shard_map/pallas_call | solution.py:49
  91.1 4.0 %shard_map.124.refs_0_.refs_1_ = f32[2,256,512]{2,1,0:T(8,128)S(1)} custom-call(bf16[256,256]{1,0:T(8,128)(2,1)} %get-tuple-element.68.refs_0_, f32[2,256,512]{2,1,0:T(8,128)S(1)} %shard_map.121.refs_0_.refs_1_), custom_call_target="tpu_custom_call" | custom-call | bytes 20000 | tf_op jit(solution)/shard_map/pallas_call | solution.py:49
  95.1 3.0 %collective-permute-done.20.refs_1_.refs_4_ = bf16[8,128,128]{2,1,0:T(8,128)(2,1)S(1)} collective-permute-done((bf16[8,128,128]{2,1,0:T(8,128)(2,1)}, bf16[8,128,128]{2,1,0:T(8,128)(2,1)S(1)}, u32[]{:S(2)}, u32[]{:S(2)}) %collective-permute-start.20) | collective-permute-done | bytes 262176 | tf_op jit(solution)/shard_map/ppermute | solution.py:66
  100.4 1.5 %collective-permute-start.24 = (bf16[8,128,128]{2,1,0:T(8,128)(2,1)}, bf16[8,128,128]{2,1,0:T(8,128)(2,1)}, u32[]{:S(2)}, u32[]{:S(2)}) collective-permute-start(bf16[8,128,128]{2,1,0:T(8,128)(2,1)} %get-tuple-element.69.refs_3_), channel_id=1, source_target_pairs={{0,16},{8,24},{16,0},{24,8},{1,17},{9,25},{17,1},{25,9},{2,18},{10... | collective-permute-start | bytes 786440 | tf_op jit(solution)/shard_map/ppermute | solution.py:66
  103.0 2.9 %shard_map.126.refs_0_.refs_2_ = bf16[2,128,256]{2,1,0:T(8,128)(2,1)S(1)} custom-call(bf16[8,128,128]{2,1,0:T(8,128)(2,1)S(1)} %get-tuple-element.71.refs_0_, f32[2,256,512]{2,1,0:T(8,128)S(1)} %shard_map.124.refs_0_.refs_1_, bf16[2,128,256]{2,1,0:T(8,128)(2,1)S(1)} %get-tuple-element.58.refs_0_.refs_4_.refs_2_), custom_call_target="tpu_custom_call" | custom-call | bytes 20000 | tf_op jit(solution)/shard_map/pallas_call | solution.py:49
  108.7 2.0 %collective-permute-start.28 = (bf16[2,128,256]{2,1,0:T(8,128)(2,1)S(1)}, bf16[2,128,256]{2,1,0:T(8,128)(2,1)}, u32[]{:S(2)}, u32[]{:S(2)}) collective-permute-start(bf16[2,128,256]{2,1,0:T(8,128)(2,1)S(1)} %shard_map.126.refs_0_.refs_2_), channel_id=1, source_target_pairs={{0,24},{8,16},{16,8},{24,0},{1,25},{9,17},{17,9},{25,1},{2,26},{10... | collective-permute-start | bytes 393224 | tf_op jit(solution)/shard_map/ppermute | solution.py:66
  112.6 2.7 %shard_map.127 = (f32[4,256,256]{2,1,0:T(8,128)}, f32[4,256,256]{2,1,0:T(8,128)}, f32[8,128]{1,0:T(8,128)S(1)}) custom-call(bf16[2,128,256]{2,1,0:T(8,128)(2,1)S(1)} %shard_map.126.refs_0_.refs_2_, bf16[8,128,128]{2,1,0:T(8,128)(2,1)S(1)} %collective-permute-done.22.refs_1_.refs_6_, bf16[8,128,128]{2,1,0:T(8,128)(2,1)S(1)} %collective-permute-done.23.refs_2_.refs_10_, ...), custom_call_target="tpu_custom_call" | custom-call | bytes 20000 | tf_op jit(solution)/shard_map/pallas_call | solution.py:49
  115.4 2.8 %shard_map.128 = (bf16[8,128,1024]{2,1,0:T(8,128)(2,1)}, f32[8,128]{1,0:T(8,128)S(1)}) custom-call(f32[8,128]{1,0:T(8,128)S(1)} %get-tuple-element.73.refs_0_, s32[3]{0:T(128)S(1)} %pad_add_fusion.place.refs_1_.refs_3_, bf16[8,128,1024]{2,1,0:T(8,128)(2,1)S(1)} %copy-done.5, bf16[8,128,128]{2,1,0:T(8,128)(2,1)} %get-tuple-element.69.refs_3_, ...), custom_call_target="tpu_custom_call" | custom-call | bytes 20000 | tf_op jit(solution)/shard_map/pallas_call | solution.py:49
  118.6 2.0 %shard_map.129 = f32[8,128,256]{2,1,0:T(8,128)} custom-call(f32[8,128]{1,0:T(8,128)S(1)} %get-tuple-element.75.refs_0_, s32[3]{0:T(128)S(1)} %pad_add_fusion.place.refs_1_.refs_3_, bf16[2,128,256]{2,1,0:T(8,128)(2,1)S(1)} %shard_map.126.refs_0_.refs_2_, bf16[2,128,256]{2,1,0:T(8,128)(2,1)S(1)} %collective-permute-done.26.refs_3_, ...), custom_call_target="tpu_custom_call" | custom-call | bytes 20000 | tf_op jit(solution)/shard_map/pallas_call | solution.py:49
  (73 shorter events, 22.3 us)
Async XLA Ops:
  7.2 104.1 %all-gather.3.cloned.1.call-start = ((), (), s32[]{:S(2)}) async-start(), calls=%async_computation | async-start | bytes 1179648 | tf_op jit(solution)/shard_map/all_gather | solution.py:518
  12.3 4.6 %collective-permute-start = (bf16[4,2,256,256]{3,2,1,0:T(8,128)(2,1)S(1)}, bf16[4,2,256,256]{3,2,1,0:T(8,128)(2,1)S(1)}, u32[]{:S(2)}, u32[]{:S(2)}) collective-permute-start(bf16[4,2,256,256]{3,2,1,0:T(8,128)(2,1)S(1)} %get-tuple-element.43), channel_id=1, source_target_pairs={{0,1},{1,0},{2,3},{3,2},{4,5},{5,4},{6,7},{7,6},{8,9},{9,8},{10,11... | collective-permute-start | bytes 3145736 | tf_op jit(solution)/shard_map/ppermute | solution.py:66
  12.8 21.4 %collective-permute-start.3 = (bf16[2,10,128,128]{3,2,1,0:T(8,128)(2,1)S(1)}, bf16[2,10,128,128]{3,2,1,0:T(8,128)(2,1)S(1)}, u32[]{:S(2)}, u32[]{:S(2)}) collective-permute-start(bf16[2,10,128,128]{3,2,1,0:T(8,128)(2,1)S(1)} %get-tuple-element.50), channel_id=1, source_target_pairs={{0,8},{8,0},{16,24},{24,16},{1,9},{9,1},{17,25},{25,17},{2,10},{10... | collective-permute-start | bytes 1966088 | tf_op jit(solution)/shard_map/ppermute | solution.py:66
  15.4 18.8 %collective-permute-start.4 = (bf16[2,10,128,128]{3,2,1,0:T(8,128)(2,1)S(1)}, bf16[2,10,128,128]{3,2,1,0:T(8,128)(2,1)S(1)}, u32[]{:S(2)}, u32[]{:S(2)}) collective-permute-start(bf16[2,10,128,128]{3,2,1,0:T(8,128)(2,1)S(1)} %get-tuple-element.51), channel_id=1, source_target_pairs={{0,16},{8,24},{16,0},{24,8},{1,17},{9,25},{17,1},{25,9},{2,18},{10... | collective-permute-start | bytes 1966088 | tf_op jit(solution)/shard_map/ppermute | solution.py:66
  16.9 17.3 %copy-start.1 = (bf16[1,8,128,1024]{3,2,1,0:T(8,128)(2,1)S(1)}, bf16[1,8,128,1024]{3,2,1,0:T(8,128)(2,1)}, u32[]{:S(2)}) copy-start(bf16[1,8,128,1024]{3,2,1,0:T(8,128)(2,1)} %refs_2_.9) | copy-start | bytes 6291460
  17.6 13.7 %collective-permute-start.1 = (bf16[2,256,256]{2,1,0:T(8,128)(2,1)S(1)}, bf16[2,256,256]{2,1,0:T(8,128)(2,1)S(1)}, u32[]{:S(2)}, u32[]{:S(2)}) collective-permute-start(bf16[2,256,256]{2,1,0:T(8,128)(2,1)S(1)} %get-tuple-element.45), channel_id=1, source_target_pairs={{0,2},{1,3},{2,0},{3,1},{4,6},{5,7},{6,4},{7,5},{8,10},{9,11},{10,... | collective-permute-start | bytes 786440 | tf_op jit(solution)/shard_map/ppermute | solution.py:66
  19.2 14.4 %collective-permute-start.2 = (bf16[2,256,256]{2,1,0:T(8,128)(2,1)S(1)}, bf16[2,256,256]{2,1,0:T(8,128)(2,1)S(1)}, u32[]{:S(2)}, u32[]{:S(2)}) collective-permute-start(bf16[2,256,256]{2,1,0:T(8,128)(2,1)S(1)} %get-tuple-element.47), channel_id=1, source_target_pairs={{0,4},{1,5},{2,6},{3,7},{4,0},{5,1},{6,2},{7,3},{8,12},{9,13},{10,... | collective-permute-start | bytes 786440 | tf_op jit(solution)/shard_map/ppermute | solution.py:66
  35.1 10.2 %collective-permute-start.7 = (bf16[10,128,128]{2,1,0:T(8,128)(2,1)S(1)}, bf16[10,128,128]{2,1,0:T(8,128)(2,1)S(1)}, u32[]{:S(2)}, u32[]{:S(2)}) collective-permute-start(bf16[10,128,128]{2,1,0:T(8,128)(2,1)S(1)} %get-tuple-element.56), channel_id=1, source_target_pairs={{0,16},{8,24},{16,0},{24,8},{1,17},{9,25},{17,1},{25,9},{2,18},{10... | collective-permute-start | bytes 983048 | tf_op jit(solution)/shard_map/ppermute | solution.py:66
  36.5 8.8 %collective-permute-start.8 = (bf16[10,128,128]{2,1,0:T(8,128)(2,1)S(1)}, bf16[10,128,128]{2,1,0:T(8,128)(2,1)S(1)}, u32[]{:S(2)}, u32[]{:S(2)}) collective-permute-start(bf16[10,128,128]{2,1,0:T(8,128)(2,1)S(1)} %get-tuple-element.57), channel_id=1, source_target_pairs={{0,8},{8,0},{16,24},{24,16},{1,9},{9,1},{17,25},{25,17},{2,10},{10... | collective-permute-start | bytes 983048 | tf_op jit(solution)/shard_map/ppermute | solution.py:66
  38.0 7.3 %collective-permute-start.5 = (bf16[1,256,256]{2,1,0:T(8,128)(2,1)S(1)}, bf16[1,256,256]{2,1,0:T(8,128)(2,1)S(1)}, u32[]{:S(2)}, u32[]{:S(2)}) collective-permute-start(bf16[1,256,256]{2,1,0:T(8,128)(2,1)S(1)} %get-tuple-element.53), channel_id=1, source_target_pairs={{0,4},{1,5},{2,6},{3,7},{4,0},{5,1},{6,2},{7,3},{8,12},{9,13},{10,... | collective-permute-start | bytes 393224 | tf_op jit(solution)/shard_map/ppermute | solution.py:66
  38.4 7.0 %collective-permute-start.6 = (bf16[1,256,256]{2,1,0:T(8,128)(2,1)S(1)}, bf16[1,256,256]{2,1,0:T(8,128)(2,1)S(1)}, u32[]{:S(2)}, u32[]{:S(2)}) collective-permute-start(bf16[1,256,256]{2,1,0:T(8,128)(2,1)S(1)} %get-tuple-element.54), channel_id=1, source_target_pairs={{0,2},{1,3},{2,0},{3,1},{4,6},{5,7},{6,4},{7,5},{8,10},{9,11},{10,... | collective-permute-start | bytes 393224 | tf_op jit(solution)/shard_map/ppermute | solution.py:66
  45.4 23.7 %copy-start.11 = (s32[8]{0:T(128)S(1)}, s32[8]{0:T(128)}, u32[]{:S(2)}) copy-start(s32[8]{0:T(128)} %refs_3_.3) | copy-start | bytes 100
  47.1 2.0 %collective-permute-start.9 = (bf16[4,256,256]{2,1,0:T(8,128)(2,1)S(1)}, bf16[4,256,256]{2,1,0:T(8,128)(2,1)S(1)}, u32[]{:S(2)}, u32[]{:S(2)}) collective-permute-start(bf16[4,256,256]{2,1,0:T(8,128)(2,1)S(1)} %get-tuple-element.60), channel_id=1, source_target_pairs={{0,1},{1,0},{2,3},{3,2},{4,5},{5,4},{6,7},{7,6},{8,9},{9,8},{10,11... | collective-permute-start | bytes 1572872 | tf_op jit(solution)/shard_map/ppermute | solution.py:66
  49.7 19.3 %collective-permute-start.10 = (bf16[512,256]{1,0:T(8,128)(2,1)S(1)}, bf16[512,256]{1,0:T(8,128)(2,1)S(1)}, u32[]{:S(2)}, u32[]{:S(2)}) collective-permute-start(bf16[512,256]{1,0:T(8,128)(2,1)S(1)} %get-tuple-element.62), channel_id=1, source_target_pairs={{0,2},{1,3},{2,0},{3,1},{4,6},{5,7},{6,4},{7,5},{8,10},{9,11},{10,... | collective-permute-start | bytes 786440 | tf_op jit(solution)/shard_map/ppermute | solution.py:66
  50.5 9.5 %collective-permute-start.13 = (bf16[2,128,256]{2,1,0:T(8,128)(2,1)S(1)}, bf16[2,128,256]{2,1,0:T(8,128)(2,1)S(1)}, u32[]{:S(2)}, u32[]{:S(2)}) collective-permute-start(bf16[2,128,256]{2,1,0:T(8,128)(2,1)S(1)} %get-tuple-element.58.refs_0_.refs_4_.refs_2_), channel_id=1, source_target_pairs={{0,4},{1,5},{2,6},{3,7},{4,0},{5,1},{6,2},{7,3},{8,12},{9,13},{10,... | collective-permute-start | bytes 393224 | tf_op jit(solution)/shard_map/ppermute | solution.py:66
  52.5 16.6 %collective-permute-start.11 = (bf16[256,256]{1,0:T(8,128)(2,1)S(1)}, bf16[256,256]{1,0:T(8,128)(2,1)S(1)}, u32[]{:S(2)}, u32[]{:S(2)}) collective-permute-start(bf16[256,256]{1,0:T(8,128)(2,1)S(1)} %get-tuple-element.63), channel_id=1, source_target_pairs={{0,4},{1,5},{2,6},{3,7},{4,0},{5,1},{6,2},{7,3},{8,12},{9,13},{10,... | collective-permute-start | bytes 393224 | tf_op jit(solution)/shard_map/ppermute | solution.py:66
  53.4 15.6 %collective-permute-start.12 = (bf16[256,256]{1,0:T(8,128)(2,1)S(1)}, bf16[256,256]{1,0:T(8,128)(2,1)S(1)}, u32[]{:S(2)}, u32[]{:S(2)}) collective-permute-start(bf16[256,256]{1,0:T(8,128)(2,1)S(1)} %get-tuple-element.64), channel_id=1, source_target_pairs={{0,6},{1,7},{2,4},{3,5},{4,2},{5,3},{6,0},{7,1},{8,14},{9,15},{10,... | collective-permute-start | bytes 393224 | tf_op jit(solution)/shard_map/ppermute | solution.py:66
  60.0 9.9 %collective-permute-start.14 = (bf16[2,128,256]{2,1,0:T(8,128)(2,1)S(1)}, bf16[2,128,256]{2,1,0:T(8,128)(2,1)S(1)}, u32[]{:S(2)}, u32[]{:S(2)}) collective-permute-start(bf16[2,128,256]{2,1,0:T(8,128)(2,1)S(1)} %collective-permute-done.13.refs_3_), channel_id=1, source_target_pairs={{0,2},{1,3},{2,0},{3,1},{4,6},{5,7},{6,4},{7,5},{8,10},{9,11},{10,... | collective-permute-start | bytes 393224 | tf_op jit(solution)/shard_map/ppermute | solution.py:66
  70.4 4.9 %collective-permute-start.15 = (f32[2,256,256]{2,1,0:T(8,128)S(1)}, f32[2,256,256]{2,1,0:T(8,128)S(1)}, u32[]{:S(2)}, u32[]{:S(2)}) collective-permute-start(f32[2,256,256]{2,1,0:T(8,128)S(1)} %shard_map.119.refs_0_.refs_1_), channel_id=1, source_target_pairs={{0,1},{1,0},{2,3},{3,2},{4,5},{5,4},{6,7},{7,6},{8,9},{9,8},{10,11... | collective-permute-start | bytes 1572872 | tf_op jit(solution)/shard_map/ppermute | solution.py:66
  70.5 12.6 %collective-permute-start.16 = (bf16[256,256]{1,0:T(8,128)(2,1)S(1)}, bf16[256,256]{1,0:T(8,128)(2,1)S(1)}, u32[]{:S(2)}, u32[]{:S(2)}) collective-permute-start(bf16[256,256]{1,0:T(8,128)(2,1)S(1)} %get-tuple-element.66.refs_0_.refs_1_), channel_id=1, source_target_pairs={{0,2},{1,3},{2,0},{3,1},{4,6},{5,7},{6,4},{7,5},{8,10},{9,11},{10,... | collective-permute-start | bytes 393224 | tf_op jit(solution)/shard_map/ppermute | solution.py:66
  72.8 12.9 %collective-permute-start.17 = (bf16[256,256]{1,0:T(8,128)(2,1)S(1)}, bf16[256,256]{1,0:T(8,128)(2,1)S(1)}, u32[]{:S(2)}, u32[]{:S(2)}) collective-permute-start(bf16[256,256]{1,0:T(8,128)(2,1)S(1)} %get-tuple-element.66.refs_0_.refs_1_), channel_id=1, source_target_pairs={{0,4},{1,5},{2,6},{3,7},{4,0},{5,1},{6,2},{7,3},{8,12},{9,13},{10,... | collective-permute-start | bytes 393224 | tf_op jit(solution)/shard_map/ppermute | solution.py:66
  73.2 12.5 %collective-permute-start.18 = (bf16[256,256]{1,0:T(8,128)(2,1)S(1)}, bf16[256,256]{1,0:T(8,128)(2,1)S(1)}, u32[]{:S(2)}, u32[]{:S(2)}) collective-permute-start(bf16[256,256]{1,0:T(8,128)(2,1)S(1)} %get-tuple-element.66.refs_0_.refs_1_), channel_id=1, source_target_pairs={{0,6},{1,7},{2,4},{3,5},{4,2},{5,3},{6,0},{7,1},{8,14},{9,15},{10,... | collective-permute-start | bytes 393224 | tf_op jit(solution)/shard_map/ppermute | solution.py:66
  85.8 2.0 %collective-permute-start.19 = (bf16[4,256,256]{2,1,0:T(8,128)(2,1)S(1)}, bf16[4,256,256]{2,1,0:T(8,128)(2,1)S(1)}, u32[]{:S(2)}, u32[]{:S(2)}) collective-permute-start(bf16[4,256,256]{2,1,0:T(8,128)(2,1)S(1)} %shard_map.122.refs_0_.refs_2_), channel_id=1, source_target_pairs={{0,1},{1,0},{2,3},{3,2},{4,5},{5,4},{6,7},{7,6},{8,9},{9,8},{10,11... | collective-permute-start | bytes 1572872 | tf_op jit(solution)/shard_map/ppermute | solution.py:66
  89.5 8.6 %collective-permute-start.20 = (bf16[8,128,128]{2,1,0:T(8,128)(2,1)}, bf16[8,128,128]{2,1,0:T(8,128)(2,1)S(1)}, u32[]{:S(2)}, u32[]{:S(2)}) collective-permute-start(bf16[8,128,128]{2,1,0:T(8,128)(2,1)} %get-tuple-element.69.refs_3_), channel_id=1, source_target_pairs={{0,8},{8,0},{16,24},{24,16},{1,9},{9,1},{17,25},{25,17},{2,10},{10... | collective-permute-start | bytes 786440 | tf_op jit(solution)/shard_map/ppermute | solution.py:66
  90.5 8.3 %collective-permute-start.21 = (bf16[8,128,128]{2,1,0:T(8,128)(2,1)}, bf16[8,128,128]{2,1,0:T(8,128)(2,1)S(1)}, u32[]{:S(2)}, u32[]{:S(2)}) collective-permute-start(bf16[8,128,128]{2,1,0:T(8,128)(2,1)} %get-tuple-element.70.refs_7_), channel_id=1, source_target_pairs={{0,16},{8,24},{16,0},{24,8},{1,17},{9,25},{17,1},{25,9},{2,18},{10... | collective-permute-start | bytes 786440 | tf_op jit(solution)/shard_map/ppermute | solution.py:66
  98.8 9.3 %collective-permute-start.22 = (bf16[8,128,128]{2,1,0:T(8,128)(2,1)S(1)}, bf16[8,128,128]{2,1,0:T(8,128)(2,1)S(1)}, u32[]{:S(2)}, u32[]{:S(2)}) collective-permute-start(bf16[8,128,128]{2,1,0:T(8,128)(2,1)S(1)} %get-tuple-element.71.refs_0_), channel_id=1, source_target_pairs={{0,16},{8,24},{16,0},{24,8},{1,17},{9,25},{17,1},{25,9},{2,18},{10... | collective-permute-start | bytes 786440 | tf_op jit(solution)/shard_map/ppermute | solution.py:66
  99.4 9.2 %collective-permute-start.23 = (bf16[8,128,128]{2,1,0:T(8,128)(2,1)S(1)}, bf16[8,128,128]{2,1,0:T(8,128)(2,1)S(1)}, u32[]{:S(2)}, u32[]{:S(2)}) collective-permute-start(bf16[8,128,128]{2,1,0:T(8,128)(2,1)S(1)} %get-tuple-element.72), channel_id=1, source_target_pairs={{0,8},{8,0},{16,24},{24,16},{1,9},{9,1},{17,25},{25,17},{2,10},{10... | collective-permute-start | bytes 786440 | tf_op jit(solution)/shard_map/ppermute | solution.py:66
  100.4 14.9 %collective-permute-start.24 = (bf16[8,128,128]{2,1,0:T(8,128)(2,1)}, bf16[8,128,128]{2,1,0:T(8,128)(2,1)}, u32[]{:S(2)}, u32[]{:S(2)}) collective-permute-start(bf16[8,128,128]{2,1,0:T(8,128)(2,1)} %get-tuple-element.69.refs_3_), channel_id=1, source_target_pairs={{0,16},{8,24},{16,0},{24,8},{1,17},{9,25},{17,1},{25,9},{2,18},{10... | collective-permute-start | bytes 786440 | tf_op jit(solution)/shard_map/ppermute | solution.py:66
  102.0 13.4 %collective-permute-start.25 = (bf16[8,128,128]{2,1,0:T(8,128)(2,1)}, bf16[8,128,128]{2,1,0:T(8,128)(2,1)}, u32[]{:S(2)}, u32[]{:S(2)}) collective-permute-start(bf16[8,128,128]{2,1,0:T(8,128)(2,1)} %get-tuple-element.70.refs_7_), channel_id=1, source_target_pairs={{0,8},{8,0},{16,24},{24,16},{1,9},{9,1},{17,25},{25,17},{2,10},{10... | collective-permute-start | bytes 786440 | tf_op jit(solution)/shard_map/ppermute | solution.py:66
  105.9 12.3 %collective-permute-start.26 = (bf16[2,128,256]{2,1,0:T(8,128)(2,1)S(1)}, bf16[2,128,256]{2,1,0:T(8,128)(2,1)S(1)}, u32[]{:S(2)}, u32[]{:S(2)}) collective-permute-start(bf16[2,128,256]{2,1,0:T(8,128)(2,1)S(1)} %shard_map.126.refs_0_.refs_2_), channel_id=1, source_target_pairs={{0,8},{8,0},{16,24},{24,16},{1,9},{9,1},{17,25},{25,17},{2,10},{10... | collective-permute-start | bytes 393224 | tf_op jit(solution)/shard_map/ppermute | solution.py:66
  108.2 10.1 %collective-permute-start.27 = (bf16[2,128,256]{2,1,0:T(8,128)(2,1)S(1)}, bf16[2,128,256]{2,1,0:T(8,128)(2,1)S(1)}, u32[]{:S(2)}, u32[]{:S(2)}) collective-permute-start(bf16[2,128,256]{2,1,0:T(8,128)(2,1)S(1)} %shard_map.126.refs_0_.refs_2_), channel_id=1, source_target_pairs={{0,16},{8,24},{16,0},{24,8},{1,17},{9,25},{17,1},{25,9},{2,18},{10... | collective-permute-start | bytes 393224 | tf_op jit(solution)/shard_map/ppermute | solution.py:66
  108.7 10.0 %collective-permute-start.28 = (bf16[2,128,256]{2,1,0:T(8,128)(2,1)S(1)}, bf16[2,128,256]{2,1,0:T(8,128)(2,1)}, u32[]{:S(2)}, u32[]{:S(2)}) collective-permute-start(bf16[2,128,256]{2,1,0:T(8,128)(2,1)S(1)} %shard_map.126.refs_0_.refs_2_), channel_id=1, source_target_pairs={{0,24},{8,16},{16,8},{24,0},{1,25},{9,17},{17,9},{25,1},{2,26},{10... | collective-permute-start | bytes 393224 | tf_op jit(solution)/shard_map/ppermute | solution.py:66
  (10 other events, 38.8 us)
Sparse Core Ops, SparseCore 0:
  89.6 21.6 all-gather.2
